TPU v7x, 32 devices: a whole 2x2x4 slice. The times are simulated.
32 devices in a mesh: gx: 8 (over z, x), gy: 2 (over y), gz: 2 (over core).
Axes of the slice: x: 2, y: 2, z: 4, core: 2. Of those that a mesh axis runs over, the one named last changes fastest.
Arguments:
- source: float32 [256, 64, 1024], P('gx', 'gz', 'gy'), may hold values from -24 to 24
- coef: float32 [256, 64, 32], P('gx', 'gz', 'gy'), may hold values from 0.01 to 0.05
- face_trace: int32 [256, 2, 32], P('gx', 'gz'), may hold values from 0 to 1023, as said below
- near_col: int32 [8, 2, 2], P('gx', 'gz', 'gy'), may hold values from 0 to 15, as said below
- far_col: int32 [8, 2, 2, 7], P('gx', 'gz', 'gy'), may hold values from 0 to 15, as said below
- near_tile: bfloat16 [8, 2, 2, 1024, 1024], P('gx', 'gz', 'gy'), may hold values from -0.1875 to 0.1875
- far_u: bfloat16 [8, 2, 2, 7, 16, 1024], P('gx', 'gz', 'gy'), may hold values from -0.375 to 0.375
- far_v: bfloat16 [8, 2, 2, 7, 16, 1024], P('gx', 'gz', 'gy'), may hold values from -0.1875 to 0.1875
Outputs:
- solution: float32 [256, 64, 1024], P('gx', 'gz', 'gy')
- flux: float32 [256, 2, 1024], P('gx', 'gz', 'gy')
Inputs may be any that keep to these rules, and one draw needn't show every extreme that they name: For every block of 32 rows of x and each face s, the entries face_trace(x, s, y) of that block are a permutation of 0 to 1023. For every row block, near_col over the slots j together with far_col over j and k name each column block 0 to 15 exactly once. `far_col`: see near_col: near and far column blocks of a row block together name every column block exactly once.
All inputs are finite; a program needn't handle non-finite values.
Results may differ from a plain program's by a relative error of at most 0.003.
Values may be sent and summed in bfloat16 or wider, within the bound.
No kernel may reach another device: no remote copies, remote signals or barrier semaphores. Data moves between devices by JAX's collectives and lax.ppermute only.
A program may use at most 64 MiB of HBM per device.

v0:
```python
import jax
import jax.numpy as jnp
from jax import lax
from jax.sharding import PartitionSpec as P

E = 32
SWEEPS = 3


def extended(block, sides, width):
    for axis, dim in sides:
        count = lax.axis_size(axis)
        forward = [(i, i + 1) for i in range(count - 1)]
        backward = [(target, source) for source, target in forward]
        low = lax.ppermute(
            lax.slice_in_dim(block, block.shape[dim] - width, None, axis=dim), axis, forward
        )
        high = lax.ppermute(lax.slice_in_dim(block, 0, width, axis=dim), axis, backward)
        block = jnp.concatenate([low, block, high], axis=dim)
    return block


def sweep(field, rhs, diag):
    slab = extended(field, (("gx", 0), ("gz", 1)), 1)
    pencil = extended(field, (("gy", 2),), E)
    beside = slab[2:, 1:-1] + slab[:-2, 1:-1] + slab[1:-1, 2:] + slab[1:-1, :-2]
    beside = beside + pencil[:, :, 2 * E :] + pencil[:, :, : -2 * E]
    return (rhs + beside) / diag


def body(source, coef, face_trace, near_col, far_col, near_tile, far_u, far_v):
    rows_x = source.shape[0]
    depth = source.shape[1]
    cells_y = coef.shape[2]
    groups = lax.axis_size("gy")
    mine_y = lax.axis_index("gy")
    face_side = lax.axis_index("gz")
    tile = near_tile.shape[3]
    far_count = far_u.shape[3]
    rank = far_u.shape[4]
    count_cols = far_count + 1
    diag = jnp.repeat(6.0 + coef, E, axis=2)
    field = jnp.zeros(source.shape, jnp.float32)
    for step in range(SWEEPS):
        field = sweep(field, source, diag)
    plane = jnp.where(face_side == 0, 0, depth - 1)
    depth_ids = jnp.arange(depth, dtype=jnp.int32)
    plane_mask = (depth_ids == plane).astype(jnp.float32)
    face_local = jnp.where(face_side == 0, field[:, 0, :], field[:, depth - 1, :]).astype(
        jnp.bfloat16
    )
    face_block = lax.all_gather(face_local, "gy", axis=1, tiled=True)
    perm = face_trace.reshape(tile)
    inverse = jnp.zeros((tile,), jnp.int32).at[perm].set(jnp.arange(tile, dtype=jnp.int32))
    block_traces = face_block.reshape(tile, E)[inverse].T
    wanted = jnp.concatenate([near_col.reshape(1), far_col.reshape(far_count)])
    share = tile // groups
    own_slice = lax.dynamic_slice_in_dim(block_traces, mine_y * share, share, 1)
    slices = lax.all_gather(own_slice[None], ("gx", "gz"), axis=0, tiled=True)
    everyone = lax.all_gather(wanted[None], "gy", axis=0, tiled=True)
    outgoing = slices[everyone]
    incoming = lax.all_to_all(outgoing, "gy", split_axis=0, concat_axis=0, tiled=True)
    chosen = incoming.transpose(1, 2, 0, 3).reshape(count_cols, E, tile)
    nearpart = lax.dot_general(
        chosen[0],
        near_tile.reshape(tile, tile),
        (((1,), (1,)), ((), ())),
        preferred_element_type=jnp.float32,
    )
    weights = jnp.einsum(
        "fet,frt->fer",
        chosen[1:],
        far_v.reshape(far_count, rank, tile),
        preferred_element_type=jnp.float32,
    ).astype(jnp.bfloat16)
    farpart = jnp.einsum(
        "fer,frt->et",
        weights,
        far_u.reshape(far_count, rank, tile),
        preferred_element_type=jnp.float32,
    )
    partial_rows = nearpart + farpart
    total = lax.psum(partial_rows, "gy")
    face_flux = total[:, perm].reshape(E, rows_x, cells_y * groups)
    mine = lax.dynamic_slice_in_dim(face_flux, mine_y * cells_y, cells_y, 2)
    flux_rows = mine.transpose(1, 2, 0).reshape(rows_x, cells_y * E)
    extra = plane_mask[None, :, None] * flux_rows[:, None, :]
    solution = sweep(field, source + extra, diag)
    return (solution, flux_rows[:, None, :])


def solution(mesh):
    return jax.shard_map(
        body,
        mesh=mesh,
        in_specs=(
            P("gx", "gz", "gy"),
            P("gx", "gz", "gy"),
            P("gx", "gz", None),
            P("gx", "gz", "gy"),
            P("gx", "gz", "gy", None),
            P("gx", "gz", "gy", None, None),
            P("gx", "gz", "gy", None, None, None),
            P("gx", "gz", "gy", None, None, None),
        ),
        out_specs=(P("gx", "gz", "gy"), P("gx", "gz", "gy")),
        check_vma=False,
    )
```

profile of v0, /device:TPU:0, one launch (start us, length us, event | category | flops | bytes accessed | tf_op | source)
XLA Modules:
  0.0 216.8 jit_solution(17377240271745328458)
XLA Ops:
  9.1 5.5 %collective-permute-start.1 = (f32[1,32,512]{2,0,1:T(1,128)}, f32[1,32,512]{2,0,1:T(1,128)S(1)}, u32[]{:S(2)}, u32[]{:S(2)}) collective-permute-start(f32[1,32,512]{2,0,1:T(1,128)} %broadcast.50), channel_id=1, source_target_pairs={{0,4},{4,8},{8,12},{12,16},{16,20},{20,24},{24,28},{1,5},{5,9},{9,... | collective-permute-start | bytes 196616 | tf_op jit(solution)/shard_map/ppermute | solution.py:15
  16.8 5.4 %collective-permute-start.5 = (f32[32,32,32]{2,0,1:T(8,128)}, f32[32,32,32]{2,0,1:T(8,128)}, u32[]{:S(2)}, u32[]{:S(2)}) collective-permute-start(f32[32,32,32]{2,0,1:T(8,128)} %broadcast.51), channel_id=1, source_target_pairs={{0,2},{1,3},{4,6},{5,7},{8,10},{9,11},{12,14},{13,15},{16,18},{17,... | collective-permute-start | bytes 393224 | tf_op jit(solution)/shard_map/ppermute | solution.py:15
  23.7 1.4 reduce.3
  25.2 4.3 %scatter_custom_fusion = s32[1024]{0:T(1024)S(1)} fusion(s32[1024]{0:T(1024)S(1)} %bitcast.51, s32[1024]{0:T(1024)S(1)} %iota.9, s32[]{:T(128)} %constant.10.clone.1), kind=kCustom, calls=%fused_computation.103 | custom fusion | bytes 4100 | tf_op jit(solution)/shard_map/scatter | solution.py:54
  30.0 4.6 %broadcast_in_dim.22 = f32[32,32,16,32]{3,2,0,1:T(8,128)} broadcast(f32[32,32,16]{2,0,1:T(8,128)S(1)} %copy.17), dimensions={0,1,2} | broadcast | bytes 2162688 | tf_op jit(solution)/shard_map/broadcast_in_dim | solution.py:42
  34.6 7.3 %reshape.72 = f32[32,32,512]{2,0,1:T(8,128)} reshape(f32[32,32,16,32]{3,2,0,1:T(8,128)} %broadcast_in_dim.22) | data formatting | bytes 4194304 | tf_op jit(solution)/shard_map/reshape | solution.py:42
  48.3 4.3 %all-reduce.4 = s32[16]{0:T(128)S(1)} all-reduce(s32[16]{0:T(128)S(1)} %add_dynamic-update-slice_fusion), channel_id=4, replica_groups=mesh['gx'=8,'gy'=2,'gz'=2] {'gy'}, use_global_device_ids=true, to_apply=%add.4 | all-reduce | flops 16 | bytes 128
  52.6 5.2 %fusion.6 = f32[32,32,512]{2,0,1:T(8,128)S(1)} fusion(f32[32,32,512]{2,0,1:T(8,128)} %reshape.72, f32[1,32,512]{2,0,1:T(1,128)S(1)} %collective-permute-done, f32[1,32,512]{2,0,1:T(1,128)S(1)} %collective-permute-done.1, f32[32,32,32]{2,0,1:T(8,128)S(1)} %collective-permute-done.4, f32[32,32,32]{2,0,1:T(8,128)} %collective-permute-done.5, ...), kind=kLoop, calls=%fused_computation.14 | loop fusion | flops 6815744 | bytes 8921088 | tf_op jit(solution)/shard_map/div | solution.py:28
  59.3 5.4 %collective-permute-start.7 = (f32[1,32,512]{2,0,1:T(1,128)S(1)}, f32[1,32,512]{2,0,1:T(1,128)S(1)}, u32[]{:S(2)}, u32[]{:S(2)}) collective-permute-start(f32[1,32,512]{2,0,1:T(1,128)S(1)} %get-tuple-element.20), channel_id=1, source_target_pairs={{0,4},{4,8},{8,12},{12,16},{16,20},{20,24},{24,28},{1,5},{5,9},{9,... | collective-permute-start | bytes 196616 | tf_op jit(solution)/shard_map/ppermute | solution.py:15
  65.9 1.9 collective-permute-start.11
  69.8 1.6 collective-permute-start.9
  72.8 6.6 %collective-permute-done.11 = f32[32,32,32]{2,0,1:T(8,128)S(1)} collective-permute-done((f32[32,32,32]{2,0,1:T(8,128)}, f32[32,32,32]{2,0,1:T(8,128)S(1)}, u32[]{:S(2)}, u32[]{:S(2)}) %collective-permute-start.11) | collective-permute-done | bytes 131104 | tf_op jit(solution)/shard_map/ppermute | solution.py:15
  79.4 4.0 %collective-permute-done.10 = f32[32,32,32]{2,0,1:T(8,128)S(1)} collective-permute-done((f32[32,32,32]{2,0,1:T(8,128)}, f32[32,32,32]{2,0,1:T(8,128)S(1)}, u32[]{:S(2)}, u32[]{:S(2)}) %collective-permute-start.10) | collective-permute-done | bytes 131104 | tf_op jit(solution)/shard_map/ppermute | solution.py:18
  83.5 10.9 %fusion.23 = f32[32,32,512]{2,0,1:T(8,128)S(1)} fusion(f32[32,32,512]{2,0,1:T(8,128)} %reshape.72, f32[32,32,512]{2,0,1:T(8,128)} %copy-done.5, f32[32,32,32]{2,0,1:T(8,128)S(1)} %collective-permute-done.11, f32[32,32,32]{2,0,1:T(8,128)S(1)} %collective-permute-done.10, f32[34,1,512]{2,0,1:T(8,128)S(1)} %collective-permute-done.9, ...), kind=kLoop, calls=%fused_computation.52 | loop fusion | flops 8912896 | bytes 8921088 | tf_op jit(solution)/shard_map/div | solution.py:28
  95.8 5.4 %collective-permute-start.13 = (f32[1,32,512]{2,0,1:T(1,128)S(1)}, f32[1,32,512]{2,0,1:T(1,128)S(1)}, u32[]{:S(2)}, u32[]{:S(2)}) collective-permute-start(f32[1,32,512]{2,0,1:T(1,128)S(1)} %get-tuple-element.16), channel_id=1, source_target_pairs={{0,4},{4,8},{8,12},{12,16},{16,20},{20,24},{24,28},{1,5},{5,9},{9,... | collective-permute-start | bytes 196616 | tf_op jit(solution)/shard_map/ppermute | solution.py:15
  101.5 1.6 collective-permute-start.17
  105.7 1.5 collective-permute-start.14
  107.2 5.4 %collective-permute-done.17 = f32[32,32,32]{2,0,1:T(8,128)S(1)} collective-permute-done((f32[32,32,32]{2,0,1:T(8,128)S(1)}, f32[32,32,32]{2,0,1:T(8,128)S(1)}, u32[]{:S(2)}, u32[]{:S(2)}) %collective-permute-start.17) | collective-permute-done | bytes 131104 | tf_op jit(solution)/shard_map/ppermute | solution.py:15
  112.6 4.1 %collective-permute-done.16 = f32[32,32,32]{2,0,1:T(8,128)S(1)} collective-permute-done((f32[32,32,32]{2,0,1:T(8,128)S(1)}, f32[32,32,32]{2,0,1:T(8,128)S(1)}, u32[]{:S(2)}, u32[]{:S(2)}) %collective-permute-start.16) | collective-permute-done | bytes 131104 | tf_op jit(solution)/shard_map/ppermute | solution.py:18
  116.7 5.4 %fusion.16 = f32[32,32,512]{2,0,1:T(8,128)S(1)} fusion(f32[32,32,512]{2,0,1:T(8,128)S(1)} %copy-done.1, f32[32,32,512]{2,0,1:T(8,128)S(1)} %fusion.23, f32[32,32,32]{2,0,1:T(8,128)S(1)} %collective-permute-done.17, f32[32,32,32]{2,0,1:T(8,128)S(1)} %collective-permute-done.16, f32[34,1,512]{2,0,1:T(8,128)S(1)} %collective-permute-done.15, ...), kind=kLoop, calls=%fused_computation.35 | loop fusion | flops 8912896 | bytes 8921088 | tf_op jit(solution)/shard_map/div | solution.py:28
  123.5 4.6 %all-gather = bf16[32,1,1024]{2,0,1:T(8,128)(2,1)S(1)} all-gather(bf16[32,1,512]{2,0,1:T(8,128)(2,1)S(1)} %fusion.34), channel_id=2, replica_groups=mesh['gx'=8,'gy'=2,'gz'=2] {'gy'}, dimensions={2}, use_global_device_ids=true | all-gather | bytes 98304 | tf_op jit(solution)/shard_map/all_gather | solution.py:52
  128.3 3.2 %gather_fusion = bf16[1024,32]{1,0:T(8,128)(2,1)S(1)} fusion(bf16[1024,32]{1,0:T(8,128)(2,1)S(1)} %reshape.73, s32[1024]{0:T(1024)S(1)} %fusion.35), kind=kCustom, calls=%fused_computation | custom fusion | bytes 135168 | tf_op jit(solution)/shard_map/gather | solution.py:55
  131.6 21.5 %all-gather.1 = bf16[512,512]{1,0:T(8,128)(2,1)S(1)} all-gather(bf16[32,512]{1,0:T(8,128)(2,1)S(1)} %copy.20), channel_id=3, replica_groups=mesh['gx'=8,'gy'=2,'gz'=2] {'gx','gz'}, dimensions={0}, use_global_device_ids=true | all-gather | bytes 557056 | tf_op jit(solution)/shard_map/all_gather | solution.py:59
  154.5 3.5 %all-to-all-start = ((bf16[2,8,32,512]{3,2,1,0:T(8,128)(2,1)}), bf16[2,8,32,512]{3,2,1,0:T(8,128)(2,1)S(1)}, u32[]{:S(2)}, u32[]{:S(2)}) async-start(bf16[2,8,32,512]{3,2,1,0:T(8,128)(2,1)} %bitcast.6), calls=%async_computation | async-start | bytes 1048576 | tf_op jit(solution)/shard_map/all_to_all | solution.py:62
  158.1 2.0 fusion.38
  161.3 4.5 %collective-permute-start.19 = (f32[1,32,512]{2,0,1:T(1,128)}, f32[1,32,512]{2,0,1:T(1,128)S(1)}, u32[]{:S(2)}, u32[]{:S(2)}) collective-permute-start(f32[1,32,512]{2,0,1:T(1,128)} %get-tuple-element.12), channel_id=1, source_target_pairs={{0,4},{4,8},{8,12},{12,16},{16,20},{20,24},{24,28},{1,5},{5,9},{9,... | collective-permute-start | bytes 196616 | tf_op jit(solution)/shard_map/ppermute | solution.py:15
  169.0 2.5 %fusion.39 = (f32[32,32,32]{2,0,1:T(8,128)}, f32[32,32,32]{2,0,1:T(8,128)}) fusion(f32[32,32,512]{2,0,1:T(8,128)} %copy-done.3), kind=kLoop, calls=%fused_computation.108 | loop fusion | bytes 524288 | tf_op jit(solution)/shard_map/slice | solution.py:18
  171.5 3.0 %collective-permute-start.23 = (f32[32,32,32]{2,0,1:T(8,128)}, f32[32,32,32]{2,0,1:T(8,128)S(1)}, u32[]{:S(2)}, u32[]{:S(2)}) collective-permute-start(f32[32,32,32]{2,0,1:T(8,128)} %get-tuple-element.15), channel_id=1, source_target_pairs={{0,2},{1,3},{4,6},{5,7},{8,10},{9,11},{12,14},{13,15},{16,18},{17,... | collective-permute-start | bytes 393224 | tf_op jit(solution)/shard_map/ppermute | solution.py:15
  179.0 10.2 %all-reduce.7.cloned.1.call-done = f32[32,1024]{1,0:T(8,128)} async-done(((f32[32,1024]{1,0:T(8,128)}), f32[32,1024]{1,0:T(8,128)}) %all-reduce.7.cloned.1.call-update) | async-done | bytes 131088 | tf_op jit(solution)/shard_map/psum | solution.py:83
  190.3 4.0 %gather_fusion.2 = f32[1024,32]{1,0:T(8,128)} fusion(f32[32,1024]{0,1:T(8,128)S(1)} %copy.23, s32[1024]{0:T(1024)S(1)} %broadcast_clamp_fusion), kind=kCustom, calls=%fused_computation.2 | custom fusion | bytes 266240 | tf_op jit(solution)/shard_map/gather | solution.py:84
  196.3 11.2 %fusion.9 = f32[32,32,512]{2,0,1:T(8,128)S(1)} fusion(f32[32,32,512]{2,0,1:T(8,128)} %reshape.72, f32[32,32,512]{2,0,1:T(8,128)} %copy-done.3, f32[32,32,32]{2,0,1:T(8,128)S(1)} %collective-permute-done.23, f32[32,32,32]{2,0,1:T(8,128)} %collective-permute-done.22, f32[34,1,512]{2,0,1:T(8,128)S(1)} %collective-permute-done.21, ...), kind=kLoop, calls=%fused_computation.18 | loop fusion | flops 9961472 | bytes 8986752 | tf_op jit(solution)/shard_map/div | solution.py:28
  207.4 2.5 %copy.25 = f32[32,32,512]{2,1,0:T(8,128)} copy(f32[32,32,512]{2,0,1:T(8,128)S(1)} %fusion.9) | data formatting | bytes 4194304
  (102 shorter events, 36.3 us)
Async XLA Ops:
  7.2 159.8 %copy-start = (bf16[1,1,1,1024,1024]{4,3,2,1,0:T(8,128)(2,1)S(1)}, bf16[1,1,1,1024,1024]{4,3,2,1,0:T(8,128)(2,1)}, u32[]{:S(2)}) copy-start(bf16[1,1,1,1024,1024]{4,3,2,1,0:T(8,128)(2,1)} %param.13) | copy-start | bytes 6291460
  7.8 36.0 %collective-permute-start = (f32[1,32,512]{2,0,1:T(1,128)}, f32[1,32,512]{2,0,1:T(1,128)S(1)}, u32[]{:S(2)}, u32[]{:S(2)}) collective-permute-start(f32[1,32,512]{2,0,1:T(1,128)} %broadcast.50), channel_id=1, source_target_pairs={{4,0},{8,4},{12,8},{16,12},{20,16},{24,20},{28,24},{5,1},{9,5},{13... | collective-permute-start | bytes 196616 | tf_op jit(solution)/shard_map/ppermute | solution.py:18
  9.1 34.7 %collective-permute-start.1 = (f32[1,32,512]{2,0,1:T(1,128)}, f32[1,32,512]{2,0,1:T(1,128)S(1)}, u32[]{:S(2)}, u32[]{:S(2)}) collective-permute-start(f32[1,32,512]{2,0,1:T(1,128)} %broadcast.50), channel_id=1, source_target_pairs={{0,4},{4,8},{8,12},{12,16},{16,20},{20,24},{24,28},{1,5},{5,9},{9,... | collective-permute-start | bytes 196616 | tf_op jit(solution)/shard_map/ppermute | solution.py:15
  15.5 37.1 %collective-permute-start.4 = (f32[32,32,32]{2,0,1:T(8,128)}, f32[32,32,32]{2,0,1:T(8,128)S(1)}, u32[]{:S(2)}, u32[]{:S(2)}) collective-permute-start(f32[32,32,32]{2,0,1:T(8,128)} %broadcast.51), channel_id=1, source_target_pairs={{2,0},{3,1},{6,4},{7,5},{10,8},{11,9},{14,12},{15,13},{18,16},{19,... | collective-permute-start | bytes 393224 | tf_op jit(solution)/shard_map/ppermute | solution.py:18
  16.8 35.8 %collective-permute-start.5 = (f32[32,32,32]{2,0,1:T(8,128)}, f32[32,32,32]{2,0,1:T(8,128)}, u32[]{:S(2)}, u32[]{:S(2)}) collective-permute-start(f32[32,32,32]{2,0,1:T(8,128)} %broadcast.51), channel_id=1, source_target_pairs={{0,2},{1,3},{4,6},{5,7},{8,10},{9,11},{12,14},{13,15},{16,18},{17,... | collective-permute-start | bytes 393224 | tf_op jit(solution)/shard_map/ppermute | solution.py:15
  34.6 8.0 %copy-start.10 = (u32[32]{0:T(128)S(1)}, u32[32]{0:T(128)}, u32[]{:S(2)}) copy-start(u32[32]{0:T(128)} %constant.44) | copy-start | bytes 388
  45.5 7.1 %collective-permute-start.3 = (f32[34,1,512]{2,0,1:T(8,128)S(1)}, f32[34,1,512]{2,0,1:T(8,128)S(1)}, u32[]{:S(2)}, u32[]{:S(2)}) collective-permute-start(f32[34,1,512]{2,0,1:T(8,128)S(1)} %get-tuple-element.11), channel_id=1, source_target_pairs={{0,1},{2,3},{4,5},{6,7},{8,9},{10,11},{12,13},{14,15},{16,17},{18,... | collective-permute-start | bytes 208904 | tf_op jit(solution)/shard_map/ppermute | solution.py:15
  46.8 5.8 %collective-permute-start.2 = (f32[34,1,512]{2,0,1:T(8,128)S(1)}, f32[34,1,512]{2,0,1:T(8,128)S(1)}, u32[]{:S(2)}, u32[]{:S(2)}) collective-permute-start(f32[34,1,512]{2,0,1:T(8,128)S(1)} %get-tuple-element.10), channel_id=1, source_target_pairs={{1,0},{3,2},{5,4},{7,6},{9,8},{11,10},{13,12},{15,14},{17,16},{19,... | collective-permute-start | bytes 208904 | tf_op jit(solution)/shard_map/ppermute | solution.py:18
  57.8 12.0 %copy-start.5 = (f32[32,32,512]{2,0,1:T(8,128)}, f32[32,32,512]{2,0,1:T(8,128)S(1)}, u32[]{:S(2)}) copy-start(f32[32,32,512]{2,0,1:T(8,128)S(1)} %fusion.6) | copy-start | bytes 6291460
  58.0 11.2 %collective-permute-start.6 = (f32[1,32,512]{2,0,1:T(1,128)S(1)}, f32[1,32,512]{2,0,1:T(1,128)S(1)}, u32[]{:S(2)}, u32[]{:S(2)}) collective-permute-start(f32[1,32,512]{2,0,1:T(1,128)S(1)} %get-tuple-element.21), channel_id=1, source_target_pairs={{4,0},{8,4},{12,8},{16,12},{20,16},{24,20},{28,24},{5,1},{9,5},{13... | collective-permute-start | bytes 196616 | tf_op jit(solution)/shard_map/ppermute | solution.py:18
  59.3 9.9 %collective-permute-start.7 = (f32[1,32,512]{2,0,1:T(1,128)S(1)}, f32[1,32,512]{2,0,1:T(1,128)S(1)}, u32[]{:S(2)}, u32[]{:S(2)}) collective-permute-start(f32[1,32,512]{2,0,1:T(1,128)S(1)} %get-tuple-element.20), channel_id=1, source_target_pairs={{0,4},{4,8},{8,12},{12,16},{16,20},{20,24},{24,28},{1,5},{5,9},{9,... | collective-permute-start | bytes 196616 | tf_op jit(solution)/shard_map/ppermute | solution.py:15
  65.9 13.5 %collective-permute-start.11 = (f32[32,32,32]{2,0,1:T(8,128)}, f32[32,32,32]{2,0,1:T(8,128)S(1)}, u32[]{:S(2)}, u32[]{:S(2)}) collective-permute-start(f32[32,32,32]{2,0,1:T(8,128)} %get-tuple-element.23), channel_id=1, source_target_pairs={{0,2},{1,3},{4,6},{5,7},{8,10},{9,11},{12,14},{13,15},{16,18},{17,... | collective-permute-start | bytes 393224 | tf_op jit(solution)/shard_map/ppermute | solution.py:15
  67.9 15.6 %collective-permute-start.10 = (f32[32,32,32]{2,0,1:T(8,128)}, f32[32,32,32]{2,0,1:T(8,128)S(1)}, u32[]{:S(2)}, u32[]{:S(2)}) collective-permute-start(f32[32,32,32]{2,0,1:T(8,128)} %get-tuple-element.22), channel_id=1, source_target_pairs={{2,0},{3,1},{6,4},{7,5},{10,8},{11,9},{14,12},{15,13},{18,16},{19,... | collective-permute-start | bytes 393224 | tf_op jit(solution)/shard_map/ppermute | solution.py:18
  69.8 13.7 %collective-permute-start.9 = (f32[34,1,512]{2,0,1:T(8,128)}, f32[34,1,512]{2,0,1:T(8,128)S(1)}, u32[]{:S(2)}, u32[]{:S(2)}) collective-permute-start(f32[34,1,512]{2,0,1:T(8,128)} %get-tuple-element.9), channel_id=1, source_target_pairs={{0,1},{2,3},{4,5},{6,7},{8,9},{10,11},{12,13},{14,15},{16,17},{18,... | collective-permute-start | bytes 208904 | tf_op jit(solution)/shard_map/ppermute | solution.py:15
  71.4 12.1 %collective-permute-start.8 = (f32[34,1,512]{2,0,1:T(8,128)S(1)}, f32[34,1,512]{2,0,1:T(8,128)S(1)}, u32[]{:S(2)}, u32[]{:S(2)}) collective-permute-start(f32[34,1,512]{2,0,1:T(8,128)S(1)} %get-tuple-element.8), channel_id=1, source_target_pairs={{1,0},{3,2},{5,4},{7,6},{9,8},{11,10},{13,12},{15,14},{17,16},{19,... | collective-permute-start | bytes 208904 | tf_op jit(solution)/shard_map/ppermute | solution.py:18
  94.5 9.9 %collective-permute-start.12 = (f32[1,32,512]{2,0,1:T(1,128)S(1)}, f32[1,32,512]{2,0,1:T(1,128)S(1)}, u32[]{:S(2)}, u32[]{:S(2)}) collective-permute-start(f32[1,32,512]{2,0,1:T(1,128)S(1)} %get-tuple-element.17), channel_id=1, source_target_pairs={{4,0},{8,4},{12,8},{16,12},{20,16},{24,20},{28,24},{5,1},{9,5},{13... | collective-permute-start | bytes 196616 | tf_op jit(solution)/shard_map/ppermute | solution.py:18
  95.8 21.0 %copy-start.1 = (f32[32,32,512]{2,0,1:T(8,128)S(1)}, f32[32,32,512]{2,0,1:T(8,128)}, u32[]{:S(2)}) copy-start(f32[32,32,512]{2,0,1:T(8,128)} %reshape.72) | copy-start | bytes 6291460
  95.8 20.9 %copy-start.2 = (f32[32,32,512]{2,1,0:T(8,128)S(1)}, f32[32,32,512]{2,1,0:T(8,128)}, u32[]{:S(2)}) copy-start(f32[32,32,512]{2,1,0:T(8,128)} %param.8) | copy-start | bytes 6291460
  95.8 8.6 %collective-permute-start.13 = (f32[1,32,512]{2,0,1:T(1,128)S(1)}, f32[1,32,512]{2,0,1:T(1,128)S(1)}, u32[]{:S(2)}, u32[]{:S(2)}) collective-permute-start(f32[1,32,512]{2,0,1:T(1,128)S(1)} %get-tuple-element.16), channel_id=1, source_target_pairs={{0,4},{4,8},{8,12},{12,16},{16,20},{20,24},{24,28},{1,5},{5,9},{9,... | collective-permute-start | bytes 196616 | tf_op jit(solution)/shard_map/ppermute | solution.py:15
  101.5 11.1 %collective-permute-start.17 = (f32[32,32,32]{2,0,1:T(8,128)S(1)}, f32[32,32,32]{2,0,1:T(8,128)S(1)}, u32[]{:S(2)}, u32[]{:S(2)}) collective-permute-start(f32[32,32,32]{2,0,1:T(8,128)S(1)} %get-tuple-element.19), channel_id=1, source_target_pairs={{0,2},{1,3},{4,6},{5,7},{8,10},{9,11},{12,14},{13,15},{16,18},{17,... | collective-permute-start | bytes 393224 | tf_op jit(solution)/shard_map/ppermute | solution.py:15
  103.0 13.7 %collective-permute-start.16 = (f32[32,32,32]{2,0,1:T(8,128)S(1)}, f32[32,32,32]{2,0,1:T(8,128)S(1)}, u32[]{:S(2)}, u32[]{:S(2)}) collective-permute-start(f32[32,32,32]{2,0,1:T(8,128)S(1)} %get-tuple-element.18), channel_id=1, source_target_pairs={{2,0},{3,1},{6,4},{7,5},{10,8},{11,9},{14,12},{15,13},{18,16},{19,... | collective-permute-start | bytes 393224 | tf_op jit(solution)/shard_map/ppermute | solution.py:18
  104.4 12.3 %collective-permute-start.15 = (f32[34,1,512]{2,0,1:T(8,128)S(1)}, f32[34,1,512]{2,0,1:T(8,128)S(1)}, u32[]{:S(2)}, u32[]{:S(2)}) collective-permute-start(f32[34,1,512]{2,0,1:T(8,128)S(1)} %get-tuple-element.7), channel_id=1, source_target_pairs={{0,1},{2,3},{4,5},{6,7},{8,9},{10,11},{12,13},{14,15},{16,17},{18,... | collective-permute-start | bytes 208904 | tf_op jit(solution)/shard_map/ppermute | solution.py:15
  105.7 11.0 %collective-permute-start.14 = (f32[34,1,512]{2,0,1:T(8,128)S(1)}, f32[34,1,512]{2,0,1:T(8,128)S(1)}, u32[]{:S(2)}, u32[]{:S(2)}) collective-permute-start(f32[34,1,512]{2,0,1:T(8,128)S(1)} %get-tuple-element.6), channel_id=1, source_target_pairs={{1,0},{3,2},{5,4},{7,6},{9,8},{11,10},{13,12},{15,14},{17,16},{19,... | collective-permute-start | bytes 208904 | tf_op jit(solution)/shard_map/ppermute | solution.py:18
  154.5 12.2 %all-to-all-start = ((bf16[2,8,32,512]{3,2,1,0:T(8,128)(2,1)}), bf16[2,8,32,512]{3,2,1,0:T(8,128)(2,1)S(1)}, u32[]{:S(2)}, u32[]{:S(2)}) async-start(bf16[2,8,32,512]{3,2,1,0:T(8,128)(2,1)} %bitcast.6), calls=%async_computation | async-start | bytes 1048576 | tf_op jit(solution)/shard_map/all_to_all | solution.py:62
  158.0 31.2 %all-reduce.7.cloned.1.call-start = ((), (), s32[]{:S(2)}) async-start(), calls=%async_computation.1 | async-start | bytes 262144 | tf_op jit(solution)/shard_map/psum | solution.py:83
  160.0 15.8 %collective-permute-start.18 = (f32[1,32,512]{2,0,1:T(1,128)}, f32[1,32,512]{2,0,1:T(1,128)S(1)}, u32[]{:S(2)}, u32[]{:S(2)}) collective-permute-start(f32[1,32,512]{2,0,1:T(1,128)} %get-tuple-element.13), channel_id=1, source_target_pairs={{4,0},{8,4},{12,8},{16,12},{20,16},{24,20},{28,24},{5,1},{9,5},{13... | collective-permute-start | bytes 196616 | tf_op jit(solution)/shard_map/ppermute | solution.py:18
  161.3 14.5 %collective-permute-start.19 = (f32[1,32,512]{2,0,1:T(1,128)}, f32[1,32,512]{2,0,1:T(1,128)S(1)}, u32[]{:S(2)}, u32[]{:S(2)}) collective-permute-start(f32[1,32,512]{2,0,1:T(1,128)} %get-tuple-element.12), channel_id=1, source_target_pairs={{0,4},{4,8},{8,12},{12,16},{16,20},{20,24},{24,28},{1,5},{5,9},{9,... | collective-permute-start | bytes 196616 | tf_op jit(solution)/shard_map/ppermute | solution.py:15
  168.9 6.9 %copy-start.4 = (f32[32,32,512]{2,0,1:T(8,128)S(1)}, f32[32,32,512]{2,0,1:T(8,128)}, u32[]{:S(2)}) copy-start(f32[32,32,512]{2,0,1:T(8,128)} %copy-done.3) | copy-start | bytes 6291460
  171.5 24.8 %collective-permute-start.23 = (f32[32,32,32]{2,0,1:T(8,128)}, f32[32,32,32]{2,0,1:T(8,128)S(1)}, u32[]{:S(2)}, u32[]{:S(2)}) collective-permute-start(f32[32,32,32]{2,0,1:T(8,128)} %get-tuple-element.15), channel_id=1, source_target_pairs={{0,2},{1,3},{4,6},{5,7},{8,10},{9,11},{12,14},{13,15},{16,18},{17,... | collective-permute-start | bytes 393224 | tf_op jit(solution)/shard_map/ppermute | solution.py:15
  174.5 21.8 %collective-permute-start.22 = (f32[32,32,32]{2,0,1:T(8,128)}, f32[32,32,32]{2,0,1:T(8,128)}, u32[]{:S(2)}, u32[]{:S(2)}) collective-permute-start(f32[32,32,32]{2,0,1:T(8,128)} %get-tuple-element.14), channel_id=1, source_target_pairs={{2,0},{3,1},{6,4},{7,5},{10,8},{11,9},{14,12},{15,13},{18,16},{19,... | collective-permute-start | bytes 393224 | tf_op jit(solution)/shard_map/ppermute | solution.py:18
  176.5 19.8 %collective-permute-start.21 = (f32[34,1,512]{2,0,1:T(8,128)}, f32[34,1,512]{2,0,1:T(8,128)S(1)}, u32[]{:S(2)}, u32[]{:S(2)}) collective-permute-start(f32[34,1,512]{2,0,1:T(8,128)} %get-tuple-element.5), channel_id=1, source_target_pairs={{0,1},{2,3},{4,5},{6,7},{8,9},{10,11},{12,13},{14,15},{16,17},{18,... | collective-permute-start | bytes 208904 | tf_op jit(solution)/shard_map/ppermute | solution.py:15
  177.7 18.5 %collective-permute-start.20 = (f32[34,1,512]{2,0,1:T(8,128)S(1)}, f32[34,1,512]{2,0,1:T(8,128)S(1)}, u32[]{:S(2)}, u32[]{:S(2)}) collective-permute-start(f32[34,1,512]{2,0,1:T(8,128)S(1)} %get-tuple-element.4), channel_id=1, source_target_pairs={{1,0},{3,2},{5,4},{7,6},{9,8},{11,10},{13,12},{15,14},{17,16},{19,... | collective-permute-start | bytes 208904 | tf_op jit(solution)/shard_map/ppermute | solution.py:18
  (5 other events, 9.0 us)
Sparse Core Ops, SparseCore 0:
  169.1 20.1 all-reduce.6
where the time goes:
time: 218 us; the launch traced here: 217 us
  starting transfers between devices  57.5 us (26%)
  local copies, waits for them, and re-layouts  43.4 us (20%)
  other arithmetic  36.5 us (17%)
  waiting for transfers between devices  31.3 us (14%)
  blocking collectives  30.4 us (14%)
  between operations  15.9 us (7%)
    ppermute x12, starting transfers between devices, extended(): lax.ppermute(lax.slice_in_dim(block, block.shape[dim] - width, None, axis...  38.3 us
    div x4, other arithmetic, sweep(): return (rhs + beside) / diag  32.6 us
    all_gather x1, blocking collectives, body(): slices = lax.all_gather(own_slice[None], ('gx', 'gz'), axis=0, tiled=True)  21.5 us
    ppermute x12, starting transfers between devices, extended(): lax.ppermute(lax.slice_in_dim(block, 0, width, axis=dim), axis, backward)  15.6 us
    ppermute x12, waiting for transfers between devices, extended(): lax.ppermute(lax.slice_in_dim(block, block.shape[dim] - width, None, axis...  12 us
    psum x1, waiting for transfers between devices, body(): total = lax.psum(partial_rows, 'gy')  10.2 us
    ppermute x12, waiting for transfers between devices, extended(): lax.ppermute(lax.slice_in_dim(block, 0, width, axis=dim), axis, backward)  8.21 us
    reshape x1, local copies, waits for them, and re-layouts, body(): diag = jnp.repeat(6.0 + coef, E, axis=2)  7.33 us
  transfers between devices with their start and end apart: 26, of which 6 were waited for; matrix products, arithmetic and copies ran while one was open for 18% of the time, Pallas kernels for 0%

commit v1 on v0

v1 whole, which is shorter than its diff:
```python
import functools

import jax
import jax.numpy as jnp
from jax import lax
from jax.experimental import pallas as pl
from jax.experimental.pallas import tpu as pltpu
from jax.sharding import PartitionSpec as P

E = 32
LANES = 128
ROWS = 8
HALO = 3
VMEM_BYTES = 56 * 1024 * 1024


def roll(value, shift, axis):
    return pltpu.roll(value, shift % value.shape[axis], axis)


def lane_ids(value):
    return lax.broadcasted_iota(jnp.int32, value.shape, value.ndim - 1)


def call(kernel, ids, operands, out_shape, in_specs=None, out_specs=None, scratch=(), flops=0, **kw):
    whole = lambda a: pl.BlockSpec(a.shape, lambda i, ids, n=len(a.shape): (0,) * n)
    if in_specs is None:
        in_specs = [None] * len(operands)
    in_specs = [whole(a) if spec is None else spec for a, spec in zip(operands, in_specs)]
    if out_specs is None:
        out_specs = [whole(a) for a in out_shape]
    moved = sum(a.size * a.dtype.itemsize for a in (*operands, *out_shape))
    return pl.pallas_call(
        kernel,
        out_shape=out_shape,
        grid_spec=pltpu.PrefetchScalarGridSpec(
            num_scalar_prefetch=1,
            grid=(1,),
            in_specs=in_specs,
            out_specs=out_specs,
            scratch_shapes=list(scratch),
        ),
        compiler_params=pltpu.CompilerParams(vmem_limit_bytes=VMEM_BYTES),
        cost_estimate=pl.CostEstimate(flops=flops, bytes_accessed=moved, transcendentals=0),
        **kw,
    )(ids, *operands)


def pairs(count):
    first = [(i, i ^ 1) for i in range(count)]
    second = [(i, i + 1) for i in range(1, count - 1, 2)]
    return first, second + [(b, a) for a, b in second]


def swap(messages, axis):
    count = lax.axis_size(axis)
    return [lax.ppermute(m, axis, p) for m, p in zip(messages, pairs(count))]


def message_count(axis):
    return 1 if lax.axis_size(axis) == 2 else 2


def choose(odd, low, high, number):
    return jnp.where(odd == number, high, low)


def from_low(odd, received):
    other = received[1] if len(received) == 2 else jnp.zeros_like(received[0])
    return jnp.where(odd == 1, received[0], other)


def from_high(odd, received):
    other = received[1] if len(received) == 2 else jnp.zeros_like(received[0])
    return jnp.where(odd == 1, other, received[0])


def spread_matrix(cells, width):
    k = lax.broadcasted_iota(jnp.int32, (LANES, width), 0)
    cell = lax.broadcasted_iota(jnp.int32, (LANES, width), 1) // E
    part = k // 32
    hit = (k - part * 32 == cell) & (part < 3) & (cell < cells)
    return jnp.where(hit, 1.0, 0.0).astype(jnp.bfloat16)


def spread(compact, width, cells):
    compact = jnp.where(lane_ids(compact) < cells, compact, 0.0)
    high = compact.astype(jnp.bfloat16).astype(jnp.float32)
    rest = compact - high
    middle = rest.astype(jnp.bfloat16).astype(jnp.float32)
    low = (rest - middle).astype(jnp.bfloat16).astype(jnp.float32)
    packed = high + roll(middle, 32, 1) + roll(low, 64, 1)
    return jnp.dot(
        packed.astype(jnp.bfloat16), spread_matrix(cells, width), preferred_element_type=jnp.float32
    )


def face_start_kernel(ids, src, inv, s_out, i_out, *messages):
    odd, side = ids[0] % 2, ids[2]
    rows_x, _, width = src.shape
    cells = width // E
    planes = []
    for d in range(3):
        s = jnp.where(side == 0, src[:, d, :], src[:, ROWS - 1 - d, :])
        c = jnp.where(side == 0, inv[:, d, :], inv[:, ROWS - 1 - d, :])
        i = spread(c, width, cells)
        s_out[d], i_out[d] = s, i
        planes.append((s, i))
    for number, message in enumerate(messages):
        for d in range(2):
            for k in range(2):
                v = planes[d][k]
                row = 4 * k + 2 * d
                message[row : row + 2, :] = choose(odd, v[:2], v[rows_x - 2 :], number)


def edge_pair(s, i):
    lane = lane_ids(s[:, :LANES])
    low = jnp.where(lane < 2 * E, s[:, :LANES], roll(i[:, :LANES], 64, 1))
    high = jnp.where(lane < 2 * E, roll(s[:, -LANES:], 64, 1), i[:, -LANES:])
    return low, high


def face_side_kernel(nx, ids, s_in, i_in, *refs):
    odd_x, odd_y = ids[0] % 2, ids[1] % 2
    got, messages = [r[...] for r in refs[:nx]], refs[nx:]
    rows_x = s_in.shape[1]
    below, above = from_low(odd_x, got), from_high(odd_x, got)
    pick = lax.broadcasted_iota(jnp.int32, below.shape, 0)
    s = jnp.where(pick == 0, roll(below, -1, 0), roll(above, 1, 0))
    i = jnp.where(pick == 0, roll(below, -5, 0), roll(above, -3, 0))
    s, i = (jnp.where(pick < 2, v, 0.0) for v in (s, i))
    parts = [edge_pair(s_in[0], i_in[0]), edge_pair(s_in[1], i_in[1]), edge_pair(s, i)]
    for number, message in enumerate(messages):
        row = 0
        for low, high in parts:
            message[row : row + low.shape[0], :] = choose(odd_y, low, high, number)
            row += low.shape[0]


def face_sweep_kernel(nx, ny, ids, s_in, i_in, *refs):
    odd_x, odd_y = ids[0] % 2, ids[1] % 2
    got_x = [r[...] for r in refs[:nx]]
    got_y = [r[...] for r in refs[nx : nx + ny]]
    out, ext_s, ext_i = refs[nx + ny :]
    _, rows_x, width = s_in.shape
    below, above = from_low(odd_x, got_x), from_high(odd_x, got_x)
    left, right = from_low(odd_y, got_y), from_high(odd_y, got_y)
    lane = lane_ids(left)
    pad_s = jnp.where(lane < 2 * E, right, roll(left, 64, 1))
    pad_i = jnp.where(lane < 2 * E, roll(right, 64, 1), left)
    ext_s[...] = jnp.zeros(ext_s.shape, jnp.float32)
    ext_i[...] = jnp.zeros(ext_i.shape, jnp.float32)
    first, last = ROWS, ROWS + rows_x
    for ext, own, pad, k in ((ext_s, s_in, pad_s, 0), (ext_i, i_in, pad_i, 1)):
        for d in range(2):
            row = 4 * k + 2 * d
            ext[d, first:last, :width] = own[d]
            ext[d, first - 2 : first, :width] = below[row : row + 2]
            ext[d, last : last + 2, :width] = above[row : row + 2]
            ext[d, first:last, width:] = pad[d * rows_x : (d + 1) * rows_x]
        ext[0, first - 1 : first, width:] = pad[2 * rows_x : 2 * rows_x + 1]
        ext[0, last : last + 1, width:] = pad[2 * rows_x + 1 : 2 * rows_x + 2]

    def around(u):
        return roll(u, 1, 0) + roll(u, -1, 0) + roll(u, E, 1) + roll(u, -E, 1)

    s0, s1, i0, i1 = ext_s[0], ext_s[1], ext_i[0], ext_i[1]
    u0, u1 = s0 * i0, s1 * i1
    deep = s_in[2] * i_in[2]
    v0 = (s0 + (around(u0) + u1)) * i0
    own = (around(u1) + u0)[first:last, :width]
    v1 = (s_in[1] + (own + deep)) * i_in[1]
    face = (s_in[0] + (around(v0)[first:last, :width] + v1)) * i_in[0]
    pieces = []
    for cell in range(width // E):
        start = cell * E // LANES * LANES
        pieces.append(roll(face[:, start : start + LANES], -(cell * E - start), 1))
    stacked = jnp.concatenate(pieces, axis=0)
    out[...] = stacked.T[:E].astype(jnp.bfloat16)


def order_kernel(ids, place, out):
    trace = lax.broadcasted_iota(jnp.int32, out.shape, 1)
    out[...] = jnp.where(place[...] == trace, 1.0, 0.0).astype(jnp.bfloat16)


def trace_kernel(ids, *refs):
    order, out = refs[-2:]
    if len(refs) == 3:
        face = refs[0][...]
    else:
        own, other = refs[0][...], refs[1][...]
        first = ids[1] == 0
        face = jnp.concatenate(
            [jnp.where(first, own, other), jnp.where(first, other, own)], axis=1
        )
    out[...] = jnp.dot(face, order[...], preferred_element_type=jnp.float32).astype(jnp.bfloat16)


ACROSS = (((1,), (1,)), ((), ()))


def operator_kernel(halves, ids, wanted, traces, near, far_v, far_u, order, *outs):
    count = wanted.shape[0] - 1
    rank = far_v.shape[0] // count
    across = functools.partial(
        lax.dot_general, dimension_numbers=ACROSS, preferred_element_type=jnp.float32
    )
    rows = across(traces[wanted[0]], near[...])
    far = jnp.concatenate([traces[wanted[1 + k]] for k in range(count)], axis=0)
    products = across(far, far_v[...])
    group = lax.broadcasted_iota(jnp.int32, (E, count * rank), 1) // rank
    weights = jnp.zeros((E, count * rank), jnp.float32)
    for k in range(count):
        weights = jnp.where(group == k, products[k * E : (k + 1) * E], weights)
    rows = rows + jnp.dot(
        weights.astype(jnp.bfloat16), far_u[...], preferred_element_type=jnp.float32
    )
    high = rows.astype(jnp.bfloat16)
    rest = rows - high.astype(jnp.float32)
    middle = rest.astype(jnp.bfloat16)
    low = (rest - middle.astype(jnp.float32)).astype(jnp.bfloat16)
    placed = across(jnp.concatenate([high, middle, low], axis=0), order[...])
    placed = placed[:E] + (placed[E : 2 * E] + placed[2 * E :])
    if halves:
        half = placed.shape[1] // 2
        first = ids[1] == 0
        outs[0][...] = jnp.where(first, placed[:, :half], placed[:, half:])
        outs[1][...] = jnp.where(first, placed[:, half:], placed[:, :half])
    else:
        outs[0][...] = placed


def finish_kernel(count, ids, *refs):
    parts, (inv, field, flux_out, out) = refs[:count], refs[count:]
    side = ids[2]
    rows_x, _, width = out.shape
    total = parts[0][...]
    if count == 2:
        total = total + parts[1][...]
    wide = jnp.concatenate([total, jnp.zeros((LANES - E, total.shape[1]), jnp.float32)], axis=0).T
    columns = []
    for start in range(0, width // E, LANES // E):
        column = wide[start * rows_x : (start + 1) * rows_x]
        for k in range(1, LANES // E):
            column = column + roll(wide[(start + k) * rows_x : (start + k + 1) * rows_x], k * E, 1)
        columns.append(column)
    flux = jnp.concatenate(columns, axis=1)
    flux_out[...] = flux
    added = (flux * inv[0])[:, None, :]
    row = lax.broadcasted_iota(jnp.int32, out.shape, 1)
    out[...] = field[...] + jnp.where(row == side * (ROWS - 1), added, 0.0)


def side_edge_kernel(ids, *refs):
    ny = len(refs) // 3
    odd = ids[1] % 2
    cells = 16
    inv = refs[ny]
    for number in range(ny):
        edge, message = refs[number], refs[ny + 1 + number]
        s, c = edge[...], inv[...]
        lane = lane_ids(s)
        width = HALO * E
        low = jnp.where(lane < width, s, roll(c, width, 2))
        high = jnp.where(lane < width, roll(s, width, 2), roll(c, width - (cells - HALO), 2))
        message[...] = choose(odd, low, high, number)


def widen(cells, ring, s, c, left, right):
    lane = lane_ids(right)
    width = HALO * E
    axis = right.ndim - 1
    zero = jnp.zeros_like(right)
    after = jnp.where(lane < width, right, zero)
    before = jnp.where(lane >= LANES - width, roll(left, LANES - width, axis), zero)
    pads = [after + before] if ring - cells == LANES // E else [after, before]
    own = jnp.where(lane < cells, c, zero)
    c_after = jnp.where((lane >= cells) & (lane < cells + HALO), roll(right, cells - width, axis), zero)
    c_before = jnp.where(
        (lane >= ring - HALO) & (lane < ring), roll(left, ring - HALO - width, axis), zero
    )
    return [s, *pads], own + c_after + c_before


def row_edge_kernel(cells, ring, ny, nx, ids, *refs):
    odd_x, odd_y = ids[0] % 2, ids[1] % 2
    s_low, s_high, c_low, c_high = refs[:4]
    y_low, y_high = refs[4 : 4 + ny], refs[4 + ny : 4 + 2 * ny]
    messages = refs[4 + 2 * ny :]
    block = s_low.shape[0]
    for k in range(HALO):
        sides = []
        for s, c, y, row in ((s_low, c_low, y_low, k), (s_high, c_high, y_high, block - HALO + k)):
            got = [r[row] for r in y]
            parts, compact = widen(
                cells, ring, s[row], c[row], from_low(odd_y, got), from_high(odd_y, got)
            )
            sides.append(jnp.concatenate([*parts, compact], axis=1))
        for number, message in enumerate(messages):
            message[k] = choose(odd_x, sides[0], sides[1], number)


def depth_edge_kernel(cells, ring, ny, nx, ids, s, c, *refs):
    odd_x, odd_y = ids[0] % 2, ids[1] % 2
    got_y, got_x, out = refs[:ny], refs[ny : ny + nx], refs[-1]
    rows_x = s.shape[0]
    got = [r[...] for r in got_y]
    parts, compact = widen(cells, ring, s[...], c[...], from_low(odd_y, got), from_high(odd_y, got))
    out[HALO : HALO + rows_x] = jnp.concatenate([*parts, compact], axis=2)
    got = [r[...] for r in got_x]
    out[:HALO] = from_low(odd_x, got)
    out[HALO + rows_x :] = from_high(odd_x, got)


def volume_kernel(cells, ring, ny, nx, ids, s, c, *refs):
    odd_x, odd_y, side = ids[0] % 2, ids[1] % 2, ids[2]
    got_y, got_x, got_z = refs[:ny], refs[ny : ny + nx], refs[ny + nx]
    out, ext_s, ext_i, one, two = refs[ny + nx + 1 :]
    rows_x, depth, width = s.shape
    wide = ring * E
    all_x = rows_x + 2 * HALO

    def place(x, parts, compact):
        row = lax.broadcasted_iota(jnp.int32, (ROWS, LANES), 0)
        zone = got_z[x]
        start = side * (ROWS - HALO)
        near = (row >= start) & (row < start + HALO)
        lanes = jnp.where(near, zone[:, wide:], 0.0)
        inverse = spread(jnp.concatenate([compact, lanes], axis=0), wide, ring)
        body = jnp.concatenate([jnp.concatenate(parts, axis=1), zone[:, :wide]], axis=0)
        ext_s[x] = body
        ext_i[x] = inverse
        one[x] = body * inverse

    def own(x, _):
        got = [r[x] for r in got_y]
        parts, compact = widen(cells, ring, s[x], c[x], from_low(odd_y, got), from_high(odd_y, got))
        place(x + HALO, parts, compact)
        return 0

    lax.fori_loop(0, rows_x, own, 0)
    for k in range(HALO):
        got = [r[k] for r in got_x]
        below, above = from_low(odd_x, got), from_high(odd_x, got)
        place(k, [below[:, :wide]], below[:, wide:])
        place(rows_x + HALO + k, [above[:, :wide]], above[:, wide:])

    def swept(old, x):
        u = old[x]
        beside = old[x - 1] + old[x + 1]
        beside = beside + (roll(u, 1, 0) + roll(u, -1, 0)) + (roll(u, E, 1) + roll(u, -E, 1))
        return (ext_s[x] + beside) * ext_i[x]

    def second(x, _):
        two[x] = swept(one, x)
        return 0

    def third(x, _):
        one[x] = swept(two, x)
        return 0

    def last(x, _):
        out[x - HALO] = swept(one, x)[:depth, :width]
        return 0

    lax.fori_loop(1, all_x - 1, second, 0)
    lax.fori_loop(2, all_x - 2, third, 0)
    lax.fori_loop(3, all_x - 3, last, 0)


def float_like(shape, dtype=jnp.float32):
    return jax.ShapeDtypeStruct(shape, dtype)


def body(source, coef, face_trace, near_col, far_col, near_tile, far_u, far_v):
    rows_x, depth, width = source.shape
    cells = coef.shape[2]
    groups = lax.axis_size("gy")
    size_x = lax.axis_size("gx")
    tile = near_tile.shape[3]
    count = far_u.shape[3]
    rank = far_u.shape[4]
    nx, ny = message_count("gx"), message_count("gy")
    at_x, at_y, at_z = (lax.axis_index(a).astype(jnp.int32) for a in ("gx", "gy", "gz"))
    ids = jnp.stack([at_x, at_y, at_z])
    slabs = depth // ROWS
    f32, bf16 = jnp.float32, jnp.bfloat16
    inv = jnp.pad(1.0 / (6.0 + coef), ((0, 0), (0, 0), (0, LANES - cells)))

    slab = lambda n: pl.BlockSpec((rows_x, ROWS, n), lambda i, ids: (0, ids[2] * (slabs - 1), 0))
    planes = float_like((3, rows_x, width))
    s_face, i_face, *out_x = call(
        face_start_kernel, ids, (source, inv),
        [planes, planes] + [float_like((ROWS, width))] * nx,
        in_specs=[slab(width), slab(LANES)],
    )
    got_x = swap(out_x, "gx")
    out_y = call(
        functools.partial(face_side_kernel, nx), ids, (s_face, i_face, *got_x),
        [float_like((2 * rows_x + ROWS, LANES))] * ny,
    )
    got_y = swap(out_y, "gy")
    ext = pltpu.VMEM((2, rows_x + 2 * ROWS, width + LANES), f32)
    part = rows_x * cells
    (face,) = call(
        functools.partial(face_sweep_kernel, nx, ny), ids, (s_face, i_face, *got_x, *got_y),
        [float_like((E, part), bf16)], scratch=(ext, ext),
    )

    place = face_trace.reshape(rows_x, cells * groups).T.reshape(tile, 1)
    (order,) = call(order_kernel, ids, (place,), [float_like((tile, tile), bf16)])
    if groups == 2:
        faces = (face, lax.ppermute(face, "gy", [(0, 1), (1, 0)]))
    else:
        faces = (lax.all_gather(face, "gy", axis=1, tiled=True),)
    (traces,) = call(
        trace_kernel, ids, (*faces, order), [float_like((E, tile), bf16)], flops=2 * E * tile * tile
    )
    traces = traces[None]
    steps = []
    step = size_x // 2
    while step:
        other = lax.ppermute(traces, "gx", [(i, i ^ step) for i in range(size_x)])
        traces = jnp.concatenate([traces, other], axis=0)
        steps.append(step)
        step //= 2
    other = lax.ppermute(traces, "gz", [(0, 1), (1, 0)])
    traces = jnp.concatenate([traces, other], axis=0)
    wanted = jnp.concatenate([near_col.reshape(1), far_col.reshape(count)])
    apart = (wanted // 2) ^ at_x
    spot = ((wanted % 2) ^ at_z) * size_x
    for n, step in enumerate(steps):
        spot = spot + jnp.where(apart & step > 0, 1 << n, 0)

    halves = groups == 2
    smem = pl.BlockSpec(memory_space=pltpu.SMEM)
    rows = call(
        functools.partial(operator_kernel, halves), ids,
        (spot, traces, near_tile.reshape(tile, tile), far_v.reshape(count * rank, tile),
         far_u.reshape(count * rank, tile), order),
        [float_like((E, part))] * 2 if halves else [float_like((E, tile))],
        in_specs=[smem] + [None] * 5, flops=8 * E * tile * tile,
    )
    if halves:
        rows = (rows[0], lax.ppermute(rows[1], "gy", [(0, 1), (1, 0)]))
    else:
        rows = (lax.psum_scatter(rows[0], "gy", scatter_dimension=1, tiled=True),)

    pad = LANES if groups == 2 else 2 * LANES
    ring = (width + pad) // E
    wide = width + pad
    blocks = width // LANES
    edge_at = lambda n: lambda i, ids: (0, 0, jnp.where(ids[1] % 2 == n, blocks - 1, 0))
    out_y = call(
        side_edge_kernel, ids, (*[source] * ny, inv), [float_like((rows_x, depth, LANES))] * ny,
        in_specs=[pl.BlockSpec((rows_x, depth, LANES), edge_at(n)) for n in range(ny)] + [None],
    )
    vol_y = swap(out_y, "gy")
    quad = lambda n, at: pl.BlockSpec((4, depth, n), lambda i, ids: (at, 0, 0))
    top = rows_x // 4 - 1
    out_x = call(
        functools.partial(row_edge_kernel, cells, ring, ny, nx), ids,
        (source, source, inv, inv, *vol_y, *vol_y),
        [float_like((HALO, depth, wide + LANES))] * nx,
        in_specs=[quad(width, 0), quad(width, top), quad(LANES, 0), quad(LANES, top)]
        + [quad(LANES, 0)] * ny + [quad(LANES, top)] * ny,
    )
    vol_x = swap(out_x, "gx")
    all_x = rows_x + 2 * HALO
    inner = lambda x, n: pl.BlockSpec(
        (x, ROWS, n), lambda i, ids: (0, (1 - ids[2]) * (slabs - 1), 0)
    )
    (out_z,) = call(
        functools.partial(depth_edge_kernel, cells, ring, ny, nx), ids,
        (source, inv, *vol_y, *vol_x), [float_like((all_x, ROWS, wide + LANES))],
        in_specs=[inner(rows_x, width), inner(rows_x, LANES)] + [inner(rows_x, LANES)] * ny
        + [inner(HALO, wide + LANES)] * nx,
    )
    vol_z = lax.ppermute(out_z, "gz", [(0, 1), (1, 0)])
    ext = pltpu.VMEM((all_x, depth + ROWS, wide), f32)
    (field,) = call(
        functools.partial(volume_kernel, cells, ring, ny, nx), ids,
        (source, inv, *vol_y, *vol_x, vol_z), [float_like(source.shape)], scratch=(ext,) * 4,
    )

    plane = pl.BlockSpec((1, rows_x, width), lambda i, ids: (0, 0, 0))
    flux, result = call(
        functools.partial(finish_kernel, len(rows)), ids, (*rows, i_face, field),
        [float_like((rows_x, width)), float_like(source.shape)],
        in_specs=[None] * len(rows) + [plane, slab(width)],
        out_specs=[pl.BlockSpec((rows_x, width), lambda i, ids: (0, 0)), slab(width)],
        input_output_aliases={len(rows) + 2: 1},
    )
    return (result, flux[:, None, :])


def solution(mesh):
    return jax.shard_map(
        body,
        mesh=mesh,
        in_specs=(
            P("gx", "gz", "gy"),
            P("gx", "gz", "gy"),
            P("gx", "gz", None),
            P("gx", "gz", "gy"),
            P("gx", "gz", "gy", None),
            P("gx", "gz", "gy", None, None),
            P("gx", "gz", "gy", None, None, None),
            P("gx", "gz", "gy", None, None, None),
        ),
        out_specs=(P("gx", "gz", "gy"), P("gx", "gz", "gy")),
        check_vma=False,
    )
```

time: 218 us -> 115 us (0.53)
  Pallas kernels: 0 us -> 60.1 us
  starting transfers between devices: 57.5 us -> 20.7 us
  other arithmetic: 36.5 us -> 2.27 us
  local copies, waits for them, and re-layouts: 43.4 us -> 11.7 us
  blocking collectives: 30.4 us -> 0 us
  between operations: 15.9 us -> 1.43 us
  waiting for transfers between devices: 31.3 us -> 17.2 us
    pallas_call x0 -> x11, Pallas kernels: none -> 60.1 us  [call(): pl.pallas_call(kernel, out_shape=out_shape, grid_spec=pltpu.PrefetchScala...]
    ppermute x24 -> x13, starting transfers between devices: 53.9 us -> 20.7 us  [the longest x3 11.3 us: body(): other = lax.ppermute(traces, 'gx', [(i, i ^ step) for i in range(size_x)])]
    div x4 -> x1, other arithmetic: 32.6 us -> 0.08 us  [body(): inv = jnp.pad(1.0 / (6.0 + coef), ((0, 0), (0, 0), (0, LANES - cells)))]
    all_gather x2 -> x0, blocking collectives: 26.1 us -> none  [the longest x1 21.5 us: body(): slices = lax.all_gather(own_slice[None], ('gx', 'gz'), axis=0, tiled=True)]
    psum x1 -> x0, waiting for transfers between devices: 10.2 us -> none  [body(): total = lax.psum(partial_rows, 'gy')]
    gather x3 -> x0, local copies, waits for them, and re-layouts: 8.58 us -> none  [the longest x1 3.99 us: body(): face_flux = total[:, perm].reshape(E, rows_x, cells_y * groups)]
    reshape x3 -> x1, local copies, waits for them, and re-layouts: 7.59 us -> 1.36 us  [body(): place = face_trace.reshape(rows_x, cells * groups).T.reshape(tile, 1)]
    slice x9 -> x0, local copies, waits for them, and re-layouts: 6.19 us -> none  [the longest x3 3.89 us: extended(): lax.slice_in_dim(block, 0, width, axis=dim)]
  transfers between devices with their start and end apart: 26 -> 13, of which waited for: 6 -> 5; matrix products, arithmetic and copies ran while one was open for 18% -> 3% of each run, Pallas kernels for 0% -> 48%
where the time goes in v1:
time: 115 us; the launch traced here: 113 us
  Pallas kernels  60.1 us (52%)
  starting transfers between devices  20.7 us (18%)
  waiting for transfers between devices  17.2 us (15%)
  local copies, waits for them, and re-layouts  11.7 us (10%)
  other arithmetic  2.27 us (2%)
  between operations  1.43 us (1%)
    pallas_call x11, Pallas kernels, call(): pl.pallas_call(kernel, out_shape=out_shape, grid_spec=pltpu.PrefetchScala...  60.1 us
    ppermute x6, waiting for transfers between devices, swap(): return [lax.ppermute(m, axis, p) for m, p in zip(messages, pairs(count))]  12.4 us
    ppermute x3, starting transfers between devices, body(): other = lax.ppermute(traces, 'gx', [(i, i ^ step) for i in range(size_x)])  11.3 us
    unnamed x32, local copies, waits for them, and re-layouts  9.37 us
    ppermute x6, starting transfers between devices, swap(): return [lax.ppermute(m, axis, p) for m, p in zip(messages, pairs(count))]  6.44 us
    ppermute x3, waiting for transfers between devices, body(): other = lax.ppermute(traces, 'gx', [(i, i ^ step) for i in range(size_x)])  2.8 us
  transfers between devices with their start and end apart: 13, of which 5 were waited for; matrix products, arithmetic and copies ran while one was open for 3% of the time, Pallas kernels for 48%

profile of v1, /device:TPU:0, one launch (start us, length us, event | category | flops | bytes accessed | tf_op | source)
XLA Modules:
  0.0 113.4 jit_solution(5001673118900487585)
XLA Ops:
  0.6 1.2 %copy.18 = f32[32,32,16]{2,1,0:T(8,128)S(1)} copy(f32[32,32,16]{1,2,0:T(8,128)} %param.9) | data formatting | bytes 131072 | tf_op args[1]
  1.9 0.8 pad.4.inv.refs_1_.refs_2_.refs_3_.c
  3.4 3.1 %shard_map.101 = f32[32,32,128]{2,1,0:T(8,128)} custom-call(s32[3]{0:T(128)} %pad_add_fusion.ids, f32[32,32,512]{2,1,0:T(8,128)} %s.3, f32[32,32,128]{2,1,0:T(8,128)} %pad.4.inv.refs_1_.refs_2_.refs_3_.c), custom_call_target="tpu_custom_call" | custom-call | bytes 3145728 | tf_op jit(solution)/shard_map/pallas_call | solution.py:33
  6.5 3.0 %collective-permute-start.9 = (f32[32,32,128]{2,1,0:T(8,128)}, f32[32,32,128]{2,1,0:T(8,128)S(1)}, u32[]{:S(2)}, u32[]{:S(2)}) collective-permute-start(f32[32,32,128]{2,1,0:T(8,128)} %shard_map.101), channel_id=1, source_target_pairs={{0,2},{2,0},{1,3},{3,1},{4,6},{6,4},{5,7},{7,5},{8,10},{10,8},{9,1... | collective-permute-start | bytes 1572872 | tf_op jit(solution)/shard_map/ppermute | solution.py:57
  9.5 2.7 %shard_map.95 = (f32[3,32,512]{2,1,0:T(8,128)}, f32[3,32,512]{2,1,0:T(8,128)}, f32[8,512]{1,0:T(8,128)}, f32[8,512]{1,0:T(8,128)}) custom-call(s32[3]{0:T(128)} %pad_add_fusion.ids, f32[32,32,512]{2,1,0:T(8,128)} %s.3, f32[32,32,128]{2,1,0:T(8,128)} %pad.4.inv.refs_1_.refs_2_.refs_3_.c), custom_call_target="tpu_custom_call" | custom-call | bytes 3047424 | tf_op jit(solution)/shard_map/pallas_call | solution.py:33
  12.2 1.5 %collective-permute-start = (f32[8,512]{1,0:T(8,128)}, f32[8,512]{1,0:T(8,128)S(1)}, u32[]{:S(2)}, u32[]{:S(2)}) collective-permute-start(f32[8,512]{1,0:T(8,128)} %get-tuple-element.14), channel_id=1, source_target_pairs={{0,4},{4,0},{8,12},{12,8},{16,20},{20,16},{24,28},{28,24},{1,5},{5... | collective-permute-start | bytes 49160 | tf_op jit(solution)/shard_map/ppermute | solution.py:57
  14.3 1.8 %collective-permute-done.refs_0_ = f32[8,512]{1,0:T(8,128)S(1)} collective-permute-done((f32[8,512]{1,0:T(8,128)}, f32[8,512]{1,0:T(8,128)S(1)}, u32[]{:S(2)}, u32[]{:S(2)}) %collective-permute-start) | collective-permute-done | bytes 16416 | tf_op jit(solution)/shard_map/ppermute | solution.py:57
  16.7 2.4 %shard_map.96 = f32[72,128]{1,0:T(8,128)} custom-call(s32[3]{0:T(128)} %pad_add_fusion.ids, f32[3,32,512]{2,1,0:T(8,128)} %get-tuple-element.12.s_in, f32[3,32,512]{2,1,0:T(8,128)} %get-tuple-element.13.i_in.refs_2_, f32[8,512]{1,0:T(8,128)} %copy-done.6, f32[8,512]{1,0:T(8,128)} %copy-done.7), custom_call_target="tpu_custom_call" | custom-call | bytes 462848 | tf_op jit(solution)/shard_map/pallas_call | solution.py:33
  19.3 4.0 %collective-permute-done.2.refs_2_ = f32[72,128]{1,0:T(8,128)S(1)} collective-permute-done((f32[72,128]{1,0:T(8,128)}, f32[72,128]{1,0:T(8,128)S(1)}, u32[]{:S(2)}, u32[]{:S(2)}) %collective-permute-start.2) | collective-permute-done | bytes 36896 | tf_op jit(solution)/shard_map/ppermute | solution.py:57
  23.9 2.7 %shard_map.97.refs_0_ = bf16[32,512]{1,0:T(8,128)(2,1)} custom-call(s32[3]{0:T(128)} %pad_add_fusion.ids, f32[3,32,512]{2,1,0:T(8,128)} %get-tuple-element.12.s_in, f32[3,32,512]{2,1,0:T(8,128)} %get-tuple-element.13.i_in.refs_2_, f32[8,512]{1,0:T(8,128)} %copy-done.6, f32[8,512]{1,0:T(8,128)} %copy-done.7, f32[72,128]{1,0:T(8,128)} %copy-done.9), custom_call_target="tpu_custom_call" | custom-call | bytes 495616 | tf_op jit(solution)/shard_map/pallas_call | solution.py:33
  26.7 0.9 collective-permute-start.3
  27.6 1.4 %reshape.32.place = s32[1024,1]{1,0:T(8,128)} reshape(s32[32,32]{1,0:T(8,128)S(1)} %copy.20) | data formatting | bytes 8192 | tf_op jit(solution)/shard_map/reshape | solution.py:412
  28.9 3.4 %shard_map.98.refs_2_.order = bf16[1024,1024]{1,0:T(8,128)(2,1)} custom-call(s32[3]{0:T(128)} %pad_add_fusion.ids, s32[1024,1]{1,0:T(8,128)} %reshape.32.place), custom_call_target="tpu_custom_call" | custom-call | bytes 2101248 | tf_op jit(solution)/shard_map/pallas_call | solution.py:33
  33.0 3.4 %shard_map.99 = bf16[32,1024]{1,0:T(8,128)(2,1)} custom-call(s32[3]{0:T(128)} %pad_add_fusion.ids, bf16[32,512]{1,0:T(8,128)(2,1)} %shard_map.97.refs_0_, bf16[32,512]{1,0:T(8,128)(2,1)} %copy-done.10, bf16[1024,1024]{1,0:T(8,128)(2,1)} %shard_map.98.refs_2_.order), custom_call_target="tpu_custom_call" | custom-call | flops 67108864 | bytes 2228224 | tf_op jit(solution)/shard_map/pallas_call | solution.py:33
  36.4 6.5 %collective-permute-start.4 = (bf16[1,32,1024]{2,1,0:T(8,128)(2,1)}, bf16[1,32,1024]{2,1,0:T(8,128)(2,1)S(1)}, u32[]{:S(2)}, u32[]{:S(2)}) collective-permute-start(bf16[1,32,1024]{2,1,0:T(8,128)(2,1)} %bitcast.16), channel_id=1, source_target_pairs={{0,16},{4,20},{8,24},{12,28},{16,0},{20,4},{24,8},{28,12},{1,17},{... | collective-permute-start | bytes 196616 | tf_op jit(solution)/shard_map/ppermute | solution.py:425
  42.9 2.8 %collective-permute-done.4 = bf16[1,32,1024]{2,1,0:T(8,128)(2,1)S(1)} collective-permute-done((bf16[1,32,1024]{2,1,0:T(8,128)(2,1)}, bf16[1,32,1024]{2,1,0:T(8,128)(2,1)S(1)}, u32[]{:S(2)}, u32[]{:S(2)}) %collective-permute-start.4) | collective-permute-done | bytes 65568 | tf_op jit(solution)/shard_map/ppermute | solution.py:425
  45.7 0.9 pad_maximum_fusion.2
  46.5 1.6 %collective-permute-start.5 = (bf16[2,32,1024]{2,1,0:T(8,128)(2,1)S(1)}, bf16[2,32,1024]{2,1,0:T(8,128)(2,1)S(1)}, u32[]{:S(2)}, u32[]{:S(2)}) collective-permute-start(bf16[2,32,1024]{2,1,0:T(8,128)(2,1)S(1)} %pad_maximum_fusion.2), channel_id=1, source_target_pairs={{0,8},{4,12},{8,0},{12,4},{16,24},{20,28},{24,16},{28,20},{1,9},{5... | collective-permute-start | bytes 393224 | tf_op jit(solution)/shard_map/ppermute | solution.py:425
  48.2 0.8 copy-done
  49.0 2.7 %shard_map.102 = (f32[3,32,768]{2,1,0:T(8,128)}, f32[3,32,768]{2,1,0:T(8,128)}) custom-call(s32[3]{0:T(128)} %pad_add_fusion.ids, f32[32,32,512]{2,1,0:T(8,128)} %s.3, f32[32,32,512]{2,1,0:T(8,128)} %s.3, f32[32,32,128]{2,1,0:T(8,128)} %pad.4.inv.refs_1_.refs_2_.refs_3_.c, f32[32,32,128]{2,1,0:T(8,128)} %pad.4.inv.refs_1_.refs_2_.refs_3_.c, ...), custom_call_target="tpu_custom_call" | custom-call | bytes 6881280 | tf_op jit(solution)/shard_map/pallas_call | solution.py:33
  53.0 3.2 %collective-permute-start.6 = (bf16[4,32,1024]{2,1,0:T(8,128)(2,1)S(1)}, bf16[4,32,1024]{2,1,0:T(8,128)(2,1)S(1)}, u32[]{:S(2)}, u32[]{:S(2)}) collective-permute-start(bf16[4,32,1024]{2,1,0:T(8,128)(2,1)S(1)} %pad_maximum_fusion.1), channel_id=1, source_target_pairs={{0,4},{4,0},{8,12},{12,8},{16,20},{20,16},{24,28},{28,24},{1,5},{5... | collective-permute-start | bytes 786440 | tf_op jit(solution)/shard_map/ppermute | solution.py:425
  56.9 6.6 %collective-permute-done.10.refs_1_ = f32[3,32,768]{2,1,0:T(8,128)S(1)} collective-permute-done((f32[3,32,768]{2,1,0:T(8,128)}, f32[3,32,768]{2,1,0:T(8,128)S(1)}, u32[]{:S(2)}, u32[]{:S(2)}) %collective-permute-start.10) | collective-permute-done | bytes 294944 | tf_op jit(solution)/shard_map/ppermute | solution.py:57
  64.2 0.7 copy-done.4
  64.9 3.0 %shard_map.103 = f32[38,8,768]{2,1,0:T(8,128)} custom-call(s32[3]{0:T(128)} %pad_add_fusion.ids, f32[32,32,512]{2,1,0:T(8,128)} %s.3, f32[32,32,128]{2,1,0:T(8,128)} %pad.4.inv.refs_1_.refs_2_.refs_3_.c, f32[32,32,128]{2,1,0:T(8,128)} %copy-done, f32[3,32,768]{2,1,0:T(8,128)} %copy-done.3, f32[3,32,768]{2,1,0:T(8,128)} %copy-done.4), custom_call_target="tpu_custom_call" | custom-call | bytes 4669440 | tf_op jit(solution)/shard_map/pallas_call | solution.py:33
  69.2 1.9 %collective-permute-done.7 = bf16[8,32,1024]{2,1,0:T(8,128)(2,1)S(1)} collective-permute-done((bf16[8,32,1024]{2,1,0:T(8,128)(2,1)S(1)}, bf16[8,32,1024]{2,1,0:T(8,128)(2,1)S(1)}, u32[]{:S(2)}, u32[]{:S(2)}) %collective-permute-start.7) | collective-permute-done | bytes 524320 | tf_op jit(solution)/shard_map/ppermute | solution.py:429
  71.2 1.0 copy-done.2
  72.1 6.6 %shard_map.100 = (f32[32,512]{1,0:T(8,128)}, f32[32,512]{1,0:T(8,128)}) custom-call(s32[3]{0:T(128)} %pad_add_fusion.ids, s32[8]{0:T(128)} %fusion.4.wanted, bf16[16,32,1024]{2,1,0:T(8,128)(2,1)} %copy-done.2, bf16[1024,1024]{1,0:T(8,128)(2,1)} %bitcast.15, bf16[112,1024]{1,0:T(8,128)(2,1)} %bitcast.20, bf16[112,1024]{1,0:T(8,128)(2,1)} %bitcast.21, ...), custom_call_target="tpu_custom_call" | custom-call | flops 268435456 | bytes 5832736 | tf_op jit(solution)/shard_map/pallas_call | solution.py:33
  78.8 1.5 %collective-permute-start.8 = (f32[32,512]{1,0:T(8,128)}, f32[32,512]{1,0:T(8,128)S(1)}, u32[]{:S(2)}, u32[]{:S(2)}) collective-permute-start(f32[32,512]{1,0:T(8,128)} %get-tuple-element.17), channel_id=1, source_target_pairs={{0,2},{2,0},{1,3},{3,1},{4,6},{6,4},{5,7},{7,5},{8,10},{10,8},{9,1... | collective-permute-start | bytes 196616 | tf_op jit(solution)/shard_map/ppermute | solution.py:447
  80.3 1.0 copy-done.5
  81.3 27.1 %shard_map.104.refs_3_ = f32[32,32,512]{2,1,0:T(8,128)} custom-call(s32[3]{0:T(128)} %pad_add_fusion.ids, f32[32,32,512]{2,1,0:T(8,128)} %s.3, f32[32,32,128]{2,1,0:T(8,128)} %pad.4.inv.refs_1_.refs_2_.refs_3_.c, f32[32,32,128]{2,1,0:T(8,128)} %copy-done, f32[3,32,768]{2,1,0:T(8,128)} %copy-done.3, f32[3,32,768]{2,1,0:T(8,128)} %copy-done.4, ...), custom_call_target="tpu_custom_call" | custom-call | bytes 6766592 | tf_op jit(solution)/shard_map/pallas_call | solution.py:33
  109.0 2.9 %shard_map.105 = (f32[32,512]{1,0:T(8,128)}, f32[32,32,512]{2,1,0:T(8,128)}) custom-call(s32[3]{0:T(128)} %pad_add_fusion.ids, f32[32,512]{1,0:T(8,128)} %get-tuple-element.16.refs_0_, f32[32,512]{1,0:T(8,128)} %copy-done.8, f32[3,32,512]{2,1,0:T(8,128)} %get-tuple-element.13.i_in.refs_2_, ...), custom_call_target="tpu_custom_call", output_to_operand_aliasing={{1}: (4, {})} | custom-call | bytes 4587520 | tf_op jit(solution)/shard_map/pallas_call | solution.py:33
  111.9 1.5 %copy.22 = f32[32,1,512]{2,1,0:T(1,128)} copy(f32[32,1,512]{2,0,1:T(8,128)} %bitcast.22) | data formatting | bytes 131072
  (47 shorter events, 7.3 us)
Async XLA Ops:
  6.5 21.0 %copy-start.11 = (s32[32,1,32]{2,1,0:T(1,128)S(1)}, s32[32,1,32]{2,1,0:T(1,128)}, u32[]{:S(2)}) copy-start(s32[32,1,32]{2,1,0:T(1,128)} %param.10) | copy-start | bytes 12292
  6.5 41.7 %collective-permute-start.9 = (f32[32,32,128]{2,1,0:T(8,128)}, f32[32,32,128]{2,1,0:T(8,128)S(1)}, u32[]{:S(2)}, u32[]{:S(2)}) collective-permute-start(f32[32,32,128]{2,1,0:T(8,128)} %shard_map.101), channel_id=1, source_target_pairs={{0,2},{2,0},{1,3},{3,1},{4,6},{6,4},{5,7},{7,5},{8,10},{10,8},{9,1... | collective-permute-start | bytes 1572872 | tf_op jit(solution)/shard_map/ppermute | solution.py:57
  12.2 3.9 %collective-permute-start = (f32[8,512]{1,0:T(8,128)}, f32[8,512]{1,0:T(8,128)S(1)}, u32[]{:S(2)}, u32[]{:S(2)}) collective-permute-start(f32[8,512]{1,0:T(8,128)} %get-tuple-element.14), channel_id=1, source_target_pairs={{0,4},{4,0},{8,12},{12,8},{16,20},{20,16},{24,28},{28,24},{1,5},{5... | collective-permute-start | bytes 49160 | tf_op jit(solution)/shard_map/ppermute | solution.py:57
  13.7 2.5 %collective-permute-start.1 = (f32[8,512]{1,0:T(8,128)}, f32[8,512]{1,0:T(8,128)S(1)}, u32[]{:S(2)}, u32[]{:S(2)}) collective-permute-start(f32[8,512]{1,0:T(8,128)} %get-tuple-element.15), channel_id=1, source_target_pairs={{4,8},{12,16},{20,24},{8,4},{16,12},{24,20},{5,9},{13,17},{21,25},... | collective-permute-start | bytes 49160 | tf_op jit(solution)/shard_map/ppermute | solution.py:57
  16.1 0.6 copy-start.6
  16.1 0.6 copy-start.7
  19.1 4.2 %collective-permute-start.2 = (f32[72,128]{1,0:T(8,128)}, f32[72,128]{1,0:T(8,128)S(1)}, u32[]{:S(2)}, u32[]{:S(2)}) collective-permute-start(f32[72,128]{1,0:T(8,128)} %shard_map.96), channel_id=1, source_target_pairs={{0,2},{2,0},{1,3},{3,1},{4,6},{6,4},{5,7},{7,5},{8,10},{10,8},{9,1... | collective-permute-start | bytes 110600 | tf_op jit(solution)/shard_map/ppermute | solution.py:57
  23.3 0.6 copy-start.9
  26.7 5.7 %collective-permute-start.3 = (bf16[32,512]{1,0:T(8,128)(2,1)}, bf16[32,512]{1,0:T(8,128)(2,1)S(1)}, u32[]{:S(2)}, u32[]{:S(2)}) collective-permute-start(bf16[32,512]{1,0:T(8,128)(2,1)} %shard_map.97.refs_0_), channel_id=1, source_target_pairs={{0,2},{2,0},{1,3},{3,1},{4,6},{6,4},{5,7},{7,5},{8,10},{10,8},{9,1... | collective-permute-start | bytes 98312 | tf_op jit(solution)/shard_map/ppermute | solution.py:415
  32.4 0.6 copy-start.10
  36.4 9.3 %collective-permute-start.4 = (bf16[1,32,1024]{2,1,0:T(8,128)(2,1)}, bf16[1,32,1024]{2,1,0:T(8,128)(2,1)S(1)}, u32[]{:S(2)}, u32[]{:S(2)}) collective-permute-start(bf16[1,32,1024]{2,1,0:T(8,128)(2,1)} %bitcast.16), channel_id=1, source_target_pairs={{0,16},{4,20},{8,24},{12,28},{16,0},{20,4},{24,8},{28,12},{1,17},{... | collective-permute-start | bytes 196616 | tf_op jit(solution)/shard_map/ppermute | solution.py:425
  46.5 6.4 %copy-start.1 = (bf16[32,1024]{1,0:T(8,128)(2,1)S(1)}, bf16[32,1024]{1,0:T(8,128)(2,1)}, u32[]{:S(2)}) copy-start(bf16[32,1024]{1,0:T(8,128)(2,1)} %shard_map.99) | copy-start | bytes 196612
  46.5 6.4 %collective-permute-start.5 = (bf16[2,32,1024]{2,1,0:T(8,128)(2,1)S(1)}, bf16[2,32,1024]{2,1,0:T(8,128)(2,1)S(1)}, u32[]{:S(2)}, u32[]{:S(2)}) collective-permute-start(bf16[2,32,1024]{2,1,0:T(8,128)(2,1)S(1)} %pad_maximum_fusion.2), channel_id=1, source_target_pairs={{0,8},{4,12},{8,0},{12,4},{16,24},{20,28},{24,16},{28,20},{1,9},{5... | collective-permute-start | bytes 393224 | tf_op jit(solution)/shard_map/ppermute | solution.py:425
  48.2 0.8 copy-start
  51.7 11.8 %collective-permute-start.10 = (f32[3,32,768]{2,1,0:T(8,128)}, f32[3,32,768]{2,1,0:T(8,128)S(1)}, u32[]{:S(2)}, u32[]{:S(2)}) collective-permute-start(f32[3,32,768]{2,1,0:T(8,128)} %get-tuple-element.18), channel_id=1, source_target_pairs={{0,4},{4,0},{8,12},{12,8},{16,20},{20,16},{24,28},{28,24},{1,5},{5... | collective-permute-start | bytes 884744 | tf_op jit(solution)/shard_map/ppermute | solution.py:57
  52.2 11.2 %collective-permute-start.11 = (f32[3,32,768]{2,1,0:T(8,128)}, f32[3,32,768]{2,1,0:T(8,128)S(1)}, u32[]{:S(2)}, u32[]{:S(2)}) collective-permute-start(f32[3,32,768]{2,1,0:T(8,128)} %get-tuple-element.19), channel_id=1, source_target_pairs={{4,8},{12,16},{20,24},{8,4},{16,12},{24,20},{5,9},{13,17},{21,25},... | collective-permute-start | bytes 884744 | tf_op jit(solution)/shard_map/ppermute | solution.py:57
  53.0 15.5 %collective-permute-start.6 = (bf16[4,32,1024]{2,1,0:T(8,128)(2,1)S(1)}, bf16[4,32,1024]{2,1,0:T(8,128)(2,1)S(1)}, u32[]{:S(2)}, u32[]{:S(2)}) collective-permute-start(bf16[4,32,1024]{2,1,0:T(8,128)(2,1)S(1)} %pad_maximum_fusion.1), channel_id=1, source_target_pairs={{0,4},{4,0},{8,12},{12,8},{16,20},{20,16},{24,28},{28,24},{1,5},{5... | collective-permute-start | bytes 786440 | tf_op jit(solution)/shard_map/ppermute | solution.py:425
  56.8 11.0 %copy-start.12 = (s32[1,1,1,7]{3,2,1,0:T(1,128)S(1)}, s32[1,1,1,7]{3,2,1,0:T(1,128)}, u32[]{:S(2)}) copy-start(s32[1,1,1,7]{3,2,1,0:T(1,128)} %param.12) | copy-start | bytes 88
  63.5 0.7 copy-start.3
  64.2 0.7 copy-start.4
  67.9 12.4 %collective-permute-start.12 = (f32[38,8,768]{2,1,0:T(8,128)}, f32[38,8,768]{2,1,0:T(8,128)S(1)}, u32[]{:S(2)}, u32[]{:S(2)}) collective-permute-start(f32[38,8,768]{2,1,0:T(8,128)} %shard_map.103), channel_id=1, source_target_pairs={{0,1},{1,0},{2,3},{3,2},{4,5},{5,4},{6,7},{7,6},{8,9},{9,8},{10,11... | collective-permute-start | bytes 2801672 | tf_op jit(solution)/shard_map/ppermute | solution.py:481
  68.5 2.6 %collective-permute-start.7 = (bf16[8,32,1024]{2,1,0:T(8,128)(2,1)S(1)}, bf16[8,32,1024]{2,1,0:T(8,128)(2,1)S(1)}, u32[]{:S(2)}, u32[]{:S(2)}) collective-permute-start(bf16[8,32,1024]{2,1,0:T(8,128)(2,1)S(1)} %pad_maximum_fusion), channel_id=1, source_target_pairs={{0,1},{1,0},{2,3},{3,2},{4,5},{5,4},{6,7},{7,6},{8,9},{9,8},{10,11... | collective-permute-start | bytes 1572872 | tf_op jit(solution)/shard_map/ppermute | solution.py:429
  71.2 1.0 copy-start.2
  78.8 29.6 %collective-permute-start.8 = (f32[32,512]{1,0:T(8,128)}, f32[32,512]{1,0:T(8,128)S(1)}, u32[]{:S(2)}, u32[]{:S(2)}) collective-permute-start(f32[32,512]{1,0:T(8,128)} %get-tuple-element.17), channel_id=1, source_target_pairs={{0,2},{2,0},{1,3},{3,1},{4,6},{6,4},{5,7},{7,5},{8,10},{10,8},{9,1... | collective-permute-start | bytes 196616 | tf_op jit(solution)/shard_map/ppermute | solution.py:447
  80.3 1.0 copy-start.5
  108.4 0.6 copy-start.8

commit v2 on v1

v2 whole, which is shorter than its diff:
```python
import functools
import math

import jax
import jax.numpy as jnp
from jax import lax
from jax.experimental import pallas as pl
from jax.experimental.pallas import tpu as pltpu
from jax.sharding import PartitionSpec as P

E = 32
LANES = 128
ROWS = 8
HALO = 3


def roll(value, shift, axis):
    return pltpu.roll(value, shift % value.shape[axis], axis)


def lane_ids(value):
    return lax.broadcasted_iota(jnp.int32, value.shape, value.ndim - 1)


def held(value):
    return pltpu.with_memory_space_constraint(value, pltpu.VMEM)


VECTOR = pl.BlockSpec(memory_space=pltpu.VMEM)
SCALAR = pl.BlockSpec(memory_space=pltpu.SMEM)
PLACED = pl.BlockSpec(memory_space=pl.ANY)


def vector(shape, dtype=jnp.float32):
    return pltpu.VMEM(shape, dtype)


def plain(shape, dtype=jnp.float32):
    return jax.ShapeDtypeStruct(shape, dtype)


def size_of(a):
    return math.prod(a.shape) * jnp.dtype(a.dtype).itemsize


def call(kernel, operands, out_shape, in_specs=None, out_specs=None, scratch=(), room=8, work=1000, **kw):
    return pl.pallas_call(
        kernel,
        out_shape=out_shape,
        in_specs=in_specs or [VECTOR] * len(operands),
        out_specs=out_specs or [VECTOR] * len(out_shape),
        scratch_shapes=list(scratch),
        compiler_params=pltpu.CompilerParams(vmem_limit_bytes=room * 1024 * 1024),
        cost_estimate=pl.CostEstimate(flops=0, bytes_accessed=work * 3000, transcendentals=0),
        **kw,
    )(*operands)


def index(axis):
    return lax.axis_index(axis).astype(jnp.int32)


def pairs(count):
    first = [(i, i ^ 1) for i in range(count)]
    second = [(i, i + 1) for i in range(1, count - 1, 2)]
    return first, second + [(b, a) for a, b in second]


def swap(messages, axis):
    count = lax.axis_size(axis)
    return [held(lax.ppermute(m, axis, p)) for m, p in zip(messages, pairs(count))]


def doubling(count):
    steps = []
    while count > 1:
        count //= 2
        steps.append(count)
    return steps


def message_count(axis):
    return 1 if lax.axis_size(axis) == 2 else 2


def choose(odd, low, high, number):
    return jnp.where(odd == number, high, low)


def from_low(odd, received):
    other = received[1] if len(received) == 2 else jnp.zeros_like(received[0])
    return jnp.where(odd == 1, received[0], other)


def from_high(odd, received):
    other = received[1] if len(received) == 2 else jnp.zeros_like(received[0])
    return jnp.where(odd == 1, other, received[0])


def spread_matrix(cells, width):
    k = lax.broadcasted_iota(jnp.int32, (LANES, width), 0)
    cell = lax.broadcasted_iota(jnp.int32, (LANES, width), 1) // E
    part = k // 32
    hit = (k - part * 32 == cell) & (part < 3) & (cell < cells)
    return jnp.where(hit, 1.0, 0.0).astype(jnp.bfloat16)


def packed(compact, cells):
    compact = jnp.where(lane_ids(compact) < cells, compact, 0.0)
    high = compact.astype(jnp.bfloat16).astype(jnp.float32)
    rest = compact - high
    middle = rest.astype(jnp.bfloat16).astype(jnp.float32)
    low = (rest - middle).astype(jnp.bfloat16).astype(jnp.float32)
    axis = compact.ndim - 1
    return (high + roll(middle, 32, axis) + roll(low, 64, axis)).astype(jnp.bfloat16)


def spread(compact, width, cells):
    return jnp.dot(
        packed(compact, cells), spread_matrix(cells, width), preferred_element_type=jnp.float32
    )


def face_start_kernel(src, coef, inv, s_out, i_out, *messages):
    odd, side = index("gx") % 2, index("gz")
    rows_x, depth, width = src.shape
    cells = width // E
    c = jnp.swapaxes(1.0 / (6.0 + coef[...]), 1, 2)
    inv[...] = jnp.concatenate(
        [c, jnp.zeros((rows_x, depth, LANES - cells), jnp.float32)], axis=2
    )
    planes = []
    for d in range(3):
        s = jnp.where(side == 0, src[:, d, :], src[:, depth - 1 - d, :])
        i = jnp.where(side == 0, inv[:, d, :], inv[:, depth - 1 - d, :])
        planes.append([s, i])
    spreads = spread(jnp.concatenate([i for _, i in planes], axis=0), width, cells)
    for d in range(3):
        planes[d][1] = spreads[d * rows_x : (d + 1) * rows_x]
        s_out[d], i_out[d] = planes[d]
    for number, message in enumerate(messages):
        for d in range(2):
            for k in range(2):
                v = planes[d][k]
                row = 4 * k + 2 * d
                message[row : row + 2, :] = choose(odd, v[:2], v[rows_x - 2 :], number)


def edge_pair(s, i):
    lane = lane_ids(s[:, :LANES])
    low = jnp.where(lane < 2 * E, s[:, :LANES], roll(i[:, :LANES], 64, 1))
    high = jnp.where(lane < 2 * E, roll(s[:, -LANES:], 64, 1), i[:, -LANES:])
    return low, high


def face_side_kernel(nx, s_in, i_in, *refs):
    odd_x, odd_y = index("gx") % 2, index("gy") % 2
    got, messages = [r[...] for r in refs[:nx]], refs[nx:]
    rows_x = s_in.shape[1]
    below, above = from_low(odd_x, got), from_high(odd_x, got)
    pick = lax.broadcasted_iota(jnp.int32, below.shape, 0)
    s = jnp.where(pick == 0, roll(below, -1, 0), roll(above, 1, 0))
    i = jnp.where(pick == 0, roll(below, -5, 0), roll(above, -3, 0))
    s, i = (jnp.where(pick < 2, v, 0.0) for v in (s, i))
    parts = [edge_pair(s_in[0], i_in[0]), edge_pair(s_in[1], i_in[1]), edge_pair(s, i)]
    for number, message in enumerate(messages):
        row = 0
        for low, high in parts:
            message[row : row + low.shape[0], :] = choose(odd_y, low, high, number)
            row += low.shape[0]


def face_sweep_kernel(nx, ny, s_in, i_in, *refs):
    odd_x, odd_y = index("gx") % 2, index("gy") % 2
    got_x = [r[...] for r in refs[:nx]]
    got_y = [r[...] for r in refs[nx : nx + ny]]
    out, ext_s, ext_i = refs[nx + ny :]
    _, rows_x, width = s_in.shape
    below, above = from_low(odd_x, got_x), from_high(odd_x, got_x)
    left, right = from_low(odd_y, got_y), from_high(odd_y, got_y)
    lane = lane_ids(left)
    pad_s = jnp.where(lane < 2 * E, right, roll(left, 64, 1))
    pad_i = jnp.where(lane < 2 * E, roll(right, 64, 1), left)
    ext_s[...] = jnp.zeros(ext_s.shape, jnp.float32)
    ext_i[...] = jnp.zeros(ext_i.shape, jnp.float32)
    first, last = ROWS, ROWS + rows_x
    for ext, own, pad, k in ((ext_s, s_in, pad_s, 0), (ext_i, i_in, pad_i, 1)):
        for d in range(2):
            row = 4 * k + 2 * d
            ext[d, first:last, :width] = own[d]
            ext[d, first - 2 : first, :width] = below[row : row + 2]
            ext[d, last : last + 2, :width] = above[row : row + 2]
            ext[d, first:last, width:] = pad[d * rows_x : (d + 1) * rows_x]
        ext[0, first - 1 : first, width:] = pad[2 * rows_x : 2 * rows_x + 1]
        ext[0, last : last + 1, width:] = pad[2 * rows_x + 1 : 2 * rows_x + 2]

    def around(u):
        return roll(u, 1, 0) + roll(u, -1, 0) + roll(u, E, 1) + roll(u, -E, 1)

    s0, s1, i0, i1 = ext_s[0], ext_s[1], ext_i[0], ext_i[1]
    u0, u1 = s0 * i0, s1 * i1
    deep = s_in[2] * i_in[2]
    v0 = (s0 + (around(u0) + u1)) * i0
    own = (around(u1) + u0)[first:last, :width]
    v1 = (s_in[1] + (own + deep)) * i_in[1]
    face = (s_in[0] + (around(v0)[first:last, :width] + v1)) * i_in[0]
    pieces = []
    for cell in range(width // E):
        start = cell * E // LANES * LANES
        pieces.append(roll(face[:, start : start + LANES], -(cell * E - start), 1))
    stacked = jnp.concatenate(pieces, axis=0)
    out[...] = stacked.T[:E].astype(jnp.bfloat16)


def order_kernel(place, near_col, far_col, order, spot):
    rows_x, _, cells_y = place.shape
    at = place[...].reshape(rows_x, cells_y) if rows_x == 1 else place[:, 0, :]
    trace = lax.broadcasted_iota(jnp.int32, (rows_x, order.shape[1]), 1)
    for y in range(cells_y):
        hit = at[:, y : y + 1] == trace
        order[y * rows_x : (y + 1) * rows_x, :] = jnp.where(hit, 1.0, 0.0).astype(jnp.bfloat16)
    at_x, at_z = index("gx"), index("gz")
    size_x = lax.axis_size("gx")
    for k in range(spot.shape[0]):
        block = near_col[0] if k == 0 else far_col[k - 1]
        apart = (block // 2) ^ at_x
        where = ((block % 2) ^ at_z) * size_x
        for n, step in enumerate(doubling(size_x)):
            where = where + jnp.where(apart & step > 0, 1 << n, 0)
        spot[k] = where


def trace_kernel(*refs):
    order, out = refs[-2:]
    if len(refs) == 3:
        face = refs[0][...]
    else:
        own, other = refs[0][...], refs[1][...]
        first = index("gy") == 0
        face = jnp.concatenate(
            [jnp.where(first, own, other), jnp.where(first, other, own)], axis=1
        )
    out[0] = jnp.dot(face, order[...], preferred_element_type=jnp.float32).astype(jnp.bfloat16)


def join_kernel(one, two, out):
    count = one.shape[0]
    out[:count] = one[...]
    out[count:] = two[...]


ACROSS = (((1,), (1,)), ((), ()))


def operator_kernel(halves, wanted, here, there, near, far_v, far_u, order, *outs):
    count = wanted.shape[0] - 1
    rank = far_v.shape[0] // count
    across = functools.partial(
        lax.dot_general, dimension_numbers=ACROSS, preferred_element_type=jnp.float32
    )
    size = here.shape[0]

    def traces(k):
        at = wanted[k] % size
        return jnp.where(wanted[k] < size, here[at], there[at])

    rows = across(traces(0), near[...])
    far = jnp.concatenate([traces(1 + k) for k in range(count)], axis=0)
    products = across(far, far_v[...])
    group = lax.broadcasted_iota(jnp.int32, (E, count * rank), 1) // rank
    weights = jnp.zeros((E, count * rank), jnp.float32)
    for k in range(count):
        weights = jnp.where(group == k, products[k * E : (k + 1) * E], weights)
    rows = rows + jnp.dot(
        weights.astype(jnp.bfloat16), far_u[...], preferred_element_type=jnp.float32
    )
    high = rows.astype(jnp.bfloat16)
    rest = rows - high.astype(jnp.float32)
    middle = rest.astype(jnp.bfloat16)
    low = (rest - middle.astype(jnp.float32)).astype(jnp.bfloat16)
    placed = across(jnp.concatenate([high, middle, low], axis=0), order[...])
    placed = placed[:E] + (placed[E : 2 * E] + placed[2 * E :])
    if halves:
        half = placed.shape[1] // 2
        first = index("gy") == 0
        outs[0][...] = jnp.where(first, placed[:, :half], placed[:, half:])
        outs[1][...] = jnp.where(first, placed[:, half:], placed[:, :half])
    else:
        outs[0][...] = placed


def finish_kernel(count, *refs):
    parts = refs[:count]
    inv, slab, _, flux_out, out, sem = refs[count:]
    side = index("gz")
    rows_x, _, width = slab.shape
    total = parts[0][...]
    if count == 2:
        total = total + parts[1][...]
    wide = jnp.concatenate([total, jnp.zeros((LANES - E, total.shape[1]), jnp.float32)], axis=0).T
    columns = []
    for start in range(0, width // E, LANES // E):
        column = wide[start * rows_x : (start + 1) * rows_x]
        for k in range(1, LANES // E):
            column = column + roll(wide[(start + k) * rows_x : (start + k + 1) * rows_x], k * E, 1)
        columns.append(column)
    flux = jnp.concatenate(columns, axis=1)
    added = (flux * inv[0])[:, None, :]
    row = lax.broadcasted_iota(jnp.int32, slab.shape, 1)
    slab[...] = slab[...] + jnp.where(row == side * (ROWS - 1), added, 0.0)
    top = pl.multiple_of(side * (out.shape[1] - ROWS), ROWS)
    copy = pltpu.make_async_copy(slab, out.at[:, pl.ds(top, ROWS), :], sem)
    copy.start()
    flux_out[...] = flux[:, None, :]
    copy.wait()


def side_edge_kernel(source, inv, *messages):
    odd = index("gy") % 2
    cells = source.shape[2] // E
    c = inv[...]
    first, last = source[:, :, :LANES], source[:, :, source.shape[2] - LANES :]
    lane = lane_ids(c)
    width = HALO * E
    low = jnp.where(lane < width, first, roll(c, width, 2))
    high = jnp.where(lane < width, roll(last, width, 2), roll(c, width - (cells - HALO), 2))
    for number, message in enumerate(messages):
        message[...] = choose(odd, low, high, number)


def widen(cells, ring, s, c, left, right):
    lane = lane_ids(right)
    width = HALO * E
    axis = right.ndim - 1
    zero = jnp.zeros_like(right)
    after = jnp.where(lane < width, right, zero)
    before = jnp.where(lane >= LANES - width, roll(left, LANES - width, axis), zero)
    pads = [after + before] if ring - cells == LANES // E else [after, before]
    own = jnp.where(lane < cells, c, zero)
    c_after = jnp.where((lane >= cells) & (lane < cells + HALO), roll(right, cells - width, axis), zero)
    c_before = jnp.where(
        (lane >= ring - HALO) & (lane < ring), roll(left, ring - HALO - width, axis), zero
    )
    return [s, *pads], own + c_after + c_before


def row_edge_kernel(cells, ring, ny, source, inv, *refs):
    odd_x, odd_y = index("gx") % 2, index("gy") % 2
    got_y, messages = refs[:ny], refs[ny:]
    rows_x = source.shape[0]
    for k in range(HALO):
        sides = []
        for row in (k, rows_x - HALO + k):
            got = [r[row] for r in got_y]
            parts, compact = widen(
                cells, ring, source[row], inv[row], from_low(odd_y, got), from_high(odd_y, got)
            )
            sides.append(jnp.concatenate([*parts, compact], axis=1))
        for number, message in enumerate(messages):
            message[k] = choose(odd_x, sides[0], sides[1], number)


def depth_edge_kernel(cells, ring, ny, nx, source, inv, *refs):
    odd_x, odd_y, side = index("gx") % 2, index("gy") % 2, index("gz")
    got_y, got_x, out = refs[:ny], refs[ny : ny + nx], refs[-1]
    rows_x, depth, _ = source.shape
    inner = lambda r: jnp.where(side == 0, r[:, depth - ROWS :, :], r[:, :ROWS, :])
    got = [inner(r) for r in got_y]
    parts, compact = widen(
        cells, ring, inner(source), inner(inv), from_low(odd_y, got), from_high(odd_y, got)
    )
    out[HALO : HALO + rows_x] = jnp.concatenate([*parts, compact], axis=2)
    got = [inner(r) for r in got_x]
    out[:HALO] = from_low(odd_x, got)
    out[HALO + rows_x :] = from_high(odd_x, got)


def assemble_kernel(cells, ring, ny, nx, source, inv, *refs):
    odd_x, odd_y, side = index("gx") % 2, index("gy") % 2, index("gz")
    got_y, got_x, got_z = refs[:ny], refs[ny : ny + nx], refs[ny + nx]
    ext_s, ext_i, one, compacts, matrix = refs[ny + nx + 1 :]
    rows_x, depth, width = source.shape
    wide = ring * E
    all_x, all_z = ext_s.shape[:2]
    matrix[...] = spread_matrix(ring, wide)
    row = lax.broadcasted_iota(jnp.int32, (ROWS, LANES), 0)
    start = side * (ROWS - HALO)
    near = (row >= start) & (row < start + HALO)

    def place(x, parts, compact):
        zone = got_z[x]
        lanes = jnp.where(near, zone[:, wide:], 0.0)
        compacts[pl.ds(pl.multiple_of(x * all_z, ROWS), depth), :] = compact
        compacts[pl.ds(pl.multiple_of(x * all_z + depth, ROWS), ROWS), :] = lanes
        at = 0
        for part in parts:
            ext_s[x, :depth, at : at + part.shape[1]] = part
            at += part.shape[1]
        ext_s[x, depth:, :] = zone[:, :wide]

    def own(x, _):
        got = [r[x] for r in got_y]
        parts, compact = widen(
            cells, ring, source[x], inv[x], from_low(odd_y, got), from_high(odd_y, got)
        )
        place(x + HALO, parts, compact)
        return 0

    lax.fori_loop(0, rows_x, own, 0)
    for k in range(HALO):
        got = [r[k] for r in got_x]
        below, above = from_low(odd_x, got), from_high(odd_x, got)
        place(k, [below[:, :wide]], below[:, wide:])
        place(rows_x + HALO + k, [above[:, :wide]], above[:, wide:])
    group = 2

    def expand(n, _):
        rows = group * all_z
        some = packed(compacts[pl.ds(pl.multiple_of(n * rows, ROWS), rows), :], ring)
        inverse = jnp.dot(some, matrix[...], preferred_element_type=jnp.float32)
        for k in range(group):
            x = n * group + k
            value = inverse[k * all_z : (k + 1) * all_z]
            ext_i[x] = value
            one[x] = ext_s[x] * value
        return 0

    lax.fori_loop(0, all_x // group, expand, 0)


def swept(ext_s, ext_i, old, x):
    u = old[x]
    beside = old[x - 1] + old[x + 1]
    beside = beside + (roll(u, 1, 0) + roll(u, -1, 0)) + (roll(u, E, 1) + roll(u, -E, 1))
    return (ext_s[x] + beside) * ext_i[x]


def sweep_kernel(margin, ext_s, ext_i, old, new):
    def step(x, _):
        new[x] = swept(ext_s, ext_i, old, x)
        return 0

    lax.fori_loop(margin, old.shape[0] - margin, step, 0)


def last_sweep_kernel(ext_s, ext_i, old, out, slab):
    side = index("gz")
    rows_x, depth, width = out.shape

    def step(x, _):
        new = swept(ext_s, ext_i, old, x + HALO)[:depth, :width]
        out[x] = new
        slab[x] = jnp.where(side == 0, new[:ROWS], new[depth - ROWS :])
        return 0

    lax.fori_loop(0, rows_x, step, 0)


def body(source, coef, face_trace, near_col, far_col, near_tile, far_u, far_v):
    rows_x, depth, width = source.shape
    cells = coef.shape[2]
    groups = lax.axis_size("gy")
    size_x = lax.axis_size("gx")
    tile = near_tile.shape[3]
    count = far_u.shape[3]
    rank = far_u.shape[4]
    nx, ny = message_count("gx"), message_count("gy")
    bf16 = jnp.bfloat16
    both = [(0, 1), (1, 0)]
    source = held(source)
    coef = held(coef.transpose(0, 2, 1))

    planes = vector((3, rows_x, width))
    inv, s_face, i_face, *out_x = call(
        face_start_kernel, (source, coef),
        [vector((rows_x, depth, LANES)), planes, planes] + [vector((ROWS, width))] * nx,
    )
    got_x = swap(out_x, "gx")
    out_y = call(
        functools.partial(face_side_kernel, nx), (s_face, i_face, *got_x),
        [vector((2 * rows_x + ROWS, LANES))] * ny, work=200,
    )
    got_y = swap(out_y, "gy")
    ext = pltpu.VMEM((2, rows_x + 2 * ROWS, width + LANES), jnp.float32)
    part = rows_x * cells
    (face,) = call(
        functools.partial(face_sweep_kernel, nx, ny), (s_face, i_face, *got_x, *got_y),
        [(vector if groups == 2 else plain)((E, part), bf16)], scratch=(ext, ext), work=500,
    )

    order, spot = call(
        order_kernel, (face_trace, near_col.reshape(1), far_col.reshape(count)),
        [vector((tile, tile), bf16), pltpu.SMEM((count + 1,), jnp.int32)],
        in_specs=[VECTOR, SCALAR, SCALAR], out_specs=[VECTOR, SCALAR],
    )
    if groups == 2:
        faces = (face, held(lax.ppermute(face, "gy", both)))
    else:
        faces = (held(lax.all_gather(face, "gy", axis=1, tiled=True)),)
    (traces,) = call(trace_kernel, (*faces, order), [vector((1, E, tile), bf16)])
    for step in doubling(size_x):
        other = held(lax.ppermute(traces, "gx", [(i, i ^ step) for i in range(size_x)]))
        both_shape = (2 * traces.shape[0], E, tile)
        (traces,) = call(join_kernel, (traces, other), [vector(both_shape, bf16)], work=300)
    other = held(lax.ppermute(traces, "gz", both))

    halves = groups == 2
    rows = call(
        functools.partial(operator_kernel, halves),
        (spot, traces, other, held(near_tile.reshape(tile, tile)), held(far_v.reshape(count * rank, tile)),
         held(far_u.reshape(count * rank, tile)), order),
        [vector((E, part))] * 2 if halves else [plain((E, tile))],
        in_specs=[SCALAR] + [VECTOR] * 6, work=3000,
    )
    if halves:
        rows = (rows[0], held(lax.ppermute(rows[1], "gy", both)))
    else:
        rows = (held(lax.psum_scatter(rows[0], "gy", scatter_dimension=1, tiled=True)),)

    pad = LANES if groups == 2 else 2 * LANES
    ring = (width + pad) // E
    wide = width + pad
    out_y = call(side_edge_kernel, (source, inv), [vector((rows_x, depth, LANES))] * ny, work=500)
    vol_y = swap(out_y, "gy")
    out_x = call(
        functools.partial(row_edge_kernel, cells, ring, ny), (source, inv, *vol_y),
        [vector((HALO, depth, wide + LANES))] * nx, work=500,
    )
    vol_x = swap(out_x, "gx")
    all_x = rows_x + 2 * HALO
    (out_z,) = call(
        functools.partial(depth_edge_kernel, cells, ring, ny, nx), (source, inv, *vol_y, *vol_x),
        [vector((all_x, ROWS, wide + LANES))], work=500,
    )
    vol_z = held(lax.ppermute(out_z, "gz", both))
    all_z = depth + ROWS
    ext = vector((all_x, all_z, wide))
    ext_s, ext_i, one = call(
        functools.partial(assemble_kernel, cells, ring, ny, nx),
        (source, inv, *vol_y, *vol_x, vol_z), [ext, ext, ext], work=2000,
        scratch=(vector((all_x * all_z, LANES)), vector((LANES, wide), bf16)),
    )
    (two,) = call(functools.partial(sweep_kernel, 1), (ext_s, ext_i, one), [ext], work=2000)
    (three,) = call(functools.partial(sweep_kernel, 2), (ext_s, ext_i, two), [ext], work=2000)
    field, slab = call(
        last_sweep_kernel, (ext_s, ext_i, three),
        [plain(source.shape), vector((rows_x, ROWS, width))], work=3000,
    )

    flux, result = call(
        functools.partial(finish_kernel, len(rows)), (*rows, i_face, slab, field),
        [plain((rows_x, 1, width)), plain(source.shape)],
        in_specs=[VECTOR] * (len(rows) + 2) + [PLACED], out_specs=[VECTOR, PLACED],
        scratch=(pltpu.SemaphoreType.DMA,), input_output_aliases={len(rows) + 2: 1},
    )
    return (result, flux)


def solution(mesh):
    return jax.shard_map(
        body,
        mesh=mesh,
        in_specs=(
            P("gx", "gz", "gy"),
            P("gx", "gz", "gy"),
            P("gx", "gz", None),
            P("gx", "gz", "gy"),
            P("gx", "gz", "gy", None),
            P("gx", "gz", "gy", None, None),
            P("gx", "gz", "gy", None, None, None),
            P("gx", "gz", "gy", None, None, None),
        ),
        out_specs=(P("gx", "gz", "gy"), P("gx", "gz", "gy")),
        check_vma=False,
    )
```

time: 115 us -> 90.4 us (0.79); the launches traced: 113 us -> 90.2 us
  Pallas kernels: 60.1 us -> 30.1 us
  waiting for transfers between devices: 17.2 us -> 33.1 us
  local copies, waits for them, and re-layouts: 11.7 us -> 2.57 us
  other arithmetic: 2.27 us -> 0 us
  starting transfers between devices: 20.7 us -> 22.9 us
    pallas_call x11 -> x17, Pallas kernels: 60.1 us -> 30.1 us  [call(): pl.pallas_call(kernel, out_shape=out_shape, in_specs=in_specs or [VECTOR]...]
    ppermute x13, waiting for transfers between devices: 17.2 us -> 33.1 us  [the longest x6 21.2 us: swap(): lax.ppermute(m, axis, p)]
    unnamed x32 -> x16, local copies, waits for them, and re-layouts: 9.37 us -> 2.57 us
    ppermute x13, starting transfers between devices: 20.7 us -> 22.9 us  [the longest x6 12 us: swap(): lax.ppermute(m, axis, p)]
    reshape x1 -> x0, local copies, waits for them, and re-layouts: 1.36 us -> none  [body(): place = face_trace.reshape(rows_x, cells * groups).T.reshape(tile, 1)]
  transfers between devices with their start and end apart: 13 -> 13, of which waited for: 5 -> 7; matrix products, arithmetic and copies ran while one was open for 3% -> 0% of each run, Pallas kernels for 48% -> 30%
where the time goes in v2:
time: 90.4 us; the launch traced here: 90.2 us
  waiting for transfers between devices  33.1 us (37%)
  Pallas kernels  30.1 us (33%)
  starting transfers between devices  22.9 us (25%)
  local copies, waits for them, and re-layouts  2.57 us (3%)
  between operations  1.49 us (2%)
    pallas_call x17, Pallas kernels, call(): pl.pallas_call(kernel, out_shape=out_shape, in_specs=in_specs or [VECTOR]...  30.1 us
    ppermute x6, waiting for transfers between devices, swap(): lax.ppermute(m, axis, p)  21.2 us
    ppermute x6, starting transfers between devices, swap(): lax.ppermute(m, axis, p)  12 us
    ppermute x3, waiting for transfers between devices, body(): lax.ppermute(traces, 'gx', [(i, i ^ step) for i in range(size_x)])  9.95 us
    ppermute x3, starting transfers between devices, body(): lax.ppermute(traces, 'gx', [(i, i ^ step) for i in range(size_x)])  7.72 us
    unnamed x16, local copies, waits for them, and re-layouts  2.57 us
    ppermute x1, waiting for transfers between devices, body(): other = held(lax.ppermute(traces, 'gz', both))  1.9 us
  transfers between devices with their start and end apart: 13, of which 7 were waited for; matrix products, arithmetic and copies ran while one was open for 0% of the time, Pallas kernels for 30%

profile of v2, /device:TPU:0, one launch (start us, length us, event | category | flops | bytes accessed | tf_op | source)
XLA Modules:
  0.0 90.2 jit_solution(12606989443657205547)
XLA Ops:
  0.6 1.6 %copy-done = f32[32,32,512]{2,1,0:T(8,128)S(1)} copy-done((f32[32,32,512]{2,1,0:T(8,128)S(1)}, f32[32,32,512]{2,1,0:T(8,128)}, u32[]{:S(2)}) %copy-start) | copy-done | bytes 2097176
  2.2 0.9 %copy-done.3 = f32[32,32,16]{1,2,0:T(8,128)S(1)} copy-done((f32[32,32,16]{1,2,0:T(8,128)S(1)}, f32[32,32,16]{1,2,0:T(8,128)}, u32[]{:S(2)}) %copy-start.3) | copy-done | bytes 65560
  3.2 0.5 shard_map.96
  3.7 0.5 shard_map.104
  4.2 3.0 %collective-permute-start.9 = (f32[32,32,128]{2,1,0:T(8,128)S(1)}, f32[32,32,128]{2,1,0:T(8,128)S(1)}, u32[]{:S(2)}, u32[]{:S(2)}) collective-permute-start(f32[32,32,128]{2,1,0:T(8,128)S(1)} %shard_map.104), channel_id=1, source_target_pairs={{0,2},{2,0},{1,3},{3,1},{4,6},{6,4},{5,7},{7,5},{8,10},{10,8},{9,1... | collective-permute-start | bytes 1572872 | tf_op jit(solution)/shard_map/ppermute | solution.py:71
  7.2 11.9 %collective-permute-done.9.refs_0_ = f32[32,32,128]{2,1,0:T(8,128)S(1)} collective-permute-done((f32[32,32,128]{2,1,0:T(8,128)S(1)}, f32[32,32,128]{2,1,0:T(8,128)S(1)}, u32[]{:S(2)}, u32[]{:S(2)}) %collective-permute-start.9) | collective-permute-done | bytes 524320 | tf_op jit(solution)/shard_map/ppermute | solution.py:71
  19.3 1.8 %collective-permute-start.10 = (f32[3,32,768]{2,1,0:T(8,128)S(1)}, f32[3,32,768]{2,1,0:T(8,128)S(1)}, u32[]{:S(2)}, u32[]{:S(2)}) collective-permute-start(f32[3,32,768]{2,1,0:T(8,128)S(1)} %get-tuple-element.29), channel_id=1, source_target_pairs={{0,4},{4,0},{8,12},{12,8},{16,20},{20,16},{24,28},{28,24},{1,5},{5... | collective-permute-start | bytes 884744 | tf_op jit(solution)/shard_map/ppermute | solution.py:71
  21.1 0.7 collective-permute-start.11
  21.7 4.3 %collective-permute-start = (f32[8,512]{1,0:T(8,128)S(1)}, f32[8,512]{1,0:T(8,128)S(1)}, u32[]{:S(2)}, u32[]{:S(2)}) collective-permute-start(f32[8,512]{1,0:T(8,128)S(1)} %get-tuple-element.23), channel_id=1, source_target_pairs={{0,4},{4,0},{8,12},{12,8},{16,20},{20,16},{24,28},{28,24},{1,5},{5... | collective-permute-start | bytes 49160 | tf_op jit(solution)/shard_map/ppermute | solution.py:71
  26.1 0.7 collective-permute-start.1
  26.7 6.8 %collective-permute-done.refs_0_ = f32[8,512]{1,0:T(8,128)S(1)} collective-permute-done((f32[8,512]{1,0:T(8,128)S(1)}, f32[8,512]{1,0:T(8,128)S(1)}, u32[]{:S(2)}, u32[]{:S(2)}) %collective-permute-start) | collective-permute-done | bytes 16416 | tf_op jit(solution)/shard_map/ppermute | solution.py:71
  33.6 1.6 %collective-permute-start.2 = (f32[72,128]{1,0:T(8,128)S(1)}, f32[72,128]{1,0:T(8,128)S(1)}, u32[]{:S(2)}, u32[]{:S(2)}) collective-permute-start(f32[72,128]{1,0:T(8,128)S(1)} %shard_map.97), channel_id=1, source_target_pairs={{0,2},{2,0},{1,3},{3,1},{4,6},{6,4},{5,7},{7,5},{8,10},{10,8},{9,1... | collective-permute-start | bytes 110600 | tf_op jit(solution)/shard_map/ppermute | solution.py:71
  35.2 2.5 %collective-permute-done.2.refs_2_ = f32[72,128]{1,0:T(8,128)S(1)} collective-permute-done((f32[72,128]{1,0:T(8,128)S(1)}, f32[72,128]{1,0:T(8,128)S(1)}, u32[]{:S(2)}, u32[]{:S(2)}) %collective-permute-start.2) | collective-permute-done | bytes 36896 | tf_op jit(solution)/shard_map/ppermute | solution.py:71
  37.7 0.4 shard_map.98.refs_0_
  38.1 1.6 %collective-permute-start.3 = (bf16[32,512]{1,0:T(8,128)(2,1)S(1)}, bf16[32,512]{1,0:T(8,128)(2,1)S(1)}, u32[]{:S(2)}, u32[]{:S(2)}) collective-permute-start(bf16[32,512]{1,0:T(8,128)(2,1)S(1)} %shard_map.98.refs_0_), channel_id=1, source_target_pairs={{0,2},{2,0},{1,3},{3,1},{4,6},{6,4},{5,7},{7,5},{8,10},{10,8},{9,1... | collective-permute-start | bytes 98312 | tf_op jit(solution)/shard_map/ppermute | solution.py:497
  40.4 1.8 %shard_map.95 = (bf16[1024,1024]{1,0:T(8,128)(2,1)S(1)}, s32[8]{0:T(128)S(4)}) custom-call(s32[32,1,32]{2,1,0:T(1,128)S(1)} %copy-done.6, s32[1]{0:T(128)} %bitcast.6.near_col, s32[7]{0:T(128)S(1)} %bitcast.11), custom_call_target="tpu_custom_call" | custom-call | bytes 3000000 | tf_op jit(solution)/shard_map/pallas_call | solution.py:47
  42.2 0.5 shard_map.99.one
  42.7 3.7 %collective-permute-start.4 = (bf16[1,32,1024]{2,1,0:T(8,128)(2,1)S(1)}, bf16[1,32,1024]{2,1,0:T(8,128)(2,1)S(1)}, u32[]{:S(2)}, u32[]{:S(2)}) collective-permute-start(bf16[1,32,1024]{2,1,0:T(8,128)(2,1)S(1)} %shard_map.99.one), channel_id=1, source_target_pairs={{0,16},{4,20},{8,24},{12,28},{16,0},{20,4},{24,8},{28,12},{1,17},{... | collective-permute-start | bytes 196616 | tf_op jit(solution)/shard_map/ppermute | solution.py:502
  46.4 2.3 %collective-permute-done.4.two = bf16[1,32,1024]{2,1,0:T(8,128)(2,1)S(1)} collective-permute-done((bf16[1,32,1024]{2,1,0:T(8,128)(2,1)S(1)}, bf16[1,32,1024]{2,1,0:T(8,128)(2,1)S(1)}, u32[]{:S(2)}, u32[]{:S(2)}) %collective-permute-start.4) | collective-permute-done | bytes 65568 | tf_op jit(solution)/shard_map/ppermute | solution.py:502
  48.7 2.6 %collective-permute-start.5 = (bf16[2,32,1024]{2,1,0:T(8,128)(2,1)S(1)}, bf16[2,32,1024]{2,1,0:T(8,128)(2,1)S(1)}, u32[]{:S(2)}, u32[]{:S(2)}) collective-permute-start(bf16[2,32,1024]{2,1,0:T(8,128)(2,1)S(1)} %shard_map.100.one), channel_id=1, source_target_pairs={{0,8},{4,12},{8,0},{12,4},{16,24},{20,28},{24,16},{28,20},{1,9},{5... | collective-permute-start | bytes 393224 | tf_op jit(solution)/shard_map/ppermute | solution.py:502
  51.3 0.2 shard_map.106
  51.6 2.6 %collective-permute-done.5.two = bf16[2,32,1024]{2,1,0:T(8,128)(2,1)S(1)} collective-permute-done((bf16[2,32,1024]{2,1,0:T(8,128)(2,1)S(1)}, bf16[2,32,1024]{2,1,0:T(8,128)(2,1)S(1)}, u32[]{:S(2)}, u32[]{:S(2)}) %collective-permute-start.5) | collective-permute-done | bytes 131104 | tf_op jit(solution)/shard_map/ppermute | solution.py:502
  54.3 1.5 %collective-permute-start.6 = (bf16[4,32,1024]{2,1,0:T(8,128)(2,1)S(1)}, bf16[4,32,1024]{2,1,0:T(8,128)(2,1)S(1)}, u32[]{:S(2)}, u32[]{:S(2)}) collective-permute-start(bf16[4,32,1024]{2,1,0:T(8,128)(2,1)S(1)} %shard_map.101.one), channel_id=1, source_target_pairs={{0,4},{4,0},{8,12},{12,8},{16,20},{20,16},{24,28},{28,24},{1,5},{5... | collective-permute-start | bytes 786440 | tf_op jit(solution)/shard_map/ppermute | solution.py:502
  55.8 5.0 %collective-permute-done.6.two = bf16[4,32,1024]{2,1,0:T(8,128)(2,1)S(1)} collective-permute-done((bf16[4,32,1024]{2,1,0:T(8,128)(2,1)S(1)}, bf16[4,32,1024]{2,1,0:T(8,128)(2,1)S(1)}, u32[]{:S(2)}, u32[]{:S(2)}) %collective-permute-start.6) | collective-permute-done | bytes 262176 | tf_op jit(solution)/shard_map/ppermute | solution.py:502
  60.8 1.9 %collective-permute-done.7.there = bf16[8,32,1024]{2,1,0:T(8,128)(2,1)S(1)} collective-permute-done((bf16[8,32,1024]{2,1,0:T(8,128)(2,1)S(1)}, bf16[8,32,1024]{2,1,0:T(8,128)(2,1)S(1)}, u32[]{:S(2)}, u32[]{:S(2)}) %collective-permute-start.7) | collective-permute-done | bytes 524320 | tf_op jit(solution)/shard_map/ppermute | solution.py:505
  62.7 2.6 %shard_map.103 = (f32[32,512]{1,0:T(8,128)S(1)}, f32[32,512]{1,0:T(8,128)S(1)}) custom-call(s32[8]{0:T(128)S(4)} %get-tuple-element.20.wanted, bf16[8,32,1024]{2,1,0:T(8,128)(2,1)S(1)} %shard_map.102.here, bf16[8,32,1024]{2,1,0:T(8,128)(2,1)S(1)} %collective-permute-done.7.there, bf16[1024,1024]{1,0:T(8,128)(2,1)S(1)} %bitcast.7, ...), custom_call_target="tpu_custom_call" | custom-call | bytes 9000000 | tf_op jit(solution)/shard_map/pallas_call | solution.py:47
  65.3 1.4 %collective-permute-start.8 = (f32[32,512]{1,0:T(8,128)S(1)}, f32[32,512]{1,0:T(8,128)S(1)}, u32[]{:S(2)}, u32[]{:S(2)}) collective-permute-start(f32[32,512]{1,0:T(8,128)S(1)} %get-tuple-element.27), channel_id=1, source_target_pairs={{0,2},{2,0},{1,3},{3,1},{4,6},{6,4},{5,7},{7,5},{8,10},{10,8},{9,1... | collective-permute-start | bytes 196616 | tf_op jit(solution)/shard_map/ppermute | solution.py:516
  66.7 7.4 %shard_map.107 = (f32[38,40,640]{2,1,0:T(8,128)S(1)}, f32[38,40,640]{2,1,0:T(8,128)S(1)}, f32[38,40,640]{2,1,0:T(8,128)S(1)}) custom-call(f32[32,32,512]{2,1,0:T(8,128)S(1)} %copy-done.1, f32[32,32,128]{2,1,0:T(8,128)S(1)} %get-tuple-element.28.inv, f32[32,32,128]{2,1,0:T(8,128)S(1)} %collective-permute-done.9.refs_0_, ...), custom_call_target="tpu_custom_call" | custom-call | bytes 6000000 | tf_op jit(solution)/shard_map/pallas_call | solution.py:47
  74.1 4.8 %shard_map.108.old = f32[38,40,640]{2,1,0:T(8,128)S(1)} custom-call(f32[38,40,640]{2,1,0:T(8,128)S(1)} %get-tuple-element.31.ext_s, f32[38,40,640]{2,1,0:T(8,128)S(1)} %get-tuple-element.32.ext_i, f32[38,40,640]{2,1,0:T(8,128)S(1)} %get-tuple-element.33.old), custom_call_target="tpu_custom_call" | custom-call | bytes 6000000 | tf_op jit(solution)/shard_map/pallas_call | solution.py:47
  78.9 4.5 %shard_map.109.old = f32[38,40,640]{2,1,0:T(8,128)S(1)} custom-call(f32[38,40,640]{2,1,0:T(8,128)S(1)} %get-tuple-element.31.ext_s, f32[38,40,640]{2,1,0:T(8,128)S(1)} %get-tuple-element.32.ext_i, f32[38,40,640]{2,1,0:T(8,128)S(1)} %shard_map.108.old), custom_call_target="tpu_custom_call" | custom-call | bytes 6000000 | tf_op jit(solution)/shard_map/pallas_call | solution.py:47
  83.4 5.0 %shard_map.110 = (f32[32,32,512]{2,1,0:T(8,128)}, f32[32,8,512]{2,1,0:T(8,128)S(1)}) custom-call(f32[38,40,640]{2,1,0:T(8,128)S(1)} %get-tuple-element.31.ext_s, f32[38,40,640]{2,1,0:T(8,128)S(1)} %get-tuple-element.32.ext_i, f32[38,40,640]{2,1,0:T(8,128)S(1)} %shard_map.109.old), custom_call_target="tpu_custom_call" | custom-call | bytes 9000000 | tf_op jit(solution)/shard_map/pallas_call | solution.py:47
  88.4 1.7 %shard_map.111 = (f32[32,1,512]{2,1,0:T(1,128)}, f32[32,32,512]{2,1,0:T(8,128)}) custom-call(f32[32,512]{1,0:T(8,128)S(1)} %get-tuple-element.26.refs_0_, f32[32,512]{1,0:T(8,128)S(1)} %collective-permute-done.8.refs_1_, f32[3,32,512]{2,1,0:T(8,128)S(1)} %get-tuple-element.22.i_in.refs_2_, ...), custom_call_target="tpu_custom_call", output_to_operand_aliasing={{1}: (4, {})} | custom-call | bytes 3000000 | tf_op jit(solution)/shard_map/pallas_call | solution.py:47
  (27 shorter events, 0.5 us)
Async XLA Ops:
  0.6 1.6 %copy-start = (f32[32,32,512]{2,1,0:T(8,128)S(1)}, f32[32,32,512]{2,1,0:T(8,128)}, u32[]{:S(2)}) copy-start(f32[32,32,512]{2,1,0:T(8,128)} %source.7) | copy-start | bytes 6291460
  2.2 0.9 %copy-start.3 = (f32[32,32,16]{1,2,0:T(8,128)S(1)}, f32[32,32,16]{1,2,0:T(8,128)}, u32[]{:S(2)}) copy-start(f32[32,32,16]{1,2,0:T(8,128)} %param.9) | copy-start | bytes 196612
  3.6 36.7 %copy-start.6 = (s32[32,1,32]{2,1,0:T(1,128)S(1)}, s32[32,1,32]{2,1,0:T(1,128)}, u32[]{:S(2)}) copy-start(s32[32,1,32]{2,1,0:T(1,128)} %place.1) | copy-start | bytes 12292
  3.6 36.7 %copy-start.7 = (s32[1,1,1,7]{3,2,1,0:T(1,128)S(1)}, s32[1,1,1,7]{3,2,1,0:T(1,128)}, u32[]{:S(2)}) copy-start(s32[1,1,1,7]{3,2,1,0:T(1,128)} %param.12) | copy-start | bytes 88
  4.1 47.2 %copy-start.1 = (f32[32,32,512]{2,1,0:T(8,128)S(1)}, f32[32,32,512]{2,1,0:T(8,128)}, u32[]{:S(2)}) copy-start(f32[32,32,512]{2,1,0:T(8,128)} %source.7) | copy-start | bytes 6291460
  4.2 15.0 %collective-permute-start.9 = (f32[32,32,128]{2,1,0:T(8,128)S(1)}, f32[32,32,128]{2,1,0:T(8,128)S(1)}, u32[]{:S(2)}, u32[]{:S(2)}) collective-permute-start(f32[32,32,128]{2,1,0:T(8,128)S(1)} %shard_map.104), channel_id=1, source_target_pairs={{0,2},{2,0},{1,3},{3,1},{4,6},{6,4},{5,7},{7,5},{8,10},{10,8},{9,1... | collective-permute-start | bytes 1572872 | tf_op jit(solution)/shard_map/ppermute | solution.py:71
  19.3 32.0 %collective-permute-start.10 = (f32[3,32,768]{2,1,0:T(8,128)S(1)}, f32[3,32,768]{2,1,0:T(8,128)S(1)}, u32[]{:S(2)}, u32[]{:S(2)}) collective-permute-start(f32[3,32,768]{2,1,0:T(8,128)S(1)} %get-tuple-element.29), channel_id=1, source_target_pairs={{0,4},{4,0},{8,12},{12,8},{16,20},{20,16},{24,28},{28,24},{1,5},{5... | collective-permute-start | bytes 884744 | tf_op jit(solution)/shard_map/ppermute | solution.py:71
  21.1 30.2 %collective-permute-start.11 = (f32[3,32,768]{2,1,0:T(8,128)S(1)}, f32[3,32,768]{2,1,0:T(8,128)S(1)}, u32[]{:S(2)}, u32[]{:S(2)}) collective-permute-start(f32[3,32,768]{2,1,0:T(8,128)S(1)} %get-tuple-element.30), channel_id=1, source_target_pairs={{4,8},{12,16},{20,24},{8,4},{16,12},{24,20},{5,9},{13,17},{21,25},... | collective-permute-start | bytes 884744 | tf_op jit(solution)/shard_map/ppermute | solution.py:71
  21.7 11.7 %collective-permute-start = (f32[8,512]{1,0:T(8,128)S(1)}, f32[8,512]{1,0:T(8,128)S(1)}, u32[]{:S(2)}, u32[]{:S(2)}) collective-permute-start(f32[8,512]{1,0:T(8,128)S(1)} %get-tuple-element.23), channel_id=1, source_target_pairs={{0,4},{4,0},{8,12},{12,8},{16,20},{20,16},{24,28},{28,24},{1,5},{5... | collective-permute-start | bytes 49160 | tf_op jit(solution)/shard_map/ppermute | solution.py:71
  26.1 7.4 %collective-permute-start.1 = (f32[8,512]{1,0:T(8,128)S(1)}, f32[8,512]{1,0:T(8,128)S(1)}, u32[]{:S(2)}, u32[]{:S(2)}) collective-permute-start(f32[8,512]{1,0:T(8,128)S(1)} %get-tuple-element.24), channel_id=1, source_target_pairs={{4,8},{12,16},{20,24},{8,4},{16,12},{24,20},{5,9},{13,17},{21,25},... | collective-permute-start | bytes 49160 | tf_op jit(solution)/shard_map/ppermute | solution.py:71
  33.6 4.1 %collective-permute-start.2 = (f32[72,128]{1,0:T(8,128)S(1)}, f32[72,128]{1,0:T(8,128)S(1)}, u32[]{:S(2)}, u32[]{:S(2)}) collective-permute-start(f32[72,128]{1,0:T(8,128)S(1)} %shard_map.97), channel_id=1, source_target_pairs={{0,2},{2,0},{1,3},{3,1},{4,6},{6,4},{5,7},{7,5},{8,10},{10,8},{9,1... | collective-permute-start | bytes 110600 | tf_op jit(solution)/shard_map/ppermute | solution.py:71
  38.1 4.1 %collective-permute-start.3 = (bf16[32,512]{1,0:T(8,128)(2,1)S(1)}, bf16[32,512]{1,0:T(8,128)(2,1)S(1)}, u32[]{:S(2)}, u32[]{:S(2)}) collective-permute-start(bf16[32,512]{1,0:T(8,128)(2,1)S(1)} %shard_map.98.refs_0_), channel_id=1, source_target_pairs={{0,2},{2,0},{1,3},{3,1},{4,6},{6,4},{5,7},{7,5},{8,10},{10,8},{9,1... | collective-permute-start | bytes 98312 | tf_op jit(solution)/shard_map/ppermute | solution.py:497
  42.2 20.5 %copy-start.2 = (bf16[1,1,1,1024,1024]{4,3,2,1,0:T(8,128)(2,1)S(1)}, bf16[1,1,1,1024,1024]{4,3,2,1,0:T(8,128)(2,1)}, u32[]{:S(2)}) copy-start(bf16[1,1,1,1024,1024]{4,3,2,1,0:T(8,128)(2,1)} %param.13) | copy-start | bytes 6291460
  42.2 20.5 %copy-start.4 = (bf16[1,1,1,7,16,1024]{5,4,3,2,1,0:T(8,128)(2,1)S(1)}, bf16[1,1,1,7,16,1024]{5,4,3,2,1,0:T(8,128)(2,1)}, u32[]{:S(2)}) copy-start(bf16[1,1,1,7,16,1024]{5,4,3,2,1,0:T(8,128)(2,1)} %param.15) | copy-start | bytes 688132
  42.2 20.5 %copy-start.5 = (bf16[1,1,1,7,16,1024]{5,4,3,2,1,0:T(8,128)(2,1)S(1)}, bf16[1,1,1,7,16,1024]{5,4,3,2,1,0:T(8,128)(2,1)}, u32[]{:S(2)}) copy-start(bf16[1,1,1,7,16,1024]{5,4,3,2,1,0:T(8,128)(2,1)} %param.14) | copy-start | bytes 688132
  42.7 6.0 %collective-permute-start.4 = (bf16[1,32,1024]{2,1,0:T(8,128)(2,1)S(1)}, bf16[1,32,1024]{2,1,0:T(8,128)(2,1)S(1)}, u32[]{:S(2)}, u32[]{:S(2)}) collective-permute-start(bf16[1,32,1024]{2,1,0:T(8,128)(2,1)S(1)} %shard_map.99.one), channel_id=1, source_target_pairs={{0,16},{4,20},{8,24},{12,28},{16,0},{20,4},{24,8},{28,12},{1,17},{... | collective-permute-start | bytes 196616 | tf_op jit(solution)/shard_map/ppermute | solution.py:502
  48.7 5.5 %collective-permute-start.5 = (bf16[2,32,1024]{2,1,0:T(8,128)(2,1)S(1)}, bf16[2,32,1024]{2,1,0:T(8,128)(2,1)S(1)}, u32[]{:S(2)}, u32[]{:S(2)}) collective-permute-start(bf16[2,32,1024]{2,1,0:T(8,128)(2,1)S(1)} %shard_map.100.one), channel_id=1, source_target_pairs={{0,8},{4,12},{8,0},{12,4},{16,24},{20,28},{24,16},{28,20},{1,9},{5... | collective-permute-start | bytes 393224 | tf_op jit(solution)/shard_map/ppermute | solution.py:502
  51.5 15.2 %collective-permute-start.12 = (f32[38,8,768]{2,1,0:T(8,128)S(1)}, f32[38,8,768]{2,1,0:T(8,128)S(1)}, u32[]{:S(2)}, u32[]{:S(2)}) collective-permute-start(f32[38,8,768]{2,1,0:T(8,128)S(1)} %shard_map.106), channel_id=1, source_target_pairs={{0,1},{1,0},{2,3},{3,2},{4,5},{5,4},{6,7},{7,6},{8,9},{9,8},{10,11... | collective-permute-start | bytes 2801672 | tf_op jit(solution)/shard_map/ppermute | solution.py:535
  54.3 6.4 %collective-permute-start.6 = (bf16[4,32,1024]{2,1,0:T(8,128)(2,1)S(1)}, bf16[4,32,1024]{2,1,0:T(8,128)(2,1)S(1)}, u32[]{:S(2)}, u32[]{:S(2)}) collective-permute-start(bf16[4,32,1024]{2,1,0:T(8,128)(2,1)S(1)} %shard_map.101.one), channel_id=1, source_target_pairs={{0,4},{4,0},{8,12},{12,8},{16,20},{20,16},{24,28},{28,24},{1,5},{5... | collective-permute-start | bytes 786440 | tf_op jit(solution)/shard_map/ppermute | solution.py:502
  60.8 2.0 %collective-permute-start.7 = (bf16[8,32,1024]{2,1,0:T(8,128)(2,1)S(1)}, bf16[8,32,1024]{2,1,0:T(8,128)(2,1)S(1)}, u32[]{:S(2)}, u32[]{:S(2)}) collective-permute-start(bf16[8,32,1024]{2,1,0:T(8,128)(2,1)S(1)} %shard_map.102.here), channel_id=1, source_target_pairs={{0,1},{1,0},{2,3},{3,2},{4,5},{5,4},{6,7},{7,6},{8,9},{9,8},{10,11... | collective-permute-start | bytes 1572872 | tf_op jit(solution)/shard_map/ppermute | solution.py:505
  65.3 23.1 %collective-permute-start.8 = (f32[32,512]{1,0:T(8,128)S(1)}, f32[32,512]{1,0:T(8,128)S(1)}, u32[]{:S(2)}, u32[]{:S(2)}) collective-permute-start(f32[32,512]{1,0:T(8,128)S(1)} %get-tuple-element.27), channel_id=1, source_target_pairs={{0,2},{2,0},{1,3},{3,1},{4,6},{6,4},{5,7},{7,5},{8,10},{10,8},{9,1... | collective-permute-start | bytes 196616 | tf_op jit(solution)/shard_map/ppermute | solution.py:516

commit v3 on v2

--- a/solution.py
+++ b/solution.py
@@ -26,9 +26,14 @@
     return pltpu.with_memory_space_constraint(value, pltpu.VMEM)
 
 
+def kept(value):
+    return pltpu.with_memory_space_constraint(value, pltpu.HBM)
+
+
 VECTOR = pl.BlockSpec(memory_space=pltpu.VMEM)
 SCALAR = pl.BlockSpec(memory_space=pltpu.SMEM)
 PLACED = pl.BlockSpec(memory_space=pl.ANY)
+MAIN = pl.BlockSpec(memory_space=pltpu.HBM)
 
 
 def vector(shape, dtype=jnp.float32):
@@ -43,17 +48,22 @@
     return math.prod(a.shape) * jnp.dtype(a.dtype).itemsize
 
 
-def call(kernel, operands, out_shape, in_specs=None, out_specs=None, scratch=(), room=8, work=1000, **kw):
+def call(kernel, operands, out_shape, in_specs=None, out_specs=None, scratch=(), room=8, work=1000, after=(), **kw):
+    given, tokens = len(operands), len(after)
+
+    def body(*refs):
+        kernel(*refs[:given], *refs[given + tokens :])
+
     return pl.pallas_call(
-        kernel,
+        body,
         out_shape=out_shape,
-        in_specs=in_specs or [VECTOR] * len(operands),
+        in_specs=(in_specs or [VECTOR] * given) + [PLACED] * tokens,
         out_specs=out_specs or [VECTOR] * len(out_shape),
         scratch_shapes=list(scratch),
         compiler_params=pltpu.CompilerParams(vmem_limit_bytes=room * 1024 * 1024),
         cost_estimate=pl.CostEstimate(flops=0, bytes_accessed=work * 3000, transcendentals=0),
         **kw,
-    )(*operands)
+    )(*operands, *after)
 
 
 def index(axis):
@@ -121,17 +131,27 @@
     )
 
 
-def face_start_kernel(src, coef, inv, s_out, i_out, *messages):
+def face_start_kernel(nx, source, coef, inv, s_out, i_out, *refs):
+    messages, (src, coefs, sems) = refs[:nx], refs[nx:]
     odd, side = index("gx") % 2, index("gz")
-    rows_x, depth, width = src.shape
+    rows_x, depth, width = source.shape
     cells = width // E
-    c = jnp.swapaxes(1.0 / (6.0 + coef[...]), 1, 2)
+    top = pl.multiple_of(side * (depth - ROWS), ROWS)
+    copies = [
+        pltpu.make_async_copy(coef, coefs, sems.at[0]),
+        pltpu.make_async_copy(source.at[:, pl.ds(top, ROWS), :], src, sems.at[1]),
+    ]
+    for copy in copies:
+        copy.start()
+    copies[0].wait()
+    c = jnp.swapaxes(1.0 / (6.0 + coefs[...]), 1, 2)
     inv[...] = jnp.concatenate(
         [c, jnp.zeros((rows_x, depth, LANES - cells), jnp.float32)], axis=2
     )
+    copies[1].wait()
     planes = []
     for d in range(3):
-        s = jnp.where(side == 0, src[:, d, :], src[:, depth - 1 - d, :])
+        s = jnp.where(side == 0, src[:, d, :], src[:, ROWS - 1 - d, :])
         i = jnp.where(side == 0, inv[:, d, :], inv[:, depth - 1 - d, :])
         planes.append([s, i])
     spreads = spread(jnp.concatenate([i for _, i in planes], axis=0), width, cells)
@@ -291,7 +311,7 @@
 
 def finish_kernel(count, *refs):
     parts = refs[:count]
-    inv, slab, _, flux_out, out, sem = refs[count:]
+    inv, slab, _, flux_out, out, held_flux, sems = refs[count:]
     side = index("gz")
     rows_x, _, width = slab.shape
     total = parts[0][...]
@@ -305,13 +325,16 @@
             column = column + roll(wide[(start + k) * rows_x : (start + k + 1) * rows_x], k * E, 1)
         columns.append(column)
     flux = jnp.concatenate(columns, axis=1)
+    held_flux[...] = flux[:, None, :]
+    out_copy = pltpu.make_async_copy(held_flux, flux_out, sems.at[0])
+    out_copy.start()
     added = (flux * inv[0])[:, None, :]
     row = lax.broadcasted_iota(jnp.int32, slab.shape, 1)
     slab[...] = slab[...] + jnp.where(row == side * (ROWS - 1), added, 0.0)
     top = pl.multiple_of(side * (out.shape[1] - ROWS), ROWS)
-    copy = pltpu.make_async_copy(slab, out.at[:, pl.ds(top, ROWS), :], sem)
+    copy = pltpu.make_async_copy(slab, out.at[:, pl.ds(top, ROWS), :], sems.at[1])
     copy.start()
-    flux_out[...] = flux[:, None, :]
+    out_copy.wait()
     copy.wait()
 
 
@@ -381,7 +404,8 @@
     ext_s, ext_i, one, compacts, matrix = refs[ny + nx + 1 :]
     rows_x, depth, width = source.shape
     wide = ring * E
-    all_x, all_z = ext_s.shape[:2]
+    all_z = depth + ROWS
+    total = ext_s.shape[0]
     matrix[...] = spread_matrix(ring, wide)
     row = lax.broadcasted_iota(jnp.int32, (ROWS, LANES), 0)
     start = side * (ROWS - HALO)
@@ -390,13 +414,15 @@
     def place(x, parts, compact):
         zone = got_z[x]
         lanes = jnp.where(near, zone[:, wide:], 0.0)
-        compacts[pl.ds(pl.multiple_of(x * all_z, ROWS), depth), :] = compact
-        compacts[pl.ds(pl.multiple_of(x * all_z + depth, ROWS), ROWS), :] = lanes
+        first = pl.ds(pl.multiple_of(x * all_z, ROWS), depth)
+        rest = pl.ds(pl.multiple_of(x * all_z + depth, ROWS), ROWS)
+        compacts[first, :] = compact
+        compacts[rest, :] = lanes
         at = 0
         for part in parts:
-            ext_s[x, :depth, at : at + part.shape[1]] = part
+            ext_s[first, at : at + part.shape[1]] = part
             at += part.shape[1]
-        ext_s[x, depth:, :] = zone[:, :wide]
+        ext_s[rest, :] = zone[:, :wide]
 
     def own(x, _):
         got = [r[x] for r in got_y]
@@ -406,54 +432,84 @@
         place(x + HALO, parts, compact)
         return 0
 
-    lax.fori_loop(0, rows_x, own, 0)
+    lax.fori_loop(0, rows_x, own, 0, unroll=2)
     for k in range(HALO):
         got = [r[k] for r in got_x]
         below, above = from_low(odd_x, got), from_high(odd_x, got)
         place(k, [below[:, :wide]], below[:, wide:])
         place(rows_x + HALO + k, [above[:, :wide]], above[:, wide:])
-    group = 2
+    chunk = max(n for n in range(2 * ROWS, 321, 2 * ROWS) if total % n == 0)
 
     def expand(n, _):
-        rows = group * all_z
-        some = packed(compacts[pl.ds(pl.multiple_of(n * rows, ROWS), rows), :], ring)
+        rows = pl.ds(pl.multiple_of(n * chunk, 2 * ROWS), chunk)
+        some = packed(compacts[rows, :], ring)
         inverse = jnp.dot(some, matrix[...], preferred_element_type=jnp.float32)
-        for k in range(group):
-            x = n * group + k
-            value = inverse[k * all_z : (k + 1) * all_z]
-            ext_i[x] = value
-            one[x] = ext_s[x] * value
+        ext_i[rows, :] = inverse
+        one[rows, :] = ext_s[rows, :] * inverse
         return 0
 
-    lax.fori_loop(0, all_x // group, expand, 0)
-
-
-def swept(ext_s, ext_i, old, x):
-    u = old[x]
-    beside = old[x - 1] + old[x + 1]
-    beside = beside + (roll(u, 1, 0) + roll(u, -1, 0)) + (roll(u, E, 1) + roll(u, -E, 1))
-    return (ext_s[x] + beside) * ext_i[x]
-
-
-def sweep_kernel(margin, ext_s, ext_i, old, new):
+    lax.fori_loop(0, total // chunk, expand, 0)
+
+
+def swept(ext_s, ext_i, old, x, all_z, depth, width, store):
+    at = lambda x, rows: pl.ds(pl.multiple_of(x * all_z, ROWS), rows)
+    tiles = old.shape[1] // LANES
+    lane = lax.broadcasted_iota(jnp.int32, (all_z, LANES), 1)
+    known = {}
+
+    def tile(j):
+        j %= tiles
+        if j not in known:
+            u = old[at(x, all_z), j * LANES : (j + 1) * LANES]
+            known[j] = (u, roll(u, E, 1), roll(u, -E, 1))
+        return known[j]
+
+    for j in range(width // LANES):
+        columns = slice(j * LANES, (j + 1) * LANES)
+        here = tile(j)
+        beside = old[at(x - 1, depth), columns] + old[at(x + 1, depth), columns]
+        up = roll(here[0], 1, 0) + roll(here[0], -1, 0)
+        side = jnp.where(lane < E, tile(j - 1)[1], here[1])
+        side = side + jnp.where(lane >= LANES - E, tile(j + 1)[2], here[2])
+        beside = beside + (up + side)[:depth]
+        new = (ext_s[at(x, depth), columns] + beside) * ext_i[at(x, depth), columns]
+        store(columns, new)
+
+
+def sweep_kernel(margin, all_z, ext_s, ext_i, old, new):
     def step(x, _):
-        new[x] = swept(ext_s, ext_i, old, x)
+        def store(columns, value):
+            new[pl.ds(pl.multiple_of(x * all_z, ROWS), all_z), columns] = value
+
+        swept(ext_s, ext_i, old, x, all_z, all_z, old.shape[1], store)
         return 0
 
-    lax.fori_loop(margin, old.shape[0] - margin, step, 0)
-
-
-def last_sweep_kernel(ext_s, ext_i, old, out, slab):
+    lax.fori_loop(margin, old.shape[0] // all_z - margin, step, 0)
+
+
+def last_sweep_kernel(ext_s, ext_i, old, out, slab, done, sems):
     side = index("gz")
     rows_x, depth, width = out.shape
+    all_z = depth + ROWS
 
     def step(x, _):
-        new = swept(ext_s, ext_i, old, x + HALO)[:depth, :width]
-        out[x] = new
-        slab[x] = jnp.where(side == 0, new[:ROWS], new[depth - ROWS :])
+        def store(columns, value):
+            done[x, :, columns] = value
+            slab[x, :, columns] = jnp.where(side == 0, value[:ROWS], value[depth - ROWS :])
+
+        swept(ext_s, ext_i, old, x + HALO, all_z, depth, width, store)
         return 0
 
-    lax.fori_loop(0, rows_x, step, 0)
+    pieces = sems.shape[0]
+    size = rows_x // pieces
+    copies = []
+    for n in range(pieces):
+        lax.fori_loop(n * size, (n + 1) * size, step, 0)
+        rows = slice(n * size, (n + 1) * size)
+        copies.append(pltpu.make_async_copy(done.at[rows], out.at[rows], sems.at[n]))
+        copies[-1].start()
+    for copy in copies:
+        copy.wait()
 
 
 def body(source, coef, face_trace, near_col, far_col, near_tile, far_u, far_v):
@@ -467,91 +523,103 @@
     nx, ny = message_count("gx"), message_count("gy")
     bf16 = jnp.bfloat16
     both = [(0, 1), (1, 0)]
-    source = held(source)
-    coef = held(coef.transpose(0, 2, 1))
+    pad = LANES if groups == 2 else 2 * LANES
+    ring = (width + pad) // E
+    wide = width + pad
+    all_x, all_z = rows_x + 2 * HALO, depth + ROWS
+    part = rows_x * cells
+    halves = groups == 2
+    coef = coef.transpose(0, 2, 1)
+    held_source = held(source)
 
     planes = vector((3, rows_x, width))
-    inv, s_face, i_face, *out_x = call(
-        face_start_kernel, (source, coef),
+    inv, s_face, i_face, *face_x = call(
+        functools.partial(face_start_kernel, nx), (kept(source), kept(coef)),
         [vector((rows_x, depth, LANES)), planes, planes] + [vector((ROWS, width))] * nx,
-    )
-    got_x = swap(out_x, "gx")
-    out_y = call(
+        in_specs=[MAIN, MAIN],
+        scratch=(vector((rows_x, ROWS, width)), vector(coef.shape), pltpu.SemaphoreType.DMA((2,))),
+    )
+    got_x = swap(face_x, "gx")
+    vol_y = call(
+        side_edge_kernel, (held_source, inv), [vector((rows_x, depth, LANES))] * ny, work=500,
+        after=face_x,
+    )
+    got_vol_y = swap(vol_y, "gy")
+    face_y = call(
         functools.partial(face_side_kernel, nx), (s_face, i_face, *got_x),
-        [vector((2 * rows_x + ROWS, LANES))] * ny, work=200,
-    )
-    got_y = swap(out_y, "gy")
+        [vector((2 * rows_x + ROWS, LANES))] * ny, work=200, after=vol_y,
+    )
+    got_y = swap(face_y, "gy")
     ext = pltpu.VMEM((2, rows_x + 2 * ROWS, width + LANES), jnp.float32)
-    part = rows_x * cells
     (face,) = call(
         functools.partial(face_sweep_kernel, nx, ny), (s_face, i_face, *got_x, *got_y),
-        [(vector if groups == 2 else plain)((E, part), bf16)], scratch=(ext, ext), work=500,
-    )
-
+        [(vector if halves else plain)((E, part), bf16)], scratch=(ext, ext), work=500,
+    )
+    if halves:
+        faces = (face, held(lax.ppermute(face, "gy", both)))
+    else:
+        faces = (held(lax.all_gather(face, "gy", axis=1, tiled=True)),)
+
+    vol_x = call(
+        functools.partial(row_edge_kernel, cells, ring, ny), (held_source, inv, *got_vol_y),
+        [vector((HALO, depth, wide + LANES))] * nx, work=500, after=(face,),
+    )
+    got_vol_x = swap(vol_x, "gx")
     order, spot = call(
         order_kernel, (face_trace, near_col.reshape(1), far_col.reshape(count)),
         [vector((tile, tile), bf16), pltpu.SMEM((count + 1,), jnp.int32)],
-        in_specs=[VECTOR, SCALAR, SCALAR], out_specs=[VECTOR, SCALAR],
-    )
-    if groups == 2:
-        faces = (face, held(lax.ppermute(face, "gy", both)))
-    else:
-        faces = (held(lax.all_gather(face, "gy", axis=1, tiled=True)),)
+        in_specs=[VECTOR, SCALAR, SCALAR], out_specs=[VECTOR, SCALAR], after=vol_x,
+    )
+
     (traces,) = call(trace_kernel, (*faces, order), [vector((1, E, tile), bf16)])
+    stages = []
     for step in doubling(size_x):
         other = held(lax.ppermute(traces, "gx", [(i, i ^ step) for i in range(size_x)]))
-        both_shape = (2 * traces.shape[0], E, tile)
-        (traces,) = call(join_kernel, (traces, other), [vector(both_shape, bf16)], work=300)
+        twice = (2 * traces.shape[0], E, tile)
+        (traces,) = call(join_kernel, (traces, other), [vector(twice, bf16)], work=300)
+        stages.append(traces)
     other = held(lax.ppermute(traces, "gz", both))
-
-    halves = groups == 2
+    (vol_z,) = call(
+        functools.partial(depth_edge_kernel, cells, ring, ny, nx),
+        (held_source, inv, *got_vol_y, *got_vol_x),
+        [vector((all_x, ROWS, wide + LANES))], work=500, after=(stages[-3],),
+    )
+    got_vol_z = held(lax.ppermute(vol_z, "gz", both))
+    ext = vector((all_x * all_z, wide))
+    ext_s, ext_i, one = call(
+        functools.partial(assemble_kernel, cells, ring, ny, nx),
+        (held_source, inv, *got_vol_y, *got_vol_x, got_vol_z), [ext, ext, ext], work=2000,
+        scratch=(vector((all_x * all_z, LANES)), vector((LANES, wide), bf16)),
+        after=(stages[-2],),
+    )
+    (two,) = call(functools.partial(sweep_kernel, 1, all_z), (ext_s, ext_i, one), [ext], work=2000)
+    (three,) = call(functools.partial(sweep_kernel, 2, all_z), (ext_s, ext_i, two), [ext], work=2000)
+
     rows = call(
         functools.partial(operator_kernel, halves),
-        (spot, traces, other, held(near_tile.reshape(tile, tile)), held(far_v.reshape(count * rank, tile)),
-         held(far_u.reshape(count * rank, tile)), order),
+        (spot, traces, other, held(near_tile.reshape(tile, tile)),
+         held(far_v.reshape(count * rank, tile)), held(far_u.reshape(count * rank, tile)), order),
         [vector((E, part))] * 2 if halves else [plain((E, tile))],
-        in_specs=[SCALAR] + [VECTOR] * 6, work=3000,
+        in_specs=[SCALAR] + [VECTOR] * 6, work=3000, after=(three,),
     )
     if halves:
-        rows = (rows[0], held(lax.ppermute(rows[1], "gy", both)))
+        sums = (rows[0], held(lax.ppermute(rows[1], "gy", both)))
     else:
-        rows = (held(lax.psum_scatter(rows[0], "gy", scatter_dimension=1, tiled=True)),)
-
-    pad = LANES if groups == 2 else 2 * LANES
-    ring = (width + pad) // E
-    wide = width + pad
-    out_y = call(side_edge_kernel, (source, inv), [vector((rows_x, depth, LANES))] * ny, work=500)
-    vol_y = swap(out_y, "gy")
-    out_x = call(
-        functools.partial(row_edge_kernel, cells, ring, ny), (source, inv, *vol_y),
-        [vector((HALO, depth, wide + LANES))] * nx, work=500,
-    )
-    vol_x = swap(out_x, "gx")
-    all_x = rows_x + 2 * HALO
-    (out_z,) = call(
-        functools.partial(depth_edge_kernel, cells, ring, ny, nx), (source, inv, *vol_y, *vol_x),
-        [vector((all_x, ROWS, wide + LANES))], work=500,
-    )
-    vol_z = held(lax.ppermute(out_z, "gz", both))
-    all_z = depth + ROWS
-    ext = vector((all_x, all_z, wide))
-    ext_s, ext_i, one = call(
-        functools.partial(assemble_kernel, cells, ring, ny, nx),
-        (source, inv, *vol_y, *vol_x, vol_z), [ext, ext, ext], work=2000,
-        scratch=(vector((all_x * all_z, LANES)), vector((LANES, wide), bf16)),
-    )
-    (two,) = call(functools.partial(sweep_kernel, 1), (ext_s, ext_i, one), [ext], work=2000)
-    (three,) = call(functools.partial(sweep_kernel, 2), (ext_s, ext_i, two), [ext], work=2000)
+        sums = (held(lax.psum_scatter(rows[0], "gy", scatter_dimension=1, tiled=True)),)
+    pieces = 4
     field, slab = call(
         last_sweep_kernel, (ext_s, ext_i, three),
-        [plain(source.shape), vector((rows_x, ROWS, width))], work=3000,
+        [plain(source.shape), vector((rows_x, ROWS, width))], work=2000,
+        out_specs=[MAIN, VECTOR], after=rows,
+        scratch=(vector(source.shape), pltpu.SemaphoreType.DMA((pieces,))),
     )
 
     flux, result = call(
-        functools.partial(finish_kernel, len(rows)), (*rows, i_face, slab, field),
+        functools.partial(finish_kernel, len(sums)), (*sums, i_face, slab, field),
         [plain((rows_x, 1, width)), plain(source.shape)],
-        in_specs=[VECTOR] * (len(rows) + 2) + [PLACED], out_specs=[VECTOR, PLACED],
-        scratch=(pltpu.SemaphoreType.DMA,), input_output_aliases={len(rows) + 2: 1},
+        in_specs=[VECTOR] * (len(sums) + 2) + [MAIN], out_specs=[MAIN, MAIN],
+        scratch=(vector((rows_x, 1, width)), pltpu.SemaphoreType.DMA((2,))),
+        input_output_aliases={len(sums) + 2: 1},
     )
     return (result, flux)
 

time: 90.4 us -> 75.6 us (0.84)
  waiting for transfers between devices: 33.1 us -> 24.7 us
  Pallas kernels: 30.1 us -> 26.8 us
  starting transfers between devices: 22.9 us -> 20.8 us
  local copies, waits for them, and re-layouts: 2.57 us -> 1.62 us
    ppermute x6, waiting for transfers between devices: 21.2 us -> 11.6 us  [swap(): lax.ppermute(m, axis, p)]
    pallas_call x17, Pallas kernels: 30.1 us -> 26.8 us  [call(): pl.pallas_call(body, out_shape=out_shape, in_specs=(in_specs or [VECTOR]...]
    ppermute x3, waiting for transfers between devices: 9.95 us -> 13.1 us  [body(): lax.ppermute(traces, 'gx', [(i, i ^ step) for i in range(size_x)])]
    ppermute x1, waiting for transfers between devices: 1.9 us -> 0.01 us  [body(): other = held(lax.ppermute(traces, 'gz', both))]
    ppermute x6, starting transfers between devices: 12 us -> 10.5 us  [swap(): lax.ppermute(m, axis, p)]
    unnamed x16 -> x14, local copies, waits for them, and re-layouts: 2.57 us -> 1.62 us
  transfers between devices with their start and end apart: 13 -> 13, of which waited for: 7 -> 6; matrix products, arithmetic and copies ran while one was open for 0% -> 0% of each run, Pallas kernels for 30% -> 27%
where the time goes in v3:
time: 75.6 us; the launch traced here: 75.4 us
  Pallas kernels  26.8 us (35%)
  waiting for transfers between devices  24.7 us (33%)
  starting transfers between devices  20.8 us (28%)
  local copies, waits for them, and re-layouts  1.62 us (2%)
  between operations  1.54 us (2%)
    pallas_call x17, Pallas kernels, call(): pl.pallas_call(body, out_shape=out_shape, in_specs=(in_specs or [VECTOR]...  26.8 us
    ppermute x3, waiting for transfers between devices, body(): lax.ppermute(traces, 'gx', [(i, i ^ step) for i in range(size_x)])  13.1 us
    ppermute x6, waiting for transfers between devices, swap(): lax.ppermute(m, axis, p)  11.6 us
    ppermute x6, starting transfers between devices, swap(): lax.ppermute(m, axis, p)  10.5 us
    ppermute x3, starting transfers between devices, body(): lax.ppermute(traces, 'gx', [(i, i ^ step) for i in range(size_x)])  6.97 us
    unnamed x14, local copies, waits for them, and re-layouts  1.62 us
    ppermute x1, starting transfers between devices, body(): sums = (rows[0], held(lax.ppermute(rows[1], 'gy', both)))  1.56 us
    ppermute x1, starting transfers between devices, body(): faces = (face, held(lax.ppermute(face, 'gy', both)))  1.52 us
  transfers between devices with their start and end apart: 13, of which 6 were waited for; matrix products, arithmetic and copies ran while one was open for 0% of the time, Pallas kernels for 27%

profile of v3, /device:TPU:0, one launch (start us, length us, event | category | flops | bytes accessed | tf_op | source)
XLA Modules:
  0.0 75.4 jit_solution(15269777603282999494)
XLA Ops:
  0.6 1.6 %shard_map.95 = (f32[32,32,128]{2,1,0:T(8,128)S(1)}, f32[3,32,512]{2,1,0:T(8,128)S(1)}, f32[3,32,512]{2,1,0:T(8,128)S(1)}, f32[8,512]{1,0:T(8,128)S(1)}, f32[8,512]{1,0:T(8,128)S(1)}) custom-call(f32[32,32,512]{2,1,0:T(8,128)} %refs_0_.11, f32[32,16,32]{2,1,0:T(8,128)} %bitcast.11), custom_call_target="tpu_custom_call" | custom-call | bytes 3000000 | tf_op jit(solution)/shard_map/pallas_call | solution.py:57
  2.3 1.6 %copy-done = f32[32,32,512]{2,1,0:T(8,128)S(1)} copy-done((f32[32,32,512]{2,1,0:T(8,128)S(1)}, f32[32,32,512]{2,1,0:T(8,128)}, u32[]{:S(2)}) %copy-start) | copy-done | bytes 2097176
  3.9 0.5 shard_map.96.refs_4_
  4.4 3.0 %collective-permute-start = (f32[32,32,128]{2,1,0:T(8,128)S(1)}, f32[32,32,128]{2,1,0:T(8,128)S(1)}, u32[]{:S(2)}, u32[]{:S(2)}) collective-permute-start(f32[32,32,128]{2,1,0:T(8,128)S(1)} %shard_map.96.refs_4_), channel_id=1, source_target_pairs={{0,2},{2,0},{1,3},{3,1},{4,6},{6,4},{5,7},{7,5},{8,10},{10,8},{9,1... | collective-permute-start | bytes 1572872 | tf_op jit(solution)/shard_map/ppermute | solution.py:81
  7.4 1.5 %collective-permute-start.1 = (f32[8,512]{1,0:T(8,128)S(1)}, f32[8,512]{1,0:T(8,128)S(1)}, u32[]{:S(2)}, u32[]{:S(2)}) collective-permute-start(f32[8,512]{1,0:T(8,128)S(1)} %get-tuple-element.21.refs_2_), channel_id=1, source_target_pairs={{0,4},{4,0},{8,12},{12,8},{16,20},{20,16},{24,28},{28,24},{1,5},{5... | collective-permute-start | bytes 49160 | tf_op jit(solution)/shard_map/ppermute | solution.py:81
  8.9 0.7 collective-permute-start.2
  9.5 1.6 %collective-permute-done.1.refs_2_ = f32[8,512]{1,0:T(8,128)S(1)} collective-permute-done((f32[8,512]{1,0:T(8,128)S(1)}, f32[8,512]{1,0:T(8,128)S(1)}, u32[]{:S(2)}, u32[]{:S(2)}) %collective-permute-start.1) | collective-permute-done | bytes 16416 | tf_op jit(solution)/shard_map/ppermute | solution.py:81
  11.1 0.1 shard_map.97
  11.2 0.1 collective-permute-start.3
  11.4 8.7 %collective-permute-done.3.refs_4_ = f32[72,128]{1,0:T(8,128)S(1)} collective-permute-done((f32[72,128]{1,0:T(8,128)S(1)}, f32[72,128]{1,0:T(8,128)S(1)}, u32[]{:S(2)}, u32[]{:S(2)}) %collective-permute-start.3) | collective-permute-done | bytes 36896 | tf_op jit(solution)/shard_map/ppermute | solution.py:81
  20.1 0.4 shard_map.98.refs_3_.refs_0_
  20.6 0.2 shard_map.99
  20.8 0.7 collective-permute-start.10
  21.4 4.6 %collective-permute-start.9 = (f32[3,32,768]{2,1,0:T(8,128)S(1)}, f32[3,32,768]{2,1,0:T(8,128)S(1)}, u32[]{:S(2)}, u32[]{:S(2)}) collective-permute-start(f32[3,32,768]{2,1,0:T(8,128)S(1)} %get-tuple-element.25.refs_3_), channel_id=1, source_target_pairs={{0,4},{4,0},{8,12},{12,8},{16,20},{20,16},{24,28},{28,24},{1,5},{5... | collective-permute-start | bytes 884744 | tf_op jit(solution)/shard_map/ppermute | solution.py:81
  26.0 1.5 %collective-permute-start.4 = (bf16[32,512]{1,0:T(8,128)(2,1)S(1)}, bf16[32,512]{1,0:T(8,128)(2,1)S(1)}, u32[]{:S(2)}, u32[]{:S(2)}) collective-permute-start(bf16[32,512]{1,0:T(8,128)(2,1)S(1)} %shard_map.98.refs_3_.refs_0_), channel_id=1, source_target_pairs={{0,2},{2,0},{1,3},{3,1},{4,6},{6,4},{5,7},{7,5},{8,10},{10,8},{9,1... | collective-permute-start | bytes 98312 | tf_op jit(solution)/shard_map/ppermute | solution.py:559
  28.2 1.8 %shard_map.100 = (bf16[1024,1024]{1,0:T(8,128)(2,1)S(1)}, s32[8]{0:T(128)S(4)}) custom-call(s32[32,1,32]{2,1,0:T(1,128)S(1)} %copy-done.5, s32[1]{0:T(128)} %bitcast.6.refs_1_, s32[7]{0:T(128)S(1)} %bitcast.10, f32[3,32,768]{2,1,0:T(8,128)S(1)} %get-tuple-element.25.refs_3_, f32[3,32,768]{2,1,0:T(8,128)S(1)} %get-tuple-element.26.refs_4_), custom_call_target="tpu_custom_call" | custom-call | bytes 3000000 | tf_op jit(solution)/shard_map/pallas_call | solution.py:57
  30.0 0.5 shard_map.101.refs_0_
  30.5 2.6 %collective-permute-start.5 = (bf16[1,32,1024]{2,1,0:T(8,128)(2,1)S(1)}, bf16[1,32,1024]{2,1,0:T(8,128)(2,1)S(1)}, u32[]{:S(2)}, u32[]{:S(2)}) collective-permute-start(bf16[1,32,1024]{2,1,0:T(8,128)(2,1)S(1)} %shard_map.101.refs_0_), channel_id=1, source_target_pairs={{0,16},{4,20},{8,24},{12,28},{16,0},{20,4},{24,8},{28,12},{1,17},{... | collective-permute-start | bytes 196616 | tf_op jit(solution)/shard_map/ppermute | solution.py:577
  33.1 2.6 %collective-permute-done.5.refs_1_ = bf16[1,32,1024]{2,1,0:T(8,128)(2,1)S(1)} collective-permute-done((bf16[1,32,1024]{2,1,0:T(8,128)(2,1)S(1)}, bf16[1,32,1024]{2,1,0:T(8,128)(2,1)S(1)}, u32[]{:S(2)}, u32[]{:S(2)}) %collective-permute-start.5) | collective-permute-done | bytes 65568 | tf_op jit(solution)/shard_map/ppermute | solution.py:577
  35.7 1.3 %collective-permute-done.9.refs_3_ = f32[3,32,768]{2,1,0:T(8,128)S(1)} collective-permute-done((f32[3,32,768]{2,1,0:T(8,128)S(1)}, f32[3,32,768]{2,1,0:T(8,128)S(1)}, u32[]{:S(2)}, u32[]{:S(2)}) %collective-permute-start.9) | collective-permute-done | bytes 294944 | tf_op jit(solution)/shard_map/ppermute | solution.py:81
  37.0 0.2 shard_map.105
  37.3 2.6 %collective-permute-start.6 = (bf16[2,32,1024]{2,1,0:T(8,128)(2,1)S(1)}, bf16[2,32,1024]{2,1,0:T(8,128)(2,1)S(1)}, u32[]{:S(2)}, u32[]{:S(2)}) collective-permute-start(bf16[2,32,1024]{2,1,0:T(8,128)(2,1)S(1)} %shard_map.102.refs_0_.refs_5_), channel_id=1, source_target_pairs={{0,8},{4,12},{8,0},{12,4},{16,24},{20,28},{24,16},{28,20},{1,9},{5... | collective-permute-start | bytes 393224 | tf_op jit(solution)/shard_map/ppermute | solution.py:577
  39.9 4.1 %collective-permute-done.6.refs_1_ = bf16[2,32,1024]{2,1,0:T(8,128)(2,1)S(1)} collective-permute-done((bf16[2,32,1024]{2,1,0:T(8,128)(2,1)S(1)}, bf16[2,32,1024]{2,1,0:T(8,128)(2,1)S(1)}, u32[]{:S(2)}, u32[]{:S(2)}) %collective-permute-start.6) | collective-permute-done | bytes 131104 | tf_op jit(solution)/shard_map/ppermute | solution.py:577
  44.0 1.7 %collective-permute-start.7 = (bf16[4,32,1024]{2,1,0:T(8,128)(2,1)S(1)}, bf16[4,32,1024]{2,1,0:T(8,128)(2,1)S(1)}, u32[]{:S(2)}, u32[]{:S(2)}) collective-permute-start(bf16[4,32,1024]{2,1,0:T(8,128)(2,1)S(1)} %shard_map.103.refs_0_.refs_6_), channel_id=1, source_target_pairs={{0,4},{4,0},{8,12},{12,8},{16,20},{20,16},{24,28},{28,24},{1,5},{5... | collective-permute-start | bytes 786440 | tf_op jit(solution)/shard_map/ppermute | solution.py:577
  45.8 6.4 %collective-permute-done.7.refs_1_ = bf16[4,32,1024]{2,1,0:T(8,128)(2,1)S(1)} collective-permute-done((bf16[4,32,1024]{2,1,0:T(8,128)(2,1)S(1)}, bf16[4,32,1024]{2,1,0:T(8,128)(2,1)S(1)}, u32[]{:S(2)}, u32[]{:S(2)}) %collective-permute-start.7) | collective-permute-done | bytes 262176 | tf_op jit(solution)/shard_map/ppermute | solution.py:577
  52.3 3.4 %shard_map.106 = (f32[1520,640]{1,0:T(8,128)S(1)}, f32[1520,640]{1,0:T(8,128)S(1)}, f32[1520,640]{1,0:T(8,128)S(1)}) custom-call(f32[32,32,512]{2,1,0:T(8,128)S(1)} %copy-done.1, f32[32,32,128]{2,1,0:T(8,128)S(1)} %get-tuple-element.20.refs_1_, f32[32,32,128]{2,1,0:T(8,128)S(1)} %collective-permute-done.refs_2_, ...), custom_call_target="tpu_custom_call" | custom-call | bytes 6000000 | tf_op jit(solution)/shard_map/pallas_call | solution.py:57
  55.6 5.1 %shard_map.107.refs_2_ = f32[1520,640]{1,0:T(8,128)S(1)} custom-call(f32[1520,640]{1,0:T(8,128)S(1)} %get-tuple-element.29.refs_0_, f32[1520,640]{1,0:T(8,128)S(1)} %get-tuple-element.30.refs_1_, f32[1520,640]{1,0:T(8,128)S(1)} %get-tuple-element.31.refs_2_), custom_call_target="tpu_custom_call" | custom-call | bytes 6000000 | tf_op jit(solution)/shard_map/pallas_call | solution.py:57
  60.7 4.8 %shard_map.108.refs_7_.refs_2_ = f32[1520,640]{1,0:T(8,128)S(1)} custom-call(f32[1520,640]{1,0:T(8,128)S(1)} %get-tuple-element.29.refs_0_, f32[1520,640]{1,0:T(8,128)S(1)} %get-tuple-element.30.refs_1_, f32[1520,640]{1,0:T(8,128)S(1)} %shard_map.107.refs_2_), custom_call_target="tpu_custom_call" | custom-call | bytes 6000000 | tf_op jit(solution)/shard_map/pallas_call | solution.py:57
  65.6 2.6 %shard_map.109 = (f32[32,512]{1,0:T(8,128)S(1)}, f32[32,512]{1,0:T(8,128)S(1)}) custom-call(s32[8]{0:T(128)S(4)} %get-tuple-element.27.refs_0_, bf16[8,32,1024]{2,1,0:T(8,128)(2,1)S(1)} %shard_map.104.refs_1_, bf16[8,32,1024]{2,1,0:T(8,128)(2,1)S(1)} %collective-permute-done.8.refs_2_, bf16[1024,1024]{1,0:T(8,128)(2,1)S(1)} %bitcast.7, ...), custom_call_target="tpu_custom_call" | custom-call | bytes 9000000 | tf_op jit(solution)/shard_map/pallas_call | solution.py:57
  68.2 1.6 %collective-permute-start.12 = (f32[32,512]{1,0:T(8,128)S(1)}, f32[32,512]{1,0:T(8,128)S(1)}, u32[]{:S(2)}, u32[]{:S(2)}) collective-permute-start(f32[32,512]{1,0:T(8,128)S(1)} %get-tuple-element.33.refs_4_), channel_id=1, source_target_pairs={{0,2},{2,0},{1,3},{3,1},{4,6},{6,4},{5,7},{7,5},{8,10},{10,8},{9,1... | collective-permute-start | bytes 196616 | tf_op jit(solution)/shard_map/ppermute | solution.py:606
  69.7 4.6 %shard_map.110 = (f32[32,32,512]{2,1,0:T(8,128)}, f32[32,8,512]{2,1,0:T(8,128)S(1)}) custom-call(f32[1520,640]{1,0:T(8,128)S(1)} %get-tuple-element.29.refs_0_, f32[1520,640]{1,0:T(8,128)S(1)} %get-tuple-element.30.refs_1_, f32[1520,640]{1,0:T(8,128)S(1)} %shard_map.108.refs_7_.refs_2_, f32[32,512]{1,0:T(8,128)S(1)} %get-tuple-element.32.refs_3_.refs_0_, ...), custom_call_target="tpu_custom_call" | custom-call | bytes 6000000 | tf_op jit(solution)/shard_map/pallas_call | solution.py:57
  74.3 1.1 %shard_map.111 = (f32[32,1,512]{2,1,0:T(1,128)}, f32[32,32,512]{2,1,0:T(8,128)}) custom-call(f32[32,512]{1,0:T(8,128)S(1)} %get-tuple-element.32.refs_3_.refs_0_, f32[32,512]{1,0:T(8,128)S(1)} %collective-permute-done.12.refs_1_, f32[3,32,512]{2,1,0:T(8,128)S(1)} %get-tuple-element.24.refs_1_.refs_2_, ...), custom_call_target="tpu_custom_call", output_to_operand_aliasing={{1}: (4, {})} | custom-call | bytes 3000000 | tf_op jit(solution)/shard_map/pallas_call | solution.py:57
  (25 shorter events, 0.3 us)
Async XLA Ops:
  0.6 19.9 %copy-start.1 = (f32[32,32,512]{2,1,0:T(8,128)S(1)}, f32[32,32,512]{2,1,0:T(8,128)}, u32[]{:S(2)}) copy-start(f32[32,32,512]{2,1,0:T(8,128)} %refs_0_.11) | copy-start | bytes 6291460
  2.3 1.6 %copy-start = (f32[32,32,512]{2,1,0:T(8,128)S(1)}, f32[32,32,512]{2,1,0:T(8,128)}, u32[]{:S(2)}) copy-start(f32[32,32,512]{2,1,0:T(8,128)} %refs_0_.11) | copy-start | bytes 6291460
  3.9 24.3 %copy-start.5 = (s32[32,1,32]{2,1,0:T(1,128)S(1)}, s32[32,1,32]{2,1,0:T(1,128)}, u32[]{:S(2)}) copy-start(s32[32,1,32]{2,1,0:T(1,128)} %refs_0_.9) | copy-start | bytes 12292
  3.9 24.3 %copy-start.6 = (s32[1,1,1,7]{3,2,1,0:T(1,128)S(1)}, s32[1,1,1,7]{3,2,1,0:T(1,128)}, u32[]{:S(2)}) copy-start(s32[1,1,1,7]{3,2,1,0:T(1,128)} %param.12) | copy-start | bytes 88
  4.4 16.2 %collective-permute-start = (f32[32,32,128]{2,1,0:T(8,128)S(1)}, f32[32,32,128]{2,1,0:T(8,128)S(1)}, u32[]{:S(2)}, u32[]{:S(2)}) collective-permute-start(f32[32,32,128]{2,1,0:T(8,128)S(1)} %shard_map.96.refs_4_), channel_id=1, source_target_pairs={{0,2},{2,0},{1,3},{3,1},{4,6},{6,4},{5,7},{7,5},{8,10},{10,8},{9,1... | collective-permute-start | bytes 1572872 | tf_op jit(solution)/shard_map/ppermute | solution.py:81
  7.4 3.7 %collective-permute-start.1 = (f32[8,512]{1,0:T(8,128)S(1)}, f32[8,512]{1,0:T(8,128)S(1)}, u32[]{:S(2)}, u32[]{:S(2)}) collective-permute-start(f32[8,512]{1,0:T(8,128)S(1)} %get-tuple-element.21.refs_2_), channel_id=1, source_target_pairs={{0,4},{4,0},{8,12},{12,8},{16,20},{20,16},{24,28},{28,24},{1,5},{5... | collective-permute-start | bytes 49160 | tf_op jit(solution)/shard_map/ppermute | solution.py:81
  8.9 2.3 %collective-permute-start.2 = (f32[8,512]{1,0:T(8,128)S(1)}, f32[8,512]{1,0:T(8,128)S(1)}, u32[]{:S(2)}, u32[]{:S(2)}) collective-permute-start(f32[8,512]{1,0:T(8,128)S(1)} %get-tuple-element.22.refs_3_), channel_id=1, source_target_pairs={{4,8},{12,16},{20,24},{8,4},{16,12},{24,20},{5,9},{13,17},{21,25},... | collective-permute-start | bytes 49160 | tf_op jit(solution)/shard_map/ppermute | solution.py:81
  11.2 8.9 %collective-permute-start.3 = (f32[72,128]{1,0:T(8,128)S(1)}, f32[72,128]{1,0:T(8,128)S(1)}, u32[]{:S(2)}, u32[]{:S(2)}) collective-permute-start(f32[72,128]{1,0:T(8,128)S(1)} %shard_map.97), channel_id=1, source_target_pairs={{0,2},{2,0},{1,3},{3,1},{4,6},{6,4},{5,7},{7,5},{8,10},{10,8},{9,1... | collective-permute-start | bytes 110600 | tf_op jit(solution)/shard_map/ppermute | solution.py:81
  20.8 14.9 %collective-permute-start.10 = (f32[3,32,768]{2,1,0:T(8,128)S(1)}, f32[3,32,768]{2,1,0:T(8,128)S(1)}, u32[]{:S(2)}, u32[]{:S(2)}) collective-permute-start(f32[3,32,768]{2,1,0:T(8,128)S(1)} %get-tuple-element.26.refs_4_), channel_id=1, source_target_pairs={{4,8},{12,16},{20,24},{8,4},{16,12},{24,20},{5,9},{13,17},{21,25},... | collective-permute-start | bytes 884744 | tf_op jit(solution)/shard_map/ppermute | solution.py:81
  21.4 15.5 %collective-permute-start.9 = (f32[3,32,768]{2,1,0:T(8,128)S(1)}, f32[3,32,768]{2,1,0:T(8,128)S(1)}, u32[]{:S(2)}, u32[]{:S(2)}) collective-permute-start(f32[3,32,768]{2,1,0:T(8,128)S(1)} %get-tuple-element.25.refs_3_), channel_id=1, source_target_pairs={{0,4},{4,0},{8,12},{12,8},{16,20},{20,16},{24,28},{28,24},{1,5},{5... | collective-permute-start | bytes 884744 | tf_op jit(solution)/shard_map/ppermute | solution.py:81
  26.0 4.0 %collective-permute-start.4 = (bf16[32,512]{1,0:T(8,128)(2,1)S(1)}, bf16[32,512]{1,0:T(8,128)(2,1)S(1)}, u32[]{:S(2)}, u32[]{:S(2)}) collective-permute-start(bf16[32,512]{1,0:T(8,128)(2,1)S(1)} %shard_map.98.refs_3_.refs_0_), channel_id=1, source_target_pairs={{0,2},{2,0},{1,3},{3,1},{4,6},{6,4},{5,7},{7,5},{8,10},{10,8},{9,1... | collective-permute-start | bytes 98312 | tf_op jit(solution)/shard_map/ppermute | solution.py:559
  30.5 5.2 %collective-permute-start.5 = (bf16[1,32,1024]{2,1,0:T(8,128)(2,1)S(1)}, bf16[1,32,1024]{2,1,0:T(8,128)(2,1)S(1)}, u32[]{:S(2)}, u32[]{:S(2)}) collective-permute-start(bf16[1,32,1024]{2,1,0:T(8,128)(2,1)S(1)} %shard_map.101.refs_0_), channel_id=1, source_target_pairs={{0,16},{4,20},{8,24},{12,28},{16,0},{20,4},{24,8},{28,12},{1,17},{... | collective-permute-start | bytes 196616 | tf_op jit(solution)/shard_map/ppermute | solution.py:577
  37.2 15.1 %collective-permute-start.11 = (f32[38,8,768]{2,1,0:T(8,128)S(1)}, f32[38,8,768]{2,1,0:T(8,128)S(1)}, u32[]{:S(2)}, u32[]{:S(2)}) collective-permute-start(f32[38,8,768]{2,1,0:T(8,128)S(1)} %shard_map.105), channel_id=1, source_target_pairs={{0,1},{1,0},{2,3},{3,2},{4,5},{5,4},{6,7},{7,6},{8,9},{9,8},{10,11... | collective-permute-start | bytes 2801672 | tf_op jit(solution)/shard_map/ppermute | solution.py:587
  37.3 6.7 %collective-permute-start.6 = (bf16[2,32,1024]{2,1,0:T(8,128)(2,1)S(1)}, bf16[2,32,1024]{2,1,0:T(8,128)(2,1)S(1)}, u32[]{:S(2)}, u32[]{:S(2)}) collective-permute-start(bf16[2,32,1024]{2,1,0:T(8,128)(2,1)S(1)} %shard_map.102.refs_0_.refs_5_), channel_id=1, source_target_pairs={{0,8},{4,12},{8,0},{12,4},{16,24},{20,28},{24,16},{28,20},{1,9},{5... | collective-permute-start | bytes 393224 | tf_op jit(solution)/shard_map/ppermute | solution.py:577
  44.0 8.1 %collective-permute-start.7 = (bf16[4,32,1024]{2,1,0:T(8,128)(2,1)S(1)}, bf16[4,32,1024]{2,1,0:T(8,128)(2,1)S(1)}, u32[]{:S(2)}, u32[]{:S(2)}) collective-permute-start(bf16[4,32,1024]{2,1,0:T(8,128)(2,1)S(1)} %shard_map.103.refs_0_.refs_6_), channel_id=1, source_target_pairs={{0,4},{4,0},{8,12},{12,8},{16,20},{20,16},{24,28},{28,24},{1,5},{5... | collective-permute-start | bytes 786440 | tf_op jit(solution)/shard_map/ppermute | solution.py:577
  52.2 13.3 %collective-permute-start.8 = (bf16[8,32,1024]{2,1,0:T(8,128)(2,1)S(1)}, bf16[8,32,1024]{2,1,0:T(8,128)(2,1)S(1)}, u32[]{:S(2)}, u32[]{:S(2)}) collective-permute-start(bf16[8,32,1024]{2,1,0:T(8,128)(2,1)S(1)} %shard_map.104.refs_1_), channel_id=1, source_target_pairs={{0,1},{1,0},{2,3},{3,2},{4,5},{5,4},{6,7},{7,6},{8,9},{9,8},{10,11... | collective-permute-start | bytes 1572872 | tf_op jit(solution)/shard_map/ppermute | solution.py:581
  60.7 4.8 %copy-start.2 = (bf16[1,1,1,1024,1024]{4,3,2,1,0:T(8,128)(2,1)S(1)}, bf16[1,1,1,1024,1024]{4,3,2,1,0:T(8,128)(2,1)}, u32[]{:S(2)}) copy-start(bf16[1,1,1,1024,1024]{4,3,2,1,0:T(8,128)(2,1)} %param.13) | copy-start | bytes 6291460
  60.7 4.8 %copy-start.3 = (bf16[1,1,1,7,16,1024]{5,4,3,2,1,0:T(8,128)(2,1)S(1)}, bf16[1,1,1,7,16,1024]{5,4,3,2,1,0:T(8,128)(2,1)}, u32[]{:S(2)}) copy-start(bf16[1,1,1,7,16,1024]{5,4,3,2,1,0:T(8,128)(2,1)} %param.15) | copy-start | bytes 688132
  60.7 4.8 %copy-start.4 = (bf16[1,1,1,7,16,1024]{5,4,3,2,1,0:T(8,128)(2,1)S(1)}, bf16[1,1,1,7,16,1024]{5,4,3,2,1,0:T(8,128)(2,1)}, u32[]{:S(2)}) copy-start(bf16[1,1,1,7,16,1024]{5,4,3,2,1,0:T(8,128)(2,1)} %param.14) | copy-start | bytes 688132
  68.2 6.1 %collective-permute-start.12 = (f32[32,512]{1,0:T(8,128)S(1)}, f32[32,512]{1,0:T(8,128)S(1)}, u32[]{:S(2)}, u32[]{:S(2)}) collective-permute-start(f32[32,512]{1,0:T(8,128)S(1)} %get-tuple-element.33.refs_4_), channel_id=1, source_target_pairs={{0,2},{2,0},{1,3},{3,1},{4,6},{6,4},{5,7},{7,5},{8,10},{10,8},{9,1... | collective-permute-start | bytes 196616 | tf_op jit(solution)/shard_map/ppermute | solution.py:606

commit v4 on v3

--- a/solution.py
+++ b/solution.py
@@ -338,17 +338,36 @@
     copy.wait()
 
 
-def side_edge_kernel(source, inv, *messages):
-    odd = index("gy") % 2
-    cells = source.shape[2] // E
-    c = inv[...]
-    first, last = source[:, :, :LANES], source[:, :, source.shape[2] - LANES :]
-    lane = lane_ids(c)
-    width = HALO * E
-    low = jnp.where(lane < width, first, roll(c, width, 2))
-    high = jnp.where(lane < width, roll(last, width, 2), roll(c, width - (cells - HALO), 2))
+def row_edge_kernel(source, inv, *messages):
+    odd = index("gx") % 2
+    rows_x, _, width = source.shape
     for number, message in enumerate(messages):
-        message[...] = choose(odd, low, high, number)
+        for k in range(HALO):
+            last = rows_x - HALO + k
+            message[k, :, :width] = choose(odd, source[k], source[last], number)
+            message[k, :, width:] = choose(odd, inv[k], inv[last], number)
+
+
+def side_edge_kernel(nx, source, inv, *refs):
+    odd_x, odd_y = index("gx") % 2, index("gy") % 2
+    got_x, messages = [r[...] for r in refs[:nx]], refs[nx:]
+    rows_x, _, width = source.shape
+    cells = width // E
+    halo = HALO * E
+
+    def put(rows, first, last, c):
+        lane = lane_ids(c)
+        low = jnp.where(lane < halo, first, roll(c, halo, 2))
+        high = jnp.where(lane < halo, roll(last, halo, 2), roll(c, halo - (cells - HALO), 2))
+        for number, message in enumerate(messages):
+            message[rows] = choose(odd_y, low, high, number)
+
+    put(slice(HALO, HALO + rows_x), source[:, :, :LANES], source[:, :, width - LANES :], inv[...])
+    for rows, edge in (
+        (slice(0, HALO), from_low(odd_x, got_x)),
+        (slice(HALO + rows_x, None), from_high(odd_x, got_x)),
+    ):
+        put(rows, edge[:, :, :LANES], edge[:, :, width - LANES : width], edge[:, :, width:])
 
 
 def widen(cells, ring, s, c, left, right):
@@ -367,41 +386,28 @@
     return [s, *pads], own + c_after + c_before
 
 
-def row_edge_kernel(cells, ring, ny, source, inv, *refs):
-    odd_x, odd_y = index("gx") % 2, index("gy") % 2
-    got_y, messages = refs[:ny], refs[ny:]
-    rows_x = source.shape[0]
-    for k in range(HALO):
-        sides = []
-        for row in (k, rows_x - HALO + k):
-            got = [r[row] for r in got_y]
-            parts, compact = widen(
-                cells, ring, source[row], inv[row], from_low(odd_y, got), from_high(odd_y, got)
-            )
-            sides.append(jnp.concatenate([*parts, compact], axis=1))
-        for number, message in enumerate(messages):
-            message[k] = choose(odd_x, sides[0], sides[1], number)
-
-
-def depth_edge_kernel(cells, ring, ny, nx, source, inv, *refs):
+def depth_edge_kernel(cells, ring, nx, ny, source, inv, *refs):
     odd_x, odd_y, side = index("gx") % 2, index("gy") % 2, index("gz")
-    got_y, got_x, out = refs[:ny], refs[ny : ny + nx], refs[-1]
-    rows_x, depth, _ = source.shape
+    got_x, got_y, out = refs[:nx], refs[nx : nx + ny], refs[-1]
+    rows_x, depth, width = source.shape
     inner = lambda r: jnp.where(side == 0, r[:, depth - ROWS :, :], r[:, :ROWS, :])
     got = [inner(r) for r in got_y]
-    parts, compact = widen(
-        cells, ring, inner(source), inner(inv), from_low(odd_y, got), from_high(odd_y, got)
-    )
-    out[HALO : HALO + rows_x] = jnp.concatenate([*parts, compact], axis=2)
-    got = [inner(r) for r in got_x]
-    out[:HALO] = from_low(odd_x, got)
-    out[HALO + rows_x :] = from_high(odd_x, got)
-
-
-def assemble_kernel(cells, ring, ny, nx, source, inv, *refs):
+    left, right = from_low(odd_y, got), from_high(odd_y, got)
+    edges = [inner(r) for r in got_x]
+    below, above = from_low(odd_x, edges), from_high(odd_x, edges)
+    for rows, s, c in (
+        (slice(0, HALO), below[:, :, :width], below[:, :, width:]),
+        (slice(HALO, HALO + rows_x), inner(source), inner(inv)),
+        (slice(HALO + rows_x, rows_x + 2 * HALO), above[:, :, :width], above[:, :, width:]),
+    ):
+        parts, compact = widen(cells, ring, s, c, left[rows], right[rows])
+        out[rows] = jnp.concatenate([*parts, compact], axis=2)
+
+
+def assemble_kernel(cells, ring, nx, ny, source, inv, *refs):
     odd_x, odd_y, side = index("gx") % 2, index("gy") % 2, index("gz")
-    got_y, got_x, got_z = refs[:ny], refs[ny : ny + nx], refs[ny + nx]
-    ext_s, ext_i, one, compacts, matrix = refs[ny + nx + 1 :]
+    got_x, got_y, got_z = refs[:nx], refs[nx : nx + ny], refs[nx + ny]
+    ext_s, ext_i, one, compacts, matrix = refs[nx + ny + 1 :]
     rows_x, depth, width = source.shape
     wide = ring * E
     all_z = depth + ROWS
@@ -411,7 +417,9 @@
     start = side * (ROWS - HALO)
     near = (row >= start) & (row < start + HALO)
 
-    def place(x, parts, compact):
+    def place(x, s, c):
+        got = [r[x] for r in got_y]
+        parts, compact = widen(cells, ring, s, c, from_low(odd_y, got), from_high(odd_y, got))
         zone = got_z[x]
         lanes = jnp.where(near, zone[:, wide:], 0.0)
         first = pl.ds(pl.multiple_of(x * all_z, ROWS), depth)
@@ -425,19 +433,15 @@
         ext_s[rest, :] = zone[:, :wide]
 
     def own(x, _):
-        got = [r[x] for r in got_y]
-        parts, compact = widen(
-            cells, ring, source[x], inv[x], from_low(odd_y, got), from_high(odd_y, got)
-        )
-        place(x + HALO, parts, compact)
+        place(x + HALO, source[x], inv[x])
         return 0
 
-    lax.fori_loop(0, rows_x, own, 0, unroll=2)
+    repeat(0, rows_x, own, 4)
     for k in range(HALO):
         got = [r[k] for r in got_x]
         below, above = from_low(odd_x, got), from_high(odd_x, got)
-        place(k, [below[:, :wide]], below[:, wide:])
-        place(rows_x + HALO + k, [above[:, :wide]], above[:, wide:])
+        place(k, below[:, :width], below[:, width:])
+        place(rows_x + HALO + k, above[:, :width], above[:, width:])
     chunk = max(n for n in range(2 * ROWS, 321, 2 * ROWS) if total % n == 0)
 
     def expand(n, _):
@@ -449,6 +453,12 @@
         return 0
 
     lax.fori_loop(0, total // chunk, expand, 0)
+
+
+def repeat(first, last, step, most):
+    count = last - first
+    unroll = max(n for n in range(1, most + 1) if count % n == 0)
+    lax.fori_loop(first, last, step, 0, unroll=unroll)
 
 
 def swept(ext_s, ext_i, old, x, all_z, depth, width, store):
@@ -476,7 +486,7 @@
         store(columns, new)
 
 
-def sweep_kernel(margin, all_z, ext_s, ext_i, old, new):
+def sweep_kernel(all_z, ext_s, ext_i, old, new):
     def step(x, _):
         def store(columns, value):
             new[pl.ds(pl.multiple_of(x * all_z, ROWS), all_z), columns] = value
@@ -484,7 +494,7 @@
         swept(ext_s, ext_i, old, x, all_z, all_z, old.shape[1], store)
         return 0
 
-    lax.fori_loop(margin, old.shape[0] // all_z - margin, step, 0)
+    repeat(1, old.shape[0] // all_z - 1, step, 6)
 
 
 def last_sweep_kernel(ext_s, ext_i, old, out, slab, done, sems):
@@ -504,7 +514,7 @@
     size = rows_x // pieces
     copies = []
     for n in range(pieces):
-        lax.fori_loop(n * size, (n + 1) * size, step, 0)
+        repeat(n * size, (n + 1) * size, step, 4)
         rows = slice(n * size, (n + 1) * size)
         copies.append(pltpu.make_async_copy(done.at[rows], out.at[rows], sems.at[n]))
         copies[-1].start()
@@ -540,15 +550,15 @@
         scratch=(vector((rows_x, ROWS, width)), vector(coef.shape), pltpu.SemaphoreType.DMA((2,))),
     )
     got_x = swap(face_x, "gx")
-    vol_y = call(
-        side_edge_kernel, (held_source, inv), [vector((rows_x, depth, LANES))] * ny, work=500,
-        after=face_x,
-    )
-    got_vol_y = swap(vol_y, "gy")
     face_y = call(
         functools.partial(face_side_kernel, nx), (s_face, i_face, *got_x),
-        [vector((2 * rows_x + ROWS, LANES))] * ny, work=200, after=vol_y,
-    )
+        [vector((2 * rows_x + ROWS, LANES))] * ny, work=200,
+    )
+    vol_x = call(
+        row_edge_kernel, (held_source, inv), [vector((HALO, depth, width + LANES))] * nx, work=200,
+        after=(face_y[0],),
+    )
+    got_vol_x = swap(vol_x, "gx")
     got_y = swap(face_y, "gy")
     ext = pltpu.VMEM((2, rows_x + 2 * ROWS, width + LANES), jnp.float32)
     (face,) = call(
@@ -560,57 +570,64 @@
     else:
         faces = (held(lax.all_gather(face, "gy", axis=1, tiled=True)),)
 
-    vol_x = call(
-        functools.partial(row_edge_kernel, cells, ring, ny), (held_source, inv, *got_vol_y),
-        [vector((HALO, depth, wide + LANES))] * nx, work=500, after=(face,),
-    )
-    got_vol_x = swap(vol_x, "gx")
     order, spot = call(
         order_kernel, (face_trace, near_col.reshape(1), far_col.reshape(count)),
         [vector((tile, tile), bf16), pltpu.SMEM((count + 1,), jnp.int32)],
-        in_specs=[VECTOR, SCALAR, SCALAR], out_specs=[VECTOR, SCALAR], after=vol_x,
-    )
-
+        in_specs=[VECTOR, SCALAR, SCALAR], out_specs=[VECTOR, SCALAR], work=2000, after=(face,),
+    )
     (traces,) = call(trace_kernel, (*faces, order), [vector((1, E, tile), bf16)])
-    stages = []
-    for step in doubling(size_x):
+    vol_y = call(
+        functools.partial(side_edge_kernel, nx), (held_source, inv, *got_vol_x),
+        [vector((all_x, depth, LANES))] * ny, work=300, after=(traces,),
+    )
+    got_vol_y = swap(vol_y, "gy")
+    steps = doubling(size_x)
+    for step in steps:
         other = held(lax.ppermute(traces, "gx", [(i, i ^ step) for i in range(size_x)]))
         twice = (2 * traces.shape[0], E, tile)
-        (traces,) = call(join_kernel, (traces, other), [vector(twice, bf16)], work=300)
-        stages.append(traces)
+        before = ()
+        if step == 1:
+            (vol_z,) = call(
+                functools.partial(depth_edge_kernel, cells, ring, nx, ny),
+                (held_source, inv, *got_vol_x, *got_vol_y),
+                [vector((all_x, ROWS, wide + LANES))], work=500, after=(traces,),
+            )
+            got_vol_z = held(lax.ppermute(vol_z, "gz", both))
+            ext = vector((all_x * all_z, wide))
+            ext_s, ext_i, one = call(
+                functools.partial(assemble_kernel, cells, ring, nx, ny),
+                (held_source, inv, *got_vol_x, *got_vol_y, got_vol_z), [ext, ext, ext], work=3000,
+                scratch=(vector((all_x * all_z, LANES)), vector((LANES, wide), bf16)),
+            )
+            before = (one,)
+        (traces,) = call(
+            join_kernel, (traces, other), [vector(twice, bf16)], work=300, after=before
+        )
     other = held(lax.ppermute(traces, "gz", both))
-    (vol_z,) = call(
-        functools.partial(depth_edge_kernel, cells, ring, ny, nx),
-        (held_source, inv, *got_vol_y, *got_vol_x),
-        [vector((all_x, ROWS, wide + LANES))], work=500, after=(stages[-3],),
-    )
-    got_vol_z = held(lax.ppermute(vol_z, "gz", both))
-    ext = vector((all_x * all_z, wide))
-    ext_s, ext_i, one = call(
-        functools.partial(assemble_kernel, cells, ring, ny, nx),
-        (held_source, inv, *got_vol_y, *got_vol_x, got_vol_z), [ext, ext, ext], work=2000,
-        scratch=(vector((all_x * all_z, LANES)), vector((LANES, wide), bf16)),
-        after=(stages[-2],),
-    )
-    (two,) = call(functools.partial(sweep_kernel, 1, all_z), (ext_s, ext_i, one), [ext], work=2000)
-    (three,) = call(functools.partial(sweep_kernel, 2, all_z), (ext_s, ext_i, two), [ext], work=2000)
+    (two,) = call(
+        functools.partial(sweep_kernel, all_z), (ext_s, ext_i, one), [ext], work=2500,
+        after=(traces,),
+    )
 
     rows = call(
         functools.partial(operator_kernel, halves),
         (spot, traces, other, held(near_tile.reshape(tile, tile)),
          held(far_v.reshape(count * rank, tile)), held(far_u.reshape(count * rank, tile)), order),
         [vector((E, part))] * 2 if halves else [plain((E, tile))],
-        in_specs=[SCALAR] + [VECTOR] * 6, work=3000, after=(three,),
+        in_specs=[SCALAR] + [VECTOR] * 6, work=2500, after=(two,),
     )
     if halves:
         sums = (rows[0], held(lax.ppermute(rows[1], "gy", both)))
     else:
         sums = (held(lax.psum_scatter(rows[0], "gy", scatter_dimension=1, tiled=True)),)
+    (three,) = call(
+        functools.partial(sweep_kernel, all_z), (ext_s, ext_i, two), [ext], work=2500, after=rows,
+    )
     pieces = 4
     field, slab = call(
         last_sweep_kernel, (ext_s, ext_i, three),
         [plain(source.shape), vector((rows_x, ROWS, width))], work=2000,
-        out_specs=[MAIN, VECTOR], after=rows,
+        out_specs=[MAIN, VECTOR],
         scratch=(vector(source.shape), pltpu.SemaphoreType.DMA((pieces,))),
     )
 

time: 75.6 us -> 61.4 us (0.81)
  waiting for transfers between devices: 24.7 us -> 12.3 us
  Pallas kernels: 26.8 us -> 21 us
  starting transfers between devices: 20.8 us -> 26.3 us
  local copies, waits for them, and re-layouts: 1.62 us -> 0.03 us
    ppermute x6, waiting for transfers between devices: 11.6 us -> 3.1 us  [swap(): lax.ppermute(m, axis, p)]
    pallas_call x17, Pallas kernels: 26.8 us -> 21 us  [call(): pl.pallas_call(body, out_shape=out_shape, in_specs=(in_specs or [VECTOR]...]
    ppermute x3, waiting for transfers between devices: 13.1 us -> 9.19 us  [body(): lax.ppermute(traces, 'gx', [(i, i ^ step) for i in range(size_x)])]
    ppermute x3, starting transfers between devices: 6.97 us -> 10.2 us  [body(): lax.ppermute(traces, 'gx', [(i, i ^ step) for i in range(size_x)])]
    ppermute x6, starting transfers between devices: 10.5 us -> 13 us  [swap(): lax.ppermute(m, axis, p)]
    unnamed x14 -> x12, local copies, waits for them, and re-layouts: 1.62 us -> 0.03 us
  transfers between devices with their start and end apart: 13 -> 13, of which waited for: 6 -> 5; matrix products, arithmetic and copies ran while one was open for 0% -> 0% of each run, Pallas kernels for 27% -> 24%
where the time goes in v4:
time: 61.4 us; the launch traced here: 61.2 us
  starting transfers between devices  26.3 us (43%)
  Pallas kernels  21 us (34%)
  waiting for transfers between devices  12.3 us (20%)
  between operations  1.56 us (3%)
    pallas_call x17, Pallas kernels, call(): pl.pallas_call(body, out_shape=out_shape, in_specs=(in_specs or [VECTOR]...  21 us
    ppermute x6, starting transfers between devices, swap(): lax.ppermute(m, axis, p)  13 us
    ppermute x3, starting transfers between devices, body(): lax.ppermute(traces, 'gx', [(i, i ^ step) for i in range(size_x)])  10.2 us
    ppermute x3, waiting for transfers between devices, body(): lax.ppermute(traces, 'gx', [(i, i ^ step) for i in range(size_x)])  9.19 us
    ppermute x6, waiting for transfers between devices, swap(): lax.ppermute(m, axis, p)  3.1 us
    ppermute x1, starting transfers between devices, body(): faces = (face, held(lax.ppermute(face, 'gy', both)))  1.99 us
  transfers between devices with their start and end apart: 13, of which 5 were waited for; matrix products, arithmetic and copies ran while one was open for 0% of the time, Pallas kernels for 24%

profile of v4, /device:TPU:0, one launch (start us, length us, event | category | flops | bytes accessed | tf_op | source)
XLA Modules:
  0.0 61.2 jit_solution(12492167472919605655)
XLA Ops:
  0.7 1.6 %shard_map.95 = (f32[32,32,128]{2,1,0:T(8,128)S(1)}, f32[3,32,512]{2,1,0:T(8,128)S(1)}, f32[3,32,512]{2,1,0:T(8,128)S(1)}, f32[8,512]{1,0:T(8,128)S(1)}, f32[8,512]{1,0:T(8,128)S(1)}) custom-call(f32[32,32,512]{2,1,0:T(8,128)} %refs_0_.11, f32[32,16,32]{2,1,0:T(8,128)} %bitcast.11), custom_call_target="tpu_custom_call" | custom-call | bytes 3000000 | tf_op jit(solution)/shard_map/pallas_call | solution.py:57
  2.3 3.0 %collective-permute-start = (f32[8,512]{1,0:T(8,128)S(1)}, f32[8,512]{1,0:T(8,128)S(1)}, u32[]{:S(2)}, u32[]{:S(2)}) collective-permute-start(f32[8,512]{1,0:T(8,128)S(1)} %get-tuple-element.22), channel_id=1, source_target_pairs={{0,4},{4,0},{8,12},{12,8},{16,20},{20,16},{24,28},{28,24},{1,5},{5... | collective-permute-start | bytes 49160 | tf_op jit(solution)/shard_map/ppermute | solution.py:81
  5.3 0.7 %collective-permute-start.1 = (f32[8,512]{1,0:T(8,128)S(1)}, f32[8,512]{1,0:T(8,128)S(1)}, u32[]{:S(2)}, u32[]{:S(2)}) collective-permute-start(f32[8,512]{1,0:T(8,128)S(1)} %get-tuple-element.23), channel_id=1, source_target_pairs={{4,8},{12,16},{20,24},{8,4},{16,12},{24,20},{5,9},{13,17},{21,25},... | collective-permute-start | bytes 49160 | tf_op jit(solution)/shard_map/ppermute | solution.py:81
  6.0 1.1 %collective-permute-done.refs_2_ = f32[8,512]{1,0:T(8,128)S(1)} collective-permute-done((f32[8,512]{1,0:T(8,128)S(1)}, f32[8,512]{1,0:T(8,128)S(1)}, u32[]{:S(2)}, u32[]{:S(2)}) %collective-permute-start) | collective-permute-done | bytes 16416 | tf_op jit(solution)/shard_map/ppermute | solution.py:81
  7.0 0.1 shard_map.96.refs_2_
  7.1 0.1 shard_map.102
  7.2 5.0 %collective-permute-start.7 = (f32[3,32,640]{2,1,0:T(8,128)S(1)}, f32[3,32,640]{2,1,0:T(8,128)S(1)}, u32[]{:S(2)}, u32[]{:S(2)}) collective-permute-start(f32[3,32,640]{2,1,0:T(8,128)S(1)} %get-tuple-element.27), channel_id=1, source_target_pairs={{0,4},{4,0},{8,12},{12,8},{16,20},{20,16},{24,28},{28,24},{1,5},{5... | collective-permute-start | bytes 737288 | tf_op jit(solution)/shard_map/ppermute | solution.py:81
  12.2 0.7 %collective-permute-start.8 = (f32[3,32,640]{2,1,0:T(8,128)S(1)}, f32[3,32,640]{2,1,0:T(8,128)S(1)}, u32[]{:S(2)}, u32[]{:S(2)}) collective-permute-start(f32[3,32,640]{2,1,0:T(8,128)S(1)} %get-tuple-element.28), channel_id=1, source_target_pairs={{4,8},{12,16},{20,24},{8,4},{16,12},{24,20},{5,9},{13,17},{21,25},... | collective-permute-start | bytes 737288 | tf_op jit(solution)/shard_map/ppermute | solution.py:81
  12.9 2.0 %collective-permute-start.2 = (f32[72,128]{1,0:T(8,128)S(1)}, f32[72,128]{1,0:T(8,128)S(1)}, u32[]{:S(2)}, u32[]{:S(2)}) collective-permute-start(f32[72,128]{1,0:T(8,128)S(1)} %shard_map.96.refs_2_), channel_id=1, source_target_pairs={{0,2},{2,0},{1,3},{3,1},{4,6},{6,4},{5,7},{7,5},{8,10},{10,8},{9,1... | collective-permute-start | bytes 110600 | tf_op jit(solution)/shard_map/ppermute | solution.py:81
  14.9 2.0 %collective-permute-done.2.refs_4_ = f32[72,128]{1,0:T(8,128)S(1)} collective-permute-done((f32[72,128]{1,0:T(8,128)S(1)}, f32[72,128]{1,0:T(8,128)S(1)}, u32[]{:S(2)}, u32[]{:S(2)}) %collective-permute-start.2) | collective-permute-done | bytes 36896 | tf_op jit(solution)/shard_map/ppermute | solution.py:81
  16.9 0.4 shard_map.97.refs_3_.refs_0_
  17.3 2.0 %collective-permute-start.3 = (bf16[32,512]{1,0:T(8,128)(2,1)S(1)}, bf16[32,512]{1,0:T(8,128)(2,1)S(1)}, u32[]{:S(2)}, u32[]{:S(2)}) collective-permute-start(bf16[32,512]{1,0:T(8,128)(2,1)S(1)} %shard_map.97.refs_3_.refs_0_), channel_id=1, source_target_pairs={{0,2},{2,0},{1,3},{3,1},{4,6},{6,4},{5,7},{7,5},{8,10},{10,8},{9,1... | collective-permute-start | bytes 98312 | tf_op jit(solution)/shard_map/ppermute | solution.py:569
  20.0 1.8 %shard_map.98 = (bf16[1024,1024]{1,0:T(8,128)(2,1)S(1)}, s32[8]{0:T(128)S(4)}) custom-call(s32[32,1,32]{2,1,0:T(1,128)S(1)} %copy-done.4, s32[1]{0:T(128)} %bitcast.6.refs_1_, s32[7]{0:T(128)S(1)} %bitcast.10, bf16[32,512]{1,0:T(8,128)(2,1)S(1)} %shard_map.97.refs_3_.refs_0_), custom_call_target="tpu_custom_call" | custom-call | bytes 6000000 | tf_op jit(solution)/shard_map/pallas_call | solution.py:57
  21.8 0.5 shard_map.99.refs_0_.refs_4_
  22.3 0.6 shard_map.103
  22.9 1.7 %collective-permute-start.9 = (f32[38,32,128]{2,1,0:T(8,128)S(1)}, f32[38,32,128]{2,1,0:T(8,128)S(1)}, u32[]{:S(2)}, u32[]{:S(2)}) collective-permute-start(f32[38,32,128]{2,1,0:T(8,128)S(1)} %shard_map.103), channel_id=1, source_target_pairs={{0,2},{2,0},{1,3},{3,1},{4,6},{6,4},{5,7},{7,5},{8,10},{10,8},{9,1... | collective-permute-start | bytes 1867784 | tf_op jit(solution)/shard_map/ppermute | solution.py:81
  24.5 5.2 %collective-permute-start.4 = (bf16[1,32,1024]{2,1,0:T(8,128)(2,1)S(1)}, bf16[1,32,1024]{2,1,0:T(8,128)(2,1)S(1)}, u32[]{:S(2)}, u32[]{:S(2)}) collective-permute-start(bf16[1,32,1024]{2,1,0:T(8,128)(2,1)S(1)} %shard_map.99.refs_0_.refs_4_), channel_id=1, source_target_pairs={{0,16},{4,20},{8,24},{12,28},{16,0},{20,4},{24,8},{28,12},{1,17},{... | collective-permute-start | bytes 196616 | tf_op jit(solution)/shard_map/ppermute | solution.py:586
  29.7 2.2 %collective-permute-done.4.refs_1_ = bf16[1,32,1024]{2,1,0:T(8,128)(2,1)S(1)} collective-permute-done((bf16[1,32,1024]{2,1,0:T(8,128)(2,1)S(1)}, bf16[1,32,1024]{2,1,0:T(8,128)(2,1)S(1)}, u32[]{:S(2)}, u32[]{:S(2)}) %collective-permute-start.4) | collective-permute-done | bytes 65568 | tf_op jit(solution)/shard_map/ppermute | solution.py:586
  32.0 2.3 %collective-permute-start.5 = (bf16[2,32,1024]{2,1,0:T(8,128)(2,1)S(1)}, bf16[2,32,1024]{2,1,0:T(8,128)(2,1)S(1)}, u32[]{:S(2)}, u32[]{:S(2)}) collective-permute-start(bf16[2,32,1024]{2,1,0:T(8,128)(2,1)S(1)} %shard_map.100.refs_0_), channel_id=1, source_target_pairs={{0,8},{4,12},{8,0},{12,4},{16,24},{20,28},{24,16},{28,20},{1,9},{5... | collective-permute-start | bytes 393224 | tf_op jit(solution)/shard_map/ppermute | solution.py:586
  34.3 2.9 %collective-permute-done.5.refs_1_ = bf16[2,32,1024]{2,1,0:T(8,128)(2,1)S(1)} collective-permute-done((bf16[2,32,1024]{2,1,0:T(8,128)(2,1)S(1)}, bf16[2,32,1024]{2,1,0:T(8,128)(2,1)S(1)}, u32[]{:S(2)}, u32[]{:S(2)}) %collective-permute-start.5) | collective-permute-done | bytes 131104 | tf_op jit(solution)/shard_map/ppermute | solution.py:586
  37.3 0.2 shard_map.104
  37.5 0.1 collective-permute-start.10
  37.6 2.6 %collective-permute-start.6 = (bf16[4,32,1024]{2,1,0:T(8,128)(2,1)S(1)}, bf16[4,32,1024]{2,1,0:T(8,128)(2,1)S(1)}, u32[]{:S(2)}, u32[]{:S(2)}) collective-permute-start(bf16[4,32,1024]{2,1,0:T(8,128)(2,1)S(1)} %shard_map.101.refs_5_.refs_0_), channel_id=1, source_target_pairs={{0,4},{4,0},{8,12},{12,8},{16,20},{20,16},{24,28},{28,24},{1,5},{5... | collective-permute-start | bytes 786440 | tf_op jit(solution)/shard_map/ppermute | solution.py:586
  40.2 2.9 %shard_map.105 = (f32[1520,640]{1,0:T(8,128)S(1)}, f32[1520,640]{1,0:T(8,128)S(1)}, f32[1520,640]{1,0:T(8,128)S(1)}) custom-call(f32[32,32,512]{2,1,0:T(8,128)S(1)} %copy-done, f32[32,32,128]{2,1,0:T(8,128)S(1)} %get-tuple-element.26.refs_1_, f32[3,32,640]{2,1,0:T(8,128)S(1)} %collective-permute-done.7.refs_2_, ...), custom_call_target="tpu_custom_call" | custom-call | bytes 9000000 | tf_op jit(solution)/shard_map/pallas_call | solution.py:57
  43.1 4.0 %collective-permute-done.6.refs_1_ = bf16[4,32,1024]{2,1,0:T(8,128)(2,1)S(1)} collective-permute-done((bf16[4,32,1024]{2,1,0:T(8,128)(2,1)S(1)}, bf16[4,32,1024]{2,1,0:T(8,128)(2,1)S(1)}, u32[]{:S(2)}, u32[]{:S(2)}) %collective-permute-start.6) | collective-permute-done | bytes 262176 | tf_op jit(solution)/shard_map/ppermute | solution.py:586
  47.2 0.1 collective-permute-start.11
  47.3 3.0 %shard_map.107.refs_7_.refs_2_ = f32[1520,640]{1,0:T(8,128)S(1)} custom-call(f32[1520,640]{1,0:T(8,128)S(1)} %get-tuple-element.30.refs_0_, f32[1520,640]{1,0:T(8,128)S(1)} %get-tuple-element.31.refs_1_, f32[1520,640]{1,0:T(8,128)S(1)} %get-tuple-element.29.refs_2_, bf16[8,32,1024]{2,1,0:T(8,128)(2,1)S(1)} %shard_map.106.refs_3_.refs_1_), custom_call_target="tpu_custom_call" | custom-call | bytes 7500000 | tf_op jit(solution)/shard_map/pallas_call | solution.py:57
  50.3 2.6 %shard_map.108 = (f32[32,512]{1,0:T(8,128)S(1)}, f32[32,512]{1,0:T(8,128)S(1)}) custom-call(s32[8]{0:T(128)S(4)} %get-tuple-element.24.refs_0_, bf16[8,32,1024]{2,1,0:T(8,128)(2,1)S(1)} %shard_map.106.refs_3_.refs_1_, bf16[8,32,1024]{2,1,0:T(8,128)(2,1)S(1)} %collective-permute-done.11.refs_2_, bf16[1024,1024]{1,0:T(8,128)(2,1)S(1)} %bitcast.7, ...), custom_call_target="tpu_custom_call" | custom-call | bytes 7500000 | tf_op jit(solution)/shard_map/pallas_call | solution.py:57
  52.9 1.0 %collective-permute-start.12 = (f32[32,512]{1,0:T(8,128)S(1)}, f32[32,512]{1,0:T(8,128)S(1)}, u32[]{:S(2)}, u32[]{:S(2)}) collective-permute-start(f32[32,512]{1,0:T(8,128)S(1)} %get-tuple-element.33.refs_4_), channel_id=1, source_target_pairs={{0,2},{2,0},{1,3},{3,1},{4,6},{6,4},{5,7},{7,5},{8,10},{10,8},{9,1... | collective-permute-start | bytes 196616 | tf_op jit(solution)/shard_map/ppermute | solution.py:620
  54.0 3.0 %shard_map.109.refs_2_ = f32[1520,640]{1,0:T(8,128)S(1)} custom-call(f32[1520,640]{1,0:T(8,128)S(1)} %get-tuple-element.30.refs_0_, f32[1520,640]{1,0:T(8,128)S(1)} %get-tuple-element.31.refs_1_, f32[1520,640]{1,0:T(8,128)S(1)} %shard_map.107.refs_7_.refs_2_, f32[32,512]{1,0:T(8,128)S(1)} %get-tuple-element.32.refs_3_.refs_0_, ...), custom_call_target="tpu_custom_call" | custom-call | bytes 7500000 | tf_op jit(solution)/shard_map/pallas_call | solution.py:57
  57.0 3.0 %shard_map.110 = (f32[32,32,512]{2,1,0:T(8,128)}, f32[32,8,512]{2,1,0:T(8,128)S(1)}) custom-call(f32[1520,640]{1,0:T(8,128)S(1)} %get-tuple-element.30.refs_0_, f32[1520,640]{1,0:T(8,128)S(1)} %get-tuple-element.31.refs_1_, f32[1520,640]{1,0:T(8,128)S(1)} %shard_map.109.refs_2_), custom_call_target="tpu_custom_call" | custom-call | bytes 6000000 | tf_op jit(solution)/shard_map/pallas_call | solution.py:57
  60.1 1.1 %shard_map.111 = (f32[32,1,512]{2,1,0:T(1,128)}, f32[32,32,512]{2,1,0:T(8,128)}) custom-call(f32[32,512]{1,0:T(8,128)S(1)} %get-tuple-element.32.refs_3_.refs_0_, f32[32,512]{1,0:T(8,128)S(1)} %collective-permute-done.12.refs_1_, f32[3,32,512]{2,1,0:T(8,128)S(1)} %get-tuple-element.21.refs_1_.refs_2_, ...), custom_call_target="tpu_custom_call", output_to_operand_aliasing={{1}: (4, {})} | custom-call | bytes 3000000 | tf_op jit(solution)/shard_map/pallas_call | solution.py:57
  (23 shorter events, 0.1 us)
Async XLA Ops:
  0.6 6.5 %copy-start = (f32[32,32,512]{2,1,0:T(8,128)S(1)}, f32[32,32,512]{2,1,0:T(8,128)}, u32[]{:S(2)}) copy-start(f32[32,32,512]{2,1,0:T(8,128)} %refs_0_.11) | copy-start | bytes 6291460
  0.6 19.3 %copy-start.5 = (s32[1,1,1,7]{3,2,1,0:T(1,128)S(1)}, s32[1,1,1,7]{3,2,1,0:T(1,128)}, u32[]{:S(2)}) copy-start(s32[1,1,1,7]{3,2,1,0:T(1,128)} %param.12) | copy-start | bytes 88
  0.7 19.3 %copy-start.4 = (s32[32,1,32]{2,1,0:T(1,128)S(1)}, s32[32,1,32]{2,1,0:T(1,128)}, u32[]{:S(2)}) copy-start(s32[32,1,32]{2,1,0:T(1,128)} %refs_0_.7) | copy-start | bytes 12292
  2.3 4.7 %collective-permute-start = (f32[8,512]{1,0:T(8,128)S(1)}, f32[8,512]{1,0:T(8,128)S(1)}, u32[]{:S(2)}, u32[]{:S(2)}) collective-permute-start(f32[8,512]{1,0:T(8,128)S(1)} %get-tuple-element.22), channel_id=1, source_target_pairs={{0,4},{4,0},{8,12},{12,8},{16,20},{20,16},{24,28},{28,24},{1,5},{5... | collective-permute-start | bytes 49160 | tf_op jit(solution)/shard_map/ppermute | solution.py:81
  5.3 1.7 %collective-permute-start.1 = (f32[8,512]{1,0:T(8,128)S(1)}, f32[8,512]{1,0:T(8,128)S(1)}, u32[]{:S(2)}, u32[]{:S(2)}) collective-permute-start(f32[8,512]{1,0:T(8,128)S(1)} %get-tuple-element.23), channel_id=1, source_target_pairs={{4,8},{12,16},{20,24},{8,4},{16,12},{24,20},{5,9},{13,17},{21,25},... | collective-permute-start | bytes 49160 | tf_op jit(solution)/shard_map/ppermute | solution.py:81
  7.2 15.1 %collective-permute-start.7 = (f32[3,32,640]{2,1,0:T(8,128)S(1)}, f32[3,32,640]{2,1,0:T(8,128)S(1)}, u32[]{:S(2)}, u32[]{:S(2)}) collective-permute-start(f32[3,32,640]{2,1,0:T(8,128)S(1)} %get-tuple-element.27), channel_id=1, source_target_pairs={{0,4},{4,0},{8,12},{12,8},{16,20},{20,16},{24,28},{28,24},{1,5},{5... | collective-permute-start | bytes 737288 | tf_op jit(solution)/shard_map/ppermute | solution.py:81
  12.2 10.1 %collective-permute-start.8 = (f32[3,32,640]{2,1,0:T(8,128)S(1)}, f32[3,32,640]{2,1,0:T(8,128)S(1)}, u32[]{:S(2)}, u32[]{:S(2)}) collective-permute-start(f32[3,32,640]{2,1,0:T(8,128)S(1)} %get-tuple-element.28), channel_id=1, source_target_pairs={{4,8},{12,16},{20,24},{8,4},{16,12},{24,20},{5,9},{13,17},{21,25},... | collective-permute-start | bytes 737288 | tf_op jit(solution)/shard_map/ppermute | solution.py:81
  12.9 4.0 %collective-permute-start.2 = (f32[72,128]{1,0:T(8,128)S(1)}, f32[72,128]{1,0:T(8,128)S(1)}, u32[]{:S(2)}, u32[]{:S(2)}) collective-permute-start(f32[72,128]{1,0:T(8,128)S(1)} %shard_map.96.refs_2_), channel_id=1, source_target_pairs={{0,2},{2,0},{1,3},{3,1},{4,6},{6,4},{5,7},{7,5},{8,10},{10,8},{9,1... | collective-permute-start | bytes 110600 | tf_op jit(solution)/shard_map/ppermute | solution.py:81
  17.3 4.5 %collective-permute-start.3 = (bf16[32,512]{1,0:T(8,128)(2,1)S(1)}, bf16[32,512]{1,0:T(8,128)(2,1)S(1)}, u32[]{:S(2)}, u32[]{:S(2)}) collective-permute-start(bf16[32,512]{1,0:T(8,128)(2,1)S(1)} %shard_map.97.refs_3_.refs_0_), channel_id=1, source_target_pairs={{0,2},{2,0},{1,3},{3,1},{4,6},{6,4},{5,7},{7,5},{8,10},{10,8},{9,1... | collective-permute-start | bytes 98312 | tf_op jit(solution)/shard_map/ppermute | solution.py:569
  22.9 14.4 %collective-permute-start.9 = (f32[38,32,128]{2,1,0:T(8,128)S(1)}, f32[38,32,128]{2,1,0:T(8,128)S(1)}, u32[]{:S(2)}, u32[]{:S(2)}) collective-permute-start(f32[38,32,128]{2,1,0:T(8,128)S(1)} %shard_map.103), channel_id=1, source_target_pairs={{0,2},{2,0},{1,3},{3,1},{4,6},{6,4},{5,7},{7,5},{8,10},{10,8},{9,1... | collective-permute-start | bytes 1867784 | tf_op jit(solution)/shard_map/ppermute | solution.py:81
  24.5 7.4 %collective-permute-start.4 = (bf16[1,32,1024]{2,1,0:T(8,128)(2,1)S(1)}, bf16[1,32,1024]{2,1,0:T(8,128)(2,1)S(1)}, u32[]{:S(2)}, u32[]{:S(2)}) collective-permute-start(bf16[1,32,1024]{2,1,0:T(8,128)(2,1)S(1)} %shard_map.99.refs_0_.refs_4_), channel_id=1, source_target_pairs={{0,16},{4,20},{8,24},{12,28},{16,0},{20,4},{24,8},{28,12},{1,17},{... | collective-permute-start | bytes 196616 | tf_op jit(solution)/shard_map/ppermute | solution.py:586
  32.0 5.3 %collective-permute-start.5 = (bf16[2,32,1024]{2,1,0:T(8,128)(2,1)S(1)}, bf16[2,32,1024]{2,1,0:T(8,128)(2,1)S(1)}, u32[]{:S(2)}, u32[]{:S(2)}) collective-permute-start(bf16[2,32,1024]{2,1,0:T(8,128)(2,1)S(1)} %shard_map.100.refs_0_), channel_id=1, source_target_pairs={{0,8},{4,12},{8,0},{12,4},{16,24},{20,28},{24,16},{28,20},{1,9},{5... | collective-permute-start | bytes 393224 | tf_op jit(solution)/shard_map/ppermute | solution.py:586
  37.5 2.7 %collective-permute-start.10 = (f32[38,8,768]{2,1,0:T(8,128)S(1)}, f32[38,8,768]{2,1,0:T(8,128)S(1)}, u32[]{:S(2)}, u32[]{:S(2)}) collective-permute-start(f32[38,8,768]{2,1,0:T(8,128)S(1)} %shard_map.104), channel_id=1, source_target_pairs={{0,1},{1,0},{2,3},{3,2},{4,5},{5,4},{6,7},{7,6},{8,9},{9,8},{10,11... | collective-permute-start | bytes 2801672 | tf_op jit(solution)/shard_map/ppermute | solution.py:595
  37.6 9.5 %collective-permute-start.6 = (bf16[4,32,1024]{2,1,0:T(8,128)(2,1)S(1)}, bf16[4,32,1024]{2,1,0:T(8,128)(2,1)S(1)}, u32[]{:S(2)}, u32[]{:S(2)}) collective-permute-start(bf16[4,32,1024]{2,1,0:T(8,128)(2,1)S(1)} %shard_map.101.refs_5_.refs_0_), channel_id=1, source_target_pairs={{0,4},{4,0},{8,12},{12,8},{16,20},{20,16},{24,28},{28,24},{1,5},{5... | collective-permute-start | bytes 786440 | tf_op jit(solution)/shard_map/ppermute | solution.py:586
  47.2 3.1 %collective-permute-start.11 = (bf16[8,32,1024]{2,1,0:T(8,128)(2,1)S(1)}, bf16[8,32,1024]{2,1,0:T(8,128)(2,1)S(1)}, u32[]{:S(2)}, u32[]{:S(2)}) collective-permute-start(bf16[8,32,1024]{2,1,0:T(8,128)(2,1)S(1)} %shard_map.106.refs_3_.refs_1_), channel_id=1, source_target_pairs={{0,1},{1,0},{2,3},{3,2},{4,5},{5,4},{6,7},{7,6},{8,9},{9,8},{10,11... | collective-permute-start | bytes 1572872 | tf_op jit(solution)/shard_map/ppermute | solution.py:606
  47.2 3.1 %copy-start.1 = (bf16[1,1,1,1024,1024]{4,3,2,1,0:T(8,128)(2,1)S(1)}, bf16[1,1,1,1024,1024]{4,3,2,1,0:T(8,128)(2,1)}, u32[]{:S(2)}) copy-start(bf16[1,1,1,1024,1024]{4,3,2,1,0:T(8,128)(2,1)} %param.13) | copy-start | bytes 6291460
  47.2 3.1 %copy-start.2 = (bf16[1,1,1,7,16,1024]{5,4,3,2,1,0:T(8,128)(2,1)S(1)}, bf16[1,1,1,7,16,1024]{5,4,3,2,1,0:T(8,128)(2,1)}, u32[]{:S(2)}) copy-start(bf16[1,1,1,7,16,1024]{5,4,3,2,1,0:T(8,128)(2,1)} %param.15) | copy-start | bytes 688132
  47.3 3.1 %copy-start.3 = (bf16[1,1,1,7,16,1024]{5,4,3,2,1,0:T(8,128)(2,1)S(1)}, bf16[1,1,1,7,16,1024]{5,4,3,2,1,0:T(8,128)(2,1)}, u32[]{:S(2)}) copy-start(bf16[1,1,1,7,16,1024]{5,4,3,2,1,0:T(8,128)(2,1)} %param.14) | copy-start | bytes 688132
  52.9 7.1 %collective-permute-start.12 = (f32[32,512]{1,0:T(8,128)S(1)}, f32[32,512]{1,0:T(8,128)S(1)}, u32[]{:S(2)}, u32[]{:S(2)}) collective-permute-start(f32[32,512]{1,0:T(8,128)S(1)} %get-tuple-element.33.refs_4_), channel_id=1, source_target_pairs={{0,2},{2,0},{1,3},{3,1},{4,6},{6,4},{5,7},{7,5},{8,10},{10,8},{9,1... | collective-permute-start | bytes 196616 | tf_op jit(solution)/shard_map/ppermute | solution.py:620

commit v5 on v4

--- a/solution.py
+++ b/solution.py
@@ -12,6 +12,7 @@
 LANES = 128
 ROWS = 8
 HALO = 3
+NEAR = 3
 
 
 def roll(value, shift, axis):
@@ -131,15 +132,14 @@
     )
 
 
-def face_start_kernel(nx, source, coef, inv, s_out, i_out, *refs):
-    messages, (src, coefs, sems) = refs[:nx], refs[nx:]
+def face_start_kernel(source, coef, held_source, inv, message, *refs):
+    edges, (coefs, sems) = refs[:-2], refs[-2:]
     odd, side = index("gx") % 2, index("gz")
     rows_x, depth, width = source.shape
     cells = width // E
-    top = pl.multiple_of(side * (depth - ROWS), ROWS)
     copies = [
         pltpu.make_async_copy(coef, coefs, sems.at[0]),
-        pltpu.make_async_copy(source.at[:, pl.ds(top, ROWS), :], src, sems.at[1]),
+        pltpu.make_async_copy(source, held_source, sems.at[1]),
     ]
     for copy in copies:
         copy.start()
@@ -148,77 +148,84 @@
     inv[...] = jnp.concatenate(
         [c, jnp.zeros((rows_x, depth, LANES - cells), jnp.float32)], axis=2
     )
+    compact = jnp.zeros((rows_x, LANES), jnp.float32)
+    for d in range(NEAR):
+        plane = jnp.where(side == 0, inv[:, d, :], inv[:, depth - 1 - d, :])
+        compact = compact + roll(plane, 32 * d, 1)
+    for n in range(rows_x // ROWS):
+        message[NEAR * rows_x :, n * LANES : (n + 1) * LANES] = compact[n * ROWS : (n + 1) * ROWS]
     copies[1].wait()
-    planes = []
-    for d in range(3):
-        s = jnp.where(side == 0, src[:, d, :], src[:, ROWS - 1 - d, :])
-        i = jnp.where(side == 0, inv[:, d, :], inv[:, depth - 1 - d, :])
-        planes.append([s, i])
-    spreads = spread(jnp.concatenate([i for _, i in planes], axis=0), width, cells)
-    for d in range(3):
-        planes[d][1] = spreads[d * rows_x : (d + 1) * rows_x]
-        s_out[d], i_out[d] = planes[d]
+    for d in range(NEAR):
+        plane = jnp.where(side == 0, held_source[:, d, :], held_source[:, depth - 1 - d, :])
+        message[d * rows_x : (d + 1) * rows_x, :] = plane
+    row_edges(odd, held_source, inv, edges)
+
+
+def row_edges(odd, source, inv, messages):
+    rows_x, _, width = source.shape
     for number, message in enumerate(messages):
-        for d in range(2):
-            for k in range(2):
-                v = planes[d][k]
+        for k in range(HALO):
+            last = rows_x - HALO + k
+            message[k, :, :width] = choose(odd, source[k], source[last], number)
+            message[k, :, width:] = choose(odd, inv[k], inv[last], number)
+
+
+def face_side_kernel(groups, own, other, s_out, i_out, i_own, *messages):
+    odd = index("gx") % 2
+    if groups == 2:
+        first = index("gy") == 0
+        parts = [jnp.where(first, own[...], other[...]), jnp.where(first, other[...], own[...])]
+    else:
+        parts = [other[n] for n in range(groups)]
+    width = own.shape[1]
+    cells = width // E
+    rows_x = i_own.shape[0]
+
+    def inverse(part):
+        pieces = [
+            part[NEAR * rows_x :, n * LANES : (n + 1) * LANES] for n in range(rows_x // ROWS)
+        ]
+        compact = jnp.concatenate(pieces, axis=0)
+        planes = jnp.concatenate([roll(compact, -32 * d, 1) for d in range(NEAR)], axis=0)
+        return spread(planes, width, cells)
+
+    i_own[...] = inverse(own[...])[:rows_x]
+    s_all = jnp.concatenate([part[: NEAR * rows_x] for part in parts], axis=1)
+    i_all = jnp.concatenate([inverse(part) for part in parts], axis=1)
+    for all_planes, out in ((s_all, s_out), (i_all, i_out)):
+        for d in range(NEAR):
+            out[d] = all_planes[d * rows_x : (d + 1) * rows_x]
+    for number, message in enumerate(messages):
+        for k, all_planes in enumerate((s_all, i_all)):
+            for d in range(2):
                 row = 4 * k + 2 * d
-                message[row : row + 2, :] = choose(odd, v[:2], v[rows_x - 2 :], number)
-
-
-def edge_pair(s, i):
-    lane = lane_ids(s[:, :LANES])
-    low = jnp.where(lane < 2 * E, s[:, :LANES], roll(i[:, :LANES], 64, 1))
-    high = jnp.where(lane < 2 * E, roll(s[:, -LANES:], 64, 1), i[:, -LANES:])
-    return low, high
-
-
-def face_side_kernel(nx, s_in, i_in, *refs):
-    odd_x, odd_y = index("gx") % 2, index("gy") % 2
-    got, messages = [r[...] for r in refs[:nx]], refs[nx:]
-    rows_x = s_in.shape[1]
-    below, above = from_low(odd_x, got), from_high(odd_x, got)
-    pick = lax.broadcasted_iota(jnp.int32, below.shape, 0)
-    s = jnp.where(pick == 0, roll(below, -1, 0), roll(above, 1, 0))
-    i = jnp.where(pick == 0, roll(below, -5, 0), roll(above, -3, 0))
-    s, i = (jnp.where(pick < 2, v, 0.0) for v in (s, i))
-    parts = [edge_pair(s_in[0], i_in[0]), edge_pair(s_in[1], i_in[1]), edge_pair(s, i)]
-    for number, message in enumerate(messages):
-        row = 0
-        for low, high in parts:
-            message[row : row + low.shape[0], :] = choose(odd_y, low, high, number)
-            row += low.shape[0]
-
-
-def face_sweep_kernel(nx, ny, s_in, i_in, *refs):
-    odd_x, odd_y = index("gx") % 2, index("gy") % 2
-    got_x = [r[...] for r in refs[:nx]]
-    got_y = [r[...] for r in refs[nx : nx + ny]]
-    out, ext_s, ext_i = refs[nx + ny :]
+                top = d * rows_x
+                message[row : row + 2, :] = choose(
+                    odd, all_planes[top : top + 2], all_planes[top + rows_x - 2 : top + rows_x], number
+                )
+
+
+def face_trace_kernel(nx, s_in, i_in, order, *refs):
+    odd = index("gx") % 2
+    got = [r[...] for r in refs[:nx]]
+    out, ext_s, ext_i = refs[nx:]
     _, rows_x, width = s_in.shape
-    below, above = from_low(odd_x, got_x), from_high(odd_x, got_x)
-    left, right = from_low(odd_y, got_y), from_high(odd_y, got_y)
-    lane = lane_ids(left)
-    pad_s = jnp.where(lane < 2 * E, right, roll(left, 64, 1))
-    pad_i = jnp.where(lane < 2 * E, roll(right, 64, 1), left)
+    below, above = from_low(odd, got), from_high(odd, got)
     ext_s[...] = jnp.zeros(ext_s.shape, jnp.float32)
     ext_i[...] = jnp.zeros(ext_i.shape, jnp.float32)
     first, last = ROWS, ROWS + rows_x
-    for ext, own, pad, k in ((ext_s, s_in, pad_s, 0), (ext_i, i_in, pad_i, 1)):
+    for ext, own, k in ((ext_s, s_in, 0), (ext_i, i_in, 1)):
         for d in range(2):
             row = 4 * k + 2 * d
             ext[d, first:last, :width] = own[d]
             ext[d, first - 2 : first, :width] = below[row : row + 2]
             ext[d, last : last + 2, :width] = above[row : row + 2]
-            ext[d, first:last, width:] = pad[d * rows_x : (d + 1) * rows_x]
-        ext[0, first - 1 : first, width:] = pad[2 * rows_x : 2 * rows_x + 1]
-        ext[0, last : last + 1, width:] = pad[2 * rows_x + 1 : 2 * rows_x + 2]
 
     def around(u):
         return roll(u, 1, 0) + roll(u, -1, 0) + roll(u, E, 1) + roll(u, -E, 1)
 
-    s0, s1, i0, i1 = ext_s[0], ext_s[1], ext_i[0], ext_i[1]
-    u0, u1 = s0 * i0, s1 * i1
+    s0, i0, i1 = ext_s[0], ext_i[0], ext_i[1]
+    u0, u1 = s0 * i0, ext_s[1] * i1
     deep = s_in[2] * i_in[2]
     v0 = (s0 + (around(u0) + u1)) * i0
     own = (around(u1) + u0)[first:last, :width]
@@ -229,7 +236,8 @@
         start = cell * E // LANES * LANES
         pieces.append(roll(face[:, start : start + LANES], -(cell * E - start), 1))
     stacked = jnp.concatenate(pieces, axis=0)
-    out[...] = stacked.T[:E].astype(jnp.bfloat16)
+    values = stacked.T[:E].astype(jnp.bfloat16)
+    out[0] = jnp.dot(values, order[...], preferred_element_type=jnp.float32).astype(jnp.bfloat16)
 
 
 def order_kernel(place, near_col, far_col, order, spot):
@@ -248,19 +256,6 @@
         for n, step in enumerate(doubling(size_x)):
             where = where + jnp.where(apart & step > 0, 1 << n, 0)
         spot[k] = where
-
-
-def trace_kernel(*refs):
-    order, out = refs[-2:]
-    if len(refs) == 3:
-        face = refs[0][...]
-    else:
-        own, other = refs[0][...], refs[1][...]
-        first = index("gy") == 0
-        face = jnp.concatenate(
-            [jnp.where(first, own, other), jnp.where(first, other, own)], axis=1
-        )
-    out[0] = jnp.dot(face, order[...], preferred_element_type=jnp.float32).astype(jnp.bfloat16)
 
 
 def join_kernel(one, two, out):
@@ -328,7 +323,7 @@
     held_flux[...] = flux[:, None, :]
     out_copy = pltpu.make_async_copy(held_flux, flux_out, sems.at[0])
     out_copy.start()
-    added = (flux * inv[0])[:, None, :]
+    added = (flux * inv[...])[:, None, :]
     row = lax.broadcasted_iota(jnp.int32, slab.shape, 1)
     slab[...] = slab[...] + jnp.where(row == side * (ROWS - 1), added, 0.0)
     top = pl.multiple_of(side * (out.shape[1] - ROWS), ROWS)
@@ -336,16 +331,6 @@
     copy.start()
     out_copy.wait()
     copy.wait()
-
-
-def row_edge_kernel(source, inv, *messages):
-    odd = index("gx") % 2
-    rows_x, _, width = source.shape
-    for number, message in enumerate(messages):
-        for k in range(HALO):
-            last = rows_x - HALO + k
-            message[k, :, :width] = choose(odd, source[k], source[last], number)
-            message[k, :, width:] = choose(odd, inv[k], inv[last], number)
 
 
 def side_edge_kernel(nx, source, inv, *refs):
@@ -388,40 +373,59 @@
 
 def depth_edge_kernel(cells, ring, nx, ny, source, inv, *refs):
     odd_x, odd_y, side = index("gx") % 2, index("gy") % 2, index("gz")
-    got_x, got_y, out = refs[:nx], refs[nx : nx + ny], refs[-1]
+    got_x, got_y, (two_out, one_out) = refs[:nx], refs[nx : nx + ny], refs[nx + ny :]
     rows_x, depth, width = source.shape
-    inner = lambda r: jnp.where(side == 0, r[:, depth - ROWS :, :], r[:, :ROWS, :])
-    got = [inner(r) for r in got_y]
-    left, right = from_low(odd_y, got), from_high(odd_y, got)
-    edges = [inner(r) for r in got_x]
-    below, above = from_low(odd_x, edges), from_high(odd_x, edges)
-    for rows, s, c in (
-        (slice(0, HALO), below[:, :, :width], below[:, :, width:]),
-        (slice(HALO, HALO + rows_x), inner(source), inner(inv)),
-        (slice(HALO + rows_x, rows_x + 2 * HALO), above[:, :, :width], above[:, :, width:]),
-    ):
-        parts, compact = widen(cells, ring, s, c, left[rows], right[rows])
-        out[rows] = jnp.concatenate([*parts, compact], axis=2)
+    wide = ring * E
+    rows = two_out.shape[1]
+    packs = jnp.zeros((rows, LANES), jnp.float32)
+    for k in range(HALO):
+        inner = lambda r: jnp.where(side == 0, r[:, depth - HALO + k, :], r[:, k, :])
+        edges = [inner(r) for r in got_x]
+        below, above = from_low(odd_x, edges), from_high(odd_x, edges)
+        empty = jnp.zeros((rows - rows_x - 2 * HALO, LANES), jnp.float32)
+        beside = [jnp.concatenate([inner(r), empty], axis=0) for r in got_y]
+        own = jnp.concatenate([inner(source), inner(inv)], axis=1)
+        blank = jnp.zeros((empty.shape[0], width + LANES), jnp.float32)
+        all_rows = jnp.concatenate([below, own, above, blank], axis=0)
+        parts, compact = widen(
+            cells, ring, all_rows[:, :width], all_rows[:, width:],
+            from_low(odd_y, beside), from_high(odd_y, beside),
+        )
+        compact = jnp.where(lane_ids(compact) < ring, compact, 0.0)
+        packs = packs + roll(compact, 32 * k, 1)
+        out = jnp.concatenate(parts, axis=1)
+        if k < 2:
+            two_out[k] = out
+        else:
+            one_out[:, :wide] = out
+    one_out[:, wide:] = packs
 
 
 def assemble_kernel(cells, ring, nx, ny, source, inv, *refs):
     odd_x, odd_y, side = index("gx") % 2, index("gy") % 2, index("gz")
-    got_x, got_y, got_z = refs[:nx], refs[nx : nx + ny], refs[nx + ny]
-    ext_s, ext_i, one, compacts, matrix = refs[nx + ny + 1 :]
+    got_x, got_y = refs[:nx], refs[nx : nx + ny]
+    z_two, z_one, ext_s, ext_i, one, compacts, matrix = refs[nx + ny :]
     rows_x, depth, width = source.shape
     wide = ring * E
     all_z = depth + ROWS
     total = ext_s.shape[0]
     matrix[...] = spread_matrix(ring, wide)
-    row = lax.broadcasted_iota(jnp.int32, (ROWS, LANES), 0)
     start = side * (ROWS - HALO)
-    near = (row >= start) & (row < start + HALO)
+
+    def spaced(rows):
+        at = lax.broadcasted_iota(jnp.int32, (ROWS, rows[0].shape[1]), 0) - start
+        tile = jnp.zeros(at.shape, jnp.float32)
+        for k, value in enumerate(rows):
+            tile = jnp.where(at == k, value, tile)
+        return tile
 
     def place(x, s, c):
         got = [r[x] for r in got_y]
         parts, compact = widen(cells, ring, s, c, from_low(odd_y, got), from_high(odd_y, got))
-        zone = got_z[x]
-        lanes = jnp.where(near, zone[:, wide:], 0.0)
+        last = z_one[pl.ds(x, 1), :]
+        zone = spaced([z_two[0, pl.ds(x, 1), :], z_two[1, pl.ds(x, 1), :], last[:, :wide]])
+        packs = jnp.broadcast_to(last[:, wide:], (ROWS, LANES))
+        lanes = spaced([roll(packs, -32 * k, 1) for k in range(HALO)])
         first = pl.ds(pl.multiple_of(x * all_z, ROWS), depth)
         rest = pl.ds(pl.multiple_of(x * all_z + depth, ROWS), ROWS)
         compacts[first, :] = compact
@@ -430,7 +434,7 @@
         for part in parts:
             ext_s[first, at : at + part.shape[1]] = part
             at += part.shape[1]
-        ext_s[rest, :] = zone[:, :wide]
+        ext_s[rest, :] = zone
 
     def own(x, _):
         place(x + HALO, source[x], inv[x])
@@ -464,14 +468,14 @@
 def swept(ext_s, ext_i, old, x, all_z, depth, width, store):
     at = lambda x, rows: pl.ds(pl.multiple_of(x * all_z, ROWS), rows)
     tiles = old.shape[1] // LANES
-    lane = lax.broadcasted_iota(jnp.int32, (all_z, LANES), 1)
+    lane = lax.broadcasted_iota(jnp.int32, (depth, LANES), 1)
     known = {}
 
     def tile(j):
         j %= tiles
         if j not in known:
             u = old[at(x, all_z), j * LANES : (j + 1) * LANES]
-            known[j] = (u, roll(u, E, 1), roll(u, -E, 1))
+            known[j] = (u, roll(u[:depth], E, 1), roll(u[:depth], -E, 1))
         return known[j]
 
     for j in range(width // LANES):
@@ -481,7 +485,7 @@
         up = roll(here[0], 1, 0) + roll(here[0], -1, 0)
         side = jnp.where(lane < E, tile(j - 1)[1], here[1])
         side = side + jnp.where(lane >= LANES - E, tile(j + 1)[2], here[2])
-        beside = beside + (up + side)[:depth]
+        beside = beside + (up[:depth] + side)
         new = (ext_s[at(x, depth), columns] + beside) * ext_i[at(x, depth), columns]
         store(columns, new)
 
@@ -494,7 +498,7 @@
         swept(ext_s, ext_i, old, x, all_z, all_z, old.shape[1], store)
         return 0
 
-    repeat(1, old.shape[0] // all_z - 1, step, 6)
+    repeat(1, old.shape[0] // all_z - 1, step, 12)
 
 
 def last_sweep_kernel(ext_s, ext_i, old, out, slab, done, sems):
@@ -514,7 +518,7 @@
     size = rows_x // pieces
     copies = []
     for n in range(pieces):
-        repeat(n * size, (n + 1) * size, step, 4)
+        repeat(n * size, (n + 1) * size, step, 8)
         rows = slice(n * size, (n + 1) * size)
         copies.append(pltpu.make_async_copy(done.at[rows], out.at[rows], sems.at[n]))
         copies[-1].start()
@@ -540,72 +544,71 @@
     part = rows_x * cells
     halves = groups == 2
     coef = coef.transpose(0, 2, 1)
-    held_source = held(source)
-
-    planes = vector((3, rows_x, width))
-    inv, s_face, i_face, *face_x = call(
-        functools.partial(face_start_kernel, nx), (kept(source), kept(coef)),
-        [vector((rows_x, depth, LANES)), planes, planes] + [vector((ROWS, width))] * nx,
+
+    held_source, inv, near, *vol_x = call(
+        face_start_kernel, (kept(source), kept(coef)),
+        [vector(source.shape), vector((rows_x, depth, LANES)), vector((NEAR * rows_x + ROWS, width))]
+        + [vector((HALO, depth, width + LANES))] * nx,
         in_specs=[MAIN, MAIN],
-        scratch=(vector((rows_x, ROWS, width)), vector(coef.shape), pltpu.SemaphoreType.DMA((2,))),
+        scratch=(vector(coef.shape), pltpu.SemaphoreType.DMA((2,))),
+    )
+    if halves:
+        other = held(lax.ppermute(near, "gy", both))
+    else:
+        other = held(lax.all_gather(near, "gy", axis=0, tiled=False))
+    got_vol_x = swap(vol_x, "gx")
+    full = vector((NEAR, rows_x, width * groups))
+    s_face, i_face, i_own, *face_x = call(
+        functools.partial(face_side_kernel, groups), (near, other),
+        [full, full, vector((rows_x, width))] + [vector((ROWS, width * groups))] * nx, work=500,
     )
     got_x = swap(face_x, "gx")
-    face_y = call(
-        functools.partial(face_side_kernel, nx), (s_face, i_face, *got_x),
-        [vector((2 * rows_x + ROWS, LANES))] * ny, work=200,
-    )
-    vol_x = call(
-        row_edge_kernel, (held_source, inv), [vector((HALO, depth, width + LANES))] * nx, work=200,
-        after=(face_y[0],),
-    )
-    got_vol_x = swap(vol_x, "gx")
-    got_y = swap(face_y, "gy")
-    ext = pltpu.VMEM((2, rows_x + 2 * ROWS, width + LANES), jnp.float32)
-    (face,) = call(
-        functools.partial(face_sweep_kernel, nx, ny), (s_face, i_face, *got_x, *got_y),
-        [(vector if halves else plain)((E, part), bf16)], scratch=(ext, ext), work=500,
-    )
-    if halves:
-        faces = (face, held(lax.ppermute(face, "gy", both)))
-    else:
-        faces = (held(lax.all_gather(face, "gy", axis=1, tiled=True)),)
-
     order, spot = call(
         order_kernel, (face_trace, near_col.reshape(1), far_col.reshape(count)),
         [vector((tile, tile), bf16), pltpu.SMEM((count + 1,), jnp.int32)],
-        in_specs=[VECTOR, SCALAR, SCALAR], out_specs=[VECTOR, SCALAR], work=2000, after=(face,),
-    )
-    (traces,) = call(trace_kernel, (*faces, order), [vector((1, E, tile), bf16)])
+        in_specs=[VECTOR, SCALAR, SCALAR], out_specs=[VECTOR, SCALAR], work=2000, after=(near,),
+    )
     vol_y = call(
         functools.partial(side_edge_kernel, nx), (held_source, inv, *got_vol_x),
-        [vector((all_x, depth, LANES))] * ny, work=300, after=(traces,),
+        [vector((all_x, depth, LANES))] * ny, work=300, after=(order, *got_x),
     )
     got_vol_y = swap(vol_y, "gy")
+
+    ext = pltpu.VMEM((2, rows_x + 2 * ROWS, width * groups + LANES), jnp.float32)
+    (traces,) = call(
+        functools.partial(face_trace_kernel, nx), (s_face, i_face, order, *got_x),
+        [vector((1, E, tile), bf16)], scratch=(ext, ext),
+    )
     steps = doubling(size_x)
     for step in steps:
         other = held(lax.ppermute(traces, "gx", [(i, i ^ step) for i in range(size_x)]))
         twice = (2 * traces.shape[0], E, tile)
         before = ()
         if step == 1:
-            (vol_z,) = call(
+            rounded = -(-all_x // ROWS) * ROWS
+            vol_z = call(
                 functools.partial(depth_edge_kernel, cells, ring, nx, ny),
                 (held_source, inv, *got_vol_x, *got_vol_y),
-                [vector((all_x, ROWS, wide + LANES))], work=500, after=(traces,),
+                [vector((2, rounded, wide)), vector((rounded, wide + LANES))], work=500,
+                after=(traces,),
             )
-            got_vol_z = held(lax.ppermute(vol_z, "gz", both))
+            got_vol_z = [held(lax.ppermute(v, "gz", both)) for v in vol_z]
             ext = vector((all_x * all_z, wide))
             ext_s, ext_i, one = call(
                 functools.partial(assemble_kernel, cells, ring, nx, ny),
-                (held_source, inv, *got_vol_x, *got_vol_y, got_vol_z), [ext, ext, ext], work=3000,
+                (held_source, inv, *got_vol_x, *got_vol_y, *got_vol_z), [ext, ext, ext], work=3000,
                 scratch=(vector((all_x * all_z, LANES)), vector((LANES, wide), bf16)),
             )
-            before = (one,)
+            (two,) = call(
+                functools.partial(sweep_kernel, all_z), (ext_s, ext_i, one), [ext], work=2500
+            )
+            before = (two,)
         (traces,) = call(
             join_kernel, (traces, other), [vector(twice, bf16)], work=300, after=before
         )
     other = held(lax.ppermute(traces, "gz", both))
-    (two,) = call(
-        functools.partial(sweep_kernel, all_z), (ext_s, ext_i, one), [ext], work=2500,
+    (three,) = call(
+        functools.partial(sweep_kernel, all_z), (ext_s, ext_i, two), [ext], work=2500,
         after=(traces,),
     )
 
@@ -614,25 +617,22 @@
         (spot, traces, other, held(near_tile.reshape(tile, tile)),
          held(far_v.reshape(count * rank, tile)), held(far_u.reshape(count * rank, tile)), order),
         [vector((E, part))] * 2 if halves else [plain((E, tile))],
-        in_specs=[SCALAR] + [VECTOR] * 6, work=2500, after=(two,),
+        in_specs=[SCALAR] + [VECTOR] * 6, work=2500, after=(three,),
     )
     if halves:
         sums = (rows[0], held(lax.ppermute(rows[1], "gy", both)))
     else:
         sums = (held(lax.psum_scatter(rows[0], "gy", scatter_dimension=1, tiled=True)),)
-    (three,) = call(
-        functools.partial(sweep_kernel, all_z), (ext_s, ext_i, two), [ext], work=2500, after=rows,
-    )
     pieces = 4
     field, slab = call(
         last_sweep_kernel, (ext_s, ext_i, three),
         [plain(source.shape), vector((rows_x, ROWS, width))], work=2000,
-        out_specs=[MAIN, VECTOR],
+        out_specs=[MAIN, VECTOR], after=rows,
         scratch=(vector(source.shape), pltpu.SemaphoreType.DMA((pieces,))),
     )
 
     flux, result = call(
-        functools.partial(finish_kernel, len(sums)), (*sums, i_face, slab, field),
+        functools.partial(finish_kernel, len(sums)), (*sums, i_own, slab, field),
         [plain((rows_x, 1, width)), plain(source.shape)],
         in_specs=[VECTOR] * (len(sums) + 2) + [MAIN], out_specs=[MAIN, MAIN],
         scratch=(vector((rows_x, 1, width)), pltpu.SemaphoreType.DMA((2,))),

time: 61.4 us -> 53 us (0.86)
  starting transfers between devices: 26.3 us -> 17.8 us
  waiting for transfers between devices: 12.3 us -> 13 us
    ppermute x6 -> x5, starting transfers between devices: 13 us -> 4.8 us  [swap(): lax.ppermute(m, axis, p)]
    ppermute x2 -> x3, waiting for transfers between devices: 0.01 us -> 4.21 us  [the longest x1 3.09 us: body(): other = held(lax.ppermute(near, 'gy', both))]
    ppermute x3, waiting for transfers between devices: 9.19 us -> 5.62 us  [body(): lax.ppermute(traces, 'gx', [(i, i ^ step) for i in range(size_x)])]
    ppermute x3, starting transfers between devices: 10.2 us -> 7.8 us  [body(): lax.ppermute(traces, 'gx', [(i, i ^ step) for i in range(size_x)])]
    ppermute x2 -> x3, starting transfers between devices: 2.06 us -> 3.6 us  [the longest x1 3.03 us: body(): other = held(lax.ppermute(near, 'gy', both))]
    ppermute x6 -> x5, waiting for transfers between devices: 3.1 us -> 2.58 us  [swap(): lax.ppermute(m, axis, p)]
    pallas_call x17 -> x15, Pallas kernels: 21 us -> 20.5 us  [call(): pl.pallas_call(body, out_shape=out_shape, in_specs=(in_specs or [VECTOR]...]
  transfers between devices with their start and end apart: 13 -> 13, of which waited for: 5 -> 6; matrix products, arithmetic and copies ran while one was open for 0% -> 0% of each run, Pallas kernels for 24% -> 27%
where the time goes in v5:
time: 53 us; the launch traced here: 52.8 us
  Pallas kernels  20.5 us (39%)
  starting transfers between devices  17.8 us (34%)
  waiting for transfers between devices  13 us (25%)
  between operations  1.48 us (3%)
    pallas_call x15, Pallas kernels, call(): pl.pallas_call(body, out_shape=out_shape, in_specs=(in_specs or [VECTOR]...  20.5 us
    ppermute x3, starting transfers between devices, body(): lax.ppermute(traces, 'gx', [(i, i ^ step) for i in range(size_x)])  7.8 us
    ppermute x3, waiting for transfers between devices, body(): lax.ppermute(traces, 'gx', [(i, i ^ step) for i in range(size_x)])  5.62 us
    ppermute x5, starting transfers between devices, swap(): lax.ppermute(m, axis, p)  4.8 us
    ppermute x1, waiting for transfers between devices, body(): other = held(lax.ppermute(near, 'gy', both))  3.09 us
    ppermute x1, starting transfers between devices, body(): other = held(lax.ppermute(near, 'gy', both))  3.03 us
    ppermute x5, waiting for transfers between devices, swap(): lax.ppermute(m, axis, p)  2.58 us
    ppermute x1, starting transfers between devices, body(): sums = (rows[0], held(lax.ppermute(rows[1], 'gy', both)))  1.29 us
  transfers between devices with their start and end apart: 13, of which 6 were waited for; matrix products, arithmetic and copies ran while one was open for 0% of the time, Pallas kernels for 27%

profile of v5, /device:TPU:0, one launch (start us, length us, event | category | flops | bytes accessed | tf_op | source)
XLA Modules:
  0.0 52.8 jit_solution(5901046192214269031)
XLA Ops:
  0.7 1.8 %shard_map.95 = (f32[32,32,512]{2,1,0:T(8,128)S(1)}, f32[32,32,128]{2,1,0:T(8,128)S(1)}, f32[104,512]{1,0:T(8,128)S(1)}, f32[3,32,640]{2,1,0:T(8,128)S(1)}, f32[3,32,640]{2,1,0:T(8,128)S(1)}) custom-call(f32[32,32,512]{2,1,0:T(8,128)} %refs_0_.2, f32[32,16,32]{2,1,0:T(8,128)} %bitcast.11), custom_call_target="tpu_custom_call" | custom-call | bytes 3000000 | tf_op jit(solution)/shard_map/pallas_call | solution.py:58
  2.5 3.0 %collective-permute-start = (f32[104,512]{1,0:T(8,128)S(1)}, f32[104,512]{1,0:T(8,128)S(1)}, u32[]{:S(2)}, u32[]{:S(2)}) collective-permute-start(f32[104,512]{1,0:T(8,128)S(1)} %get-tuple-element.25.refs_3_.refs_0_), channel_id=1, source_target_pairs={{0,2},{2,0},{1,3},{3,1},{4,6},{6,4},{5,7},{7,5},{8,10},{10,8},{9,1... | collective-permute-start | bytes 638984 | tf_op jit(solution)/shard_map/ppermute | solution.py:556
  5.5 1.5 %collective-permute-start.6 = (f32[3,32,640]{2,1,0:T(8,128)S(1)}, f32[3,32,640]{2,1,0:T(8,128)S(1)}, u32[]{:S(2)}, u32[]{:S(2)}) collective-permute-start(f32[3,32,640]{2,1,0:T(8,128)S(1)} %get-tuple-element.34), channel_id=1, source_target_pairs={{0,4},{4,0},{8,12},{12,8},{16,20},{20,16},{24,28},{28,24},{1,5},{5... | collective-permute-start | bytes 737288 | tf_op jit(solution)/shard_map/ppermute | solution.py:82
  7.0 0.7 %collective-permute-start.7 = (f32[3,32,640]{2,1,0:T(8,128)S(1)}, f32[3,32,640]{2,1,0:T(8,128)S(1)}, u32[]{:S(2)}, u32[]{:S(2)}) collective-permute-start(f32[3,32,640]{2,1,0:T(8,128)S(1)} %get-tuple-element.35), channel_id=1, source_target_pairs={{4,8},{12,16},{20,24},{8,4},{16,12},{24,20},{5,9},{13,17},{21,25},... | collective-permute-start | bytes 737288 | tf_op jit(solution)/shard_map/ppermute | solution.py:82
  7.7 3.1 %collective-permute-done.refs_1_ = f32[104,512]{1,0:T(8,128)S(1)} collective-permute-done((f32[104,512]{1,0:T(8,128)S(1)}, f32[104,512]{1,0:T(8,128)S(1)}, u32[]{:S(2)}, u32[]{:S(2)}) %collective-permute-start) | collective-permute-done | bytes 213024 | tf_op jit(solution)/shard_map/ppermute | solution.py:556
  10.8 0.4 shard_map.97
  11.1 1.8 %collective-permute-start.1 = (f32[8,1024]{1,0:T(8,128)S(1)}, f32[8,1024]{1,0:T(8,128)S(1)}, u32[]{:S(2)}, u32[]{:S(2)}) collective-permute-start(f32[8,1024]{1,0:T(8,128)S(1)} %get-tuple-element.30), channel_id=1, source_target_pairs={{0,4},{4,0},{8,12},{12,8},{16,20},{20,16},{24,28},{28,24},{1,5},{5... | collective-permute-start | bytes 98312 | tf_op jit(solution)/shard_map/ppermute | solution.py:82
  12.9 0.7 %collective-permute-start.2 = (f32[8,1024]{1,0:T(8,128)S(1)}, f32[8,1024]{1,0:T(8,128)S(1)}, u32[]{:S(2)}, u32[]{:S(2)}) collective-permute-start(f32[8,1024]{1,0:T(8,128)S(1)} %get-tuple-element.31), channel_id=1, source_target_pairs={{4,8},{12,16},{20,24},{8,4},{16,12},{24,20},{5,9},{13,17},{21,25},... | collective-permute-start | bytes 98312 | tf_op jit(solution)/shard_map/ppermute | solution.py:82
  14.2 1.8 %shard_map.96 = (bf16[1024,1024]{1,0:T(8,128)(2,1)S(1)}, s32[8]{0:T(128)S(4)}) custom-call(s32[32,1,32]{2,1,0:T(1,128)S(1)} %copy-done.3, s32[1]{0:T(128)} %bitcast.6.refs_1_, s32[7]{0:T(128)S(1)} %bitcast.10, f32[104,512]{1,0:T(8,128)S(1)} %get-tuple-element.25.refs_3_.refs_0_), custom_call_target="tpu_custom_call" | custom-call | bytes 6000000 | tf_op jit(solution)/shard_map/pallas_call | solution.py:58
  16.0 2.6 %collective-permute-done.1.refs_3_.refs_5_ = f32[8,1024]{1,0:T(8,128)S(1)} collective-permute-done((f32[8,1024]{1,0:T(8,128)S(1)}, f32[8,1024]{1,0:T(8,128)S(1)}, u32[]{:S(2)}, u32[]{:S(2)}) %collective-permute-start.1) | collective-permute-done | bytes 32800 | tf_op jit(solution)/shard_map/ppermute | solution.py:82
  18.6 0.5 %shard_map.101 = f32[38,32,128]{2,1,0:T(8,128)S(1)} custom-call(f32[32,32,512]{2,1,0:T(8,128)S(1)} %get-tuple-element.32.refs_0_, f32[32,32,128]{2,1,0:T(8,128)S(1)} %get-tuple-element.33.refs_1_, f32[3,32,640]{2,1,0:T(8,128)S(1)} %collective-permute-done.6.refs_2_, f32[3,32,640]{2,1,0:T(8,128)S(1)} %collective-permute-done.7.refs_3_, ...), custom_call_target="tpu_custom_call" | custom-call | bytes 900000 | tf_op jit(solution)/shard_map/pallas_call | solution.py:58
  19.2 0.2 collective-permute-start.8
  19.4 0.9 %shard_map.98.refs_0_ = bf16[1,32,1024]{2,1,0:T(8,128)(2,1)S(1)} custom-call(f32[3,32,1024]{2,1,0:T(8,128)S(1)} %get-tuple-element.27.refs_0_, f32[3,32,1024]{2,1,0:T(8,128)S(1)} %get-tuple-element.28.refs_1_, bf16[1024,1024]{1,0:T(8,128)(2,1)S(1)} %get-tuple-element.29.refs_2_.refs_4_.refs_6_, f32[8,1024]{1,0:T(8,128)S(1)} %collective-permute-done.1.refs_3_.refs_5_, ...), custom_call_target="tpu_custom_call" | custom-call | bytes 3000000 | tf_op jit(solution)/shard_map/pallas_call | solution.py:58
  20.3 5.0 %collective-permute-start.3 = (bf16[1,32,1024]{2,1,0:T(8,128)(2,1)S(1)}, bf16[1,32,1024]{2,1,0:T(8,128)(2,1)S(1)}, u32[]{:S(2)}, u32[]{:S(2)}) collective-permute-start(bf16[1,32,1024]{2,1,0:T(8,128)(2,1)S(1)} %shard_map.98.refs_0_), channel_id=1, source_target_pairs={{0,16},{4,20},{8,24},{12,28},{16,0},{20,4},{24,8},{28,12},{1,17},{... | collective-permute-start | bytes 196616 | tf_op jit(solution)/shard_map/ppermute | solution.py:584
  25.3 2.4 %collective-permute-done.3.refs_1_ = bf16[1,32,1024]{2,1,0:T(8,128)(2,1)S(1)} collective-permute-done((bf16[1,32,1024]{2,1,0:T(8,128)(2,1)S(1)}, bf16[1,32,1024]{2,1,0:T(8,128)(2,1)S(1)}, u32[]{:S(2)}, u32[]{:S(2)}) %collective-permute-start.3) | collective-permute-done | bytes 65568 | tf_op jit(solution)/shard_map/ppermute | solution.py:584
  27.7 1.8 %collective-permute-start.4 = (bf16[2,32,1024]{2,1,0:T(8,128)(2,1)S(1)}, bf16[2,32,1024]{2,1,0:T(8,128)(2,1)S(1)}, u32[]{:S(2)}, u32[]{:S(2)}) collective-permute-start(bf16[2,32,1024]{2,1,0:T(8,128)(2,1)S(1)} %shard_map.99.refs_0_), channel_id=1, source_target_pairs={{0,8},{4,12},{8,0},{12,4},{16,24},{20,28},{24,16},{28,20},{1,9},{5... | collective-permute-start | bytes 393224 | tf_op jit(solution)/shard_map/ppermute | solution.py:584
  29.5 3.2 %collective-permute-done.4.refs_1_ = bf16[2,32,1024]{2,1,0:T(8,128)(2,1)S(1)} collective-permute-done((bf16[2,32,1024]{2,1,0:T(8,128)(2,1)S(1)}, bf16[2,32,1024]{2,1,0:T(8,128)(2,1)S(1)}, u32[]{:S(2)}, u32[]{:S(2)}) %collective-permute-start.4) | collective-permute-done | bytes 131104 | tf_op jit(solution)/shard_map/ppermute | solution.py:584
  32.8 1.0 %collective-permute-start.5 = (bf16[4,32,1024]{2,1,0:T(8,128)(2,1)S(1)}, bf16[4,32,1024]{2,1,0:T(8,128)(2,1)S(1)}, u32[]{:S(2)}, u32[]{:S(2)}) collective-permute-start(bf16[4,32,1024]{2,1,0:T(8,128)(2,1)S(1)} %shard_map.100.refs_5_.refs_0_), channel_id=1, source_target_pairs={{0,4},{4,0},{8,12},{12,8},{16,20},{20,16},{24,28},{28,24},{1,5},{5... | collective-permute-start | bytes 786440 | tf_op jit(solution)/shard_map/ppermute | solution.py:584
  33.8 0.2 shard_map.102
  34.0 0.1 collective-permute-start.9
  34.1 0.5 collective-permute-start.10
  34.6 1.1 %collective-permute-done.10.refs_6_ = f32[40,768]{1,0:T(8,128)S(1)} collective-permute-done((f32[40,768]{1,0:T(8,128)S(1)}, f32[40,768]{1,0:T(8,128)S(1)}, u32[]{:S(2)}, u32[]{:S(2)}) %collective-permute-start.10) | collective-permute-done | bytes 122912 | tf_op jit(solution)/shard_map/ppermute | solution.py:595
  35.7 2.9 %shard_map.103 = (f32[1520,640]{1,0:T(8,128)S(1)}, f32[1520,640]{1,0:T(8,128)S(1)}, f32[1520,640]{1,0:T(8,128)S(1)}) custom-call(f32[32,32,512]{2,1,0:T(8,128)S(1)} %get-tuple-element.32.refs_0_, f32[32,32,128]{2,1,0:T(8,128)S(1)} %get-tuple-element.33.refs_1_, f32[3,32,640]{2,1,0:T(8,128)S(1)} %collective-permute-done.6.refs_2_, ...), custom_call_target="tpu_custom_call" | custom-call | bytes 9000000 | tf_op jit(solution)/shard_map/pallas_call | solution.py:58
  38.7 2.8 %shard_map.104.refs_2_ = f32[1520,640]{1,0:T(8,128)S(1)} custom-call(f32[1520,640]{1,0:T(8,128)S(1)} %get-tuple-element.38.refs_0_, f32[1520,640]{1,0:T(8,128)S(1)} %get-tuple-element.39.refs_1_, f32[1520,640]{1,0:T(8,128)S(1)} %get-tuple-element.40.refs_2_), custom_call_target="tpu_custom_call" | custom-call | bytes 7500000 | tf_op jit(solution)/shard_map/pallas_call | solution.py:58
  41.6 0.0 copy-start.1
  41.6 0.3 collective-permute-start.11
  41.9 2.8 %shard_map.106.refs_7_.refs_2_ = f32[1520,640]{1,0:T(8,128)S(1)} custom-call(f32[1520,640]{1,0:T(8,128)S(1)} %get-tuple-element.38.refs_0_, f32[1520,640]{1,0:T(8,128)S(1)} %get-tuple-element.39.refs_1_, f32[1520,640]{1,0:T(8,128)S(1)} %shard_map.104.refs_2_, bf16[8,32,1024]{2,1,0:T(8,128)(2,1)S(1)} %shard_map.105.refs_3_.refs_1_), custom_call_target="tpu_custom_call" | custom-call | bytes 7500000 | tf_op jit(solution)/shard_map/pallas_call | solution.py:58
  44.7 2.6 %shard_map.107 = (f32[32,512]{1,0:T(8,128)S(1)}, f32[32,512]{1,0:T(8,128)S(1)}) custom-call(s32[8]{0:T(128)S(4)} %get-tuple-element.26.refs_0_, bf16[8,32,1024]{2,1,0:T(8,128)(2,1)S(1)} %shard_map.105.refs_3_.refs_1_, bf16[8,32,1024]{2,1,0:T(8,128)(2,1)S(1)} %collective-permute-done.11.refs_2_, bf16[1024,1024]{1,0:T(8,128)(2,1)S(1)} %bitcast.7, ...), custom_call_target="tpu_custom_call" | custom-call | bytes 7500000 | tf_op jit(solution)/shard_map/pallas_call | solution.py:58
  47.3 1.3 %collective-permute-start.12 = (f32[32,512]{1,0:T(8,128)S(1)}, f32[32,512]{1,0:T(8,128)S(1)}, u32[]{:S(2)}, u32[]{:S(2)}) collective-permute-start(f32[32,512]{1,0:T(8,128)S(1)} %get-tuple-element.42.refs_4_), channel_id=1, source_target_pairs={{0,2},{2,0},{1,3},{3,1},{4,6},{6,4},{5,7},{7,5},{8,10},{10,8},{9,1... | collective-permute-start | bytes 196616 | tf_op jit(solution)/shard_map/ppermute | solution.py:623
  48.6 2.5 %shard_map.108 = (f32[32,32,512]{2,1,0:T(8,128)}, f32[32,8,512]{2,1,0:T(8,128)S(1)}) custom-call(f32[1520,640]{1,0:T(8,128)S(1)} %get-tuple-element.38.refs_0_, f32[1520,640]{1,0:T(8,128)S(1)} %get-tuple-element.39.refs_1_, f32[1520,640]{1,0:T(8,128)S(1)} %shard_map.106.refs_7_.refs_2_, f32[32,512]{1,0:T(8,128)S(1)} %get-tuple-element.41.refs_3_.refs_0_, ...), custom_call_target="tpu_custom_call" | custom-call | bytes 6000000 | tf_op jit(solution)/shard_map/pallas_call | solution.py:58
  51.1 0.5 %collective-permute-done.12.refs_1_ = f32[32,512]{1,0:T(8,128)S(1)} collective-permute-done((f32[32,512]{1,0:T(8,128)S(1)}, f32[32,512]{1,0:T(8,128)S(1)}, u32[]{:S(2)}, u32[]{:S(2)}) %collective-permute-start.12) | collective-permute-done | bytes 65568 | tf_op jit(solution)/shard_map/ppermute | solution.py:623
  51.7 1.1 %shard_map.109 = (f32[32,1,512]{2,1,0:T(1,128)}, f32[32,32,512]{2,1,0:T(8,128)}) custom-call(f32[32,512]{1,0:T(8,128)S(1)} %get-tuple-element.41.refs_3_.refs_0_, f32[32,512]{1,0:T(8,128)S(1)} %collective-permute-done.12.refs_1_, f32[32,512]{1,0:T(8,128)S(1)} %get-tuple-element.43.refs_2_, ...), custom_call_target="tpu_custom_call", output_to_operand_aliasing={{1}: (4, {})} | custom-call | bytes 3000000 | tf_op jit(solution)/shard_map/pallas_call | solution.py:58
  (19 shorter events, 0.1 us)
Async XLA Ops:
  0.6 13.6 %copy-start.4 = (s32[1,1,1,7]{3,2,1,0:T(1,128)S(1)}, s32[1,1,1,7]{3,2,1,0:T(1,128)}, u32[]{:S(2)}) copy-start(s32[1,1,1,7]{3,2,1,0:T(1,128)} %param.12) | copy-start | bytes 88
  0.6 13.6 %copy-start.3 = (s32[32,1,32]{2,1,0:T(1,128)S(1)}, s32[32,1,32]{2,1,0:T(1,128)}, u32[]{:S(2)}) copy-start(s32[32,1,32]{2,1,0:T(1,128)} %refs_0_.3) | copy-start | bytes 12292
  2.5 8.3 %collective-permute-start = (f32[104,512]{1,0:T(8,128)S(1)}, f32[104,512]{1,0:T(8,128)S(1)}, u32[]{:S(2)}, u32[]{:S(2)}) collective-permute-start(f32[104,512]{1,0:T(8,128)S(1)} %get-tuple-element.25.refs_3_.refs_0_), channel_id=1, source_target_pairs={{0,2},{2,0},{1,3},{3,1},{4,6},{6,4},{5,7},{7,5},{8,10},{10,8},{9,1... | collective-permute-start | bytes 638984 | tf_op jit(solution)/shard_map/ppermute | solution.py:556
  5.5 13.1 %collective-permute-start.6 = (f32[3,32,640]{2,1,0:T(8,128)S(1)}, f32[3,32,640]{2,1,0:T(8,128)S(1)}, u32[]{:S(2)}, u32[]{:S(2)}) collective-permute-start(f32[3,32,640]{2,1,0:T(8,128)S(1)} %get-tuple-element.34), channel_id=1, source_target_pairs={{0,4},{4,0},{8,12},{12,8},{16,20},{20,16},{24,28},{28,24},{1,5},{5... | collective-permute-start | bytes 737288 | tf_op jit(solution)/shard_map/ppermute | solution.py:82
  7.0 11.6 %collective-permute-start.7 = (f32[3,32,640]{2,1,0:T(8,128)S(1)}, f32[3,32,640]{2,1,0:T(8,128)S(1)}, u32[]{:S(2)}, u32[]{:S(2)}) collective-permute-start(f32[3,32,640]{2,1,0:T(8,128)S(1)} %get-tuple-element.35), channel_id=1, source_target_pairs={{4,8},{12,16},{20,24},{8,4},{16,12},{24,20},{5,9},{13,17},{21,25},... | collective-permute-start | bytes 737288 | tf_op jit(solution)/shard_map/ppermute | solution.py:82
  11.1 7.5 %collective-permute-start.1 = (f32[8,1024]{1,0:T(8,128)S(1)}, f32[8,1024]{1,0:T(8,128)S(1)}, u32[]{:S(2)}, u32[]{:S(2)}) collective-permute-start(f32[8,1024]{1,0:T(8,128)S(1)} %get-tuple-element.30), channel_id=1, source_target_pairs={{0,4},{4,0},{8,12},{12,8},{16,20},{20,16},{24,28},{28,24},{1,5},{5... | collective-permute-start | bytes 98312 | tf_op jit(solution)/shard_map/ppermute | solution.py:82
  12.9 5.7 %collective-permute-start.2 = (f32[8,1024]{1,0:T(8,128)S(1)}, f32[8,1024]{1,0:T(8,128)S(1)}, u32[]{:S(2)}, u32[]{:S(2)}) collective-permute-start(f32[8,1024]{1,0:T(8,128)S(1)} %get-tuple-element.31), channel_id=1, source_target_pairs={{4,8},{12,16},{20,24},{8,4},{16,12},{24,20},{5,9},{13,17},{21,25},... | collective-permute-start | bytes 98312 | tf_op jit(solution)/shard_map/ppermute | solution.py:82
  19.2 14.6 %collective-permute-start.8 = (f32[38,32,128]{2,1,0:T(8,128)S(1)}, f32[38,32,128]{2,1,0:T(8,128)S(1)}, u32[]{:S(2)}, u32[]{:S(2)}) collective-permute-start(f32[38,32,128]{2,1,0:T(8,128)S(1)} %shard_map.101), channel_id=1, source_target_pairs={{0,2},{2,0},{1,3},{3,1},{4,6},{6,4},{5,7},{7,5},{8,10},{10,8},{9,1... | collective-permute-start | bytes 1867784 | tf_op jit(solution)/shard_map/ppermute | solution.py:82
  20.3 7.4 %collective-permute-start.3 = (bf16[1,32,1024]{2,1,0:T(8,128)(2,1)S(1)}, bf16[1,32,1024]{2,1,0:T(8,128)(2,1)S(1)}, u32[]{:S(2)}, u32[]{:S(2)}) collective-permute-start(bf16[1,32,1024]{2,1,0:T(8,128)(2,1)S(1)} %shard_map.98.refs_0_), channel_id=1, source_target_pairs={{0,16},{4,20},{8,24},{12,28},{16,0},{20,4},{24,8},{28,12},{1,17},{... | collective-permute-start | bytes 196616 | tf_op jit(solution)/shard_map/ppermute | solution.py:584
  27.7 5.0 %collective-permute-start.4 = (bf16[2,32,1024]{2,1,0:T(8,128)(2,1)S(1)}, bf16[2,32,1024]{2,1,0:T(8,128)(2,1)S(1)}, u32[]{:S(2)}, u32[]{:S(2)}) collective-permute-start(bf16[2,32,1024]{2,1,0:T(8,128)(2,1)S(1)} %shard_map.99.refs_0_), channel_id=1, source_target_pairs={{0,8},{4,12},{8,0},{12,4},{16,24},{20,28},{24,16},{28,20},{1,9},{5... | collective-permute-start | bytes 393224 | tf_op jit(solution)/shard_map/ppermute | solution.py:584
  32.8 8.7 %collective-permute-start.5 = (bf16[4,32,1024]{2,1,0:T(8,128)(2,1)S(1)}, bf16[4,32,1024]{2,1,0:T(8,128)(2,1)S(1)}, u32[]{:S(2)}, u32[]{:S(2)}) collective-permute-start(bf16[4,32,1024]{2,1,0:T(8,128)(2,1)S(1)} %shard_map.100.refs_5_.refs_0_), channel_id=1, source_target_pairs={{0,4},{4,0},{8,12},{12,8},{16,20},{20,16},{24,28},{28,24},{1,5},{5... | collective-permute-start | bytes 786440 | tf_op jit(solution)/shard_map/ppermute | solution.py:584
  34.0 1.7 %collective-permute-start.9 = (f32[2,40,640]{2,1,0:T(8,128)S(1)}, f32[2,40,640]{2,1,0:T(8,128)S(1)}, u32[]{:S(2)}, u32[]{:S(2)}) collective-permute-start(f32[2,40,640]{2,1,0:T(8,128)S(1)} %get-tuple-element.36), channel_id=1, source_target_pairs={{0,1},{1,0},{2,3},{3,2},{4,5},{5,4},{6,7},{7,6},{8,9},{9,8},{10,11... | collective-permute-start | bytes 614408 | tf_op jit(solution)/shard_map/ppermute | solution.py:595
  34.1 1.6 %collective-permute-start.10 = (f32[40,768]{1,0:T(8,128)S(1)}, f32[40,768]{1,0:T(8,128)S(1)}, u32[]{:S(2)}, u32[]{:S(2)}) collective-permute-start(f32[40,768]{1,0:T(8,128)S(1)} %get-tuple-element.37), channel_id=1, source_target_pairs={{0,1},{1,0},{2,3},{3,2},{4,5},{5,4},{6,7},{7,6},{8,9},{9,8},{10,11... | collective-permute-start | bytes 368648 | tf_op jit(solution)/shard_map/ppermute | solution.py:595
  41.5 3.2 %copy-start = (bf16[1,1,1,1024,1024]{4,3,2,1,0:T(8,128)(2,1)S(1)}, bf16[1,1,1,1024,1024]{4,3,2,1,0:T(8,128)(2,1)}, u32[]{:S(2)}) copy-start(bf16[1,1,1,1024,1024]{4,3,2,1,0:T(8,128)(2,1)} %param.13) | copy-start | bytes 6291460
  41.6 3.2 %copy-start.1 = (bf16[1,1,1,7,16,1024]{5,4,3,2,1,0:T(8,128)(2,1)S(1)}, bf16[1,1,1,7,16,1024]{5,4,3,2,1,0:T(8,128)(2,1)}, u32[]{:S(2)}) copy-start(bf16[1,1,1,7,16,1024]{5,4,3,2,1,0:T(8,128)(2,1)} %param.15) | copy-start | bytes 688132
  41.6 3.2 %copy-start.2 = (bf16[1,1,1,7,16,1024]{5,4,3,2,1,0:T(8,128)(2,1)S(1)}, bf16[1,1,1,7,16,1024]{5,4,3,2,1,0:T(8,128)(2,1)}, u32[]{:S(2)}) copy-start(bf16[1,1,1,7,16,1024]{5,4,3,2,1,0:T(8,128)(2,1)} %param.14) | copy-start | bytes 688132
  41.6 3.1 %collective-permute-start.11 = (bf16[8,32,1024]{2,1,0:T(8,128)(2,1)S(1)}, bf16[8,32,1024]{2,1,0:T(8,128)(2,1)S(1)}, u32[]{:S(2)}, u32[]{:S(2)}) collective-permute-start(bf16[8,32,1024]{2,1,0:T(8,128)(2,1)S(1)} %shard_map.105.refs_3_.refs_1_), channel_id=1, source_target_pairs={{0,1},{1,0},{2,3},{3,2},{4,5},{5,4},{6,7},{7,6},{8,9},{9,8},{10,11... | collective-permute-start | bytes 1572872 | tf_op jit(solution)/shard_map/ppermute | solution.py:609
  47.3 4.3 %collective-permute-start.12 = (f32[32,512]{1,0:T(8,128)S(1)}, f32[32,512]{1,0:T(8,128)S(1)}, u32[]{:S(2)}, u32[]{:S(2)}) collective-permute-start(f32[32,512]{1,0:T(8,128)S(1)} %get-tuple-element.42.refs_4_), channel_id=1, source_target_pairs={{0,2},{2,0},{1,3},{3,1},{4,6},{6,4},{5,7},{7,5},{8,10},{10,8},{9,1... | collective-permute-start | bytes 196616 | tf_op jit(solution)/shard_map/ppermute | solution.py:623

commit v6 on v5

--- a/solution.py
+++ b/solution.py
@@ -162,12 +162,23 @@
 
 
 def row_edges(odd, source, inv, messages):
-    rows_x, _, width = source.shape
+    rows_x, depth, width = source.shape
     for number, message in enumerate(messages):
+        packs = jnp.zeros((depth, LANES), jnp.float32)
         for k in range(HALO):
             last = rows_x - HALO + k
-            message[k, :, :width] = choose(odd, source[k], source[last], number)
-            message[k, :, width:] = choose(odd, inv[k], inv[last], number)
+            message[k * depth : (k + 1) * depth, :] = choose(odd, source[k], source[last], number)
+            packs = packs + roll(choose(odd, inv[k], inv[last], number), 32 * k, 1)
+        for n in range(depth // ROWS):
+            message[HALO * depth :, n * LANES : (n + 1) * LANES] = packs[n * ROWS : (n + 1) * ROWS]
+
+
+def row_layers(message, depth):
+    packs = jnp.concatenate(
+        [message[HALO * depth :, n * LANES : (n + 1) * LANES] for n in range(depth // ROWS)], axis=0
+    )
+    planes = [message[k * depth : (k + 1) * depth] for k in range(HALO)]
+    return planes, [jnp.where(lane_ids(packs) < 32, roll(packs, -32 * k, 1), 0.0) for k in range(HALO)]
 
 
 def face_side_kernel(groups, own, other, s_out, i_out, i_own, *messages):
@@ -267,7 +278,21 @@
 ACROSS = (((1,), (1,)), ((), ()))
 
 
-def operator_kernel(halves, wanted, here, there, near, far_v, far_u, order, *outs):
+def row_order_kernel(order, near, far_u, near_out, far_out):
+    size = 2 * LANES
+
+    def step(n, _):
+        columns = pl.ds(pl.multiple_of(n * size, size), size)
+        rows = jnp.dot(order[...], near[:, columns], preferred_element_type=jnp.float32)
+        near_out[:, columns] = rows.astype(jnp.bfloat16)
+        return 0
+
+    lax.fori_loop(0, near.shape[1] // size, step, 0)
+    rows = lax.dot_general(far_u[...], order[...], ACROSS, preferred_element_type=jnp.float32)
+    far_out[...] = rows.astype(jnp.bfloat16)
+
+
+def operator_kernel(halves, wanted, here, there, near, far_v, far_u, *outs):
     count = wanted.shape[0] - 1
     rank = far_v.shape[0] // count
     across = functools.partial(
@@ -289,19 +314,13 @@
     rows = rows + jnp.dot(
         weights.astype(jnp.bfloat16), far_u[...], preferred_element_type=jnp.float32
     )
-    high = rows.astype(jnp.bfloat16)
-    rest = rows - high.astype(jnp.float32)
-    middle = rest.astype(jnp.bfloat16)
-    low = (rest - middle.astype(jnp.float32)).astype(jnp.bfloat16)
-    placed = across(jnp.concatenate([high, middle, low], axis=0), order[...])
-    placed = placed[:E] + (placed[E : 2 * E] + placed[2 * E :])
     if halves:
-        half = placed.shape[1] // 2
+        half = rows.shape[1] // 2
         first = index("gy") == 0
-        outs[0][...] = jnp.where(first, placed[:, :half], placed[:, half:])
-        outs[1][...] = jnp.where(first, placed[:, half:], placed[:, :half])
+        outs[0][...] = jnp.where(first, rows[:, :half], rows[:, half:])
+        outs[1][...] = jnp.where(first, rows[:, half:], rows[:, :half])
     else:
-        outs[0][...] = placed
+        outs[0][...] = rows
 
 
 def finish_kernel(count, *refs):
@@ -336,23 +355,28 @@
 def side_edge_kernel(nx, source, inv, *refs):
     odd_x, odd_y = index("gx") % 2, index("gy") % 2
     got_x, messages = [r[...] for r in refs[:nx]], refs[nx:]
-    rows_x, _, width = source.shape
+    rows_x, depth, width = source.shape
     cells = width // E
     halo = HALO * E
 
     def put(rows, first, last, c):
         lane = lane_ids(c)
-        low = jnp.where(lane < halo, first, roll(c, halo, 2))
-        high = jnp.where(lane < halo, roll(last, halo, 2), roll(c, halo - (cells - HALO), 2))
+        axis = c.ndim - 1
+        low = jnp.where(lane < halo, first, roll(c, halo, axis))
+        high = jnp.where(lane < halo, roll(last, halo, axis), roll(c, halo - (cells - HALO), axis))
         for number, message in enumerate(messages):
             message[rows] = choose(odd_y, low, high, number)
 
-    put(slice(HALO, HALO + rows_x), source[:, :, :LANES], source[:, :, width - LANES :], inv[...])
-    for rows, edge in (
-        (slice(0, HALO), from_low(odd_x, got_x)),
-        (slice(HALO + rows_x, None), from_high(odd_x, got_x)),
+    own = slice(HALO - 1, HALO - 1 + rows_x)
+    put(own, source[:, :, :LANES], source[:, :, width - LANES :], inv[...])
+    for start, skip, edge in (
+        (0, 1, from_low(odd_x, got_x)),
+        (HALO - 1 + rows_x, 0, from_high(odd_x, got_x)),
     ):
-        put(rows, edge[:, :, :LANES], edge[:, :, width - LANES : width], edge[:, :, width:])
+        planes, compacts = row_layers(edge, depth)
+        for k in range(HALO - 1):
+            s, c = planes[k + skip], compacts[k + skip]
+            put(start + k, s[:, :LANES], s[:, width - LANES :], c)
 
 
 def widen(cells, ring, s, c, left, right):
@@ -378,14 +402,25 @@
     wide = ring * E
     rows = two_out.shape[1]
     packs = jnp.zeros((rows, LANES), jnp.float32)
+
+    def layer(message, z):
+        lanes = message[HALO * depth + z % ROWS : HALO * depth + z % ROWS + 1, z // ROWS * LANES :]
+        lanes = lanes[:, :LANES]
+        lines = []
+        for n in range(HALO):
+            line = message[n * depth + z : n * depth + z + 1, :]
+            compact = jnp.where(lane_ids(lanes) < 32, roll(lanes, -32 * n, 1), 0.0)
+            lines.append(jnp.concatenate([line, compact], axis=1))
+        return jnp.concatenate(lines, axis=0)
+
     for k in range(HALO):
         inner = lambda r: jnp.where(side == 0, r[:, depth - HALO + k, :], r[:, k, :])
-        edges = [inner(r) for r in got_x]
+        edges = [jnp.where(side == 0, layer(r, depth - HALO + k), layer(r, k)) for r in got_x]
         below, above = from_low(odd_x, edges), from_high(odd_x, edges)
-        empty = jnp.zeros((rows - rows_x - 2 * HALO, LANES), jnp.float32)
-        beside = [jnp.concatenate([inner(r), empty], axis=0) for r in got_y]
+        empty = jnp.zeros((rows - rows_x - 2 * HALO + 1, LANES), jnp.float32)
+        beside = [jnp.concatenate([empty[:1], inner(r), empty], axis=0) for r in got_y]
         own = jnp.concatenate([inner(source), inner(inv)], axis=1)
-        blank = jnp.zeros((empty.shape[0], width + LANES), jnp.float32)
+        blank = jnp.zeros((rows - rows_x - 2 * HALO, width + LANES), jnp.float32)
         all_rows = jnp.concatenate([below, own, above, blank], axis=0)
         parts, compact = widen(
             cells, ring, all_rows[:, :width], all_rows[:, width:],
@@ -419,8 +454,7 @@
             tile = jnp.where(at == k, value, tile)
         return tile
 
-    def place(x, s, c):
-        got = [r[x] for r in got_y]
+    def place(x, s, c, got):
         parts, compact = widen(cells, ring, s, c, from_low(odd_y, got), from_high(odd_y, got))
         last = z_one[pl.ds(x, 1), :]
         zone = spaced([z_two[0, pl.ds(x, 1), :], z_two[1, pl.ds(x, 1), :], last[:, :wide]])
@@ -437,15 +471,19 @@
         ext_s[rest, :] = zone
 
     def own(x, _):
-        place(x + HALO, source[x], inv[x])
+        place(x + HALO, source[x], inv[x], [r[x + HALO - 1] for r in got_y])
         return 0
 
     repeat(0, rows_x, own, 4)
-    for k in range(HALO):
-        got = [r[k] for r in got_x]
-        below, above = from_low(odd_x, got), from_high(odd_x, got)
-        place(k, below[:, :width], below[:, width:])
-        place(rows_x + HALO + k, above[:, :width], above[:, width:])
+    got = [r[...] for r in got_x]
+    for base, skip, edge in ((0, 0, from_low(odd_x, got)), (rows_x + HALO, 2, from_high(odd_x, got))):
+        planes, compact = row_layers(edge, depth)
+        for k in range(HALO):
+            if k == skip:
+                beside = [jnp.zeros((depth, LANES), jnp.float32) for _ in got_y]
+            else:
+                beside = [r[base + k - 1] for r in got_y]
+            place(base + k, planes[k], compact[k], beside)
     chunk = max(n for n in range(2 * ROWS, 321, 2 * ROWS) if total % n == 0)
 
     def expand(n, _):
@@ -490,7 +528,9 @@
         store(columns, new)
 
 
-def sweep_kernel(all_z, ext_s, ext_i, old, new):
+def sweep_kernel(all_z, first, last, ext_s, ext_i, old, *refs):
+    new = refs[-1]
+
     def step(x, _):
         def store(columns, value):
             new[pl.ds(pl.multiple_of(x * all_z, ROWS), all_z), columns] = value
@@ -498,7 +538,7 @@
         swept(ext_s, ext_i, old, x, all_z, all_z, old.shape[1], store)
         return 0
 
-    repeat(1, old.shape[0] // all_z - 1, step, 12)
+    repeat(first, last, step, 12)
 
 
 def last_sweep_kernel(ext_s, ext_i, old, out, slab, done, sems):
@@ -548,7 +588,7 @@
     held_source, inv, near, *vol_x = call(
         face_start_kernel, (kept(source), kept(coef)),
         [vector(source.shape), vector((rows_x, depth, LANES)), vector((NEAR * rows_x + ROWS, width))]
-        + [vector((HALO, depth, width + LANES))] * nx,
+        + [vector((HALO * depth + ROWS, width))] * nx,
         in_specs=[MAIN, MAIN],
         scratch=(vector(coef.shape), pltpu.SemaphoreType.DMA((2,))),
     )
@@ -570,7 +610,7 @@
     )
     vol_y = call(
         functools.partial(side_edge_kernel, nx), (held_source, inv, *got_vol_x),
-        [vector((all_x, depth, LANES))] * ny, work=300, after=(order, *got_x),
+        [vector((all_x - 2, depth, LANES))] * ny, work=300, after=(order, *got_x),
     )
     got_vol_y = swap(vol_y, "gy")
 
@@ -584,6 +624,14 @@
         other = held(lax.ppermute(traces, "gx", [(i, i ^ step) for i in range(size_x)]))
         twice = (2 * traces.shape[0], E, tile)
         before = ()
+        if step == steps[-2]:
+            near, far_rows = call(
+                row_order_kernel,
+                (order, held(near_tile.reshape(tile, tile)), held(far_u.reshape(count * rank, tile))),
+                [vector((tile, tile), bf16), vector((count * rank, tile), bf16)], work=3000,
+                after=(traces,),
+            )
+            before = (near,)
         if step == 1:
             rounded = -(-all_x // ROWS) * ROWS
             vol_z = call(
@@ -600,34 +648,40 @@
                 scratch=(vector((all_x * all_z, LANES)), vector((LANES, wide), bf16)),
             )
             (two,) = call(
-                functools.partial(sweep_kernel, all_z), (ext_s, ext_i, one), [ext], work=2500
+                functools.partial(sweep_kernel, all_z, 1, all_x - 1), (ext_s, ext_i, one), [ext],
+                work=2500,
             )
             before = (two,)
         (traces,) = call(
             join_kernel, (traces, other), [vector(twice, bf16)], work=300, after=before
         )
     other = held(lax.ppermute(traces, "gz", both))
+    count_x = (all_x - 4) // 2
+    middle = 2 + count_x - count_x % 4
     (three,) = call(
-        functools.partial(sweep_kernel, all_z), (ext_s, ext_i, two), [ext], work=2500,
+        functools.partial(sweep_kernel, all_z, 2, middle), (ext_s, ext_i, two), [ext], work=1400,
         after=(traces,),
     )
 
     rows = call(
         functools.partial(operator_kernel, halves),
-        (spot, traces, other, held(near_tile.reshape(tile, tile)),
-         held(far_v.reshape(count * rank, tile)), held(far_u.reshape(count * rank, tile)), order),
+        (spot, traces, other, near, held(far_v.reshape(count * rank, tile)), far_rows),
         [vector((E, part))] * 2 if halves else [plain((E, tile))],
-        in_specs=[SCALAR] + [VECTOR] * 6, work=2500, after=(three,),
+        in_specs=[SCALAR] + [VECTOR] * 5, work=2500, after=(three,),
     )
     if halves:
         sums = (rows[0], held(lax.ppermute(rows[1], "gy", both)))
     else:
         sums = (held(lax.psum_scatter(rows[0], "gy", scatter_dimension=1, tiled=True)),)
+    (three,) = call(
+        functools.partial(sweep_kernel, all_z, middle, all_x - 2), (ext_s, ext_i, two, three), [ext],
+        work=1400, input_output_aliases={3: 0}, after=rows,
+    )
     pieces = 4
     field, slab = call(
         last_sweep_kernel, (ext_s, ext_i, three),
         [plain(source.shape), vector((rows_x, ROWS, width))], work=2000,
-        out_specs=[MAIN, VECTOR], after=rows,
+        out_specs=[MAIN, VECTOR],
         scratch=(vector(source.shape), pltpu.SemaphoreType.DMA((pieces,))),
     )
 

time: 53 us -> 51 us (0.962)
  waiting for transfers between devices: 13 us -> 7.85 us
  Pallas kernels: 20.5 us -> 22.9 us
  starting transfers between devices: 17.8 us -> 18.6 us
    ppermute x3, waiting for transfers between devices: 5.62 us -> 2.42 us  [body(): lax.ppermute(traces, 'gx', [(i, i ^ step) for i in range(size_x)])]
    pallas_call x15 -> x17, Pallas kernels: 20.5 us -> 22.9 us  [call(): pl.pallas_call(body, out_shape=out_shape, in_specs=(in_specs or [VECTOR]...]
    ppermute x5, waiting for transfers between devices: 2.58 us -> 0.82 us  [swap(): lax.ppermute(m, axis, p)]
    ppermute x3, starting transfers between devices: 7.8 us -> 8.75 us  [body(): lax.ppermute(traces, 'gx', [(i, i ^ step) for i in range(size_x)])]
    ppermute x1, starting transfers between devices: 1.29 us -> 0.54 us  [body(): sums = (rows[0], held(lax.ppermute(rows[1], 'gy', both)))]
    ppermute x5, starting transfers between devices: 4.8 us -> 5.39 us  [swap(): lax.ppermute(m, axis, p)]
    ppermute x1, waiting for transfers between devices: 0.55 us -> 0.01 us  [body(): sums = (rows[0], held(lax.ppermute(rows[1], 'gy', both)))]
  transfers between devices with their start and end apart: 13 -> 13, of which waited for: 6 -> 6; matrix products, arithmetic and copies ran while one was open for 0% -> 0% of each run, Pallas kernels for 27% -> 36%
where the time goes in v6:
time: 51 us; the launch traced here: 50.8 us
  Pallas kernels  22.9 us (45%)
  starting transfers between devices  18.6 us (36%)
  waiting for transfers between devices  7.85 us (15%)
  between operations  1.49 us (3%)
    pallas_call x17, Pallas kernels, call(): pl.pallas_call(body, out_shape=out_shape, in_specs=(in_specs or [VECTOR]...  22.9 us
    ppermute x3, starting transfers between devices, body(): lax.ppermute(traces, 'gx', [(i, i ^ step) for i in range(size_x)])  8.75 us
    ppermute x5, starting transfers between devices, swap(): lax.ppermute(m, axis, p)  5.39 us
    ppermute x1, waiting for transfers between devices, body(): other = held(lax.ppermute(near, 'gy', both))  3.09 us
    ppermute x1, starting transfers between devices, body(): other = held(lax.ppermute(near, 'gy', both))  3.03 us
    ppermute x3, waiting for transfers between devices, body(): lax.ppermute(traces, 'gx', [(i, i ^ step) for i in range(size_x)])  2.42 us
    ppermute x2, waiting for transfers between devices, body(): got_vol_z = [held(lax.ppermute(v, 'gz', both)) for v in vol_z]  1.12 us
  transfers between devices with their start and end apart: 13, of which 6 were waited for; matrix products, arithmetic and copies ran while one was open for 0% of the time, Pallas kernels for 36%

profile of v6, /device:TPU:0, one launch (start us, length us, event | category | flops | bytes accessed | tf_op | source)
XLA Modules:
  0.0 50.8 jit_solution(9772496112868113547)
XLA Ops:
  0.7 1.9 %shard_map.95 = (f32[32,32,512]{2,1,0:T(8,128)S(1)}, f32[32,32,128]{2,1,0:T(8,128)S(1)}, f32[104,512]{1,0:T(8,128)S(1)}, f32[104,512]{1,0:T(8,128)S(1)}, f32[104,512]{1,0:T(8,128)S(1)}) custom-call(f32[32,32,512]{2,1,0:T(8,128)} %refs_0_.2, f32[32,16,32]{2,1,0:T(8,128)} %bitcast.11), custom_call_target="tpu_custom_call" | custom-call | bytes 3000000 | tf_op jit(solution)/shard_map/pallas_call | solution.py:58
  2.5 3.0 %collective-permute-start = (f32[104,512]{1,0:T(8,128)S(1)}, f32[104,512]{1,0:T(8,128)S(1)}, u32[]{:S(2)}, u32[]{:S(2)}) collective-permute-start(f32[104,512]{1,0:T(8,128)S(1)} %get-tuple-element.27.refs_3_.refs_0_), channel_id=1, source_target_pairs={{0,2},{2,0},{1,3},{3,1},{4,6},{6,4},{5,7},{7,5},{8,10},{10,8},{9,1... | collective-permute-start | bytes 638984 | tf_op jit(solution)/shard_map/ppermute | solution.py:596
  5.6 1.5 %collective-permute-start.6 = (f32[104,512]{1,0:T(8,128)S(1)}, f32[104,512]{1,0:T(8,128)S(1)}, u32[]{:S(2)}, u32[]{:S(2)}) collective-permute-start(f32[104,512]{1,0:T(8,128)S(1)} %get-tuple-element.37), channel_id=1, source_target_pairs={{0,4},{4,0},{8,12},{12,8},{16,20},{20,16},{24,28},{28,24},{1,5},{5... | collective-permute-start | bytes 638984 | tf_op jit(solution)/shard_map/ppermute | solution.py:82
  7.1 0.7 %collective-permute-start.7 = (f32[104,512]{1,0:T(8,128)S(1)}, f32[104,512]{1,0:T(8,128)S(1)}, u32[]{:S(2)}, u32[]{:S(2)}) collective-permute-start(f32[104,512]{1,0:T(8,128)S(1)} %get-tuple-element.38), channel_id=1, source_target_pairs={{4,8},{12,16},{20,24},{8,4},{16,12},{24,20},{5,9},{13,17},{21,25},... | collective-permute-start | bytes 638984 | tf_op jit(solution)/shard_map/ppermute | solution.py:82
  7.7 3.1 %collective-permute-done.refs_1_ = f32[104,512]{1,0:T(8,128)S(1)} collective-permute-done((f32[104,512]{1,0:T(8,128)S(1)}, f32[104,512]{1,0:T(8,128)S(1)}, u32[]{:S(2)}, u32[]{:S(2)}) %collective-permute-start) | collective-permute-done | bytes 213024 | tf_op jit(solution)/shard_map/ppermute | solution.py:596
  10.8 0.4 shard_map.97
  11.2 1.8 %collective-permute-start.1 = (f32[8,1024]{1,0:T(8,128)S(1)}, f32[8,1024]{1,0:T(8,128)S(1)}, u32[]{:S(2)}, u32[]{:S(2)}) collective-permute-start(f32[8,1024]{1,0:T(8,128)S(1)} %get-tuple-element.32), channel_id=1, source_target_pairs={{0,4},{4,0},{8,12},{12,8},{16,20},{20,16},{24,28},{28,24},{1,5},{5... | collective-permute-start | bytes 98312 | tf_op jit(solution)/shard_map/ppermute | solution.py:82
  13.0 0.7 %collective-permute-start.2 = (f32[8,1024]{1,0:T(8,128)S(1)}, f32[8,1024]{1,0:T(8,128)S(1)}, u32[]{:S(2)}, u32[]{:S(2)}) collective-permute-start(f32[8,1024]{1,0:T(8,128)S(1)} %get-tuple-element.33), channel_id=1, source_target_pairs={{4,8},{12,16},{20,24},{8,4},{16,12},{24,20},{5,9},{13,17},{21,25},... | collective-permute-start | bytes 98312 | tf_op jit(solution)/shard_map/ppermute | solution.py:82
  14.3 1.8 %shard_map.96 = (bf16[1024,1024]{1,0:T(8,128)(2,1)S(1)}, s32[8]{0:T(128)S(4)}) custom-call(s32[32,1,32]{2,1,0:T(1,128)S(1)} %copy-done.3, s32[1]{0:T(128)} %bitcast.6.refs_1_, s32[7]{0:T(128)S(1)} %bitcast.10, f32[104,512]{1,0:T(8,128)S(1)} %get-tuple-element.27.refs_3_.refs_0_), custom_call_target="tpu_custom_call" | custom-call | bytes 6000000 | tf_op jit(solution)/shard_map/pallas_call | solution.py:58
  16.1 0.5 collective-permute-done.6.refs_2_
  16.6 0.3 collective-permute-done.1.refs_3_.refs_5_
  16.9 0.6 %shard_map.102 = f32[36,32,128]{2,1,0:T(8,128)S(1)} custom-call(f32[32,32,512]{2,1,0:T(8,128)S(1)} %get-tuple-element.35.refs_0_, f32[32,32,128]{2,1,0:T(8,128)S(1)} %get-tuple-element.36.refs_1_, f32[104,512]{1,0:T(8,128)S(1)} %collective-permute-done.6.refs_2_, f32[104,512]{1,0:T(8,128)S(1)} %collective-permute-done.7.refs_3_, ...), custom_call_target="tpu_custom_call" | custom-call | bytes 900000 | tf_op jit(solution)/shard_map/pallas_call | solution.py:58
  17.5 0.8 %collective-permute-start.8 = (f32[36,32,128]{2,1,0:T(8,128)S(1)}, f32[36,32,128]{2,1,0:T(8,128)S(1)}, u32[]{:S(2)}, u32[]{:S(2)}) collective-permute-start(f32[36,32,128]{2,1,0:T(8,128)S(1)} %shard_map.102), channel_id=1, source_target_pairs={{0,2},{2,0},{1,3},{3,1},{4,6},{6,4},{5,7},{7,5},{8,10},{10,8},{9,1... | collective-permute-start | bytes 1769480 | tf_op jit(solution)/shard_map/ppermute | solution.py:82
  18.3 0.9 %shard_map.98.refs_0_ = bf16[1,32,1024]{2,1,0:T(8,128)(2,1)S(1)} custom-call(f32[3,32,1024]{2,1,0:T(8,128)S(1)} %get-tuple-element.29.refs_0_, f32[3,32,1024]{2,1,0:T(8,128)S(1)} %get-tuple-element.30.refs_1_, bf16[1024,1024]{1,0:T(8,128)(2,1)S(1)} %get-tuple-element.31.refs_2_.refs_0_.refs_4_, f32[8,1024]{1,0:T(8,128)S(1)} %collective-permute-done.1.refs_3_.refs_5_, ...), custom_call_target="tpu_custom_call" | custom-call | bytes 3000000 | tf_op jit(solution)/shard_map/pallas_call | solution.py:58
  19.3 6.1 %collective-permute-start.3 = (bf16[1,32,1024]{2,1,0:T(8,128)(2,1)S(1)}, bf16[1,32,1024]{2,1,0:T(8,128)(2,1)S(1)}, u32[]{:S(2)}, u32[]{:S(2)}) collective-permute-start(bf16[1,32,1024]{2,1,0:T(8,128)(2,1)S(1)} %shard_map.98.refs_0_), channel_id=1, source_target_pairs={{0,16},{4,20},{8,24},{12,28},{16,0},{20,4},{24,8},{28,12},{1,17},{... | collective-permute-start | bytes 196616 | tf_op jit(solution)/shard_map/ppermute | solution.py:624
  25.4 2.4 %collective-permute-done.3.refs_1_ = bf16[1,32,1024]{2,1,0:T(8,128)(2,1)S(1)} collective-permute-done((bf16[1,32,1024]{2,1,0:T(8,128)(2,1)S(1)}, bf16[1,32,1024]{2,1,0:T(8,128)(2,1)S(1)}, u32[]{:S(2)}, u32[]{:S(2)}) %collective-permute-start.3) | collective-permute-done | bytes 65568 | tf_op jit(solution)/shard_map/ppermute | solution.py:624
  27.8 1.8 %collective-permute-start.4 = (bf16[2,32,1024]{2,1,0:T(8,128)(2,1)S(1)}, bf16[2,32,1024]{2,1,0:T(8,128)(2,1)S(1)}, u32[]{:S(2)}, u32[]{:S(2)}) collective-permute-start(bf16[2,32,1024]{2,1,0:T(8,128)(2,1)S(1)} %shard_map.99.refs_3_.refs_0_), channel_id=1, source_target_pairs={{0,8},{4,12},{8,0},{12,4},{16,24},{20,28},{24,16},{28,20},{1,9},{5... | collective-permute-start | bytes 393224 | tf_op jit(solution)/shard_map/ppermute | solution.py:624
  29.6 3.7 %shard_map.100 = (bf16[1024,1024]{1,0:T(8,128)(2,1)S(1)}, bf16[112,1024]{1,0:T(8,128)(2,1)S(1)}) custom-call(bf16[1024,1024]{1,0:T(8,128)(2,1)S(1)} %get-tuple-element.31.refs_2_.refs_0_.refs_4_, bf16[1024,1024]{1,0:T(8,128)(2,1)S(1)} %bitcast.7, bf16[112,1024]{1,0:T(8,128)(2,1)S(1)} %bitcast.8, bf16[2,32,1024]{2,1,0:T(8,128)(2,1)S(1)} %shard_map.99.refs_3_.refs_0_), custom_call_target="tpu_custom_call" | custom-call | bytes 9000000 | tf_op jit(solution)/shard_map/pallas_call | solution.py:58
  33.4 0.8 %collective-permute-start.5 = (bf16[4,32,1024]{2,1,0:T(8,128)(2,1)S(1)}, bf16[4,32,1024]{2,1,0:T(8,128)(2,1)S(1)}, u32[]{:S(2)}, u32[]{:S(2)}) collective-permute-start(bf16[4,32,1024]{2,1,0:T(8,128)(2,1)S(1)} %shard_map.101.refs_5_.refs_0_), channel_id=1, source_target_pairs={{0,4},{4,0},{8,12},{12,8},{16,20},{20,16},{24,28},{28,24},{1,5},{5... | collective-permute-start | bytes 786440 | tf_op jit(solution)/shard_map/ppermute | solution.py:624
  34.2 0.3 shard_map.103
  34.6 0.5 collective-permute-start.10
  35.1 1.1 %collective-permute-done.10.refs_6_ = f32[40,768]{1,0:T(8,128)S(1)} collective-permute-done((f32[40,768]{1,0:T(8,128)S(1)}, f32[40,768]{1,0:T(8,128)S(1)}, u32[]{:S(2)}, u32[]{:S(2)}) %collective-permute-start.10) | collective-permute-done | bytes 122912 | tf_op jit(solution)/shard_map/ppermute | solution.py:643
  36.2 3.0 %shard_map.104 = (f32[1520,640]{1,0:T(8,128)S(1)}, f32[1520,640]{1,0:T(8,128)S(1)}, f32[1520,640]{1,0:T(8,128)S(1)}) custom-call(f32[32,32,512]{2,1,0:T(8,128)S(1)} %get-tuple-element.35.refs_0_, f32[32,32,128]{2,1,0:T(8,128)S(1)} %get-tuple-element.36.refs_1_, f32[104,512]{1,0:T(8,128)S(1)} %collective-permute-done.6.refs_2_, ...), custom_call_target="tpu_custom_call" | custom-call | bytes 9000000 | tf_op jit(solution)/shard_map/pallas_call | solution.py:58
  39.2 2.8 %shard_map.105.refs_2_ = f32[1520,640]{1,0:T(8,128)S(1)} custom-call(f32[1520,640]{1,0:T(8,128)S(1)} %get-tuple-element.41.refs_0_, f32[1520,640]{1,0:T(8,128)S(1)} %get-tuple-element.42.refs_1_, f32[1520,640]{1,0:T(8,128)S(1)} %get-tuple-element.43.refs_2_), custom_call_target="tpu_custom_call" | custom-call | bytes 7500000 | tf_op jit(solution)/shard_map/pallas_call | solution.py:58
  42.1 0.3 collective-permute-start.11
  42.4 1.3 %shard_map.107.refs_6_.refs_3_ = f32[1520,640]{1,0:T(8,128)S(1)} custom-call(f32[1520,640]{1,0:T(8,128)S(1)} %get-tuple-element.41.refs_0_, f32[1520,640]{1,0:T(8,128)S(1)} %get-tuple-element.42.refs_1_, f32[1520,640]{1,0:T(8,128)S(1)} %shard_map.105.refs_2_, bf16[8,32,1024]{2,1,0:T(8,128)(2,1)S(1)} %shard_map.106.refs_3_.refs_1_), custom_call_target="tpu_custom_call" | custom-call | bytes 4200000 | tf_op jit(solution)/shard_map/pallas_call | solution.py:58
  43.6 0.4 collective-permute-done.11.refs_2_
  44.1 1.1 %shard_map.108 = (f32[32,512]{1,0:T(8,128)S(1)}, f32[32,512]{1,0:T(8,128)S(1)}) custom-call(s32[8]{0:T(128)S(4)} %get-tuple-element.28.refs_0_, bf16[8,32,1024]{2,1,0:T(8,128)(2,1)S(1)} %shard_map.106.refs_3_.refs_1_, bf16[8,32,1024]{2,1,0:T(8,128)(2,1)S(1)} %collective-permute-done.11.refs_2_, bf16[1024,1024]{1,0:T(8,128)(2,1)S(1)} %get-tuple-element.34.refs_2_.refs_3_, ...), custom_call_target="tpu_custom_call" | custom-call | bytes 7500000 | tf_op jit(solution)/shard_map/pallas_call | solution.py:58
  45.2 0.5 %collective-permute-start.12 = (f32[32,512]{1,0:T(8,128)S(1)}, f32[32,512]{1,0:T(8,128)S(1)}, u32[]{:S(2)}, u32[]{:S(2)}) collective-permute-start(f32[32,512]{1,0:T(8,128)S(1)} %get-tuple-element.46.refs_5_), channel_id=1, source_target_pairs={{0,2},{2,0},{1,3},{3,1},{4,6},{6,4},{5,7},{7,5},{8,10},{10,8},{9,1... | collective-permute-start | bytes 196616 | tf_op jit(solution)/shard_map/ppermute | solution.py:673
  45.7 1.4 %shard_map.109.refs_2_ = f32[1520,640]{1,0:T(8,128)S(1)} custom-call(f32[1520,640]{1,0:T(8,128)S(1)} %get-tuple-element.41.refs_0_, f32[1520,640]{1,0:T(8,128)S(1)} %get-tuple-element.42.refs_1_, f32[1520,640]{1,0:T(8,128)S(1)} %shard_map.105.refs_2_, f32[1520,640]{1,0:T(8,128)S(1)} %shard_map.107.refs_6_.refs_3_, ...), custom_call_target="tpu_custom_call", output_to_operand_aliasing={{}: (3, {})} | custom-call | bytes 4200000 | tf_op jit(solution)/shard_map/pallas_call | solution.py:58
  47.2 2.5 %shard_map.110 = (f32[32,32,512]{2,1,0:T(8,128)}, f32[32,8,512]{2,1,0:T(8,128)S(1)}) custom-call(f32[1520,640]{1,0:T(8,128)S(1)} %get-tuple-element.41.refs_0_, f32[1520,640]{1,0:T(8,128)S(1)} %get-tuple-element.42.refs_1_, f32[1520,640]{1,0:T(8,128)S(1)} %shard_map.109.refs_2_), custom_call_target="tpu_custom_call" | custom-call | bytes 6000000 | tf_op jit(solution)/shard_map/pallas_call | solution.py:58
  49.7 1.1 %shard_map.111 = (f32[32,1,512]{2,1,0:T(1,128)}, f32[32,32,512]{2,1,0:T(8,128)}) custom-call(f32[32,512]{1,0:T(8,128)S(1)} %get-tuple-element.45.refs_4_.refs_0_, f32[32,512]{1,0:T(8,128)S(1)} %collective-permute-done.12.refs_1_, f32[32,512]{1,0:T(8,128)S(1)} %get-tuple-element.47.refs_2_, ...), custom_call_target="tpu_custom_call", output_to_operand_aliasing={{1}: (4, {})} | custom-call | bytes 3000000 | tf_op jit(solution)/shard_map/pallas_call | solution.py:58
  (21 shorter events, 0.2 us)
Async XLA Ops:
  0.6 13.7 %copy-start.4 = (s32[1,1,1,7]{3,2,1,0:T(1,128)S(1)}, s32[1,1,1,7]{3,2,1,0:T(1,128)}, u32[]{:S(2)}) copy-start(s32[1,1,1,7]{3,2,1,0:T(1,128)} %param.12) | copy-start | bytes 88
  0.6 13.7 %copy-start.3 = (s32[32,1,32]{2,1,0:T(1,128)S(1)}, s32[32,1,32]{2,1,0:T(1,128)}, u32[]{:S(2)}) copy-start(s32[32,1,32]{2,1,0:T(1,128)} %refs_0_.3) | copy-start | bytes 12292
  2.5 8.3 %collective-permute-start = (f32[104,512]{1,0:T(8,128)S(1)}, f32[104,512]{1,0:T(8,128)S(1)}, u32[]{:S(2)}, u32[]{:S(2)}) collective-permute-start(f32[104,512]{1,0:T(8,128)S(1)} %get-tuple-element.27.refs_3_.refs_0_), channel_id=1, source_target_pairs={{0,2},{2,0},{1,3},{3,1},{4,6},{6,4},{5,7},{7,5},{8,10},{10,8},{9,1... | collective-permute-start | bytes 638984 | tf_op jit(solution)/shard_map/ppermute | solution.py:596
  5.6 11.0 %collective-permute-start.6 = (f32[104,512]{1,0:T(8,128)S(1)}, f32[104,512]{1,0:T(8,128)S(1)}, u32[]{:S(2)}, u32[]{:S(2)}) collective-permute-start(f32[104,512]{1,0:T(8,128)S(1)} %get-tuple-element.37), channel_id=1, source_target_pairs={{0,4},{4,0},{8,12},{12,8},{16,20},{20,16},{24,28},{28,24},{1,5},{5... | collective-permute-start | bytes 638984 | tf_op jit(solution)/shard_map/ppermute | solution.py:82
  7.1 9.5 %collective-permute-start.7 = (f32[104,512]{1,0:T(8,128)S(1)}, f32[104,512]{1,0:T(8,128)S(1)}, u32[]{:S(2)}, u32[]{:S(2)}) collective-permute-start(f32[104,512]{1,0:T(8,128)S(1)} %get-tuple-element.38), channel_id=1, source_target_pairs={{4,8},{12,16},{20,24},{8,4},{16,12},{24,20},{5,9},{13,17},{21,25},... | collective-permute-start | bytes 638984 | tf_op jit(solution)/shard_map/ppermute | solution.py:82
  11.2 5.7 %collective-permute-start.1 = (f32[8,1024]{1,0:T(8,128)S(1)}, f32[8,1024]{1,0:T(8,128)S(1)}, u32[]{:S(2)}, u32[]{:S(2)}) collective-permute-start(f32[8,1024]{1,0:T(8,128)S(1)} %get-tuple-element.32), channel_id=1, source_target_pairs={{0,4},{4,0},{8,12},{12,8},{16,20},{20,16},{24,28},{28,24},{1,5},{5... | collective-permute-start | bytes 98312 | tf_op jit(solution)/shard_map/ppermute | solution.py:82
  13.0 3.9 %collective-permute-start.2 = (f32[8,1024]{1,0:T(8,128)S(1)}, f32[8,1024]{1,0:T(8,128)S(1)}, u32[]{:S(2)}, u32[]{:S(2)}) collective-permute-start(f32[8,1024]{1,0:T(8,128)S(1)} %get-tuple-element.33), channel_id=1, source_target_pairs={{4,8},{12,16},{20,24},{8,4},{16,12},{24,20},{5,9},{13,17},{21,25},... | collective-permute-start | bytes 98312 | tf_op jit(solution)/shard_map/ppermute | solution.py:82
  17.5 12.1 %copy-start = (bf16[1,1,1,1024,1024]{4,3,2,1,0:T(8,128)(2,1)S(1)}, bf16[1,1,1,1024,1024]{4,3,2,1,0:T(8,128)(2,1)}, u32[]{:S(2)}) copy-start(bf16[1,1,1,1024,1024]{4,3,2,1,0:T(8,128)(2,1)} %param.13) | copy-start | bytes 6291460
  17.5 12.1 %copy-start.1 = (bf16[1,1,1,7,16,1024]{5,4,3,2,1,0:T(8,128)(2,1)S(1)}, bf16[1,1,1,7,16,1024]{5,4,3,2,1,0:T(8,128)(2,1)}, u32[]{:S(2)}) copy-start(bf16[1,1,1,7,16,1024]{5,4,3,2,1,0:T(8,128)(2,1)} %param.14) | copy-start | bytes 688132
  17.5 16.7 %collective-permute-start.8 = (f32[36,32,128]{2,1,0:T(8,128)S(1)}, f32[36,32,128]{2,1,0:T(8,128)S(1)}, u32[]{:S(2)}, u32[]{:S(2)}) collective-permute-start(f32[36,32,128]{2,1,0:T(8,128)S(1)} %shard_map.102), channel_id=1, source_target_pairs={{0,2},{2,0},{1,3},{3,1},{4,6},{6,4},{5,7},{7,5},{8,10},{10,8},{9,1... | collective-permute-start | bytes 1769480 | tf_op jit(solution)/shard_map/ppermute | solution.py:82
  19.3 8.6 %collective-permute-start.3 = (bf16[1,32,1024]{2,1,0:T(8,128)(2,1)S(1)}, bf16[1,32,1024]{2,1,0:T(8,128)(2,1)S(1)}, u32[]{:S(2)}, u32[]{:S(2)}) collective-permute-start(bf16[1,32,1024]{2,1,0:T(8,128)(2,1)S(1)} %shard_map.98.refs_0_), channel_id=1, source_target_pairs={{0,16},{4,20},{8,24},{12,28},{16,0},{20,4},{24,8},{28,12},{1,17},{... | collective-permute-start | bytes 196616 | tf_op jit(solution)/shard_map/ppermute | solution.py:624
  27.8 5.5 %collective-permute-start.4 = (bf16[2,32,1024]{2,1,0:T(8,128)(2,1)S(1)}, bf16[2,32,1024]{2,1,0:T(8,128)(2,1)S(1)}, u32[]{:S(2)}, u32[]{:S(2)}) collective-permute-start(bf16[2,32,1024]{2,1,0:T(8,128)(2,1)S(1)} %shard_map.99.refs_3_.refs_0_), channel_id=1, source_target_pairs={{0,8},{4,12},{8,0},{12,4},{16,24},{20,28},{24,16},{28,20},{1,9},{5... | collective-permute-start | bytes 393224 | tf_op jit(solution)/shard_map/ppermute | solution.py:624
  33.4 8.6 %collective-permute-start.5 = (bf16[4,32,1024]{2,1,0:T(8,128)(2,1)S(1)}, bf16[4,32,1024]{2,1,0:T(8,128)(2,1)S(1)}, u32[]{:S(2)}, u32[]{:S(2)}) collective-permute-start(bf16[4,32,1024]{2,1,0:T(8,128)(2,1)S(1)} %shard_map.101.refs_5_.refs_0_), channel_id=1, source_target_pairs={{0,4},{4,0},{8,12},{12,8},{16,20},{20,16},{24,28},{28,24},{1,5},{5... | collective-permute-start | bytes 786440 | tf_op jit(solution)/shard_map/ppermute | solution.py:624
  34.5 1.7 %collective-permute-start.9 = (f32[2,40,640]{2,1,0:T(8,128)S(1)}, f32[2,40,640]{2,1,0:T(8,128)S(1)}, u32[]{:S(2)}, u32[]{:S(2)}) collective-permute-start(f32[2,40,640]{2,1,0:T(8,128)S(1)} %get-tuple-element.39), channel_id=1, source_target_pairs={{0,1},{1,0},{2,3},{3,2},{4,5},{5,4},{6,7},{7,6},{8,9},{9,8},{10,11... | collective-permute-start | bytes 614408 | tf_op jit(solution)/shard_map/ppermute | solution.py:643
  34.6 1.6 %collective-permute-start.10 = (f32[40,768]{1,0:T(8,128)S(1)}, f32[40,768]{1,0:T(8,128)S(1)}, u32[]{:S(2)}, u32[]{:S(2)}) collective-permute-start(f32[40,768]{1,0:T(8,128)S(1)} %get-tuple-element.40), channel_id=1, source_target_pairs={{0,1},{1,0},{2,3},{3,2},{4,5},{5,4},{6,7},{7,6},{8,9},{9,8},{10,11... | collective-permute-start | bytes 368648 | tf_op jit(solution)/shard_map/ppermute | solution.py:643
  42.1 2.0 %copy-start.2 = (bf16[1,1,1,7,16,1024]{5,4,3,2,1,0:T(8,128)(2,1)S(1)}, bf16[1,1,1,7,16,1024]{5,4,3,2,1,0:T(8,128)(2,1)}, u32[]{:S(2)}) copy-start(bf16[1,1,1,7,16,1024]{5,4,3,2,1,0:T(8,128)(2,1)} %param.15) | copy-start | bytes 688132
  42.1 2.0 %collective-permute-start.11 = (bf16[8,32,1024]{2,1,0:T(8,128)(2,1)S(1)}, bf16[8,32,1024]{2,1,0:T(8,128)(2,1)S(1)}, u32[]{:S(2)}, u32[]{:S(2)}) collective-permute-start(bf16[8,32,1024]{2,1,0:T(8,128)(2,1)S(1)} %shard_map.106.refs_3_.refs_1_), channel_id=1, source_target_pairs={{0,1},{1,0},{2,3},{3,2},{4,5},{5,4},{6,7},{7,6},{8,9},{9,8},{10,11... | collective-permute-start | bytes 1572872 | tf_op jit(solution)/shard_map/ppermute | solution.py:658
  45.2 4.5 %collective-permute-start.12 = (f32[32,512]{1,0:T(8,128)S(1)}, f32[32,512]{1,0:T(8,128)S(1)}, u32[]{:S(2)}, u32[]{:S(2)}) collective-permute-start(f32[32,512]{1,0:T(8,128)S(1)} %get-tuple-element.46.refs_5_), channel_id=1, source_target_pairs={{0,2},{2,0},{1,3},{3,1},{4,6},{6,4},{5,7},{7,5},{8,10},{10,8},{9,1... | collective-permute-start | bytes 196616 | tf_op jit(solution)/shard_map/ppermute | solution.py:673

commit v7 on v6

--- a/solution.py
+++ b/solution.py
@@ -218,7 +218,7 @@
 
 def face_trace_kernel(nx, s_in, i_in, order, *refs):
     odd = index("gx") % 2
-    got = [r[...] for r in refs[:nx]]
+    got = [r[:ROWS] for r in refs[:nx]]
     out, ext_s, ext_i = refs[nx:]
     _, rows_x, width = s_in.shape
     below, above = from_low(odd, got), from_high(odd, got)
@@ -251,17 +251,20 @@
     out[0] = jnp.dot(values, order[...], preferred_element_type=jnp.float32).astype(jnp.bfloat16)
 
 
-def order_kernel(place, near_col, far_col, order, spot):
+def order_kernel(place, order):
     rows_x, _, cells_y = place.shape
-    at = place[...].reshape(rows_x, cells_y) if rows_x == 1 else place[:, 0, :]
+    at = place[:, 0, :]
     trace = lax.broadcasted_iota(jnp.int32, (rows_x, order.shape[1]), 1)
     for y in range(cells_y):
         hit = at[:, y : y + 1] == trace
         order[y * rows_x : (y + 1) * rows_x, :] = jnp.where(hit, 1.0, 0.0).astype(jnp.bfloat16)
+
+
+def spot_kernel(near_col, far_col, spot):
     at_x, at_z = index("gx"), index("gz")
     size_x = lax.axis_size("gx")
     for k in range(spot.shape[0]):
-        block = near_col[0] if k == 0 else far_col[k - 1]
+        block = near_col[0, 0, 0] if k == 0 else far_col[0, 0, 0, k - 1]
         apart = (block // 2) ^ at_x
         where = ((block % 2) ^ at_z) * size_x
         for n, step in enumerate(doubling(size_x)):
@@ -287,7 +290,7 @@
         near_out[:, columns] = rows.astype(jnp.bfloat16)
         return 0
 
-    lax.fori_loop(0, near.shape[1] // size, step, 0)
+    repeat(0, near.shape[1] // size, step, 4)
     rows = lax.dot_general(far_u[...], order[...], ACROSS, preferred_element_type=jnp.float32)
     far_out[...] = rows.astype(jnp.bfloat16)
 
@@ -325,9 +328,15 @@
 
 def finish_kernel(count, *refs):
     parts = refs[:count]
-    inv, slab, _, flux_out, out, held_flux, sems = refs[count:]
+    inv, slab, tail, _, flux_out, out, held_flux, sems = refs[count:]
     side = index("gz")
     rows_x, _, width = slab.shape
+    size, depth, _ = tail.shape
+    columns = off_face(side, depth)
+    tail_copy = pltpu.make_async_copy(
+        tail.at[:, columns, :], out.at[rows_x - size :, columns, :], sems.at[2]
+    )
+    tail_copy.start()
     total = parts[0][...]
     if count == 2:
         total = total + parts[1][...]
@@ -348,6 +357,7 @@
     top = pl.multiple_of(side * (out.shape[1] - ROWS), ROWS)
     copy = pltpu.make_async_copy(slab, out.at[:, pl.ds(top, ROWS), :], sems.at[1])
     copy.start()
+    tail_copy.wait()
     out_copy.wait()
     copy.wait()
 
@@ -474,7 +484,7 @@
         place(x + HALO, source[x], inv[x], [r[x + HALO - 1] for r in got_y])
         return 0
 
-    repeat(0, rows_x, own, 4)
+    repeat(0, rows_x, own, 16)
     got = [r[...] for r in got_x]
     for base, skip, edge in ((0, 0, from_low(odd_x, got)), (rows_x + HALO, 2, from_high(odd_x, got))):
         planes, compact = row_layers(edge, depth)
@@ -494,7 +504,7 @@
         one[rows, :] = ext_s[rows, :] * inverse
         return 0
 
-    lax.fori_loop(0, total // chunk, expand, 0)
+    repeat(0, total // chunk, expand, 5)
 
 
 def repeat(first, last, step, most):
@@ -541,27 +551,34 @@
     repeat(first, last, step, 12)
 
 
-def last_sweep_kernel(ext_s, ext_i, old, out, slab, done, sems):
+def off_face(side, depth):
+    return pl.ds(pl.multiple_of((1 - side) * ROWS, ROWS), depth - ROWS)
+
+
+def last_sweep_kernel(pieces, ext_s, ext_i, old, out, slab, tail, done, sems):
     side = index("gz")
     rows_x, depth, width = out.shape
     all_z = depth + ROWS
-
-    def step(x, _):
-        def store(columns, value):
-            done[x, :, columns] = value
-            slab[x, :, columns] = jnp.where(side == 0, value[:ROWS], value[depth - ROWS :])
-
-        swept(ext_s, ext_i, old, x + HALO, all_z, depth, width, store)
-        return 0
-
-    pieces = sems.shape[0]
     size = rows_x // pieces
     copies = []
     for n in range(pieces):
+        target, shift = (tail, n * size) if n == pieces - 1 else (done, 0)
+
+        def step(x, _, target=target, shift=shift):
+            def store(columns, value):
+                target[x - shift, :, columns] = value
+                slab[x, :, columns] = jnp.where(side == 0, value[:ROWS], value[depth - ROWS :])
+
+            swept(ext_s, ext_i, old, x + HALO, all_z, depth, width, store)
+            return 0
+
         repeat(n * size, (n + 1) * size, step, 8)
-        rows = slice(n * size, (n + 1) * size)
-        copies.append(pltpu.make_async_copy(done.at[rows], out.at[rows], sems.at[n]))
-        copies[-1].start()
+        if n < pieces - 1:
+            rows, columns = slice(n * size, (n + 1) * size), off_face(side, depth)
+            copies.append(
+                pltpu.make_async_copy(done.at[rows, columns, :], out.at[rows, columns, :], sems.at[n])
+            )
+            copies[-1].start()
     for copy in copies:
         copy.wait()
 
@@ -600,14 +617,11 @@
     full = vector((NEAR, rows_x, width * groups))
     s_face, i_face, i_own, *face_x = call(
         functools.partial(face_side_kernel, groups), (near, other),
-        [full, full, vector((rows_x, width))] + [vector((ROWS, width * groups))] * nx, work=500,
+        [full, full, vector((rows_x, width))]
+        + [vector(((1 + n) * ROWS, width * groups)) for n in range(nx)], work=500,
     )
     got_x = swap(face_x, "gx")
-    order, spot = call(
-        order_kernel, (face_trace, near_col.reshape(1), far_col.reshape(count)),
-        [vector((tile, tile), bf16), pltpu.SMEM((count + 1,), jnp.int32)],
-        in_specs=[VECTOR, SCALAR, SCALAR], out_specs=[VECTOR, SCALAR], work=2000, after=(near,),
-    )
+    (order,) = call(order_kernel, (face_trace,), [vector((tile, tile), bf16)], after=(near,))
     vol_y = call(
         functools.partial(side_edge_kernel, nx), (held_source, inv, *got_vol_x),
         [vector((all_x - 2, depth, LANES))] * ny, work=300, after=(order, *got_x),
@@ -624,6 +638,12 @@
         other = held(lax.ppermute(traces, "gx", [(i, i ^ step) for i in range(size_x)]))
         twice = (2 * traces.shape[0], E, tile)
         before = ()
+        if step == steps[0]:
+            (spot,) = call(
+                spot_kernel, (near_col, far_col), [pltpu.SMEM((count + 1,), jnp.int32)],
+                in_specs=[SCALAR, SCALAR], out_specs=[SCALAR], after=(traces,),
+            )
+            before = (spot,)
         if step == steps[-2]:
             near, far_rows = call(
                 row_order_kernel,
@@ -631,7 +651,7 @@
                 [vector((tile, tile), bf16), vector((count * rank, tile), bf16)], work=3000,
                 after=(traces,),
             )
-            before = (near,)
+            before = (*before, near)
         if step == 1:
             rounded = -(-all_x // ROWS) * ROWS
             vol_z = call(
@@ -678,19 +698,20 @@
         work=1400, input_output_aliases={3: 0}, after=rows,
     )
     pieces = 4
-    field, slab = call(
-        last_sweep_kernel, (ext_s, ext_i, three),
-        [plain(source.shape), vector((rows_x, ROWS, width))], work=2000,
-        out_specs=[MAIN, VECTOR],
-        scratch=(vector(source.shape), pltpu.SemaphoreType.DMA((pieces,))),
+    size = rows_x // pieces
+    field, slab, tail = call(
+        functools.partial(last_sweep_kernel, pieces), (ext_s, ext_i, three),
+        [plain(source.shape), vector((rows_x, ROWS, width)), vector((size, depth, width))],
+        out_specs=[MAIN, VECTOR, VECTOR], work=2000,
+        scratch=(vector((rows_x - size, depth, width)), pltpu.SemaphoreType.DMA((pieces - 1,))),
     )
 
     flux, result = call(
-        functools.partial(finish_kernel, len(sums)), (*sums, i_own, slab, field),
+        functools.partial(finish_kernel, len(sums)), (*sums, i_own, slab, tail, field),
         [plain((rows_x, 1, width)), plain(source.shape)],
-        in_specs=[VECTOR] * (len(sums) + 2) + [MAIN], out_specs=[MAIN, MAIN],
-        scratch=(vector((rows_x, 1, width)), pltpu.SemaphoreType.DMA((2,))),
-        input_output_aliases={len(sums) + 2: 1},
+        in_specs=[VECTOR] * (len(sums) + 3) + [MAIN], out_specs=[MAIN, MAIN],
+        scratch=(vector((rows_x, 1, width)), pltpu.SemaphoreType.DMA((3,))),
+        input_output_aliases={len(sums) + 3: 1},
     )
     return (result, flux)
 

time: 51 us -> 49.4 us (0.969)
  Pallas kernels: 22.9 us -> 20.6 us
  starting transfers between devices: 18.6 us -> 20 us
  waiting for transfers between devices: 7.85 us -> 7.06 us
    ppermute x5, starting transfers between devices: 5.39 us -> 8.97 us  [swap(): lax.ppermute(m, axis, p)]
    pallas_call x17 -> x18, Pallas kernels: 22.9 us -> 20.6 us  [call(): pl.pallas_call(body, out_shape=out_shape, in_specs=(in_specs or [VECTOR]...]
    ppermute x3, starting transfers between devices: 8.75 us -> 6.63 us  [body(): lax.ppermute(traces, 'gx', [(i, i ^ step) for i in range(size_x)])]
    ppermute x3, waiting for transfers between devices: 2.42 us -> 1.55 us  [body(): lax.ppermute(traces, 'gx', [(i, i ^ step) for i in range(size_x)])]
  transfers between devices with their start and end apart: 13 -> 13, of which waited for: 6 -> 7; matrix products, arithmetic and copies ran while one was open for 0% -> 0% of each run, Pallas kernels for 36% -> 32%
where the time goes in v7:
time: 49.4 us; the launch traced here: 49.2 us
  Pallas kernels  20.6 us (42%)
  starting transfers between devices  20 us (40%)
  waiting for transfers between devices  7.06 us (14%)
  between operations  1.48 us (3%)
    pallas_call x18, Pallas kernels, call(): pl.pallas_call(body, out_shape=out_shape, in_specs=(in_specs or [VECTOR]...  20.6 us
    ppermute x5, starting transfers between devices, swap(): lax.ppermute(m, axis, p)  8.97 us
    ppermute x3, starting transfers between devices, body(): lax.ppermute(traces, 'gx', [(i, i ^ step) for i in range(size_x)])  6.63 us
    ppermute x1, waiting for transfers between devices, body(): other = held(lax.ppermute(near, 'gy', both))  3.09 us
    ppermute x1, starting transfers between devices, body(): other = held(lax.ppermute(near, 'gy', both))  3.03 us
    ppermute x3, waiting for transfers between devices, body(): lax.ppermute(traces, 'gx', [(i, i ^ step) for i in range(size_x)])  1.55 us
    ppermute x2, waiting for transfers between devices, body(): got_vol_z = [held(lax.ppermute(v, 'gz', both)) for v in vol_z]  1.12 us
  transfers between devices with their start and end apart: 13, of which 7 were waited for; matrix products, arithmetic and copies ran while one was open for 0% of the time, Pallas kernels for 32%

profile of v7, /device:TPU:0, one launch (start us, length us, event | category | flops | bytes accessed | tf_op | source)
XLA Modules:
  0.0 49.2 jit_solution(9465820951633396342)
XLA Ops:
  0.6 1.9 %shard_map.95 = (f32[32,32,512]{2,1,0:T(8,128)S(1)}, f32[32,32,128]{2,1,0:T(8,128)S(1)}, f32[104,512]{1,0:T(8,128)S(1)}, f32[104,512]{1,0:T(8,128)S(1)}, f32[104,512]{1,0:T(8,128)S(1)}) custom-call(f32[32,32,512]{2,1,0:T(8,128)} %refs_0_.3, f32[32,16,32]{2,1,0:T(8,128)} %bitcast.7), custom_call_target="tpu_custom_call" | custom-call | bytes 3000000 | tf_op jit(solution)/shard_map/pallas_call | solution.py:58
  2.5 3.0 %collective-permute-start = (f32[104,512]{1,0:T(8,128)S(1)}, f32[104,512]{1,0:T(8,128)S(1)}, u32[]{:S(2)}, u32[]{:S(2)}) collective-permute-start(f32[104,512]{1,0:T(8,128)S(1)} %get-tuple-element.26.refs_0_.refs_1_), channel_id=1, source_target_pairs={{0,2},{2,0},{1,3},{3,1},{4,6},{6,4},{5,7},{7,5},{8,10},{10,8},{9,1... | collective-permute-start | bytes 638984 | tf_op jit(solution)/shard_map/ppermute | solution.py:613
  5.6 1.5 %collective-permute-start.6 = (f32[104,512]{1,0:T(8,128)S(1)}, f32[104,512]{1,0:T(8,128)S(1)}, u32[]{:S(2)}, u32[]{:S(2)}) collective-permute-start(f32[104,512]{1,0:T(8,128)S(1)} %get-tuple-element.34), channel_id=1, source_target_pairs={{0,4},{4,0},{8,12},{12,8},{16,20},{20,16},{24,28},{28,24},{1,5},{5... | collective-permute-start | bytes 638984 | tf_op jit(solution)/shard_map/ppermute | solution.py:82
  7.1 0.7 %collective-permute-start.7 = (f32[104,512]{1,0:T(8,128)S(1)}, f32[104,512]{1,0:T(8,128)S(1)}, u32[]{:S(2)}, u32[]{:S(2)}) collective-permute-start(f32[104,512]{1,0:T(8,128)S(1)} %get-tuple-element.35), channel_id=1, source_target_pairs={{4,8},{12,16},{20,24},{8,4},{16,12},{24,20},{5,9},{13,17},{21,25},... | collective-permute-start | bytes 638984 | tf_op jit(solution)/shard_map/ppermute | solution.py:82
  7.7 3.1 %collective-permute-done.refs_1_ = f32[104,512]{1,0:T(8,128)S(1)} collective-permute-done((f32[104,512]{1,0:T(8,128)S(1)}, f32[104,512]{1,0:T(8,128)S(1)}, u32[]{:S(2)}, u32[]{:S(2)}) %collective-permute-start) | collective-permute-done | bytes 213024 | tf_op jit(solution)/shard_map/ppermute | solution.py:613
  10.8 0.4 shard_map.96
  11.2 0.7 %collective-permute-start.2 = (f32[16,1024]{1,0:T(8,128)S(1)}, f32[16,1024]{1,0:T(8,128)S(1)}, u32[]{:S(2)}, u32[]{:S(2)}) collective-permute-start(f32[16,1024]{1,0:T(8,128)S(1)} %get-tuple-element.30), channel_id=1, source_target_pairs={{4,8},{12,16},{20,24},{8,4},{16,12},{24,20},{5,9},{13,17},{21,25},... | collective-permute-start | bytes 196616 | tf_op jit(solution)/shard_map/ppermute | solution.py:82
  11.9 4.6 %collective-permute-start.1 = (f32[8,1024]{1,0:T(8,128)S(1)}, f32[8,1024]{1,0:T(8,128)S(1)}, u32[]{:S(2)}, u32[]{:S(2)}) collective-permute-start(f32[8,1024]{1,0:T(8,128)S(1)} %get-tuple-element.29), channel_id=1, source_target_pairs={{0,4},{4,0},{8,12},{12,8},{16,20},{20,16},{24,28},{28,24},{1,5},{5... | collective-permute-start | bytes 98312 | tf_op jit(solution)/shard_map/ppermute | solution.py:82
  16.4 1.2 %shard_map.97.refs_2_.refs_0_.refs_4_ = bf16[1024,1024]{1,0:T(8,128)(2,1)S(1)} custom-call(s32[32,1,32]{2,1,0:T(1,128)S(1)} %copy-done.3, f32[104,512]{1,0:T(8,128)S(1)} %get-tuple-element.26.refs_0_.refs_1_), custom_call_target="tpu_custom_call" | custom-call | bytes 3000000 | tf_op jit(solution)/shard_map/pallas_call | solution.py:58
  17.7 0.6 %collective-permute-done.1.refs_3_.refs_5_ = f32[8,1024]{1,0:T(8,128)S(1)} collective-permute-done((f32[8,1024]{1,0:T(8,128)S(1)}, f32[8,1024]{1,0:T(8,128)S(1)}, u32[]{:S(2)}, u32[]{:S(2)}) %collective-permute-start.1) | collective-permute-done | bytes 32800 | tf_op jit(solution)/shard_map/ppermute | solution.py:82
  18.3 0.6 %shard_map.103 = f32[36,32,128]{2,1,0:T(8,128)S(1)} custom-call(f32[32,32,512]{2,1,0:T(8,128)S(1)} %get-tuple-element.32.refs_0_, f32[32,32,128]{2,1,0:T(8,128)S(1)} %get-tuple-element.33.refs_1_, f32[104,512]{1,0:T(8,128)S(1)} %collective-permute-done.6.refs_2_, f32[104,512]{1,0:T(8,128)S(1)} %collective-permute-done.7.refs_3_, ...), custom_call_target="tpu_custom_call" | custom-call | bytes 900000 | tf_op jit(solution)/shard_map/pallas_call | solution.py:58
  19.0 1.6 %collective-permute-start.8 = (f32[36,32,128]{2,1,0:T(8,128)S(1)}, f32[36,32,128]{2,1,0:T(8,128)S(1)}, u32[]{:S(2)}, u32[]{:S(2)}) collective-permute-start(f32[36,32,128]{2,1,0:T(8,128)S(1)} %shard_map.103), channel_id=1, source_target_pairs={{0,2},{2,0},{1,3},{3,1},{4,6},{6,4},{5,7},{7,5},{8,10},{10,8},{9,1... | collective-permute-start | bytes 1769480 | tf_op jit(solution)/shard_map/ppermute | solution.py:82
  20.5 0.9 %shard_map.98.refs_2_.refs_0_ = bf16[1,32,1024]{2,1,0:T(8,128)(2,1)S(1)} custom-call(f32[3,32,1024]{2,1,0:T(8,128)S(1)} %get-tuple-element.27.refs_0_, f32[3,32,1024]{2,1,0:T(8,128)S(1)} %get-tuple-element.28.refs_1_, bf16[1024,1024]{1,0:T(8,128)(2,1)S(1)} %shard_map.97.refs_2_.refs_0_.refs_4_, f32[8,1024]{1,0:T(8,128)S(1)} %collective-permute-done.1.refs_3_.refs_5_, ...), custom_call_target="tpu_custom_call" | custom-call | bytes 3000000 | tf_op jit(solution)/shard_map/pallas_call | solution.py:58
  21.5 3.1 %collective-permute-start.3 = (bf16[1,32,1024]{2,1,0:T(8,128)(2,1)S(1)}, bf16[1,32,1024]{2,1,0:T(8,128)(2,1)S(1)}, u32[]{:S(2)}, u32[]{:S(2)}) collective-permute-start(bf16[1,32,1024]{2,1,0:T(8,128)(2,1)S(1)} %shard_map.98.refs_2_.refs_0_), channel_id=1, source_target_pairs={{0,16},{4,20},{8,24},{12,28},{16,0},{20,4},{24,8},{28,12},{1,17},{... | collective-permute-start | bytes 196616 | tf_op jit(solution)/shard_map/ppermute | solution.py:638
  25.2 0.6 %shard_map.99.refs_2_.refs_0_ = s32[8]{0:T(128)S(4)} custom-call(s32[1,1,1]{2,1,0:T(1,128)S(6)} %copy.14.refs_0_, s32[1,1,1,7]{3,2,1,0:T(1,128)S(1)} %copy-done.4, bf16[1,32,1024]{2,1,0:T(8,128)(2,1)S(1)} %shard_map.98.refs_2_.refs_0_), custom_call_target="tpu_custom_call" | custom-call | bytes 3000000 | tf_op jit(solution)/shard_map/pallas_call | solution.py:58
  25.9 1.2 %collective-permute-done.3.refs_1_ = bf16[1,32,1024]{2,1,0:T(8,128)(2,1)S(1)} collective-permute-done((bf16[1,32,1024]{2,1,0:T(8,128)(2,1)S(1)}, bf16[1,32,1024]{2,1,0:T(8,128)(2,1)S(1)}, u32[]{:S(2)}, u32[]{:S(2)}) %collective-permute-start.3) | collective-permute-done | bytes 65568 | tf_op jit(solution)/shard_map/ppermute | solution.py:638
  27.1 1.7 %collective-permute-start.4 = (bf16[2,32,1024]{2,1,0:T(8,128)(2,1)S(1)}, bf16[2,32,1024]{2,1,0:T(8,128)(2,1)S(1)}, u32[]{:S(2)}, u32[]{:S(2)}) collective-permute-start(bf16[2,32,1024]{2,1,0:T(8,128)(2,1)S(1)} %shard_map.100.refs_3_.refs_0_), channel_id=1, source_target_pairs={{0,8},{4,12},{8,0},{12,4},{16,24},{20,28},{24,16},{28,20},{1,9},{5... | collective-permute-start | bytes 393224 | tf_op jit(solution)/shard_map/ppermute | solution.py:638
  28.8 2.9 %shard_map.101 = (bf16[1024,1024]{1,0:T(8,128)(2,1)S(1)}, bf16[112,1024]{1,0:T(8,128)(2,1)S(1)}) custom-call(bf16[1024,1024]{1,0:T(8,128)(2,1)S(1)} %shard_map.97.refs_2_.refs_0_.refs_4_, bf16[1024,1024]{1,0:T(8,128)(2,1)S(1)} %bitcast.4, bf16[112,1024]{1,0:T(8,128)(2,1)S(1)} %bitcast.5, bf16[2,32,1024]{2,1,0:T(8,128)(2,1)S(1)} %shard_map.100.refs_3_.refs_0_), custom_call_target="tpu_custom_call" | custom-call | bytes 9000000 | tf_op jit(solution)/shard_map/pallas_call | solution.py:58
  31.7 0.4 collective-permute-done.4.refs_1_
  32.1 1.8 %collective-permute-start.5 = (bf16[4,32,1024]{2,1,0:T(8,128)(2,1)S(1)}, bf16[4,32,1024]{2,1,0:T(8,128)(2,1)S(1)}, u32[]{:S(2)}, u32[]{:S(2)}) collective-permute-start(bf16[4,32,1024]{2,1,0:T(8,128)(2,1)S(1)} %shard_map.102.refs_5_.refs_0_), channel_id=1, source_target_pairs={{0,4},{4,0},{8,12},{12,8},{16,20},{20,16},{24,28},{28,24},{1,5},{5... | collective-permute-start | bytes 786440 | tf_op jit(solution)/shard_map/ppermute | solution.py:638
  33.9 0.3 shard_map.104
  34.3 0.5 %collective-permute-start.10 = (f32[40,768]{1,0:T(8,128)S(1)}, f32[40,768]{1,0:T(8,128)S(1)}, u32[]{:S(2)}, u32[]{:S(2)}) collective-permute-start(f32[40,768]{1,0:T(8,128)S(1)} %get-tuple-element.37), channel_id=1, source_target_pairs={{0,1},{1,0},{2,3},{3,2},{4,5},{5,4},{6,7},{7,6},{8,9},{9,8},{10,11... | collective-permute-start | bytes 368648 | tf_op jit(solution)/shard_map/ppermute | solution.py:663
  34.8 1.1 %collective-permute-done.10.refs_6_ = f32[40,768]{1,0:T(8,128)S(1)} collective-permute-done((f32[40,768]{1,0:T(8,128)S(1)}, f32[40,768]{1,0:T(8,128)S(1)}, u32[]{:S(2)}, u32[]{:S(2)}) %collective-permute-start.10) | collective-permute-done | bytes 122912 | tf_op jit(solution)/shard_map/ppermute | solution.py:663
  35.9 1.8 %shard_map.105 = (f32[1520,640]{1,0:T(8,128)S(1)}, f32[1520,640]{1,0:T(8,128)S(1)}, f32[1520,640]{1,0:T(8,128)S(1)}) custom-call(f32[32,32,512]{2,1,0:T(8,128)S(1)} %get-tuple-element.32.refs_0_, f32[32,32,128]{2,1,0:T(8,128)S(1)} %get-tuple-element.33.refs_1_, f32[104,512]{1,0:T(8,128)S(1)} %collective-permute-done.6.refs_2_, ...), custom_call_target="tpu_custom_call" | custom-call | bytes 9000000 | tf_op jit(solution)/shard_map/pallas_call | solution.py:58
  37.7 2.8 %shard_map.106.refs_2_ = f32[1520,640]{1,0:T(8,128)S(1)} custom-call(f32[1520,640]{1,0:T(8,128)S(1)} %get-tuple-element.38.refs_0_, f32[1520,640]{1,0:T(8,128)S(1)} %get-tuple-element.39.refs_1_, f32[1520,640]{1,0:T(8,128)S(1)} %get-tuple-element.40.refs_2_), custom_call_target="tpu_custom_call" | custom-call | bytes 7500000 | tf_op jit(solution)/shard_map/pallas_call | solution.py:58
  40.9 1.3 %shard_map.108.refs_6_.refs_3_ = f32[1520,640]{1,0:T(8,128)S(1)} custom-call(f32[1520,640]{1,0:T(8,128)S(1)} %get-tuple-element.38.refs_0_, f32[1520,640]{1,0:T(8,128)S(1)} %get-tuple-element.39.refs_1_, f32[1520,640]{1,0:T(8,128)S(1)} %shard_map.106.refs_2_, bf16[8,32,1024]{2,1,0:T(8,128)(2,1)S(1)} %shard_map.107.refs_3_.refs_1_), custom_call_target="tpu_custom_call" | custom-call | bytes 4200000 | tf_op jit(solution)/shard_map/pallas_call | solution.py:58
  42.2 0.4 collective-permute-done.11.refs_2_
  42.6 1.1 %shard_map.109 = (f32[32,512]{1,0:T(8,128)S(1)}, f32[32,512]{1,0:T(8,128)S(1)}) custom-call(s32[8]{0:T(128)S(4)} %shard_map.99.refs_2_.refs_0_, bf16[8,32,1024]{2,1,0:T(8,128)(2,1)S(1)} %shard_map.107.refs_3_.refs_1_, bf16[8,32,1024]{2,1,0:T(8,128)(2,1)S(1)} %collective-permute-done.11.refs_2_, bf16[1024,1024]{1,0:T(8,128)(2,1)S(1)} %get-tuple-element.31.refs_2_.refs_3_, ...), custom_call_target="tpu_custom_call" | custom-call | bytes 7500000 | tf_op jit(solution)/shard_map/pallas_call | solution.py:58
  43.7 0.6 %collective-permute-start.12 = (f32[32,512]{1,0:T(8,128)S(1)}, f32[32,512]{1,0:T(8,128)S(1)}, u32[]{:S(2)}, u32[]{:S(2)}) collective-permute-start(f32[32,512]{1,0:T(8,128)S(1)} %get-tuple-element.43.refs_5_), channel_id=1, source_target_pairs={{0,2},{2,0},{1,3},{3,1},{4,6},{6,4},{5,7},{7,5},{8,10},{10,8},{9,1... | collective-permute-start | bytes 196616 | tf_op jit(solution)/shard_map/ppermute | solution.py:693
  44.3 1.4 %shard_map.110.refs_2_ = f32[1520,640]{1,0:T(8,128)S(1)} custom-call(f32[1520,640]{1,0:T(8,128)S(1)} %get-tuple-element.38.refs_0_, f32[1520,640]{1,0:T(8,128)S(1)} %get-tuple-element.39.refs_1_, f32[1520,640]{1,0:T(8,128)S(1)} %shard_map.106.refs_2_, f32[1520,640]{1,0:T(8,128)S(1)} %shard_map.108.refs_6_.refs_3_, ...), custom_call_target="tpu_custom_call", output_to_operand_aliasing={{}: (3, {})} | custom-call | bytes 4200000 | tf_op jit(solution)/shard_map/pallas_call | solution.py:58
  45.7 2.0 %shard_map.111 = (f32[32,32,512]{2,1,0:T(8,128)}, f32[32,8,512]{2,1,0:T(8,128)S(1)}, f32[8,32,512]{2,1,0:T(8,128)S(1)}) custom-call(f32[1520,640]{1,0:T(8,128)S(1)} %get-tuple-element.38.refs_0_, f32[1520,640]{1,0:T(8,128)S(1)} %get-tuple-element.39.refs_1_, f32[1520,640]{1,0:T(8,128)S(1)} %shard_map.110.refs_2_), custom_call_target="tpu_custom_call" | custom-call | bytes 6000000 | tf_op jit(solution)/shard_map/pallas_call | solution.py:58
  48.0 1.2 %shard_map.112 = (f32[32,1,512]{2,1,0:T(1,128)}, f32[32,32,512]{2,1,0:T(8,128)}) custom-call(f32[32,512]{1,0:T(8,128)S(1)} %get-tuple-element.42.refs_4_.refs_0_, f32[32,512]{1,0:T(8,128)S(1)} %collective-permute-done.12.refs_1_, f32[32,512]{1,0:T(8,128)S(1)} %get-tuple-element.44.refs_2_, ...), custom_call_target="tpu_custom_call", output_to_operand_aliasing={{1}: (5, {})} | custom-call | bytes 3000000 | tf_op jit(solution)/shard_map/pallas_call | solution.py:58
  (22 shorter events, 0.7 us)
Async XLA Ops:
  0.6 15.8 %copy-start.3 = (s32[32,1,32]{2,1,0:T(1,128)S(1)}, s32[32,1,32]{2,1,0:T(1,128)}, u32[]{:S(2)}) copy-start(s32[32,1,32]{2,1,0:T(1,128)} %refs_0_.4) | copy-start | bytes 12292
  2.5 8.3 %collective-permute-start = (f32[104,512]{1,0:T(8,128)S(1)}, f32[104,512]{1,0:T(8,128)S(1)}, u32[]{:S(2)}, u32[]{:S(2)}) collective-permute-start(f32[104,512]{1,0:T(8,128)S(1)} %get-tuple-element.26.refs_0_.refs_1_), channel_id=1, source_target_pairs={{0,2},{2,0},{1,3},{3,1},{4,6},{6,4},{5,7},{7,5},{8,10},{10,8},{9,1... | collective-permute-start | bytes 638984 | tf_op jit(solution)/shard_map/ppermute | solution.py:613
  5.6 12.1 %collective-permute-start.6 = (f32[104,512]{1,0:T(8,128)S(1)}, f32[104,512]{1,0:T(8,128)S(1)}, u32[]{:S(2)}, u32[]{:S(2)}) collective-permute-start(f32[104,512]{1,0:T(8,128)S(1)} %get-tuple-element.34), channel_id=1, source_target_pairs={{0,4},{4,0},{8,12},{12,8},{16,20},{20,16},{24,28},{28,24},{1,5},{5... | collective-permute-start | bytes 638984 | tf_op jit(solution)/shard_map/ppermute | solution.py:82
  7.1 10.6 %collective-permute-start.7 = (f32[104,512]{1,0:T(8,128)S(1)}, f32[104,512]{1,0:T(8,128)S(1)}, u32[]{:S(2)}, u32[]{:S(2)}) collective-permute-start(f32[104,512]{1,0:T(8,128)S(1)} %get-tuple-element.35), channel_id=1, source_target_pairs={{4,8},{12,16},{20,24},{8,4},{16,12},{24,20},{5,9},{13,17},{21,25},... | collective-permute-start | bytes 638984 | tf_op jit(solution)/shard_map/ppermute | solution.py:82
  11.2 7.1 %collective-permute-start.2 = (f32[16,1024]{1,0:T(8,128)S(1)}, f32[16,1024]{1,0:T(8,128)S(1)}, u32[]{:S(2)}, u32[]{:S(2)}) collective-permute-start(f32[16,1024]{1,0:T(8,128)S(1)} %get-tuple-element.30), channel_id=1, source_target_pairs={{4,8},{12,16},{20,24},{8,4},{16,12},{24,20},{5,9},{13,17},{21,25},... | collective-permute-start | bytes 196616 | tf_op jit(solution)/shard_map/ppermute | solution.py:82
  11.9 6.5 %collective-permute-start.1 = (f32[8,1024]{1,0:T(8,128)S(1)}, f32[8,1024]{1,0:T(8,128)S(1)}, u32[]{:S(2)}, u32[]{:S(2)}) collective-permute-start(f32[8,1024]{1,0:T(8,128)S(1)} %get-tuple-element.29), channel_id=1, source_target_pairs={{0,4},{4,0},{8,12},{12,8},{16,20},{20,16},{24,28},{28,24},{1,5},{5... | collective-permute-start | bytes 98312 | tf_op jit(solution)/shard_map/ppermute | solution.py:82
  18.9 6.3 %copy-start.4 = (s32[1,1,1,7]{3,2,1,0:T(1,128)S(1)}, s32[1,1,1,7]{3,2,1,0:T(1,128)}, u32[]{:S(2)}) copy-start(s32[1,1,1,7]{3,2,1,0:T(1,128)} %refs_1_.1) | copy-start | bytes 88
  18.9 9.9 %copy-start = (bf16[1,1,1,1024,1024]{4,3,2,1,0:T(8,128)(2,1)S(1)}, bf16[1,1,1,1024,1024]{4,3,2,1,0:T(8,128)(2,1)}, u32[]{:S(2)}) copy-start(bf16[1,1,1,1024,1024]{4,3,2,1,0:T(8,128)(2,1)} %param.13) | copy-start | bytes 6291460
  18.9 9.9 %copy-start.1 = (bf16[1,1,1,7,16,1024]{5,4,3,2,1,0:T(8,128)(2,1)S(1)}, bf16[1,1,1,7,16,1024]{5,4,3,2,1,0:T(8,128)(2,1)}, u32[]{:S(2)}) copy-start(bf16[1,1,1,7,16,1024]{5,4,3,2,1,0:T(8,128)(2,1)} %param.14) | copy-start | bytes 688132
  19.0 14.9 %collective-permute-start.8 = (f32[36,32,128]{2,1,0:T(8,128)S(1)}, f32[36,32,128]{2,1,0:T(8,128)S(1)}, u32[]{:S(2)}, u32[]{:S(2)}) collective-permute-start(f32[36,32,128]{2,1,0:T(8,128)S(1)} %shard_map.103), channel_id=1, source_target_pairs={{0,2},{2,0},{1,3},{3,1},{4,6},{6,4},{5,7},{7,5},{8,10},{10,8},{9,1... | collective-permute-start | bytes 1769480 | tf_op jit(solution)/shard_map/ppermute | solution.py:82
  21.5 5.6 %collective-permute-start.3 = (bf16[1,32,1024]{2,1,0:T(8,128)(2,1)S(1)}, bf16[1,32,1024]{2,1,0:T(8,128)(2,1)S(1)}, u32[]{:S(2)}, u32[]{:S(2)}) collective-permute-start(bf16[1,32,1024]{2,1,0:T(8,128)(2,1)S(1)} %shard_map.98.refs_2_.refs_0_), channel_id=1, source_target_pairs={{0,16},{4,20},{8,24},{12,28},{16,0},{20,4},{24,8},{28,12},{1,17},{... | collective-permute-start | bytes 196616 | tf_op jit(solution)/shard_map/ppermute | solution.py:638
  27.1 5.0 %collective-permute-start.4 = (bf16[2,32,1024]{2,1,0:T(8,128)(2,1)S(1)}, bf16[2,32,1024]{2,1,0:T(8,128)(2,1)S(1)}, u32[]{:S(2)}, u32[]{:S(2)}) collective-permute-start(bf16[2,32,1024]{2,1,0:T(8,128)(2,1)S(1)} %shard_map.100.refs_3_.refs_0_), channel_id=1, source_target_pairs={{0,8},{4,12},{8,0},{12,4},{16,24},{20,28},{24,16},{28,20},{1,9},{5... | collective-permute-start | bytes 393224 | tf_op jit(solution)/shard_map/ppermute | solution.py:638
  32.1 8.4 %collective-permute-start.5 = (bf16[4,32,1024]{2,1,0:T(8,128)(2,1)S(1)}, bf16[4,32,1024]{2,1,0:T(8,128)(2,1)S(1)}, u32[]{:S(2)}, u32[]{:S(2)}) collective-permute-start(bf16[4,32,1024]{2,1,0:T(8,128)(2,1)S(1)} %shard_map.102.refs_5_.refs_0_), channel_id=1, source_target_pairs={{0,4},{4,0},{8,12},{12,8},{16,20},{20,16},{24,28},{28,24},{1,5},{5... | collective-permute-start | bytes 786440 | tf_op jit(solution)/shard_map/ppermute | solution.py:638
  34.2 1.7 %collective-permute-start.9 = (f32[2,40,640]{2,1,0:T(8,128)S(1)}, f32[2,40,640]{2,1,0:T(8,128)S(1)}, u32[]{:S(2)}, u32[]{:S(2)}) collective-permute-start(f32[2,40,640]{2,1,0:T(8,128)S(1)} %get-tuple-element.36), channel_id=1, source_target_pairs={{0,1},{1,0},{2,3},{3,2},{4,5},{5,4},{6,7},{7,6},{8,9},{9,8},{10,11... | collective-permute-start | bytes 614408 | tf_op jit(solution)/shard_map/ppermute | solution.py:663
  34.3 1.6 %collective-permute-start.10 = (f32[40,768]{1,0:T(8,128)S(1)}, f32[40,768]{1,0:T(8,128)S(1)}, u32[]{:S(2)}, u32[]{:S(2)}) collective-permute-start(f32[40,768]{1,0:T(8,128)S(1)} %get-tuple-element.37), channel_id=1, source_target_pairs={{0,1},{1,0},{2,3},{3,2},{4,5},{5,4},{6,7},{7,6},{8,9},{9,8},{10,11... | collective-permute-start | bytes 368648 | tf_op jit(solution)/shard_map/ppermute | solution.py:663
  40.6 2.0 %copy-start.2 = (bf16[1,1,1,7,16,1024]{5,4,3,2,1,0:T(8,128)(2,1)S(1)}, bf16[1,1,1,7,16,1024]{5,4,3,2,1,0:T(8,128)(2,1)}, u32[]{:S(2)}) copy-start(bf16[1,1,1,7,16,1024]{5,4,3,2,1,0:T(8,128)(2,1)} %param.15) | copy-start | bytes 688132
  40.6 2.0 %collective-permute-start.11 = (bf16[8,32,1024]{2,1,0:T(8,128)(2,1)S(1)}, bf16[8,32,1024]{2,1,0:T(8,128)(2,1)S(1)}, u32[]{:S(2)}, u32[]{:S(2)}) collective-permute-start(bf16[8,32,1024]{2,1,0:T(8,128)(2,1)S(1)} %shard_map.107.refs_3_.refs_1_), channel_id=1, source_target_pairs={{0,1},{1,0},{2,3},{3,2},{4,5},{5,4},{6,7},{7,6},{8,9},{9,8},{10,11... | collective-permute-start | bytes 1572872 | tf_op jit(solution)/shard_map/ppermute | solution.py:678
  43.7 4.3 %collective-permute-start.12 = (f32[32,512]{1,0:T(8,128)S(1)}, f32[32,512]{1,0:T(8,128)S(1)}, u32[]{:S(2)}, u32[]{:S(2)}) collective-permute-start(f32[32,512]{1,0:T(8,128)S(1)} %get-tuple-element.43.refs_5_), channel_id=1, source_target_pairs={{0,2},{2,0},{1,3},{3,1},{4,6},{6,4},{5,7},{7,5},{8,10},{10,8},{9,1... | collective-permute-start | bytes 196616 | tf_op jit(solution)/shard_map/ppermute | solution.py:693

commit v8 on v7

--- a/solution.py
+++ b/solution.py
@@ -362,23 +362,28 @@
     copy.wait()
 
 
-def side_edge_kernel(nx, source, inv, *refs):
+def put_side(cells, odd, messages, rows, first, last, c):
+    halo = HALO * E
+    lane = lane_ids(c)
+    axis = c.ndim - 1
+    low = jnp.where(lane < halo, first, roll(c, halo, axis))
+    high = jnp.where(lane < halo, roll(last, halo, axis), roll(c, halo - (cells - HALO), axis))
+    for number, message in enumerate(messages):
+        message[rows] = choose(odd, low, high, number)
+
+
+def side_edge_kernel(source, inv, *messages):
+    rows_x, _, width = source.shape
+    first, last = source[:, :, :LANES], source[:, :, width - LANES :]
+    own = slice(HALO - 1, HALO - 1 + rows_x)
+    put_side(width // E, index("gy") % 2, messages, own, first, last, inv[...])
+
+
+def side_halo_kernel(nx, ny, depth, *refs):
     odd_x, odd_y = index("gx") % 2, index("gy") % 2
-    got_x, messages = [r[...] for r in refs[:nx]], refs[nx:]
-    rows_x, depth, width = source.shape
-    cells = width // E
-    halo = HALO * E
-
-    def put(rows, first, last, c):
-        lane = lane_ids(c)
-        axis = c.ndim - 1
-        low = jnp.where(lane < halo, first, roll(c, halo, axis))
-        high = jnp.where(lane < halo, roll(last, halo, axis), roll(c, halo - (cells - HALO), axis))
-        for number, message in enumerate(messages):
-            message[rows] = choose(odd_y, low, high, number)
-
-    own = slice(HALO - 1, HALO - 1 + rows_x)
-    put(own, source[:, :, :LANES], source[:, :, width - LANES :], inv[...])
+    got_x, messages = [r[...] for r in refs[:nx]], refs[nx + ny :]
+    width = got_x[0].shape[1]
+    rows_x = messages[0].shape[0] - 2 * (HALO - 1)
     for start, skip, edge in (
         (0, 1, from_low(odd_x, got_x)),
         (HALO - 1 + rows_x, 0, from_high(odd_x, got_x)),
@@ -386,7 +391,8 @@
         planes, compacts = row_layers(edge, depth)
         for k in range(HALO - 1):
             s, c = planes[k + skip], compacts[k + skip]
-            put(start + k, s[:, :LANES], s[:, width - LANES :], c)
+            first, last = s[:, :LANES], s[:, width - LANES :]
+            put_side(width // E, odd_y, messages, start + k, first, last, c)
 
 
 def widen(cells, ring, s, c, left, right):
@@ -447,44 +453,28 @@
 
 
 def assemble_kernel(cells, ring, nx, ny, source, inv, *refs):
-    odd_x, odd_y, side = index("gx") % 2, index("gy") % 2, index("gz")
+    odd_x, odd_y = index("gx") % 2, index("gy") % 2
     got_x, got_y = refs[:nx], refs[nx : nx + ny]
-    z_two, z_one, ext_s, ext_i, one, compacts, matrix = refs[nx + ny :]
+    ext_s, ext_i, one, compacts, matrix = refs[nx + ny :]
     rows_x, depth, width = source.shape
     wide = ring * E
     all_z = depth + ROWS
     total = ext_s.shape[0]
     matrix[...] = spread_matrix(ring, wide)
-    start = side * (ROWS - HALO)
-
-    def spaced(rows):
-        at = lax.broadcasted_iota(jnp.int32, (ROWS, rows[0].shape[1]), 0) - start
-        tile = jnp.zeros(at.shape, jnp.float32)
-        for k, value in enumerate(rows):
-            tile = jnp.where(at == k, value, tile)
-        return tile
-
     def place(x, s, c, got):
         parts, compact = widen(cells, ring, s, c, from_low(odd_y, got), from_high(odd_y, got))
-        last = z_one[pl.ds(x, 1), :]
-        zone = spaced([z_two[0, pl.ds(x, 1), :], z_two[1, pl.ds(x, 1), :], last[:, :wide]])
-        packs = jnp.broadcast_to(last[:, wide:], (ROWS, LANES))
-        lanes = spaced([roll(packs, -32 * k, 1) for k in range(HALO)])
         first = pl.ds(pl.multiple_of(x * all_z, ROWS), depth)
-        rest = pl.ds(pl.multiple_of(x * all_z + depth, ROWS), ROWS)
         compacts[first, :] = compact
-        compacts[rest, :] = lanes
         at = 0
         for part in parts:
             ext_s[first, at : at + part.shape[1]] = part
             at += part.shape[1]
-        ext_s[rest, :] = zone
 
     def own(x, _):
         place(x + HALO, source[x], inv[x], [r[x + HALO - 1] for r in got_y])
         return 0
 
-    repeat(0, rows_x, own, 16)
+    repeat(0, rows_x, own, 32)
     got = [r[...] for r in got_x]
     for base, skip, edge in ((0, 0, from_low(odd_x, got)), (rows_x + HALO, 2, from_high(odd_x, got))):
         planes, compact = row_layers(edge, depth)
@@ -507,6 +497,47 @@
     repeat(0, total // chunk, expand, 5)
 
 
+def depth_rows_kernel(ring, z_two, z_one, _s, _i, _o, ext_s, ext_i, one, compacts, inverses, matrix):
+    all_x = compacts.shape[0] // ROWS
+    all_z = ext_s.shape[0] // all_x
+    depth, wide = all_z - ROWS, ring * E
+    matrix[...] = spread_matrix(ring, wide)
+    start = index("gz") * (ROWS - HALO)
+
+    def rest(x):
+        return pl.ds(pl.multiple_of(x * all_z + depth, ROWS), ROWS)
+
+    def tile_of(x):
+        return pl.ds(pl.multiple_of(x * ROWS, ROWS), ROWS)
+
+    def spaced(rows):
+        at = lax.broadcasted_iota(jnp.int32, (ROWS, rows[0].shape[1]), 0) - start
+        tile = jnp.zeros(at.shape, jnp.float32)
+        for k, value in enumerate(rows):
+            tile = jnp.where(at == k, value, tile)
+        return tile
+
+    def zone(x, _):
+        last = z_one[pl.ds(x, 1), :]
+        ext_s[rest(x), :] = spaced(
+            [z_two[0, pl.ds(x, 1), :], z_two[1, pl.ds(x, 1), :], last[:, :wide]]
+        )
+        packs = jnp.broadcast_to(last[:, wide:], (ROWS, LANES))
+        compacts[tile_of(x), :] = spaced([roll(packs, -32 * k, 1) for k in range(HALO)])
+        return 0
+
+    def spread_out(x, _):
+        i = inverses[tile_of(x), :]
+        ext_i[rest(x), :] = i
+        one[rest(x), :] = ext_s[rest(x), :] * i
+        return 0
+
+    repeat(0, all_x, zone, 38)
+    some = packed(compacts[...], ring)
+    inverses[...] = jnp.dot(some, matrix[...], preferred_element_type=jnp.float32)
+    repeat(0, all_x, spread_out, 38)
+
+
 def repeat(first, last, step, most):
     count = last - first
     unroll = max(n for n in range(1, most + 1) if count % n == 0)
@@ -548,7 +579,7 @@
         swept(ext_s, ext_i, old, x, all_z, all_z, old.shape[1], store)
         return 0
 
-    repeat(first, last, step, 12)
+    repeat(first, last, step, 36)
 
 
 def off_face(side, depth):
@@ -622,9 +653,11 @@
     )
     got_x = swap(face_x, "gx")
     (order,) = call(order_kernel, (face_trace,), [vector((tile, tile), bf16)], after=(near,))
+    sides = [vector((all_x - 2, depth, LANES))] * ny
+    vol_y = call(side_edge_kernel, (held_source, inv), sides, after=(near,))
     vol_y = call(
-        functools.partial(side_edge_kernel, nx), (held_source, inv, *got_vol_x),
-        [vector((all_x - 2, depth, LANES))] * ny, work=300, after=(order, *got_x),
+        functools.partial(side_halo_kernel, nx, ny, depth), (*got_vol_x, *vol_y), sides,
+        after=(order, *got_x), input_output_aliases={nx + n: n for n in range(ny)},
     )
     got_vol_y = swap(vol_y, "gy")
 
@@ -662,10 +695,19 @@
             )
             got_vol_z = [held(lax.ppermute(v, "gz", both)) for v in vol_z]
             ext = vector((all_x * all_z, wide))
+            most = call(
+                functools.partial(assemble_kernel, cells, ring, nx, ny),
+                (held_source, inv, *got_vol_x, *got_vol_y), [ext, ext, ext],
+                scratch=(vector((all_x * all_z, LANES)), vector((LANES, wide), bf16)),
+                after=vol_z,
+            )
             ext_s, ext_i, one = call(
-                functools.partial(assemble_kernel, cells, ring, nx, ny),
-                (held_source, inv, *got_vol_x, *got_vol_y, *got_vol_z), [ext, ext, ext], work=3000,
-                scratch=(vector((all_x * all_z, LANES)), vector((LANES, wide), bf16)),
+                functools.partial(depth_rows_kernel, ring), (*got_vol_z, *most), [ext, ext, ext],
+                scratch=(
+                    vector((all_x * ROWS, LANES)), vector((all_x * ROWS, wide)),
+                    vector((LANES, wide), bf16),
+                ),
+                input_output_aliases={2: 0, 3: 1, 4: 2},
             )
             (two,) = call(
                 functools.partial(sweep_kernel, all_z, 1, all_x - 1), (ext_s, ext_i, one), [ext],
@@ -676,8 +718,7 @@
             join_kernel, (traces, other), [vector(twice, bf16)], work=300, after=before
         )
     other = held(lax.ppermute(traces, "gz", both))
-    count_x = (all_x - 4) // 2
-    middle = 2 + count_x - count_x % 4
+    middle = 2 + (all_x - 4) * 3 // 5
     (three,) = call(
         functools.partial(sweep_kernel, all_z, 2, middle), (ext_s, ext_i, two), [ext], work=1400,
         after=(traces,),

time: 49.4 us -> 47.7 us (0.966)
  waiting for transfers between devices: 7.06 us -> 5.58 us
  local copies, waits for them, and re-layouts: 0.03 us -> 0.74 us
  starting transfers between devices: 20 us -> 19.4 us
    ppermute x2, waiting for transfers between devices: 1.12 us -> 0.01 us  [body(): got_vol_z = [held(lax.ppermute(v, 'gz', both)) for v in vol_z]]
    ppermute x3, starting transfers between devices: 6.63 us -> 5.76 us  [body(): lax.ppermute(traces, 'gx', [(i, i ^ step) for i in range(size_x)])]
    unnamed x10, local copies, waits for them, and re-layouts: 0.03 us -> 0.74 us
    ppermute x5, waiting for transfers between devices: 0.64 us -> 0.01 us  [swap(): lax.ppermute(m, axis, p)]
    pallas_call x18 -> x20, Pallas kernels: 20.6 us -> 20.2 us  [call(): pl.pallas_call(body, out_shape=out_shape, in_specs=(in_specs or [VECTOR]...]
  transfers between devices with their start and end apart: 13 -> 13, of which waited for: 7 -> 5; matrix products, arithmetic and copies ran while one was open for 0% -> 0% of each run, Pallas kernels for 32% -> 33%
where the time goes in v8:
time: 47.7 us; the launch traced here: 47.5 us
  Pallas kernels  20.2 us (42%)
  starting transfers between devices  19.4 us (41%)
  waiting for transfers between devices  5.58 us (12%)
  between operations  1.52 us (3%)
  local copies, waits for them, and re-layouts  0.74 us (2%)
    pallas_call x20, Pallas kernels, call(): pl.pallas_call(body, out_shape=out_shape, in_specs=(in_specs or [VECTOR]...  20.2 us
    ppermute x5, starting transfers between devices, swap(): lax.ppermute(m, axis, p)  8.97 us
    ppermute x3, starting transfers between devices, body(): lax.ppermute(traces, 'gx', [(i, i ^ step) for i in range(size_x)])  5.76 us
    ppermute x1, waiting for transfers between devices, body(): other = held(lax.ppermute(near, 'gy', both))  3.09 us
    ppermute x1, starting transfers between devices, body(): other = held(lax.ppermute(near, 'gy', both))  3.03 us
    ppermute x3, waiting for transfers between devices, body(): lax.ppermute(traces, 'gx', [(i, i ^ step) for i in range(size_x)])  1.8 us
  transfers between devices with their start and end apart: 13, of which 5 were waited for; matrix products, arithmetic and copies ran while one was open for 0% of the time, Pallas kernels for 33%

profile of v8, /device:TPU:0, one launch (start us, length us, event | category | flops | bytes accessed | tf_op | source)
XLA Modules:
  0.0 47.5 jit_solution(6413460440996910554)
XLA Ops:
  0.6 1.9 %shard_map.95 = (f32[32,32,512]{2,1,0:T(8,128)S(1)}, f32[32,32,128]{2,1,0:T(8,128)S(1)}, f32[104,512]{1,0:T(8,128)S(1)}, f32[104,512]{1,0:T(8,128)S(1)}, f32[104,512]{1,0:T(8,128)S(1)}) custom-call(f32[32,32,512]{2,1,0:T(8,128)} %refs_0_.3, f32[32,16,32]{2,1,0:T(8,128)} %bitcast.7), custom_call_target="tpu_custom_call" | custom-call | bytes 3000000 | tf_op jit(solution)/shard_map/pallas_call | solution.py:58
  2.5 3.0 %collective-permute-start = (f32[104,512]{1,0:T(8,128)S(1)}, f32[104,512]{1,0:T(8,128)S(1)}, u32[]{:S(2)}, u32[]{:S(2)}) collective-permute-start(f32[104,512]{1,0:T(8,128)S(1)} %get-tuple-element.29.refs_0_.refs_1_.refs_2_), channel_id=1, source_target_pairs={{0,2},{2,0},{1,3},{3,1},{4,6},{6,4},{5,7},{7,5},{8,10},{10,8},{9,1... | collective-permute-start | bytes 638984 | tf_op jit(solution)/shard_map/ppermute | solution.py:644
  5.5 1.5 %collective-permute-start.6 = (f32[104,512]{1,0:T(8,128)S(1)}, f32[104,512]{1,0:T(8,128)S(1)}, u32[]{:S(2)}, u32[]{:S(2)}) collective-permute-start(f32[104,512]{1,0:T(8,128)S(1)} %get-tuple-element.37), channel_id=1, source_target_pairs={{0,4},{4,0},{8,12},{12,8},{16,20},{20,16},{24,28},{28,24},{1,5},{5... | collective-permute-start | bytes 638984 | tf_op jit(solution)/shard_map/ppermute | solution.py:82
  7.0 0.7 %collective-permute-start.7 = (f32[104,512]{1,0:T(8,128)S(1)}, f32[104,512]{1,0:T(8,128)S(1)}, u32[]{:S(2)}, u32[]{:S(2)}) collective-permute-start(f32[104,512]{1,0:T(8,128)S(1)} %get-tuple-element.38), channel_id=1, source_target_pairs={{4,8},{12,16},{20,24},{8,4},{16,12},{24,20},{5,9},{13,17},{21,25},... | collective-permute-start | bytes 638984 | tf_op jit(solution)/shard_map/ppermute | solution.py:82
  7.7 3.1 %collective-permute-done.refs_1_ = f32[104,512]{1,0:T(8,128)S(1)} collective-permute-done((f32[104,512]{1,0:T(8,128)S(1)}, f32[104,512]{1,0:T(8,128)S(1)}, u32[]{:S(2)}, u32[]{:S(2)}) %collective-permute-start) | collective-permute-done | bytes 213024 | tf_op jit(solution)/shard_map/ppermute | solution.py:644
  10.8 0.4 shard_map.96
  11.2 0.7 %collective-permute-start.2 = (f32[16,1024]{1,0:T(8,128)S(1)}, f32[16,1024]{1,0:T(8,128)S(1)}, u32[]{:S(2)}, u32[]{:S(2)}) collective-permute-start(f32[16,1024]{1,0:T(8,128)S(1)} %get-tuple-element.33), channel_id=1, source_target_pairs={{4,8},{12,16},{20,24},{8,4},{16,12},{24,20},{5,9},{13,17},{21,25},... | collective-permute-start | bytes 196616 | tf_op jit(solution)/shard_map/ppermute | solution.py:82
  11.8 4.6 %collective-permute-start.1 = (f32[8,1024]{1,0:T(8,128)S(1)}, f32[8,1024]{1,0:T(8,128)S(1)}, u32[]{:S(2)}, u32[]{:S(2)}) collective-permute-start(f32[8,1024]{1,0:T(8,128)S(1)} %get-tuple-element.32), channel_id=1, source_target_pairs={{0,4},{4,0},{8,12},{12,8},{16,20},{20,16},{24,28},{28,24},{1,5},{5... | collective-permute-start | bytes 98312 | tf_op jit(solution)/shard_map/ppermute | solution.py:82
  16.4 0.7 %copy-done.3 = s32[32,1,32]{2,1,0:T(1,128)S(1)} copy-done((s32[32,1,32]{2,1,0:T(1,128)S(1)}, s32[32,1,32]{2,1,0:T(1,128)}, u32[]{:S(2)}) %copy-start.3) | copy-done | bytes 4120
  17.1 1.2 %shard_map.97.refs_2_.refs_0_.refs_3_ = bf16[1024,1024]{1,0:T(8,128)(2,1)S(1)} custom-call(s32[32,1,32]{2,1,0:T(1,128)S(1)} %copy-done.3, f32[104,512]{1,0:T(8,128)S(1)} %get-tuple-element.29.refs_0_.refs_1_.refs_2_), custom_call_target="tpu_custom_call" | custom-call | bytes 3000000 | tf_op jit(solution)/shard_map/pallas_call | solution.py:58
  18.4 0.5 shard_map.103.refs_2_
  19.1 1.6 %collective-permute-start.8 = (f32[36,32,128]{2,1,0:T(8,128)S(1)}, f32[36,32,128]{2,1,0:T(8,128)S(1)}, u32[]{:S(2)}, u32[]{:S(2)}) collective-permute-start(f32[36,32,128]{2,1,0:T(8,128)S(1)} %shard_map.104), channel_id=1, source_target_pairs={{0,2},{2,0},{1,3},{3,1},{4,6},{6,4},{5,7},{7,5},{8,10},{10,8},{9,1... | collective-permute-start | bytes 1769480 | tf_op jit(solution)/shard_map/ppermute | solution.py:82
  20.7 0.9 %shard_map.98.refs_2_.refs_0_ = bf16[1,32,1024]{2,1,0:T(8,128)(2,1)S(1)} custom-call(f32[3,32,1024]{2,1,0:T(8,128)S(1)} %get-tuple-element.30.refs_0_, f32[3,32,1024]{2,1,0:T(8,128)S(1)} %get-tuple-element.31.refs_1_, bf16[1024,1024]{1,0:T(8,128)(2,1)S(1)} %shard_map.97.refs_2_.refs_0_.refs_3_, f32[8,1024]{1,0:T(8,128)S(1)} %collective-permute-done.1.refs_3_.refs_4_, ...), custom_call_target="tpu_custom_call" | custom-call | bytes 3000000 | tf_op jit(solution)/shard_map/pallas_call | solution.py:58
  21.6 2.6 %collective-permute-start.3 = (bf16[1,32,1024]{2,1,0:T(8,128)(2,1)S(1)}, bf16[1,32,1024]{2,1,0:T(8,128)(2,1)S(1)}, u32[]{:S(2)}, u32[]{:S(2)}) collective-permute-start(bf16[1,32,1024]{2,1,0:T(8,128)(2,1)S(1)} %shard_map.98.refs_2_.refs_0_), channel_id=1, source_target_pairs={{0,16},{4,20},{8,24},{12,28},{16,0},{20,4},{24,8},{28,12},{1,17},{... | collective-permute-start | bytes 196616 | tf_op jit(solution)/shard_map/ppermute | solution.py:671
  24.9 0.6 %shard_map.99.refs_2_.refs_0_ = s32[8]{0:T(128)S(4)} custom-call(s32[1,1,1]{2,1,0:T(1,128)S(6)} %copy.22.refs_0_, s32[1,1,1,7]{3,2,1,0:T(1,128)S(1)} %copy-done.4, bf16[1,32,1024]{2,1,0:T(8,128)(2,1)S(1)} %shard_map.98.refs_2_.refs_0_), custom_call_target="tpu_custom_call" | custom-call | bytes 3000000 | tf_op jit(solution)/shard_map/pallas_call | solution.py:58
  25.5 1.3 %collective-permute-done.3.refs_1_ = bf16[1,32,1024]{2,1,0:T(8,128)(2,1)S(1)} collective-permute-done((bf16[1,32,1024]{2,1,0:T(8,128)(2,1)S(1)}, bf16[1,32,1024]{2,1,0:T(8,128)(2,1)S(1)}, u32[]{:S(2)}, u32[]{:S(2)}) %collective-permute-start.3) | collective-permute-done | bytes 65568 | tf_op jit(solution)/shard_map/ppermute | solution.py:671
  26.9 1.6 %collective-permute-start.4 = (bf16[2,32,1024]{2,1,0:T(8,128)(2,1)S(1)}, bf16[2,32,1024]{2,1,0:T(8,128)(2,1)S(1)}, u32[]{:S(2)}, u32[]{:S(2)}) collective-permute-start(bf16[2,32,1024]{2,1,0:T(8,128)(2,1)S(1)} %shard_map.100.refs_3_.refs_0_), channel_id=1, source_target_pairs={{0,8},{4,12},{8,0},{12,4},{16,24},{20,28},{24,16},{28,20},{1,9},{5... | collective-permute-start | bytes 393224 | tf_op jit(solution)/shard_map/ppermute | solution.py:671
  28.5 2.9 %shard_map.101 = (bf16[1024,1024]{1,0:T(8,128)(2,1)S(1)}, bf16[112,1024]{1,0:T(8,128)(2,1)S(1)}) custom-call(bf16[1024,1024]{1,0:T(8,128)(2,1)S(1)} %shard_map.97.refs_2_.refs_0_.refs_3_, bf16[1024,1024]{1,0:T(8,128)(2,1)S(1)} %bitcast.4, bf16[112,1024]{1,0:T(8,128)(2,1)S(1)} %bitcast.5, bf16[2,32,1024]{2,1,0:T(8,128)(2,1)S(1)} %shard_map.100.refs_3_.refs_0_), custom_call_target="tpu_custom_call" | custom-call | bytes 9000000 | tf_op jit(solution)/shard_map/pallas_call | solution.py:58
  31.4 0.5 %collective-permute-done.4.refs_1_ = bf16[2,32,1024]{2,1,0:T(8,128)(2,1)S(1)} collective-permute-done((bf16[2,32,1024]{2,1,0:T(8,128)(2,1)S(1)}, bf16[2,32,1024]{2,1,0:T(8,128)(2,1)S(1)}, u32[]{:S(2)}, u32[]{:S(2)}) %collective-permute-start.4) | collective-permute-done | bytes 131104 | tf_op jit(solution)/shard_map/ppermute | solution.py:671
  31.9 1.5 %collective-permute-start.5 = (bf16[4,32,1024]{2,1,0:T(8,128)(2,1)S(1)}, bf16[4,32,1024]{2,1,0:T(8,128)(2,1)S(1)}, u32[]{:S(2)}, u32[]{:S(2)}) collective-permute-start(bf16[4,32,1024]{2,1,0:T(8,128)(2,1)S(1)} %shard_map.102.refs_5_.refs_0_), channel_id=1, source_target_pairs={{0,4},{4,0},{8,12},{12,8},{16,20},{20,16},{24,28},{28,24},{1,5},{5... | collective-permute-start | bytes 786440 | tf_op jit(solution)/shard_map/ppermute | solution.py:671
  33.4 0.3 shard_map.105
  33.8 0.5 %collective-permute-start.10 = (f32[40,768]{1,0:T(8,128)S(1)}, f32[40,768]{1,0:T(8,128)S(1)}, u32[]{:S(2)}, u32[]{:S(2)}) collective-permute-start(f32[40,768]{1,0:T(8,128)S(1)} %get-tuple-element.40.refs_6_), channel_id=1, source_target_pairs={{0,1},{1,0},{2,3},{3,2},{4,5},{5,4},{6,7},{7,6},{8,9},{9,8},{10,11... | collective-permute-start | bytes 368648 | tf_op jit(solution)/shard_map/ppermute | solution.py:696
  34.3 1.2 %shard_map.106 = (f32[1520,640]{1,0:T(8,128)S(1)}, f32[1520,640]{1,0:T(8,128)S(1)}, f32[1520,640]{1,0:T(8,128)S(1)}) custom-call(f32[32,32,512]{2,1,0:T(8,128)S(1)} %get-tuple-element.35.refs_0_, f32[32,32,128]{2,1,0:T(8,128)S(1)} %get-tuple-element.36.refs_1_, f32[104,512]{1,0:T(8,128)S(1)} %collective-permute-done.6.refs_0_.refs_2_, ...), custom_call_target="tpu_custom_call" | custom-call | bytes 3000000 | tf_op jit(solution)/shard_map/pallas_call | solution.py:58
  35.6 0.6 %shard_map.107 = (f32[1520,640]{1,0:T(8,128)S(1)}, f32[1520,640]{1,0:T(8,128)S(1)}, f32[1520,640]{1,0:T(8,128)S(1)}) custom-call(f32[2,40,640]{2,1,0:T(8,128)S(1)} %collective-permute-done.9.refs_0_, f32[40,768]{1,0:T(8,128)S(1)} %collective-permute-done.10.refs_1_, ...), custom_call_target="tpu_custom_call", output_to_operand_aliasing={{0}: (2, {}), {1}: (3, {}), {2}: (4, {})} | custom-call | bytes 3000000 | tf_op jit(solution)/shard_map/pallas_call | solution.py:58
  36.2 2.7 %shard_map.108.refs_2_ = f32[1520,640]{1,0:T(8,128)S(1)} custom-call(f32[1520,640]{1,0:T(8,128)S(1)} %get-tuple-element.44.refs_0_, f32[1520,640]{1,0:T(8,128)S(1)} %get-tuple-element.45.refs_1_, f32[1520,640]{1,0:T(8,128)S(1)} %get-tuple-element.46.refs_2_), custom_call_target="tpu_custom_call" | custom-call | bytes 7500000 | tf_op jit(solution)/shard_map/pallas_call | solution.py:58
  39.0 1.5 %shard_map.110.refs_6_.refs_3_ = f32[1520,640]{1,0:T(8,128)S(1)} custom-call(f32[1520,640]{1,0:T(8,128)S(1)} %get-tuple-element.44.refs_0_, f32[1520,640]{1,0:T(8,128)S(1)} %get-tuple-element.45.refs_1_, f32[1520,640]{1,0:T(8,128)S(1)} %shard_map.108.refs_2_, bf16[8,32,1024]{2,1,0:T(8,128)(2,1)S(1)} %shard_map.109.refs_3_.refs_1_), custom_call_target="tpu_custom_call" | custom-call | bytes 4200000 | tf_op jit(solution)/shard_map/pallas_call | solution.py:58
  40.5 0.4 collective-permute-done.11.refs_2_
  40.9 1.1 %shard_map.111 = (f32[32,512]{1,0:T(8,128)S(1)}, f32[32,512]{1,0:T(8,128)S(1)}) custom-call(s32[8]{0:T(128)S(4)} %shard_map.99.refs_2_.refs_0_, bf16[8,32,1024]{2,1,0:T(8,128)(2,1)S(1)} %shard_map.109.refs_3_.refs_1_, bf16[8,32,1024]{2,1,0:T(8,128)(2,1)S(1)} %collective-permute-done.11.refs_2_, bf16[1024,1024]{1,0:T(8,128)(2,1)S(1)} %get-tuple-element.34.refs_2_.refs_3_, ...), custom_call_target="tpu_custom_call" | custom-call | bytes 7500000 | tf_op jit(solution)/shard_map/pallas_call | solution.py:58
  42.0 0.9 %collective-permute-start.12 = (f32[32,512]{1,0:T(8,128)S(1)}, f32[32,512]{1,0:T(8,128)S(1)}, u32[]{:S(2)}, u32[]{:S(2)}) collective-permute-start(f32[32,512]{1,0:T(8,128)S(1)} %get-tuple-element.49.refs_5_), channel_id=1, source_target_pairs={{0,2},{2,0},{1,3},{3,1},{4,6},{6,4},{5,7},{7,5},{8,10},{10,8},{9,1... | collective-permute-start | bytes 196616 | tf_op jit(solution)/shard_map/ppermute | solution.py:734
  42.9 1.0 %shard_map.112.refs_2_ = f32[1520,640]{1,0:T(8,128)S(1)} custom-call(f32[1520,640]{1,0:T(8,128)S(1)} %get-tuple-element.44.refs_0_, f32[1520,640]{1,0:T(8,128)S(1)} %get-tuple-element.45.refs_1_, f32[1520,640]{1,0:T(8,128)S(1)} %shard_map.108.refs_2_, f32[1520,640]{1,0:T(8,128)S(1)} %shard_map.110.refs_6_.refs_3_, ...), custom_call_target="tpu_custom_call", output_to_operand_aliasing={{}: (3, {})} | custom-call | bytes 4200000 | tf_op jit(solution)/shard_map/pallas_call | solution.py:58
  44.0 2.0 %shard_map.113 = (f32[32,32,512]{2,1,0:T(8,128)}, f32[32,8,512]{2,1,0:T(8,128)S(1)}, f32[8,32,512]{2,1,0:T(8,128)S(1)}) custom-call(f32[1520,640]{1,0:T(8,128)S(1)} %get-tuple-element.44.refs_0_, f32[1520,640]{1,0:T(8,128)S(1)} %get-tuple-element.45.refs_1_, f32[1520,640]{1,0:T(8,128)S(1)} %shard_map.112.refs_2_), custom_call_target="tpu_custom_call" | custom-call | bytes 6000000 | tf_op jit(solution)/shard_map/pallas_call | solution.py:58
  46.3 1.2 %shard_map.114 = (f32[32,1,512]{2,1,0:T(1,128)}, f32[32,32,512]{2,1,0:T(8,128)}) custom-call(f32[32,512]{1,0:T(8,128)S(1)} %get-tuple-element.48.refs_4_.refs_0_, f32[32,512]{1,0:T(8,128)S(1)} %collective-permute-done.12.refs_1_, f32[32,512]{1,0:T(8,128)S(1)} %get-tuple-element.50.refs_2_, ...), custom_call_target="tpu_custom_call", output_to_operand_aliasing={{1}: (5, {})} | custom-call | bytes 3000000 | tf_op jit(solution)/shard_map/pallas_call | solution.py:58
  (24 shorter events, 0.8 us)
Async XLA Ops:
  2.5 8.3 %collective-permute-start = (f32[104,512]{1,0:T(8,128)S(1)}, f32[104,512]{1,0:T(8,128)S(1)}, u32[]{:S(2)}, u32[]{:S(2)}) collective-permute-start(f32[104,512]{1,0:T(8,128)S(1)} %get-tuple-element.29.refs_0_.refs_1_.refs_2_), channel_id=1, source_target_pairs={{0,2},{2,0},{1,3},{3,1},{4,6},{6,4},{5,7},{7,5},{8,10},{10,8},{9,1... | collective-permute-start | bytes 638984 | tf_op jit(solution)/shard_map/ppermute | solution.py:644
  5.5 13.3 %collective-permute-start.6 = (f32[104,512]{1,0:T(8,128)S(1)}, f32[104,512]{1,0:T(8,128)S(1)}, u32[]{:S(2)}, u32[]{:S(2)}) collective-permute-start(f32[104,512]{1,0:T(8,128)S(1)} %get-tuple-element.37), channel_id=1, source_target_pairs={{0,4},{4,0},{8,12},{12,8},{16,20},{20,16},{24,28},{28,24},{1,5},{5... | collective-permute-start | bytes 638984 | tf_op jit(solution)/shard_map/ppermute | solution.py:82
  7.0 11.9 %collective-permute-start.7 = (f32[104,512]{1,0:T(8,128)S(1)}, f32[104,512]{1,0:T(8,128)S(1)}, u32[]{:S(2)}, u32[]{:S(2)}) collective-permute-start(f32[104,512]{1,0:T(8,128)S(1)} %get-tuple-element.38), channel_id=1, source_target_pairs={{4,8},{12,16},{20,24},{8,4},{16,12},{24,20},{5,9},{13,17},{21,25},... | collective-permute-start | bytes 638984 | tf_op jit(solution)/shard_map/ppermute | solution.py:82
  11.2 7.7 %collective-permute-start.2 = (f32[16,1024]{1,0:T(8,128)S(1)}, f32[16,1024]{1,0:T(8,128)S(1)}, u32[]{:S(2)}, u32[]{:S(2)}) collective-permute-start(f32[16,1024]{1,0:T(8,128)S(1)} %get-tuple-element.33), channel_id=1, source_target_pairs={{4,8},{12,16},{20,24},{8,4},{16,12},{24,20},{5,9},{13,17},{21,25},... | collective-permute-start | bytes 196616 | tf_op jit(solution)/shard_map/ppermute | solution.py:82
  11.8 7.1 %collective-permute-start.1 = (f32[8,1024]{1,0:T(8,128)S(1)}, f32[8,1024]{1,0:T(8,128)S(1)}, u32[]{:S(2)}, u32[]{:S(2)}) collective-permute-start(f32[8,1024]{1,0:T(8,128)S(1)} %get-tuple-element.32), channel_id=1, source_target_pairs={{0,4},{4,0},{8,12},{12,8},{16,20},{20,16},{24,28},{28,24},{1,5},{5... | collective-permute-start | bytes 98312 | tf_op jit(solution)/shard_map/ppermute | solution.py:82
  16.4 0.7 %copy-start.3 = (s32[32,1,32]{2,1,0:T(1,128)S(1)}, s32[32,1,32]{2,1,0:T(1,128)}, u32[]{:S(2)}) copy-start(s32[32,1,32]{2,1,0:T(1,128)} %refs_0_.4) | copy-start | bytes 12292
  18.9 6.0 %copy-start.4 = (s32[1,1,1,7]{3,2,1,0:T(1,128)S(1)}, s32[1,1,1,7]{3,2,1,0:T(1,128)}, u32[]{:S(2)}) copy-start(s32[1,1,1,7]{3,2,1,0:T(1,128)} %refs_1_.1) | copy-start | bytes 88
  18.9 9.6 %copy-start = (bf16[1,1,1,1024,1024]{4,3,2,1,0:T(8,128)(2,1)S(1)}, bf16[1,1,1,1024,1024]{4,3,2,1,0:T(8,128)(2,1)}, u32[]{:S(2)}) copy-start(bf16[1,1,1,1024,1024]{4,3,2,1,0:T(8,128)(2,1)} %param.13) | copy-start | bytes 6291460
  18.9 9.6 %copy-start.1 = (bf16[1,1,1,7,16,1024]{5,4,3,2,1,0:T(8,128)(2,1)S(1)}, bf16[1,1,1,7,16,1024]{5,4,3,2,1,0:T(8,128)(2,1)}, u32[]{:S(2)}) copy-start(bf16[1,1,1,7,16,1024]{5,4,3,2,1,0:T(8,128)(2,1)} %param.14) | copy-start | bytes 688132
  19.1 14.3 %collective-permute-start.8 = (f32[36,32,128]{2,1,0:T(8,128)S(1)}, f32[36,32,128]{2,1,0:T(8,128)S(1)}, u32[]{:S(2)}, u32[]{:S(2)}) collective-permute-start(f32[36,32,128]{2,1,0:T(8,128)S(1)} %shard_map.104), channel_id=1, source_target_pairs={{0,2},{2,0},{1,3},{3,1},{4,6},{6,4},{5,7},{7,5},{8,10},{10,8},{9,1... | collective-permute-start | bytes 1769480 | tf_op jit(solution)/shard_map/ppermute | solution.py:82
  21.6 5.2 %collective-permute-start.3 = (bf16[1,32,1024]{2,1,0:T(8,128)(2,1)S(1)}, bf16[1,32,1024]{2,1,0:T(8,128)(2,1)S(1)}, u32[]{:S(2)}, u32[]{:S(2)}) collective-permute-start(bf16[1,32,1024]{2,1,0:T(8,128)(2,1)S(1)} %shard_map.98.refs_2_.refs_0_), channel_id=1, source_target_pairs={{0,16},{4,20},{8,24},{12,28},{16,0},{20,4},{24,8},{28,12},{1,17},{... | collective-permute-start | bytes 196616 | tf_op jit(solution)/shard_map/ppermute | solution.py:671
  26.9 5.0 %collective-permute-start.4 = (bf16[2,32,1024]{2,1,0:T(8,128)(2,1)S(1)}, bf16[2,32,1024]{2,1,0:T(8,128)(2,1)S(1)}, u32[]{:S(2)}, u32[]{:S(2)}) collective-permute-start(bf16[2,32,1024]{2,1,0:T(8,128)(2,1)S(1)} %shard_map.100.refs_3_.refs_0_), channel_id=1, source_target_pairs={{0,8},{4,12},{8,0},{12,4},{16,24},{20,28},{24,16},{28,20},{1,9},{5... | collective-permute-start | bytes 393224 | tf_op jit(solution)/shard_map/ppermute | solution.py:671
  31.9 6.9 %collective-permute-start.5 = (bf16[4,32,1024]{2,1,0:T(8,128)(2,1)S(1)}, bf16[4,32,1024]{2,1,0:T(8,128)(2,1)S(1)}, u32[]{:S(2)}, u32[]{:S(2)}) collective-permute-start(bf16[4,32,1024]{2,1,0:T(8,128)(2,1)S(1)} %shard_map.102.refs_5_.refs_0_), channel_id=1, source_target_pairs={{0,4},{4,0},{8,12},{12,8},{16,20},{20,16},{24,28},{28,24},{1,5},{5... | collective-permute-start | bytes 786440 | tf_op jit(solution)/shard_map/ppermute | solution.py:671
  33.8 1.8 %collective-permute-start.9 = (f32[2,40,640]{2,1,0:T(8,128)S(1)}, f32[2,40,640]{2,1,0:T(8,128)S(1)}, u32[]{:S(2)}, u32[]{:S(2)}) collective-permute-start(f32[2,40,640]{2,1,0:T(8,128)S(1)} %get-tuple-element.39.refs_5_), channel_id=1, source_target_pairs={{0,1},{1,0},{2,3},{3,2},{4,5},{5,4},{6,7},{7,6},{8,9},{9,8},{10,11... | collective-permute-start | bytes 614408 | tf_op jit(solution)/shard_map/ppermute | solution.py:696
  33.8 1.7 %collective-permute-start.10 = (f32[40,768]{1,0:T(8,128)S(1)}, f32[40,768]{1,0:T(8,128)S(1)}, u32[]{:S(2)}, u32[]{:S(2)}) collective-permute-start(f32[40,768]{1,0:T(8,128)S(1)} %get-tuple-element.40.refs_6_), channel_id=1, source_target_pairs={{0,1},{1,0},{2,3},{3,2},{4,5},{5,4},{6,7},{7,6},{8,9},{9,8},{10,11... | collective-permute-start | bytes 368648 | tf_op jit(solution)/shard_map/ppermute | solution.py:696
  38.9 2.0 %copy-start.2 = (bf16[1,1,1,7,16,1024]{5,4,3,2,1,0:T(8,128)(2,1)S(1)}, bf16[1,1,1,7,16,1024]{5,4,3,2,1,0:T(8,128)(2,1)}, u32[]{:S(2)}) copy-start(bf16[1,1,1,7,16,1024]{5,4,3,2,1,0:T(8,128)(2,1)} %param.15) | copy-start | bytes 688132
  38.9 2.0 %collective-permute-start.11 = (bf16[8,32,1024]{2,1,0:T(8,128)(2,1)S(1)}, bf16[8,32,1024]{2,1,0:T(8,128)(2,1)S(1)}, u32[]{:S(2)}, u32[]{:S(2)}) collective-permute-start(bf16[8,32,1024]{2,1,0:T(8,128)(2,1)S(1)} %shard_map.109.refs_3_.refs_1_), channel_id=1, source_target_pairs={{0,1},{1,0},{2,3},{3,2},{4,5},{5,4},{6,7},{7,6},{8,9},{9,8},{10,11... | collective-permute-start | bytes 1572872 | tf_op jit(solution)/shard_map/ppermute | solution.py:720
  42.0 4.3 %collective-permute-start.12 = (f32[32,512]{1,0:T(8,128)S(1)}, f32[32,512]{1,0:T(8,128)S(1)}, u32[]{:S(2)}, u32[]{:S(2)}) collective-permute-start(f32[32,512]{1,0:T(8,128)S(1)} %get-tuple-element.49.refs_5_), channel_id=1, source_target_pairs={{0,2},{2,0},{1,3},{3,1},{4,6},{6,4},{5,7},{7,5},{8,10},{10,8},{9,1... | collective-permute-start | bytes 196616 | tf_op jit(solution)/shard_map/ppermute | solution.py:734

commit v9 on v8

--- a/solution.py
+++ b/solution.py
@@ -132,7 +132,7 @@
     )
 
 
-def face_start_kernel(source, coef, held_source, inv, message, *refs):
+def face_start_kernel(source, coef, trace, held_source, held_trace, inv, message, *refs):
     edges, (coefs, sems) = refs[:-2], refs[-2:]
     odd, side = index("gx") % 2, index("gz")
     rows_x, depth, width = source.shape
@@ -140,6 +140,7 @@
     copies = [
         pltpu.make_async_copy(coef, coefs, sems.at[0]),
         pltpu.make_async_copy(source, held_source, sems.at[1]),
+        pltpu.make_async_copy(trace, held_trace, sems.at[2]),
     ]
     for copy in copies:
         copy.start()
@@ -159,6 +160,7 @@
         plane = jnp.where(side == 0, held_source[:, d, :], held_source[:, depth - 1 - d, :])
         message[d * rows_x : (d + 1) * rows_x, :] = plane
     row_edges(odd, held_source, inv, edges)
+    copies[2].wait()
 
 
 def row_edges(odd, source, inv, messages):
@@ -633,12 +635,13 @@
     halves = groups == 2
     coef = coef.transpose(0, 2, 1)
 
-    held_source, inv, near, *vol_x = call(
-        face_start_kernel, (kept(source), kept(coef)),
-        [vector(source.shape), vector((rows_x, depth, LANES)), vector((NEAR * rows_x + ROWS, width))]
+    held_source, held_trace, inv, near, *vol_x = call(
+        face_start_kernel, (kept(source), kept(coef), kept(face_trace)),
+        [vector(source.shape), vector(face_trace.shape, jnp.int32), vector((rows_x, depth, LANES)),
+          vector((NEAR * rows_x + ROWS, width))]
         + [vector((HALO * depth + ROWS, width))] * nx,
-        in_specs=[MAIN, MAIN],
-        scratch=(vector(coef.shape), pltpu.SemaphoreType.DMA((2,))),
+        in_specs=[MAIN] * 3,
+        scratch=(vector(coef.shape), pltpu.SemaphoreType.DMA((3,))),
     )
     if halves:
         other = held(lax.ppermute(near, "gy", both))
@@ -652,7 +655,7 @@
         + [vector(((1 + n) * ROWS, width * groups)) for n in range(nx)], work=500,
     )
     got_x = swap(face_x, "gx")
-    (order,) = call(order_kernel, (face_trace,), [vector((tile, tile), bf16)], after=(near,))
+    (order,) = call(order_kernel, (held_trace,), [vector((tile, tile), bf16)], after=(near,))
     sides = [vector((all_x - 2, depth, LANES))] * ny
     vol_y = call(side_edge_kernel, (held_source, inv), sides, after=(near,))
     vol_y = call(
@@ -718,7 +721,7 @@
             join_kernel, (traces, other), [vector(twice, bf16)], work=300, after=before
         )
     other = held(lax.ppermute(traces, "gz", both))
-    middle = 2 + (all_x - 4) * 3 // 5
+    middle = 2 + (all_x - 4) * 2 // 3
     (three,) = call(
         functools.partial(sweep_kernel, all_z, 2, middle), (ext_s, ext_i, two), [ext], work=1400,
         after=(traces,),

time: 47.7 us -> 47.7 us (level)
  local copies, waits for them, and re-layouts: 0.74 us -> 0.03 us
  starting transfers between devices: 19.4 us -> 19.9 us
    ppermute x3, starting transfers between devices: 5.76 us -> 6.62 us  [body(): lax.ppermute(traces, 'gx', [(i, i ^ step) for i in range(size_x)])]
    unnamed x10 -> x8, local copies, waits for them, and re-layouts: 0.74 us -> 0.03 us
    ppermute x1, waiting for transfers between devices: 0.31 us -> 0.81 us  [body(): sums = (rows[0], held(lax.ppermute(rows[1], 'gy', both)))]
  transfers between devices with their start and end apart: 13 -> 13, of which waited for: 5 -> 6; matrix products, arithmetic and copies ran while one was open for 0% -> 0% of each run, Pallas kernels for 33% -> 33%
where the time goes in v9:
time: 47.7 us; the launch traced here: 47.5 us
  Pallas kernels  20.3 us (43%)
  starting transfers between devices  19.9 us (42%)
  waiting for transfers between devices  5.8 us (12%)
  between operations  1.5 us (3%)
    pallas_call x20, Pallas kernels, call(): pl.pallas_call(body, out_shape=out_shape, in_specs=(in_specs or [VECTOR]...  20.3 us
    ppermute x5, starting transfers between devices, swap(): lax.ppermute(m, axis, p)  8.97 us
    ppermute x3, starting transfers between devices, body(): lax.ppermute(traces, 'gx', [(i, i ^ step) for i in range(size_x)])  6.62 us
    ppermute x1, waiting for transfers between devices, body(): other = held(lax.ppermute(near, 'gy', both))  3.09 us
    ppermute x1, starting transfers between devices, body(): other = held(lax.ppermute(near, 'gy', both))  3.03 us
    ppermute x3, waiting for transfers between devices, body(): lax.ppermute(traces, 'gx', [(i, i ^ step) for i in range(size_x)])  1.56 us
  transfers between devices with their start and end apart: 13, of which 6 were waited for; matrix products, arithmetic and copies ran while one was open for 0% of the time, Pallas kernels for 33%

profile of v9, /device:TPU:0, one launch (start us, length us, event | category | flops | bytes accessed | tf_op | source)
XLA Modules:
  0.0 47.5 jit_solution(10596021590001872011)
XLA Ops:
  0.6 1.9 %shard_map.95 = (f32[32,32,512]{2,1,0:T(8,128)S(1)}, s32[32,1,32]{2,1,0:T(1,128)S(1)}, f32[32,32,128]{2,1,0:T(8,128)S(1)}, f32[104,512]{1,0:T(8,128)S(1)}, f32[1...) custom-call(f32[32,32,512]{2,1,0:T(8,128)} %refs_0_.2, f32[32,16,32]{2,1,0:T(8,128)} %bitcast.7, s32[32,1,32]{2,1,0:T(1,128)} %refs_2_.1), custom_call_target="tpu_custom_call" | custom-call | bytes 3000000 | tf_op jit(solution)/shard_map/pallas_call | solution.py:58
  2.5 3.0 %collective-permute-start = (f32[104,512]{1,0:T(8,128)S(1)}, f32[104,512]{1,0:T(8,128)S(1)}, u32[]{:S(2)}, u32[]{:S(2)}) collective-permute-start(f32[104,512]{1,0:T(8,128)S(1)} %get-tuple-element.30.refs_0_.refs_1_.refs_2_), channel_id=1, source_target_pairs={{0,2},{2,0},{1,3},{3,1},{4,6},{6,4},{5,7},{7,5},{8,10},{10,8},{9,1... | collective-permute-start | bytes 638984 | tf_op jit(solution)/shard_map/ppermute | solution.py:647
  5.6 1.5 %collective-permute-start.6 = (f32[104,512]{1,0:T(8,128)S(1)}, f32[104,512]{1,0:T(8,128)S(1)}, u32[]{:S(2)}, u32[]{:S(2)}) collective-permute-start(f32[104,512]{1,0:T(8,128)S(1)} %get-tuple-element.39), channel_id=1, source_target_pairs={{0,4},{4,0},{8,12},{12,8},{16,20},{20,16},{24,28},{28,24},{1,5},{5... | collective-permute-start | bytes 638984 | tf_op jit(solution)/shard_map/ppermute | solution.py:82
  7.0 0.7 %collective-permute-start.7 = (f32[104,512]{1,0:T(8,128)S(1)}, f32[104,512]{1,0:T(8,128)S(1)}, u32[]{:S(2)}, u32[]{:S(2)}) collective-permute-start(f32[104,512]{1,0:T(8,128)S(1)} %get-tuple-element.40), channel_id=1, source_target_pairs={{4,8},{12,16},{20,24},{8,4},{16,12},{24,20},{5,9},{13,17},{21,25},... | collective-permute-start | bytes 638984 | tf_op jit(solution)/shard_map/ppermute | solution.py:82
  7.7 3.1 %collective-permute-done.refs_1_ = f32[104,512]{1,0:T(8,128)S(1)} collective-permute-done((f32[104,512]{1,0:T(8,128)S(1)}, f32[104,512]{1,0:T(8,128)S(1)}, u32[]{:S(2)}, u32[]{:S(2)}) %collective-permute-start) | collective-permute-done | bytes 213024 | tf_op jit(solution)/shard_map/ppermute | solution.py:647
  10.8 0.4 shard_map.96
  11.2 0.7 %collective-permute-start.2 = (f32[16,1024]{1,0:T(8,128)S(1)}, f32[16,1024]{1,0:T(8,128)S(1)}, u32[]{:S(2)}, u32[]{:S(2)}) collective-permute-start(f32[16,1024]{1,0:T(8,128)S(1)} %get-tuple-element.35), channel_id=1, source_target_pairs={{4,8},{12,16},{20,24},{8,4},{16,12},{24,20},{5,9},{13,17},{21,25},... | collective-permute-start | bytes 196616 | tf_op jit(solution)/shard_map/ppermute | solution.py:82
  11.9 4.6 %collective-permute-start.1 = (f32[8,1024]{1,0:T(8,128)S(1)}, f32[8,1024]{1,0:T(8,128)S(1)}, u32[]{:S(2)}, u32[]{:S(2)}) collective-permute-start(f32[8,1024]{1,0:T(8,128)S(1)} %get-tuple-element.34), channel_id=1, source_target_pairs={{0,4},{4,0},{8,12},{12,8},{16,20},{20,16},{24,28},{28,24},{1,5},{5... | collective-permute-start | bytes 98312 | tf_op jit(solution)/shard_map/ppermute | solution.py:82
  16.4 1.2 %shard_map.97.refs_2_.refs_0_.refs_3_ = bf16[1024,1024]{1,0:T(8,128)(2,1)S(1)} custom-call(s32[32,1,32]{2,1,0:T(1,128)S(1)} %get-tuple-element.33.refs_0_, f32[104,512]{1,0:T(8,128)S(1)} %get-tuple-element.30.refs_0_.refs_1_.refs_2_), custom_call_target="tpu_custom_call" | custom-call | bytes 3000000 | tf_op jit(solution)/shard_map/pallas_call | solution.py:58
  17.7 0.5 shard_map.103.refs_2_
  18.5 1.6 %collective-permute-start.8 = (f32[36,32,128]{2,1,0:T(8,128)S(1)}, f32[36,32,128]{2,1,0:T(8,128)S(1)}, u32[]{:S(2)}, u32[]{:S(2)}) collective-permute-start(f32[36,32,128]{2,1,0:T(8,128)S(1)} %shard_map.104), channel_id=1, source_target_pairs={{0,2},{2,0},{1,3},{3,1},{4,6},{6,4},{5,7},{7,5},{8,10},{10,8},{9,1... | collective-permute-start | bytes 1769480 | tf_op jit(solution)/shard_map/ppermute | solution.py:82
  20.1 0.9 %shard_map.98.refs_2_.refs_0_ = bf16[1,32,1024]{2,1,0:T(8,128)(2,1)S(1)} custom-call(f32[3,32,1024]{2,1,0:T(8,128)S(1)} %get-tuple-element.31.refs_0_, f32[3,32,1024]{2,1,0:T(8,128)S(1)} %get-tuple-element.32.refs_1_, bf16[1024,1024]{1,0:T(8,128)(2,1)S(1)} %shard_map.97.refs_2_.refs_0_.refs_3_, f32[8,1024]{1,0:T(8,128)S(1)} %collective-permute-done.1.refs_3_.refs_4_, ...), custom_call_target="tpu_custom_call" | custom-call | bytes 3000000 | tf_op jit(solution)/shard_map/pallas_call | solution.py:58
  21.0 3.1 %collective-permute-start.3 = (bf16[1,32,1024]{2,1,0:T(8,128)(2,1)S(1)}, bf16[1,32,1024]{2,1,0:T(8,128)(2,1)S(1)}, u32[]{:S(2)}, u32[]{:S(2)}) collective-permute-start(bf16[1,32,1024]{2,1,0:T(8,128)(2,1)S(1)} %shard_map.98.refs_2_.refs_0_), channel_id=1, source_target_pairs={{0,16},{4,20},{8,24},{12,28},{16,0},{20,4},{24,8},{28,12},{1,17},{... | collective-permute-start | bytes 196616 | tf_op jit(solution)/shard_map/ppermute | solution.py:674
  24.8 0.6 %shard_map.99.refs_2_.refs_0_ = s32[8]{0:T(128)S(4)} custom-call(s32[1,1,1]{2,1,0:T(1,128)S(6)} %copy.22.refs_0_, s32[1,1,1,7]{3,2,1,0:T(1,128)S(1)} %copy-done.3, bf16[1,32,1024]{2,1,0:T(8,128)(2,1)S(1)} %shard_map.98.refs_2_.refs_0_), custom_call_target="tpu_custom_call" | custom-call | bytes 3000000 | tf_op jit(solution)/shard_map/pallas_call | solution.py:58
  25.4 1.2 %collective-permute-done.3.refs_1_ = bf16[1,32,1024]{2,1,0:T(8,128)(2,1)S(1)} collective-permute-done((bf16[1,32,1024]{2,1,0:T(8,128)(2,1)S(1)}, bf16[1,32,1024]{2,1,0:T(8,128)(2,1)S(1)}, u32[]{:S(2)}, u32[]{:S(2)}) %collective-permute-start.3) | collective-permute-done | bytes 65568 | tf_op jit(solution)/shard_map/ppermute | solution.py:674
  26.6 1.7 %collective-permute-start.4 = (bf16[2,32,1024]{2,1,0:T(8,128)(2,1)S(1)}, bf16[2,32,1024]{2,1,0:T(8,128)(2,1)S(1)}, u32[]{:S(2)}, u32[]{:S(2)}) collective-permute-start(bf16[2,32,1024]{2,1,0:T(8,128)(2,1)S(1)} %shard_map.100.refs_3_.refs_0_), channel_id=1, source_target_pairs={{0,8},{4,12},{8,0},{12,4},{16,24},{20,28},{24,16},{28,20},{1,9},{5... | collective-permute-start | bytes 393224 | tf_op jit(solution)/shard_map/ppermute | solution.py:674
  28.4 2.9 %shard_map.101 = (bf16[1024,1024]{1,0:T(8,128)(2,1)S(1)}, bf16[112,1024]{1,0:T(8,128)(2,1)S(1)}) custom-call(bf16[1024,1024]{1,0:T(8,128)(2,1)S(1)} %shard_map.97.refs_2_.refs_0_.refs_3_, bf16[1024,1024]{1,0:T(8,128)(2,1)S(1)} %bitcast.4, bf16[112,1024]{1,0:T(8,128)(2,1)S(1)} %bitcast.5, bf16[2,32,1024]{2,1,0:T(8,128)(2,1)S(1)} %shard_map.100.refs_3_.refs_0_), custom_call_target="tpu_custom_call" | custom-call | bytes 9000000 | tf_op jit(solution)/shard_map/pallas_call | solution.py:58
  31.3 0.4 collective-permute-done.4.refs_1_
  31.7 1.8 %collective-permute-start.5 = (bf16[4,32,1024]{2,1,0:T(8,128)(2,1)S(1)}, bf16[4,32,1024]{2,1,0:T(8,128)(2,1)S(1)}, u32[]{:S(2)}, u32[]{:S(2)}) collective-permute-start(bf16[4,32,1024]{2,1,0:T(8,128)(2,1)S(1)} %shard_map.102.refs_5_.refs_0_), channel_id=1, source_target_pairs={{0,4},{4,0},{8,12},{12,8},{16,20},{20,16},{24,28},{28,24},{1,5},{5... | collective-permute-start | bytes 786440 | tf_op jit(solution)/shard_map/ppermute | solution.py:674
  33.5 0.3 shard_map.105
  33.8 0.5 %collective-permute-start.10 = (f32[40,768]{1,0:T(8,128)S(1)}, f32[40,768]{1,0:T(8,128)S(1)}, u32[]{:S(2)}, u32[]{:S(2)}) collective-permute-start(f32[40,768]{1,0:T(8,128)S(1)} %get-tuple-element.42.refs_6_), channel_id=1, source_target_pairs={{0,1},{1,0},{2,3},{3,2},{4,5},{5,4},{6,7},{7,6},{8,9},{9,8},{10,11... | collective-permute-start | bytes 368648 | tf_op jit(solution)/shard_map/ppermute | solution.py:699
  34.3 1.2 %shard_map.106 = (f32[1520,640]{1,0:T(8,128)S(1)}, f32[1520,640]{1,0:T(8,128)S(1)}, f32[1520,640]{1,0:T(8,128)S(1)}) custom-call(f32[32,32,512]{2,1,0:T(8,128)S(1)} %get-tuple-element.37.refs_0_, f32[32,32,128]{2,1,0:T(8,128)S(1)} %get-tuple-element.38.refs_1_, f32[104,512]{1,0:T(8,128)S(1)} %collective-permute-done.6.refs_0_.refs_2_, ...), custom_call_target="tpu_custom_call" | custom-call | bytes 3000000 | tf_op jit(solution)/shard_map/pallas_call | solution.py:58
  35.6 0.6 %shard_map.107 = (f32[1520,640]{1,0:T(8,128)S(1)}, f32[1520,640]{1,0:T(8,128)S(1)}, f32[1520,640]{1,0:T(8,128)S(1)}) custom-call(f32[2,40,640]{2,1,0:T(8,128)S(1)} %collective-permute-done.9.refs_0_, f32[40,768]{1,0:T(8,128)S(1)} %collective-permute-done.10.refs_1_, ...), custom_call_target="tpu_custom_call", output_to_operand_aliasing={{0}: (2, {}), {1}: (3, {}), {2}: (4, {})} | custom-call | bytes 3000000 | tf_op jit(solution)/shard_map/pallas_call | solution.py:58
  36.2 2.7 %shard_map.108.refs_2_ = f32[1520,640]{1,0:T(8,128)S(1)} custom-call(f32[1520,640]{1,0:T(8,128)S(1)} %get-tuple-element.46.refs_0_, f32[1520,640]{1,0:T(8,128)S(1)} %get-tuple-element.47.refs_1_, f32[1520,640]{1,0:T(8,128)S(1)} %get-tuple-element.48.refs_2_), custom_call_target="tpu_custom_call" | custom-call | bytes 7500000 | tf_op jit(solution)/shard_map/pallas_call | solution.py:58
  39.1 1.6 %shard_map.110.refs_6_.refs_3_ = f32[1520,640]{1,0:T(8,128)S(1)} custom-call(f32[1520,640]{1,0:T(8,128)S(1)} %get-tuple-element.46.refs_0_, f32[1520,640]{1,0:T(8,128)S(1)} %get-tuple-element.47.refs_1_, f32[1520,640]{1,0:T(8,128)S(1)} %shard_map.108.refs_2_, bf16[8,32,1024]{2,1,0:T(8,128)(2,1)S(1)} %shard_map.109.refs_3_.refs_1_), custom_call_target="tpu_custom_call" | custom-call | bytes 4200000 | tf_op jit(solution)/shard_map/pallas_call | solution.py:58
  40.7 0.2 collective-permute-done.11.refs_2_
  40.9 1.1 %shard_map.111 = (f32[32,512]{1,0:T(8,128)S(1)}, f32[32,512]{1,0:T(8,128)S(1)}) custom-call(s32[8]{0:T(128)S(4)} %shard_map.99.refs_2_.refs_0_, bf16[8,32,1024]{2,1,0:T(8,128)(2,1)S(1)} %shard_map.109.refs_3_.refs_1_, bf16[8,32,1024]{2,1,0:T(8,128)(2,1)S(1)} %collective-permute-done.11.refs_2_, bf16[1024,1024]{1,0:T(8,128)(2,1)S(1)} %get-tuple-element.36.refs_2_.refs_3_, ...), custom_call_target="tpu_custom_call" | custom-call | bytes 7500000 | tf_op jit(solution)/shard_map/pallas_call | solution.py:58
  42.0 0.6 %collective-permute-start.12 = (f32[32,512]{1,0:T(8,128)S(1)}, f32[32,512]{1,0:T(8,128)S(1)}, u32[]{:S(2)}, u32[]{:S(2)}) collective-permute-start(f32[32,512]{1,0:T(8,128)S(1)} %get-tuple-element.51.refs_5_), channel_id=1, source_target_pairs={{0,2},{2,0},{1,3},{3,1},{4,6},{6,4},{5,7},{7,5},{8,10},{10,8},{9,1... | collective-permute-start | bytes 196616 | tf_op jit(solution)/shard_map/ppermute | solution.py:737
  42.6 0.9 %shard_map.112.refs_2_ = f32[1520,640]{1,0:T(8,128)S(1)} custom-call(f32[1520,640]{1,0:T(8,128)S(1)} %get-tuple-element.46.refs_0_, f32[1520,640]{1,0:T(8,128)S(1)} %get-tuple-element.47.refs_1_, f32[1520,640]{1,0:T(8,128)S(1)} %shard_map.108.refs_2_, f32[1520,640]{1,0:T(8,128)S(1)} %shard_map.110.refs_6_.refs_3_, ...), custom_call_target="tpu_custom_call", output_to_operand_aliasing={{}: (3, {})} | custom-call | bytes 4200000 | tf_op jit(solution)/shard_map/pallas_call | solution.py:58
  43.5 2.0 %shard_map.113 = (f32[32,32,512]{2,1,0:T(8,128)}, f32[32,8,512]{2,1,0:T(8,128)S(1)}, f32[8,32,512]{2,1,0:T(8,128)S(1)}) custom-call(f32[1520,640]{1,0:T(8,128)S(1)} %get-tuple-element.46.refs_0_, f32[1520,640]{1,0:T(8,128)S(1)} %get-tuple-element.47.refs_1_, f32[1520,640]{1,0:T(8,128)S(1)} %shard_map.112.refs_2_), custom_call_target="tpu_custom_call" | custom-call | bytes 6000000 | tf_op jit(solution)/shard_map/pallas_call | solution.py:58
  45.5 0.8 %collective-permute-done.12.refs_1_ = f32[32,512]{1,0:T(8,128)S(1)} collective-permute-done((f32[32,512]{1,0:T(8,128)S(1)}, f32[32,512]{1,0:T(8,128)S(1)}, u32[]{:S(2)}, u32[]{:S(2)}) %collective-permute-start.12) | collective-permute-done | bytes 65568 | tf_op jit(solution)/shard_map/ppermute | solution.py:737
  46.3 1.2 %shard_map.114 = (f32[32,1,512]{2,1,0:T(1,128)}, f32[32,32,512]{2,1,0:T(8,128)}) custom-call(f32[32,512]{1,0:T(8,128)S(1)} %get-tuple-element.50.refs_4_.refs_0_, f32[32,512]{1,0:T(8,128)S(1)} %collective-permute-done.12.refs_1_, f32[32,512]{1,0:T(8,128)S(1)} %get-tuple-element.52.refs_2_, ...), custom_call_target="tpu_custom_call", output_to_operand_aliasing={{1}: (5, {})} | custom-call | bytes 3000000 | tf_op jit(solution)/shard_map/pallas_call | solution.py:58
  (22 shorter events, 0.6 us)
Async XLA Ops:
  2.5 8.3 %collective-permute-start = (f32[104,512]{1,0:T(8,128)S(1)}, f32[104,512]{1,0:T(8,128)S(1)}, u32[]{:S(2)}, u32[]{:S(2)}) collective-permute-start(f32[104,512]{1,0:T(8,128)S(1)} %get-tuple-element.30.refs_0_.refs_1_.refs_2_), channel_id=1, source_target_pairs={{0,2},{2,0},{1,3},{3,1},{4,6},{6,4},{5,7},{7,5},{8,10},{10,8},{9,1... | collective-permute-start | bytes 638984 | tf_op jit(solution)/shard_map/ppermute | solution.py:647
  5.6 12.6 %collective-permute-start.6 = (f32[104,512]{1,0:T(8,128)S(1)}, f32[104,512]{1,0:T(8,128)S(1)}, u32[]{:S(2)}, u32[]{:S(2)}) collective-permute-start(f32[104,512]{1,0:T(8,128)S(1)} %get-tuple-element.39), channel_id=1, source_target_pairs={{0,4},{4,0},{8,12},{12,8},{16,20},{20,16},{24,28},{28,24},{1,5},{5... | collective-permute-start | bytes 638984 | tf_op jit(solution)/shard_map/ppermute | solution.py:82
  7.0 11.1 %collective-permute-start.7 = (f32[104,512]{1,0:T(8,128)S(1)}, f32[104,512]{1,0:T(8,128)S(1)}, u32[]{:S(2)}, u32[]{:S(2)}) collective-permute-start(f32[104,512]{1,0:T(8,128)S(1)} %get-tuple-element.40), channel_id=1, source_target_pairs={{4,8},{12,16},{20,24},{8,4},{16,12},{24,20},{5,9},{13,17},{21,25},... | collective-permute-start | bytes 638984 | tf_op jit(solution)/shard_map/ppermute | solution.py:82
  11.2 7.1 %collective-permute-start.2 = (f32[16,1024]{1,0:T(8,128)S(1)}, f32[16,1024]{1,0:T(8,128)S(1)}, u32[]{:S(2)}, u32[]{:S(2)}) collective-permute-start(f32[16,1024]{1,0:T(8,128)S(1)} %get-tuple-element.35), channel_id=1, source_target_pairs={{4,8},{12,16},{20,24},{8,4},{16,12},{24,20},{5,9},{13,17},{21,25},... | collective-permute-start | bytes 196616 | tf_op jit(solution)/shard_map/ppermute | solution.py:82
  11.9 6.5 %collective-permute-start.1 = (f32[8,1024]{1,0:T(8,128)S(1)}, f32[8,1024]{1,0:T(8,128)S(1)}, u32[]{:S(2)}, u32[]{:S(2)}) collective-permute-start(f32[8,1024]{1,0:T(8,128)S(1)} %get-tuple-element.34), channel_id=1, source_target_pairs={{0,4},{4,0},{8,12},{12,8},{16,20},{20,16},{24,28},{28,24},{1,5},{5... | collective-permute-start | bytes 98312 | tf_op jit(solution)/shard_map/ppermute | solution.py:82
  18.1 6.6 %copy-start.3 = (s32[1,1,1,7]{3,2,1,0:T(1,128)S(1)}, s32[1,1,1,7]{3,2,1,0:T(1,128)}, u32[]{:S(2)}) copy-start(s32[1,1,1,7]{3,2,1,0:T(1,128)} %refs_1_.1) | copy-start | bytes 88
  18.2 10.2 %copy-start = (bf16[1,1,1,1024,1024]{4,3,2,1,0:T(8,128)(2,1)S(1)}, bf16[1,1,1,1024,1024]{4,3,2,1,0:T(8,128)(2,1)}, u32[]{:S(2)}) copy-start(bf16[1,1,1,1024,1024]{4,3,2,1,0:T(8,128)(2,1)} %param.13) | copy-start | bytes 6291460
  18.2 10.2 %copy-start.1 = (bf16[1,1,1,7,16,1024]{5,4,3,2,1,0:T(8,128)(2,1)S(1)}, bf16[1,1,1,7,16,1024]{5,4,3,2,1,0:T(8,128)(2,1)}, u32[]{:S(2)}) copy-start(bf16[1,1,1,7,16,1024]{5,4,3,2,1,0:T(8,128)(2,1)} %param.14) | copy-start | bytes 688132
  18.5 14.9 %collective-permute-start.8 = (f32[36,32,128]{2,1,0:T(8,128)S(1)}, f32[36,32,128]{2,1,0:T(8,128)S(1)}, u32[]{:S(2)}, u32[]{:S(2)}) collective-permute-start(f32[36,32,128]{2,1,0:T(8,128)S(1)} %shard_map.104), channel_id=1, source_target_pairs={{0,2},{2,0},{1,3},{3,1},{4,6},{6,4},{5,7},{7,5},{8,10},{10,8},{9,1... | collective-permute-start | bytes 1769480 | tf_op jit(solution)/shard_map/ppermute | solution.py:82
  21.0 5.6 %collective-permute-start.3 = (bf16[1,32,1024]{2,1,0:T(8,128)(2,1)S(1)}, bf16[1,32,1024]{2,1,0:T(8,128)(2,1)S(1)}, u32[]{:S(2)}, u32[]{:S(2)}) collective-permute-start(bf16[1,32,1024]{2,1,0:T(8,128)(2,1)S(1)} %shard_map.98.refs_2_.refs_0_), channel_id=1, source_target_pairs={{0,16},{4,20},{8,24},{12,28},{16,0},{20,4},{24,8},{28,12},{1,17},{... | collective-permute-start | bytes 196616 | tf_op jit(solution)/shard_map/ppermute | solution.py:674
  26.6 5.0 %collective-permute-start.4 = (bf16[2,32,1024]{2,1,0:T(8,128)(2,1)S(1)}, bf16[2,32,1024]{2,1,0:T(8,128)(2,1)S(1)}, u32[]{:S(2)}, u32[]{:S(2)}) collective-permute-start(bf16[2,32,1024]{2,1,0:T(8,128)(2,1)S(1)} %shard_map.100.refs_3_.refs_0_), channel_id=1, source_target_pairs={{0,8},{4,12},{8,0},{12,4},{16,24},{20,28},{24,16},{28,20},{1,9},{5... | collective-permute-start | bytes 393224 | tf_op jit(solution)/shard_map/ppermute | solution.py:674
  31.7 7.2 %collective-permute-start.5 = (bf16[4,32,1024]{2,1,0:T(8,128)(2,1)S(1)}, bf16[4,32,1024]{2,1,0:T(8,128)(2,1)S(1)}, u32[]{:S(2)}, u32[]{:S(2)}) collective-permute-start(bf16[4,32,1024]{2,1,0:T(8,128)(2,1)S(1)} %shard_map.102.refs_5_.refs_0_), channel_id=1, source_target_pairs={{0,4},{4,0},{8,12},{12,8},{16,20},{20,16},{24,28},{28,24},{1,5},{5... | collective-permute-start | bytes 786440 | tf_op jit(solution)/shard_map/ppermute | solution.py:674
  33.8 1.8 %collective-permute-start.9 = (f32[2,40,640]{2,1,0:T(8,128)S(1)}, f32[2,40,640]{2,1,0:T(8,128)S(1)}, u32[]{:S(2)}, u32[]{:S(2)}) collective-permute-start(f32[2,40,640]{2,1,0:T(8,128)S(1)} %get-tuple-element.41.refs_5_), channel_id=1, source_target_pairs={{0,1},{1,0},{2,3},{3,2},{4,5},{5,4},{6,7},{7,6},{8,9},{9,8},{10,11... | collective-permute-start | bytes 614408 | tf_op jit(solution)/shard_map/ppermute | solution.py:699
  33.8 1.7 %collective-permute-start.10 = (f32[40,768]{1,0:T(8,128)S(1)}, f32[40,768]{1,0:T(8,128)S(1)}, u32[]{:S(2)}, u32[]{:S(2)}) collective-permute-start(f32[40,768]{1,0:T(8,128)S(1)} %get-tuple-element.42.refs_6_), channel_id=1, source_target_pairs={{0,1},{1,0},{2,3},{3,2},{4,5},{5,4},{6,7},{7,6},{8,9},{9,8},{10,11... | collective-permute-start | bytes 368648 | tf_op jit(solution)/shard_map/ppermute | solution.py:699
  38.9 2.0 %copy-start.2 = (bf16[1,1,1,7,16,1024]{5,4,3,2,1,0:T(8,128)(2,1)S(1)}, bf16[1,1,1,7,16,1024]{5,4,3,2,1,0:T(8,128)(2,1)}, u32[]{:S(2)}) copy-start(bf16[1,1,1,7,16,1024]{5,4,3,2,1,0:T(8,128)(2,1)} %param.15) | copy-start | bytes 688132
  38.9 2.0 %collective-permute-start.11 = (bf16[8,32,1024]{2,1,0:T(8,128)(2,1)S(1)}, bf16[8,32,1024]{2,1,0:T(8,128)(2,1)S(1)}, u32[]{:S(2)}, u32[]{:S(2)}) collective-permute-start(bf16[8,32,1024]{2,1,0:T(8,128)(2,1)S(1)} %shard_map.109.refs_3_.refs_1_), channel_id=1, source_target_pairs={{0,1},{1,0},{2,3},{3,2},{4,5},{5,4},{6,7},{7,6},{8,9},{9,8},{10,11... | collective-permute-start | bytes 1572872 | tf_op jit(solution)/shard_map/ppermute | solution.py:723
  42.0 4.3 %collective-permute-start.12 = (f32[32,512]{1,0:T(8,128)S(1)}, f32[32,512]{1,0:T(8,128)S(1)}, u32[]{:S(2)}, u32[]{:S(2)}) collective-permute-start(f32[32,512]{1,0:T(8,128)S(1)} %get-tuple-element.51.refs_5_), channel_id=1, source_target_pairs={{0,2},{2,0},{1,3},{3,1},{4,6},{6,4},{5,7},{7,5},{8,10},{10,8},{9,1... | collective-permute-start | bytes 196616 | tf_op jit(solution)/shard_map/ppermute | solution.py:737

commit v10 on v9

--- a/solution.py
+++ b/solution.py
@@ -652,7 +652,7 @@
     s_face, i_face, i_own, *face_x = call(
         functools.partial(face_side_kernel, groups), (near, other),
         [full, full, vector((rows_x, width))]
-        + [vector(((1 + n) * ROWS, width * groups)) for n in range(nx)], work=500,
+        + [vector((ROWS, width * groups))] * nx, work=500,
     )
     got_x = swap(face_x, "gx")
     (order,) = call(order_kernel, (held_trace,), [vector((tile, tile), bf16)], after=(near,))

time: 47.7 us -> 47.7 us (level)
  waiting for transfers between devices: 5.8 us -> 7.35 us
  starting transfers between devices: 19.9 us -> 18.4 us
    ppermute x5, starting transfers between devices: 8.97 us -> 5.18 us  [swap(): lax.ppermute(m, axis, p)]
    ppermute x3, starting transfers between devices: 6.62 us -> 9.01 us  [body(): lax.ppermute(traces, 'gx', [(i, i ^ step) for i in range(size_x)])]
    ppermute x5, waiting for transfers between devices: 0.13 us -> 1.52 us  [swap(): lax.ppermute(m, axis, p)]
  transfers between devices with their start and end apart: 13 -> 13, of which waited for: 6 -> 8; matrix products, arithmetic and copies ran while one was open for 0% -> 0% of each run, Pallas kernels for 33% -> 33%
where the time goes in v10:
time: 47.7 us; the launch traced here: 47.5 us
  Pallas kernels  20.3 us (43%)
  starting transfers between devices  18.4 us (39%)
  waiting for transfers between devices  7.35 us (15%)
  between operations  1.48 us (3%)
    pallas_call x20, Pallas kernels, call(): pl.pallas_call(body, out_shape=out_shape, in_specs=(in_specs or [VECTOR]...  20.3 us
    ppermute x3, starting transfers between devices, body(): lax.ppermute(traces, 'gx', [(i, i ^ step) for i in range(size_x)])  9.01 us
    ppermute x5, starting transfers between devices, swap(): lax.ppermute(m, axis, p)  5.18 us
    ppermute x1, waiting for transfers between devices, body(): other = held(lax.ppermute(near, 'gy', both))  3.09 us
    ppermute x1, starting transfers between devices, body(): other = held(lax.ppermute(near, 'gy', both))  3.03 us
    ppermute x3, waiting for transfers between devices, body(): lax.ppermute(traces, 'gx', [(i, i ^ step) for i in range(size_x)])  1.61 us
    ppermute x5, waiting for transfers between devices, swap(): lax.ppermute(m, axis, p)  1.52 us
  transfers between devices with their start and end apart: 13, of which 8 were waited for; matrix products, arithmetic and copies ran while one was open for 0% of the time, Pallas kernels for 33%

profile of v10, /device:TPU:0, one launch (start us, length us, event | category | flops | bytes accessed | tf_op | source)
XLA Modules:
  0.0 47.5 jit_solution(1570264272737680571)
XLA Ops:
  0.6 1.9 %shard_map.95 = (f32[32,32,512]{2,1,0:T(8,128)S(1)}, s32[32,1,32]{2,1,0:T(1,128)S(1)}, f32[32,32,128]{2,1,0:T(8,128)S(1)}, f32[104,512]{1,0:T(8,128)S(1)}, f32[1...) custom-call(f32[32,32,512]{2,1,0:T(8,128)} %refs_0_.2, f32[32,16,32]{2,1,0:T(8,128)} %bitcast.7, s32[32,1,32]{2,1,0:T(1,128)} %refs_2_.1), custom_call_target="tpu_custom_call" | custom-call | bytes 3000000 | tf_op jit(solution)/shard_map/pallas_call | solution.py:58
  2.5 3.0 %collective-permute-start = (f32[104,512]{1,0:T(8,128)S(1)}, f32[104,512]{1,0:T(8,128)S(1)}, u32[]{:S(2)}, u32[]{:S(2)}) collective-permute-start(f32[104,512]{1,0:T(8,128)S(1)} %get-tuple-element.30.refs_0_.refs_1_.refs_2_), channel_id=1, source_target_pairs={{0,2},{2,0},{1,3},{3,1},{4,6},{6,4},{5,7},{7,5},{8,10},{10,8},{9,1... | collective-permute-start | bytes 638984 | tf_op jit(solution)/shard_map/ppermute | solution.py:647
  5.6 1.5 %collective-permute-start.6 = (f32[104,512]{1,0:T(8,128)S(1)}, f32[104,512]{1,0:T(8,128)S(1)}, u32[]{:S(2)}, u32[]{:S(2)}) collective-permute-start(f32[104,512]{1,0:T(8,128)S(1)} %get-tuple-element.39), channel_id=1, source_target_pairs={{0,4},{4,0},{8,12},{12,8},{16,20},{20,16},{24,28},{28,24},{1,5},{5... | collective-permute-start | bytes 638984 | tf_op jit(solution)/shard_map/ppermute | solution.py:82
  7.0 0.7 %collective-permute-start.7 = (f32[104,512]{1,0:T(8,128)S(1)}, f32[104,512]{1,0:T(8,128)S(1)}, u32[]{:S(2)}, u32[]{:S(2)}) collective-permute-start(f32[104,512]{1,0:T(8,128)S(1)} %get-tuple-element.40), channel_id=1, source_target_pairs={{4,8},{12,16},{20,24},{8,4},{16,12},{24,20},{5,9},{13,17},{21,25},... | collective-permute-start | bytes 638984 | tf_op jit(solution)/shard_map/ppermute | solution.py:82
  7.7 3.1 %collective-permute-done.refs_1_ = f32[104,512]{1,0:T(8,128)S(1)} collective-permute-done((f32[104,512]{1,0:T(8,128)S(1)}, f32[104,512]{1,0:T(8,128)S(1)}, u32[]{:S(2)}, u32[]{:S(2)}) %collective-permute-start) | collective-permute-done | bytes 213024 | tf_op jit(solution)/shard_map/ppermute | solution.py:647
  10.8 0.4 shard_map.96
  11.2 1.8 %collective-permute-start.1 = (f32[8,1024]{1,0:T(8,128)S(1)}, f32[8,1024]{1,0:T(8,128)S(1)}, u32[]{:S(2)}, u32[]{:S(2)}) collective-permute-start(f32[8,1024]{1,0:T(8,128)S(1)} %get-tuple-element.34), channel_id=1, source_target_pairs={{0,4},{4,0},{8,12},{12,8},{16,20},{20,16},{24,28},{28,24},{1,5},{5... | collective-permute-start | bytes 98312 | tf_op jit(solution)/shard_map/ppermute | solution.py:82
  13.0 0.7 %collective-permute-start.2 = (f32[8,1024]{1,0:T(8,128)S(1)}, f32[8,1024]{1,0:T(8,128)S(1)}, u32[]{:S(2)}, u32[]{:S(2)}) collective-permute-start(f32[8,1024]{1,0:T(8,128)S(1)} %get-tuple-element.35), channel_id=1, source_target_pairs={{4,8},{12,16},{20,24},{8,4},{16,12},{24,20},{5,9},{13,17},{21,25},... | collective-permute-start | bytes 98312 | tf_op jit(solution)/shard_map/ppermute | solution.py:82
  13.6 1.2 %shard_map.97.refs_2_.refs_0_.refs_3_ = bf16[1024,1024]{1,0:T(8,128)(2,1)S(1)} custom-call(s32[32,1,32]{2,1,0:T(1,128)S(1)} %get-tuple-element.33.refs_0_, f32[104,512]{1,0:T(8,128)S(1)} %get-tuple-element.30.refs_0_.refs_1_.refs_2_), custom_call_target="tpu_custom_call" | custom-call | bytes 3000000 | tf_op jit(solution)/shard_map/pallas_call | solution.py:58
  14.9 0.5 shard_map.103.refs_2_
  15.4 1.2 %collective-permute-done.6.refs_0_.refs_2_ = f32[104,512]{1,0:T(8,128)S(1)} collective-permute-done((f32[104,512]{1,0:T(8,128)S(1)}, f32[104,512]{1,0:T(8,128)S(1)}, u32[]{:S(2)}, u32[]{:S(2)}) %collective-permute-start.6) | collective-permute-done | bytes 213024 | tf_op jit(solution)/shard_map/ppermute | solution.py:82
  16.5 0.3 collective-permute-done.1.refs_3_.refs_4_
  17.1 0.6 %collective-permute-start.8 = (f32[36,32,128]{2,1,0:T(8,128)S(1)}, f32[36,32,128]{2,1,0:T(8,128)S(1)}, u32[]{:S(2)}, u32[]{:S(2)}) collective-permute-start(f32[36,32,128]{2,1,0:T(8,128)S(1)} %shard_map.104), channel_id=1, source_target_pairs={{0,2},{2,0},{1,3},{3,1},{4,6},{6,4},{5,7},{7,5},{8,10},{10,8},{9,1... | collective-permute-start | bytes 1769480 | tf_op jit(solution)/shard_map/ppermute | solution.py:82
  17.7 0.9 %shard_map.98.refs_2_.refs_0_ = bf16[1,32,1024]{2,1,0:T(8,128)(2,1)S(1)} custom-call(f32[3,32,1024]{2,1,0:T(8,128)S(1)} %get-tuple-element.31.refs_0_, f32[3,32,1024]{2,1,0:T(8,128)S(1)} %get-tuple-element.32.refs_1_, bf16[1024,1024]{1,0:T(8,128)(2,1)S(1)} %shard_map.97.refs_2_.refs_0_.refs_3_, f32[8,1024]{1,0:T(8,128)S(1)} %collective-permute-done.1.refs_3_.refs_4_, ...), custom_call_target="tpu_custom_call" | custom-call | bytes 3000000 | tf_op jit(solution)/shard_map/pallas_call | solution.py:58
  18.6 6.3 %collective-permute-start.3 = (bf16[1,32,1024]{2,1,0:T(8,128)(2,1)S(1)}, bf16[1,32,1024]{2,1,0:T(8,128)(2,1)S(1)}, u32[]{:S(2)}, u32[]{:S(2)}) collective-permute-start(bf16[1,32,1024]{2,1,0:T(8,128)(2,1)S(1)} %shard_map.98.refs_2_.refs_0_), channel_id=1, source_target_pairs={{0,16},{4,20},{8,24},{12,28},{16,0},{20,4},{24,8},{28,12},{1,17},{... | collective-permute-start | bytes 196616 | tf_op jit(solution)/shard_map/ppermute | solution.py:674
  25.6 0.6 %shard_map.99.refs_2_.refs_0_ = s32[8]{0:T(128)S(4)} custom-call(s32[1,1,1]{2,1,0:T(1,128)S(6)} %copy.22.refs_0_, s32[1,1,1,7]{3,2,1,0:T(1,128)S(1)} %copy-done.3, bf16[1,32,1024]{2,1,0:T(8,128)(2,1)S(1)} %shard_map.98.refs_2_.refs_0_), custom_call_target="tpu_custom_call" | custom-call | bytes 3000000 | tf_op jit(solution)/shard_map/pallas_call | solution.py:58
  26.3 1.1 %collective-permute-done.3.refs_1_ = bf16[1,32,1024]{2,1,0:T(8,128)(2,1)S(1)} collective-permute-done((bf16[1,32,1024]{2,1,0:T(8,128)(2,1)S(1)}, bf16[1,32,1024]{2,1,0:T(8,128)(2,1)S(1)}, u32[]{:S(2)}, u32[]{:S(2)}) %collective-permute-start.3) | collective-permute-done | bytes 65568 | tf_op jit(solution)/shard_map/ppermute | solution.py:674
  27.4 1.8 %collective-permute-start.4 = (bf16[2,32,1024]{2,1,0:T(8,128)(2,1)S(1)}, bf16[2,32,1024]{2,1,0:T(8,128)(2,1)S(1)}, u32[]{:S(2)}, u32[]{:S(2)}) collective-permute-start(bf16[2,32,1024]{2,1,0:T(8,128)(2,1)S(1)} %shard_map.100.refs_3_.refs_0_), channel_id=1, source_target_pairs={{0,8},{4,12},{8,0},{12,4},{16,24},{20,28},{24,16},{28,20},{1,9},{5... | collective-permute-start | bytes 393224 | tf_op jit(solution)/shard_map/ppermute | solution.py:674
  29.2 2.9 %shard_map.101 = (bf16[1024,1024]{1,0:T(8,128)(2,1)S(1)}, bf16[112,1024]{1,0:T(8,128)(2,1)S(1)}) custom-call(bf16[1024,1024]{1,0:T(8,128)(2,1)S(1)} %shard_map.97.refs_2_.refs_0_.refs_3_, bf16[1024,1024]{1,0:T(8,128)(2,1)S(1)} %bitcast.4, bf16[112,1024]{1,0:T(8,128)(2,1)S(1)} %bitcast.5, bf16[2,32,1024]{2,1,0:T(8,128)(2,1)S(1)} %shard_map.100.refs_3_.refs_0_), custom_call_target="tpu_custom_call" | custom-call | bytes 9000000 | tf_op jit(solution)/shard_map/pallas_call | solution.py:58
  32.4 0.9 %collective-permute-start.5 = (bf16[4,32,1024]{2,1,0:T(8,128)(2,1)S(1)}, bf16[4,32,1024]{2,1,0:T(8,128)(2,1)S(1)}, u32[]{:S(2)}, u32[]{:S(2)}) collective-permute-start(bf16[4,32,1024]{2,1,0:T(8,128)(2,1)S(1)} %shard_map.102.refs_5_.refs_0_), channel_id=1, source_target_pairs={{0,4},{4,0},{8,12},{12,8},{16,20},{20,16},{24,28},{28,24},{1,5},{5... | collective-permute-start | bytes 786440 | tf_op jit(solution)/shard_map/ppermute | solution.py:674
  33.3 0.3 shard_map.105
  33.7 0.5 %collective-permute-start.10 = (f32[40,768]{1,0:T(8,128)S(1)}, f32[40,768]{1,0:T(8,128)S(1)}, u32[]{:S(2)}, u32[]{:S(2)}) collective-permute-start(f32[40,768]{1,0:T(8,128)S(1)} %get-tuple-element.42.refs_6_), channel_id=1, source_target_pairs={{0,1},{1,0},{2,3},{3,2},{4,5},{5,4},{6,7},{7,6},{8,9},{9,8},{10,11... | collective-permute-start | bytes 368648 | tf_op jit(solution)/shard_map/ppermute | solution.py:699
  34.2 1.2 %shard_map.106 = (f32[1520,640]{1,0:T(8,128)S(1)}, f32[1520,640]{1,0:T(8,128)S(1)}, f32[1520,640]{1,0:T(8,128)S(1)}) custom-call(f32[32,32,512]{2,1,0:T(8,128)S(1)} %get-tuple-element.37.refs_0_, f32[32,32,128]{2,1,0:T(8,128)S(1)} %get-tuple-element.38.refs_1_, f32[104,512]{1,0:T(8,128)S(1)} %collective-permute-done.6.refs_0_.refs_2_, ...), custom_call_target="tpu_custom_call" | custom-call | bytes 3000000 | tf_op jit(solution)/shard_map/pallas_call | solution.py:58
  35.4 0.6 %shard_map.107 = (f32[1520,640]{1,0:T(8,128)S(1)}, f32[1520,640]{1,0:T(8,128)S(1)}, f32[1520,640]{1,0:T(8,128)S(1)}) custom-call(f32[2,40,640]{2,1,0:T(8,128)S(1)} %collective-permute-done.9.refs_0_, f32[40,768]{1,0:T(8,128)S(1)} %collective-permute-done.10.refs_1_, ...), custom_call_target="tpu_custom_call", output_to_operand_aliasing={{0}: (2, {}), {1}: (3, {}), {2}: (4, {})} | custom-call | bytes 3000000 | tf_op jit(solution)/shard_map/pallas_call | solution.py:58
  36.0 2.7 %shard_map.108.refs_2_ = f32[1520,640]{1,0:T(8,128)S(1)} custom-call(f32[1520,640]{1,0:T(8,128)S(1)} %get-tuple-element.46.refs_0_, f32[1520,640]{1,0:T(8,128)S(1)} %get-tuple-element.47.refs_1_, f32[1520,640]{1,0:T(8,128)S(1)} %get-tuple-element.48.refs_2_), custom_call_target="tpu_custom_call" | custom-call | bytes 7500000 | tf_op jit(solution)/shard_map/pallas_call | solution.py:58
  39.0 1.6 %shard_map.110.refs_6_.refs_3_ = f32[1520,640]{1,0:T(8,128)S(1)} custom-call(f32[1520,640]{1,0:T(8,128)S(1)} %get-tuple-element.46.refs_0_, f32[1520,640]{1,0:T(8,128)S(1)} %get-tuple-element.47.refs_1_, f32[1520,640]{1,0:T(8,128)S(1)} %shard_map.108.refs_2_, bf16[8,32,1024]{2,1,0:T(8,128)(2,1)S(1)} %shard_map.109.refs_3_.refs_1_), custom_call_target="tpu_custom_call" | custom-call | bytes 4200000 | tf_op jit(solution)/shard_map/pallas_call | solution.py:58
  40.9 1.1 %shard_map.111 = (f32[32,512]{1,0:T(8,128)S(1)}, f32[32,512]{1,0:T(8,128)S(1)}) custom-call(s32[8]{0:T(128)S(4)} %shard_map.99.refs_2_.refs_0_, bf16[8,32,1024]{2,1,0:T(8,128)(2,1)S(1)} %shard_map.109.refs_3_.refs_1_, bf16[8,32,1024]{2,1,0:T(8,128)(2,1)S(1)} %collective-permute-done.11.refs_2_, bf16[1024,1024]{1,0:T(8,128)(2,1)S(1)} %get-tuple-element.36.refs_2_.refs_3_, ...), custom_call_target="tpu_custom_call" | custom-call | bytes 7500000 | tf_op jit(solution)/shard_map/pallas_call | solution.py:58
  42.0 0.5 %collective-permute-start.12 = (f32[32,512]{1,0:T(8,128)S(1)}, f32[32,512]{1,0:T(8,128)S(1)}, u32[]{:S(2)}, u32[]{:S(2)}) collective-permute-start(f32[32,512]{1,0:T(8,128)S(1)} %get-tuple-element.51.refs_5_), channel_id=1, source_target_pairs={{0,2},{2,0},{1,3},{3,1},{4,6},{6,4},{5,7},{7,5},{8,10},{10,8},{9,1... | collective-permute-start | bytes 196616 | tf_op jit(solution)/shard_map/ppermute | solution.py:737
  42.6 0.9 %shard_map.112.refs_2_ = f32[1520,640]{1,0:T(8,128)S(1)} custom-call(f32[1520,640]{1,0:T(8,128)S(1)} %get-tuple-element.46.refs_0_, f32[1520,640]{1,0:T(8,128)S(1)} %get-tuple-element.47.refs_1_, f32[1520,640]{1,0:T(8,128)S(1)} %shard_map.108.refs_2_, f32[1520,640]{1,0:T(8,128)S(1)} %shard_map.110.refs_6_.refs_3_, ...), custom_call_target="tpu_custom_call", output_to_operand_aliasing={{}: (3, {})} | custom-call | bytes 4200000 | tf_op jit(solution)/shard_map/pallas_call | solution.py:58
  43.5 2.0 %shard_map.113 = (f32[32,32,512]{2,1,0:T(8,128)}, f32[32,8,512]{2,1,0:T(8,128)S(1)}, f32[8,32,512]{2,1,0:T(8,128)S(1)}) custom-call(f32[1520,640]{1,0:T(8,128)S(1)} %get-tuple-element.46.refs_0_, f32[1520,640]{1,0:T(8,128)S(1)} %get-tuple-element.47.refs_1_, f32[1520,640]{1,0:T(8,128)S(1)} %shard_map.112.refs_2_), custom_call_target="tpu_custom_call" | custom-call | bytes 6000000 | tf_op jit(solution)/shard_map/pallas_call | solution.py:58
  45.5 0.8 %collective-permute-done.12.refs_1_ = f32[32,512]{1,0:T(8,128)S(1)} collective-permute-done((f32[32,512]{1,0:T(8,128)S(1)}, f32[32,512]{1,0:T(8,128)S(1)}, u32[]{:S(2)}, u32[]{:S(2)}) %collective-permute-start.12) | collective-permute-done | bytes 65568 | tf_op jit(solution)/shard_map/ppermute | solution.py:737
  46.3 1.2 %shard_map.114 = (f32[32,1,512]{2,1,0:T(1,128)}, f32[32,32,512]{2,1,0:T(8,128)}) custom-call(f32[32,512]{1,0:T(8,128)S(1)} %get-tuple-element.50.refs_4_.refs_0_, f32[32,512]{1,0:T(8,128)S(1)} %collective-permute-done.12.refs_1_, f32[32,512]{1,0:T(8,128)S(1)} %get-tuple-element.52.refs_2_, ...), custom_call_target="tpu_custom_call", output_to_operand_aliasing={{1}: (5, {})} | custom-call | bytes 3000000 | tf_op jit(solution)/shard_map/pallas_call | solution.py:58
  (22 shorter events, 1.2 us)
Async XLA Ops:
  2.5 8.3 %collective-permute-start = (f32[104,512]{1,0:T(8,128)S(1)}, f32[104,512]{1,0:T(8,128)S(1)}, u32[]{:S(2)}, u32[]{:S(2)}) collective-permute-start(f32[104,512]{1,0:T(8,128)S(1)} %get-tuple-element.30.refs_0_.refs_1_.refs_2_), channel_id=1, source_target_pairs={{0,2},{2,0},{1,3},{3,1},{4,6},{6,4},{5,7},{7,5},{8,10},{10,8},{9,1... | collective-permute-start | bytes 638984 | tf_op jit(solution)/shard_map/ppermute | solution.py:647
  5.6 11.0 %collective-permute-start.6 = (f32[104,512]{1,0:T(8,128)S(1)}, f32[104,512]{1,0:T(8,128)S(1)}, u32[]{:S(2)}, u32[]{:S(2)}) collective-permute-start(f32[104,512]{1,0:T(8,128)S(1)} %get-tuple-element.39), channel_id=1, source_target_pairs={{0,4},{4,0},{8,12},{12,8},{16,20},{20,16},{24,28},{28,24},{1,5},{5... | collective-permute-start | bytes 638984 | tf_op jit(solution)/shard_map/ppermute | solution.py:82
  7.0 9.5 %collective-permute-start.7 = (f32[104,512]{1,0:T(8,128)S(1)}, f32[104,512]{1,0:T(8,128)S(1)}, u32[]{:S(2)}, u32[]{:S(2)}) collective-permute-start(f32[104,512]{1,0:T(8,128)S(1)} %get-tuple-element.40), channel_id=1, source_target_pairs={{4,8},{12,16},{20,24},{8,4},{16,12},{24,20},{5,9},{13,17},{21,25},... | collective-permute-start | bytes 638984 | tf_op jit(solution)/shard_map/ppermute | solution.py:82
  11.2 5.7 %collective-permute-start.1 = (f32[8,1024]{1,0:T(8,128)S(1)}, f32[8,1024]{1,0:T(8,128)S(1)}, u32[]{:S(2)}, u32[]{:S(2)}) collective-permute-start(f32[8,1024]{1,0:T(8,128)S(1)} %get-tuple-element.34), channel_id=1, source_target_pairs={{0,4},{4,0},{8,12},{12,8},{16,20},{20,16},{24,28},{28,24},{1,5},{5... | collective-permute-start | bytes 98312 | tf_op jit(solution)/shard_map/ppermute | solution.py:82
  13.0 3.9 %collective-permute-start.2 = (f32[8,1024]{1,0:T(8,128)S(1)}, f32[8,1024]{1,0:T(8,128)S(1)}, u32[]{:S(2)}, u32[]{:S(2)}) collective-permute-start(f32[8,1024]{1,0:T(8,128)S(1)} %get-tuple-element.35), channel_id=1, source_target_pairs={{4,8},{12,16},{20,24},{8,4},{16,12},{24,20},{5,9},{13,17},{21,25},... | collective-permute-start | bytes 98312 | tf_op jit(solution)/shard_map/ppermute | solution.py:82
  15.3 10.3 %copy-start.3 = (s32[1,1,1,7]{3,2,1,0:T(1,128)S(1)}, s32[1,1,1,7]{3,2,1,0:T(1,128)}, u32[]{:S(2)}) copy-start(s32[1,1,1,7]{3,2,1,0:T(1,128)} %refs_1_.1) | copy-start | bytes 88
  15.4 13.8 %copy-start = (bf16[1,1,1,1024,1024]{4,3,2,1,0:T(8,128)(2,1)S(1)}, bf16[1,1,1,1024,1024]{4,3,2,1,0:T(8,128)(2,1)}, u32[]{:S(2)}) copy-start(bf16[1,1,1,1024,1024]{4,3,2,1,0:T(8,128)(2,1)} %param.13) | copy-start | bytes 6291460
  15.4 13.8 %copy-start.1 = (bf16[1,1,1,7,16,1024]{5,4,3,2,1,0:T(8,128)(2,1)S(1)}, bf16[1,1,1,7,16,1024]{5,4,3,2,1,0:T(8,128)(2,1)}, u32[]{:S(2)}) copy-start(bf16[1,1,1,7,16,1024]{5,4,3,2,1,0:T(8,128)(2,1)} %param.14) | copy-start | bytes 688132
  17.1 16.2 %collective-permute-start.8 = (f32[36,32,128]{2,1,0:T(8,128)S(1)}, f32[36,32,128]{2,1,0:T(8,128)S(1)}, u32[]{:S(2)}, u32[]{:S(2)}) collective-permute-start(f32[36,32,128]{2,1,0:T(8,128)S(1)} %shard_map.104), channel_id=1, source_target_pairs={{0,2},{2,0},{1,3},{3,1},{4,6},{6,4},{5,7},{7,5},{8,10},{10,8},{9,1... | collective-permute-start | bytes 1769480 | tf_op jit(solution)/shard_map/ppermute | solution.py:82
  18.6 8.8 %collective-permute-start.3 = (bf16[1,32,1024]{2,1,0:T(8,128)(2,1)S(1)}, bf16[1,32,1024]{2,1,0:T(8,128)(2,1)S(1)}, u32[]{:S(2)}, u32[]{:S(2)}) collective-permute-start(bf16[1,32,1024]{2,1,0:T(8,128)(2,1)S(1)} %shard_map.98.refs_2_.refs_0_), channel_id=1, source_target_pairs={{0,16},{4,20},{8,24},{12,28},{16,0},{20,4},{24,8},{28,12},{1,17},{... | collective-permute-start | bytes 196616 | tf_op jit(solution)/shard_map/ppermute | solution.py:674
  27.4 5.0 %collective-permute-start.4 = (bf16[2,32,1024]{2,1,0:T(8,128)(2,1)S(1)}, bf16[2,32,1024]{2,1,0:T(8,128)(2,1)S(1)}, u32[]{:S(2)}, u32[]{:S(2)}) collective-permute-start(bf16[2,32,1024]{2,1,0:T(8,128)(2,1)S(1)} %shard_map.100.refs_3_.refs_0_), channel_id=1, source_target_pairs={{0,8},{4,12},{8,0},{12,4},{16,24},{20,28},{24,16},{28,20},{1,9},{5... | collective-permute-start | bytes 393224 | tf_op jit(solution)/shard_map/ppermute | solution.py:674
  32.4 6.4 %collective-permute-start.5 = (bf16[4,32,1024]{2,1,0:T(8,128)(2,1)S(1)}, bf16[4,32,1024]{2,1,0:T(8,128)(2,1)S(1)}, u32[]{:S(2)}, u32[]{:S(2)}) collective-permute-start(bf16[4,32,1024]{2,1,0:T(8,128)(2,1)S(1)} %shard_map.102.refs_5_.refs_0_), channel_id=1, source_target_pairs={{0,4},{4,0},{8,12},{12,8},{16,20},{20,16},{24,28},{28,24},{1,5},{5... | collective-permute-start | bytes 786440 | tf_op jit(solution)/shard_map/ppermute | solution.py:674
  33.6 1.8 %collective-permute-start.9 = (f32[2,40,640]{2,1,0:T(8,128)S(1)}, f32[2,40,640]{2,1,0:T(8,128)S(1)}, u32[]{:S(2)}, u32[]{:S(2)}) collective-permute-start(f32[2,40,640]{2,1,0:T(8,128)S(1)} %get-tuple-element.41.refs_5_), channel_id=1, source_target_pairs={{0,1},{1,0},{2,3},{3,2},{4,5},{5,4},{6,7},{7,6},{8,9},{9,8},{10,11... | collective-permute-start | bytes 614408 | tf_op jit(solution)/shard_map/ppermute | solution.py:699
  33.7 1.7 %collective-permute-start.10 = (f32[40,768]{1,0:T(8,128)S(1)}, f32[40,768]{1,0:T(8,128)S(1)}, u32[]{:S(2)}, u32[]{:S(2)}) collective-permute-start(f32[40,768]{1,0:T(8,128)S(1)} %get-tuple-element.42.refs_6_), channel_id=1, source_target_pairs={{0,1},{1,0},{2,3},{3,2},{4,5},{5,4},{6,7},{7,6},{8,9},{9,8},{10,11... | collective-permute-start | bytes 368648 | tf_op jit(solution)/shard_map/ppermute | solution.py:699
  38.9 2.0 %copy-start.2 = (bf16[1,1,1,7,16,1024]{5,4,3,2,1,0:T(8,128)(2,1)S(1)}, bf16[1,1,1,7,16,1024]{5,4,3,2,1,0:T(8,128)(2,1)}, u32[]{:S(2)}) copy-start(bf16[1,1,1,7,16,1024]{5,4,3,2,1,0:T(8,128)(2,1)} %param.15) | copy-start | bytes 688132
  38.9 2.0 %collective-permute-start.11 = (bf16[8,32,1024]{2,1,0:T(8,128)(2,1)S(1)}, bf16[8,32,1024]{2,1,0:T(8,128)(2,1)S(1)}, u32[]{:S(2)}, u32[]{:S(2)}) collective-permute-start(bf16[8,32,1024]{2,1,0:T(8,128)(2,1)S(1)} %shard_map.109.refs_3_.refs_1_), channel_id=1, source_target_pairs={{0,1},{1,0},{2,3},{3,2},{4,5},{5,4},{6,7},{7,6},{8,9},{9,8},{10,11... | collective-permute-start | bytes 1572872 | tf_op jit(solution)/shard_map/ppermute | solution.py:723
  42.0 4.3 %collective-permute-start.12 = (f32[32,512]{1,0:T(8,128)S(1)}, f32[32,512]{1,0:T(8,128)S(1)}, u32[]{:S(2)}, u32[]{:S(2)}) collective-permute-start(f32[32,512]{1,0:T(8,128)S(1)} %get-tuple-element.51.refs_5_), channel_id=1, source_target_pairs={{0,2},{2,0},{1,3},{3,1},{4,6},{6,4},{5,7},{7,5},{8,10},{10,8},{9,1... | collective-permute-start | bytes 196616 | tf_op jit(solution)/shard_map/ppermute | solution.py:737
